TPU v7x, 32 devices: a whole 2x2x4 slice. The times are simulated.
32 devices in a mesh: row: 4 (over x, core), th: 2 (over y), ph: 4 (over z).
Axes of the slice: x: 2, y: 2, z: 4, core: 2. Of those that a mesh axis runs over, the one named last changes fastest.
Arguments:
- right_side: float32 [8, 16, 8, 256], P(None, 'ph', 'th', 'row'), may hold values from -14 to 14
- conduct: float32 [8, 16, 8, 256], P(None, 'ph', 'th', 'row'), may hold values from 0.05 to 0.3
- coupling: float32 [8, 8], replicated, may hold values from -0.6 to 0.6
- inverse: bfloat16 [16, 8, 16, 128, 128], P('ph', 'th', 'row'), may hold values from -0.45 to 1.45
- face_codes: int32 [2, 16, 8], P(None, 'ph', 'th'), may hold values from 0 to 2
Outputs:
- correction: float32 [8, 16, 8, 256], P(None, 'ph', 'th', 'row')
- residual: float32 [8, 16, 8, 256], P(None, 'ph', 'th', 'row')
Inputs may be any that keep to these rules, and one draw needn't show every extreme that they name: `face_codes`: 0 marks a fixed radial face, 1 an outflow face, 2 a reflecting face.
All inputs are finite; a program needn't handle non-finite values.
Results may differ from a plain program's by a relative error of at most 0.0095.
The roundings to bfloat16 on the way count: a program that leaves them out, or rounds other values in their place, can miss the bound.
Values sent between devices are 32-bit elements; how exact they have to be, the bound alone decides.
No kernel may reach another device: no remote copies, remote signals or barrier semaphores. Data moves between devices by JAX's collectives and lax.ppermute only.
A program may use at most 64 MiB of HBM per device.

v0:
```python
import jax
import jax.numpy as jnp
from jax import lax
from jax.sharding import PartitionSpec as P

VARS = 8
BLK = 16
S = 4


def with_halo(array, sides, width):
    for axis, dim in sides:
        count, length = (lax.axis_size(axis), array.shape[dim])
        up = [(i, (i + 1) % count) for i in range(count)]
        down = [(j, i) for i, j in up]
        last = lax.slice_in_dim(array, length - width, length, axis=dim)
        first = lax.slice_in_dim(array, 0, width, axis=dim)
        before = lax.ppermute(last, axis, up)
        after = lax.ppermute(first, axis, down)
        array = jnp.concatenate([before, array, after], axis=dim)
    return array


def face_factor(codes):
    return (codes == 1).astype(jnp.float32) - (codes == 2).astype(jnp.float32)


def operate(field, conduct, coupling, face_codes):
    padded = with_halo(field, (("row", 3), ("th", 2), ("ph", 1)), 1)
    azimuth_sum = padded[:, :-2, 1:-1, 1:-1] + padded[:, 2:, 1:-1, 1:-1]
    polar_low = padded[:, 1:-1, :-2, 1:-1]
    polar_high = padded[:, 1:-1, 2:, 1:-1]
    radial_low = padded[:, 1:-1, 1:-1, :-2]
    radial_high = padded[:, 1:-1, 1:-1, 2:]
    polar_pos = lax.broadcasted_iota(jnp.int32, field.shape, 2)
    radial_pos = lax.broadcasted_iota(jnp.int32, field.shape, 3)
    polar_start = lax.axis_index("th") == 0
    polar_end = lax.axis_index("th") == lax.axis_size("th") - 1
    radial_start = lax.axis_index("row") == 0
    radial_end = lax.axis_index("row") == lax.axis_size("row") - 1
    polar_low = jnp.where((polar_pos == 0) & polar_start, 0.0, polar_low)
    polar_high = jnp.where((polar_pos == field.shape[2] - 1) & polar_end, 0.0, polar_high)
    inner_ghost = face_factor(face_codes[0])[None, :, :, None] * field[..., :1]
    outer_ghost = face_factor(face_codes[1])[None, :, :, None] * field[..., -1:]
    radial_low = jnp.where((radial_pos == 0) & radial_start, inner_ghost, radial_low)
    radial_high = jnp.where(
        (radial_pos == field.shape[3] - 1) & radial_end, outer_ghost, radial_high
    )
    mixed = jnp.einsum("kj,jpqr->kpqr", coupling, field, precision=lax.Precision.HIGHEST)
    neighbours = radial_low + radial_high + polar_low + polar_high + azimuth_sum
    return field + mixed + conduct * (6.0 * field - neighbours)


def precondition(field, inverse):
    ph_cells = field.shape[1]
    th_cells = field.shape[2]
    nblocks = field.shape[3] // BLK
    rounded = field.astype(jnp.bfloat16)
    blocked = (
        rounded.reshape(VARS, ph_cells, th_cells, nblocks, BLK)
        .transpose(1, 2, 3, 0, 4)
        .reshape(ph_cells, th_cells, nblocks, VARS * BLK)
    )
    result = jnp.einsum("pqbij,pqbj->pqbi", inverse, blocked, preferred_element_type=jnp.float32)
    return (
        result.reshape(ph_cells, th_cells, nblocks, VARS, BLK)
        .transpose(3, 0, 1, 2, 4)
        .reshape(field.shape)
    )


def solve_small(upper_factor):
    matrix = upper_factor[:, :S] + upper_factor[:, 1:]
    target = upper_factor[:, 0]
    normal = jnp.dot(matrix.T, matrix, precision=lax.Precision.HIGHEST)
    moment = jnp.dot(matrix.T, target, precision=lax.Precision.HIGHEST)
    lower = jnp.linalg.cholesky(normal)
    forward = []
    for target_row in range(S):
        summed = moment[target_row]
        for source_row in range(target_row):
            summed = summed - lower[target_row, source_row] * forward[source_row]
        forward.append(summed / lower[target_row, target_row])
    backward = [None] * S
    for target_row in reversed(range(S)):
        summed = forward[target_row]
        for source_row in range(target_row + 1, S):
            summed = summed - lower[source_row, target_row] * backward[source_row]
        backward[target_row] = summed / lower[target_row, target_row]
    return backward


def local(right_side, conduct, coupling, inverse, face_codes):
    correction = jnp.zeros_like(right_side)
    residual = right_side
    krylov = [residual]
    directions = []
    for column in range(S):
        smoothed = precondition(krylov[column], inverse)
        directions.append(smoothed)
        krylov.append(operate(smoothed, conduct, coupling, face_codes) - krylov[column])
    flat = jnp.stack(krylov).reshape(S + 1, -1)
    local_products = jnp.dot(flat, flat.T, precision=lax.Precision.HIGHEST)
    products = lax.psum(local_products, ("row", "th", "ph"))
    upper_factor = jnp.linalg.cholesky(products).T
    weights = solve_small(upper_factor)
    residual = krylov[0]
    for column in range(S):
        correction = correction + weights[column] * directions[column]
        residual = residual - weights[column] * (krylov[column + 1] + krylov[column])
    return (correction, residual)


def solution(mesh):
    placed = (
        P(None, "ph", "th", "row"),
        P(None, "ph", "th", "row"),
        P(),
        P("ph", "th", "row", None, None),
        P(None, "ph", "th"),
    )
    return jax.shard_map(
        local,
        mesh=mesh,
        in_specs=placed,
        out_specs=(P(None, "ph", "th", "row"), P(None, "ph", "th", "row")),
        check_vma=False,
    )
```

profile of v0, /device:TPU:0, one launch (start us, length us, event | category | flops | bytes accessed | tf_op | source)
XLA Modules:
  0.0 136.0 jit_solution(337439843982767926)
XLA Ops:
  0.6 0.9 subtract_bitcast_fusion
  1.5 0.9 convert_element_type.56
  2.7 1.2 fusion.68
  4.3 0.2 multiply_reduce_fusion.7
  4.5 0.5 collective-permute-start
  5.1 2.0 %collective-permute-start.1 = (f32[8,4,4,1]{3,0,2,1:T(8,128)S(1)}, f32[8,4,4,1]{3,0,2,1:T(8,128)S(1)}, u32[]{:S(2)}, u32[]{:S(2)}) collective-permute-start(f32[8,4,4,1]{3,0,2,1:T(8,128)S(1)} %get-tuple-element.37), channel_id=1, source_target_pairs={{8,0},{16,8},{24,16},{0,24},{9,1},{17,9},{25,17},{1,25},{10,2},{18... | collective-permute-start | bytes 1544 | tf_op jit(solution)/shard_map/ppermute | solution.py:19
  7.1 1.8 %collective-permute-done = f32[8,4,4,1]{3,0,2,1:T(8,128)S(1)} collective-permute-done((f32[8,4,4,1]{3,0,2,1:T(8,128)S(1)}, f32[8,4,4,1]{3,0,2,1:T(8,128)S(1)}, u32[]{:S(2)}, u32[]{:S(2)}) %collective-permute-start) | collective-permute-done | bytes 544 | tf_op jit(solution)/shard_map/ppermute | solution.py:18
  8.9 0.5 collective-permute-done.1
  9.5 1.9 %collective-permute-start.2 = (f32[8,4,1,66]{3,0,2,1:T(8,128)S(1)}, f32[8,4,1,66]{3,0,2,1:T(8,128)S(1)}, u32[]{:S(2)}, u32[]{:S(2)}) collective-permute-start(f32[8,4,1,66]{3,0,2,1:T(8,128)S(1)} %get-tuple-element.28), channel_id=1, source_target_pairs={{0,4},{4,0},{1,5},{5,1},{2,6},{6,2},{3,7},{7,3},{8,12},{12,8},{9,1... | collective-permute-start | bytes 25352 | tf_op jit(solution)/shard_map/ppermute | solution.py:18
  11.6 1.7 %collective-permute-done.2 = f32[8,4,1,66]{3,0,2,1:T(8,128)S(1)} collective-permute-done((f32[8,4,1,66]{3,0,2,1:T(8,128)S(1)}, f32[8,4,1,66]{3,0,2,1:T(8,128)S(1)}, u32[]{:S(2)}, u32[]{:S(2)}) %collective-permute-start.2) | collective-permute-done | bytes 8480 | tf_op jit(solution)/shard_map/ppermute | solution.py:18
  13.3 1.8 %collective-permute-done.3 = f32[8,4,1,66]{3,0,2,1:T(8,128)S(1)} collective-permute-done((f32[8,4,1,66]{3,0,2,1:T(8,128)S(1)}, f32[8,4,1,66]{3,0,2,1:T(8,128)S(1)}, u32[]{:S(2)}, u32[]{:S(2)}) %collective-permute-start.3) | collective-permute-done | bytes 8480 | tf_op jit(solution)/shard_map/ppermute | solution.py:19
  15.2 1.6 %collective-permute-start.4 = (f32[8,1,6,66]{3,0,2,1:T(8,128)S(1)}, f32[8,1,6,66]{3,0,2,1:T(8,128)S(1)}, u32[]{:S(2)}, u32[]{:S(2)}) collective-permute-start(f32[8,1,6,66]{3,0,2,1:T(8,128)S(1)} %get-tuple-element.20), channel_id=1, source_target_pairs={{0,1},{1,2},{2,3},{3,0},{4,5},{5,6},{6,7},{7,4},{8,9},{9,10},{10,1... | collective-permute-start | bytes 38024 | tf_op jit(solution)/shard_map/ppermute | solution.py:18
  16.9 2.2 %collective-permute-start.5 = (f32[8,1,6,66]{3,0,2,1:T(8,128)S(1)}, f32[8,1,6,66]{3,0,2,1:T(8,128)S(1)}, u32[]{:S(2)}, u32[]{:S(2)}) collective-permute-start(f32[8,1,6,66]{3,0,2,1:T(8,128)S(1)} %get-tuple-element.21), channel_id=1, source_target_pairs={{1,0},{2,1},{3,2},{0,3},{5,4},{6,5},{7,6},{4,7},{9,8},{10,9},{11,1... | collective-permute-start | bytes 38024 | tf_op jit(solution)/shard_map/ppermute | solution.py:19
  19.1 1.8 %collective-permute-done.4 = f32[8,1,6,66]{3,0,2,1:T(8,128)S(1)} collective-permute-done((f32[8,1,6,66]{3,0,2,1:T(8,128)S(1)}, f32[8,1,6,66]{3,0,2,1:T(8,128)S(1)}, u32[]{:S(2)}, u32[]{:S(2)}) %collective-permute-start.4) | collective-permute-done | bytes 12704 | tf_op jit(solution)/shard_map/ppermute | solution.py:18
  21.0 0.3 bitcast_dynamic-update-slice_fusion.3
  21.6 1.2 fusion.69
  23.2 0.2 multiply_reduce_fusion.5
  23.5 1.7 %collective-permute-start.7 = (f32[8,4,4,1]{3,0,2,1:T(8,128)S(1)}, f32[8,4,4,1]{3,0,2,1:T(8,128)S(1)}, u32[]{:S(2)}, u32[]{:S(2)}) collective-permute-start(f32[8,4,4,1]{3,0,2,1:T(8,128)S(1)} %get-tuple-element.35), channel_id=1, source_target_pairs={{8,0},{16,8},{24,16},{0,24},{9,1},{17,9},{25,17},{1,25},{10,2},{18... | collective-permute-start | bytes 1544 | tf_op jit(solution)/shard_map/ppermute | solution.py:19
  25.2 1.9 %collective-permute-done.6 = f32[8,4,4,1]{3,0,2,1:T(8,128)S(1)} collective-permute-done((f32[8,4,4,1]{3,0,2,1:T(8,128)S(1)}, f32[8,4,4,1]{3,0,2,1:T(8,128)S(1)}, u32[]{:S(2)}, u32[]{:S(2)}) %collective-permute-start.6) | collective-permute-done | bytes 544 | tf_op jit(solution)/shard_map/ppermute | solution.py:18
  27.2 0.9 collective-permute-start.8
  28.1 1.2 collective-permute-start.9
  29.3 1.7 %collective-permute-done.8 = f32[8,4,1,66]{3,0,2,1:T(8,128)S(1)} collective-permute-done((f32[8,4,1,66]{3,0,2,1:T(8,128)S(1)}, f32[8,4,1,66]{3,0,2,1:T(8,128)S(1)}, u32[]{:S(2)}, u32[]{:S(2)}) %collective-permute-start.8) | collective-permute-done | bytes 8480 | tf_op jit(solution)/shard_map/ppermute | solution.py:18
  31.0 0.8 collective-permute-done.9
  32.0 1.2 collective-permute-start.10
  33.1 2.7 %collective-permute-start.11 = (f32[8,1,6,66]{3,0,2,1:T(8,128)S(1)}, f32[8,1,6,66]{3,0,2,1:T(8,128)S(1)}, u32[]{:S(2)}, u32[]{:S(2)}) collective-permute-start(f32[8,1,6,66]{3,0,2,1:T(8,128)S(1)} %get-tuple-element.19), channel_id=1, source_target_pairs={{1,0},{2,1},{3,2},{0,3},{5,4},{6,5},{7,6},{4,7},{9,8},{10,9},{11,1... | collective-permute-start | bytes 38024 | tf_op jit(solution)/shard_map/ppermute | solution.py:19
  35.9 1.8 %collective-permute-done.10 = f32[8,1,6,66]{3,0,2,1:T(8,128)S(1)} collective-permute-done((f32[8,1,6,66]{3,0,2,1:T(8,128)S(1)}, f32[8,1,6,66]{3,0,2,1:T(8,128)S(1)}, u32[]{:S(2)}, u32[]{:S(2)}) %collective-permute-start.10) | collective-permute-done | bytes 12704 | tf_op jit(solution)/shard_map/ppermute | solution.py:18
  37.7 0.3 bitcast_dynamic-update-slice_fusion.2
  38.3 1.2 fusion.70
  39.9 0.2 multiply_reduce_fusion.3
  40.1 1.7 %collective-permute-start.13 = (f32[8,4,4,1]{3,0,2,1:T(8,128)S(1)}, f32[8,4,4,1]{3,0,2,1:T(8,128)S(1)}, u32[]{:S(2)}, u32[]{:S(2)}) collective-permute-start(f32[8,4,4,1]{3,0,2,1:T(8,128)S(1)} %get-tuple-element.33), channel_id=1, source_target_pairs={{8,0},{16,8},{24,16},{0,24},{9,1},{17,9},{25,17},{1,25},{10,2},{18... | collective-permute-start | bytes 1544 | tf_op jit(solution)/shard_map/ppermute | solution.py:19
  41.9 1.9 %collective-permute-done.12 = f32[8,4,4,1]{3,0,2,1:T(8,128)S(1)} collective-permute-done((f32[8,4,4,1]{3,0,2,1:T(8,128)S(1)}, f32[8,4,4,1]{3,0,2,1:T(8,128)S(1)}, u32[]{:S(2)}, u32[]{:S(2)}) %collective-permute-start.12) | collective-permute-done | bytes 544 | tf_op jit(solution)/shard_map/ppermute | solution.py:18
  43.8 0.5 collective-permute-done.13
  44.5 0.7 collective-permute-start.14
  45.2 1.4 %collective-permute-start.15 = (f32[8,4,1,66]{3,0,2,1:T(8,128)S(1)}, f32[8,4,1,66]{3,0,2,1:T(8,128)S(1)}, u32[]{:S(2)}, u32[]{:S(2)}) collective-permute-start(f32[8,4,1,66]{3,0,2,1:T(8,128)S(1)} %get-tuple-element.25), channel_id=1, source_target_pairs={{4,0},{0,4},{5,1},{1,5},{6,2},{2,6},{7,3},{3,7},{12,8},{8,12},{13,... | collective-permute-start | bytes 25352 | tf_op jit(solution)/shard_map/ppermute | solution.py:19
  46.5 1.7 %collective-permute-done.14 = f32[8,4,1,66]{3,0,2,1:T(8,128)S(1)} collective-permute-done((f32[8,4,1,66]{3,0,2,1:T(8,128)S(1)}, f32[8,4,1,66]{3,0,2,1:T(8,128)S(1)}, u32[]{:S(2)}, u32[]{:S(2)}) %collective-permute-start.14) | collective-permute-done | bytes 8480 | tf_op jit(solution)/shard_map/ppermute | solution.py:18
  48.3 0.6 collective-permute-done.15
  49.0 1.1 collective-permute-start.16
  50.1 2.8 %collective-permute-start.17 = (f32[8,1,6,66]{3,0,2,1:T(8,128)S(1)}, f32[8,1,6,66]{3,0,2,1:T(8,128)S(1)}, u32[]{:S(2)}, u32[]{:S(2)}) collective-permute-start(f32[8,1,6,66]{3,0,2,1:T(8,128)S(1)} %get-tuple-element.17), channel_id=1, source_target_pairs={{1,0},{2,1},{3,2},{0,3},{5,4},{6,5},{7,6},{4,7},{9,8},{10,9},{11,1... | collective-permute-start | bytes 38024 | tf_op jit(solution)/shard_map/ppermute | solution.py:19
  52.9 1.9 %collective-permute-done.16 = f32[8,1,6,66]{3,0,2,1:T(8,128)S(1)} collective-permute-done((f32[8,1,6,66]{3,0,2,1:T(8,128)S(1)}, f32[8,1,6,66]{3,0,2,1:T(8,128)S(1)}, u32[]{:S(2)}, u32[]{:S(2)}) %collective-permute-start.16) | collective-permute-done | bytes 12704 | tf_op jit(solution)/shard_map/ppermute | solution.py:18
  54.8 0.3 bitcast_dynamic-update-slice_fusion.1
  55.4 1.2 fusion.71
  57.0 0.2 multiply_reduce_fusion.1
  57.3 1.7 %collective-permute-start.19 = (f32[8,4,4,1]{3,0,2,1:T(8,128)S(1)}, f32[8,4,4,1]{3,0,2,1:T(8,128)S(1)}, u32[]{:S(2)}, u32[]{:S(2)}) collective-permute-start(f32[8,4,4,1]{3,0,2,1:T(8,128)S(1)} %get-tuple-element.31), channel_id=1, source_target_pairs={{8,0},{16,8},{24,16},{0,24},{9,1},{17,9},{25,17},{1,25},{10,2},{18... | collective-permute-start | bytes 1544 | tf_op jit(solution)/shard_map/ppermute | solution.py:19
  59.0 1.9 %collective-permute-done.18 = f32[8,4,4,1]{3,0,2,1:T(8,128)S(1)} collective-permute-done((f32[8,4,4,1]{3,0,2,1:T(8,128)S(1)}, f32[8,4,4,1]{3,0,2,1:T(8,128)S(1)}, u32[]{:S(2)}, u32[]{:S(2)}) %collective-permute-start.18) | collective-permute-done | bytes 544 | tf_op jit(solution)/shard_map/ppermute | solution.py:18
  61.2 1.8 %collective-permute-start.20 = (f32[8,4,1,66]{3,0,2,1:T(8,128)S(1)}, f32[8,4,1,66]{3,0,2,1:T(8,128)S(1)}, u32[]{:S(2)}, u32[]{:S(2)}) collective-permute-start(f32[8,4,1,66]{3,0,2,1:T(8,128)S(1)} %get-tuple-element.22), channel_id=1, source_target_pairs={{0,4},{4,0},{1,5},{5,1},{2,6},{6,2},{3,7},{7,3},{8,12},{12,8},{9,1... | collective-permute-start | bytes 25352 | tf_op jit(solution)/shard_map/ppermute | solution.py:18
  63.0 0.3 collective-permute-start.21
  63.3 1.7 %collective-permute-done.20 = f32[8,4,1,66]{3,0,2,1:T(8,128)S(1)} collective-permute-done((f32[8,4,1,66]{3,0,2,1:T(8,128)S(1)}, f32[8,4,1,66]{3,0,2,1:T(8,128)S(1)}, u32[]{:S(2)}, u32[]{:S(2)}) %collective-permute-start.20) | collective-permute-done | bytes 8480 | tf_op jit(solution)/shard_map/ppermute | solution.py:18
  65.0 1.7 %collective-permute-done.21 = f32[8,4,1,66]{3,0,2,1:T(8,128)S(1)} collective-permute-done((f32[8,4,1,66]{3,0,2,1:T(8,128)S(1)}, f32[8,4,1,66]{3,0,2,1:T(8,128)S(1)}, u32[]{:S(2)}, u32[]{:S(2)}) %collective-permute-start.21) | collective-permute-done | bytes 8480 | tf_op jit(solution)/shard_map/ppermute | solution.py:19
  66.8 1.0 collective-permute-start.22
  67.8 2.9 %collective-permute-start.23 = (f32[8,1,6,66]{3,0,2,1:T(8,128)S(1)}, f32[8,1,6,66]{3,0,2,1:T(8,128)S(1)}, u32[]{:S(2)}, u32[]{:S(2)}) collective-permute-start(f32[8,1,6,66]{3,0,2,1:T(8,128)S(1)} %get-tuple-element.15), channel_id=1, source_target_pairs={{1,0},{2,1},{3,2},{0,3},{5,4},{6,5},{7,6},{4,7},{9,8},{10,9},{11,1... | collective-permute-start | bytes 38024 | tf_op jit(solution)/shard_map/ppermute | solution.py:19
  70.7 2.0 %collective-permute-done.22 = f32[8,1,6,66]{3,0,2,1:T(8,128)S(1)} collective-permute-done((f32[8,1,6,66]{3,0,2,1:T(8,128)S(1)}, f32[8,1,6,66]{3,0,2,1:T(8,128)S(1)}, u32[]{:S(2)}, u32[]{:S(2)}) %collective-permute-start.22) | collective-permute-done | bytes 12704 | tf_op jit(solution)/shard_map/ppermute | solution.py:18
  72.7 0.3 bitcast_dynamic-update-slice_fusion
  73.0 1.2 convolution_bitcast_fusion.4
  74.3 39.9 %psum.7 = f32[5,5]{0,1:T(8,128)S(1)} all-reduce(f32[5,5]{0,1:T(8,128)S(1)} %convolution_bitcast_fusion.4), channel_id=1, replica_groups=mesh['row'=4,'th'=2,'ph'=4] {'row','th','ph'}, use_global_device_ids=true, to_apply=%region_0.1 | all-reduce | flops 25 | bytes 200 | tf_op jit(solution)/shard_map/psum | solution.py:104
  114.3 0.4 cholesky.34
  114.8 0.6 compare_reduce_fusion.1
  115.4 0.6 select_bitcast_fusion
  116.3 0.6 fusion.67
  117.1 0.4 cholesky.67
  117.5 0.7 compare_reduce_fusion
  118.1 0.6 select_select_fusion
  118.8 0.7 fusion.66
  134.8 0.6 copy.43
  135.4 0.6 copy.44
  (66 shorter events, 4.5 us)
Async XLA Ops:
  0.6 2.1 %copy-start = (bf16[4,4,4,128,128]{4,3,2,1,0:T(8,128)(2,1)S(1)}, bf16[4,4,4,128,128]{4,3,2,1,0:T(8,128)(2,1)}, u32[]{:S(2)}) copy-start(bf16[4,4,4,128,128]{4,3,2,1,0:T(8,128)(2,1)} %param.8) | copy-start | bytes 6291460
  2.4 4.7 %copy-start.1 = (f32[8,4,4,64]{3,2,1,0:T(4,128)S(1)}, f32[8,4,4,64]{3,2,1,0:T(4,128)}, u32[]{:S(2)}) copy-start(f32[8,4,4,64]{3,2,1,0:T(4,128)} %param.5) | copy-start | bytes 98308
  2.7 18.2 %copy-start.2 = (f32[8,4,4,64]{3,2,1,0:T(4,128)S(1)}, f32[8,4,4,64]{3,2,1,0:T(4,128)}, u32[]{:S(2)}) copy-start(f32[8,4,4,64]{3,2,1,0:T(4,128)} %param.6) | copy-start | bytes 98308
  2.7 18.2 %copy-start.3 = (f32[8,8]{1,0:T(8,128)S(1)}, f32[8,8]{1,0:T(8,128)}, u32[]{:S(2)}) copy-start(f32[8,8]{1,0:T(8,128)} %param.7) | copy-start | bytes 772
  4.5 4.4 %collective-permute-start = (f32[8,4,4,1]{3,0,2,1:T(8,128)S(1)}, f32[8,4,4,1]{3,0,2,1:T(8,128)S(1)}, u32[]{:S(2)}, u32[]{:S(2)}) collective-permute-start(f32[8,4,4,1]{3,0,2,1:T(8,128)S(1)} %get-tuple-element.36), channel_id=1, source_target_pairs={{0,8},{8,16},{16,24},{24,0},{1,9},{9,17},{17,25},{25,1},{2,10},{10... | collective-permute-start | bytes 1544 | tf_op jit(solution)/shard_map/ppermute | solution.py:18
  5.1 4.4 %collective-permute-start.1 = (f32[8,4,4,1]{3,0,2,1:T(8,128)S(1)}, f32[8,4,4,1]{3,0,2,1:T(8,128)S(1)}, u32[]{:S(2)}, u32[]{:S(2)}) collective-permute-start(f32[8,4,4,1]{3,0,2,1:T(8,128)S(1)} %get-tuple-element.37), channel_id=1, source_target_pairs={{8,0},{16,8},{24,16},{0,24},{9,1},{17,9},{25,17},{1,25},{10,2},{18... | collective-permute-start | bytes 1544 | tf_op jit(solution)/shard_map/ppermute | solution.py:19
  9.5 3.8 %collective-permute-start.2 = (f32[8,4,1,66]{3,0,2,1:T(8,128)S(1)}, f32[8,4,1,66]{3,0,2,1:T(8,128)S(1)}, u32[]{:S(2)}, u32[]{:S(2)}) collective-permute-start(f32[8,4,1,66]{3,0,2,1:T(8,128)S(1)} %get-tuple-element.28), channel_id=1, source_target_pairs={{0,4},{4,0},{1,5},{5,1},{2,6},{6,2},{3,7},{7,3},{8,12},{12,8},{9,1... | collective-permute-start | bytes 25352 | tf_op jit(solution)/shard_map/ppermute | solution.py:18
  11.4 3.7 %collective-permute-start.3 = (f32[8,4,1,66]{3,0,2,1:T(8,128)S(1)}, f32[8,4,1,66]{3,0,2,1:T(8,128)S(1)}, u32[]{:S(2)}, u32[]{:S(2)}) collective-permute-start(f32[8,4,1,66]{3,0,2,1:T(8,128)S(1)} %get-tuple-element.29), channel_id=1, source_target_pairs={{4,0},{0,4},{5,1},{1,5},{6,2},{2,6},{7,3},{3,7},{12,8},{8,12},{13,... | collective-permute-start | bytes 25352 | tf_op jit(solution)/shard_map/ppermute | solution.py:19
  15.2 5.7 %collective-permute-start.4 = (f32[8,1,6,66]{3,0,2,1:T(8,128)S(1)}, f32[8,1,6,66]{3,0,2,1:T(8,128)S(1)}, u32[]{:S(2)}, u32[]{:S(2)}) collective-permute-start(f32[8,1,6,66]{3,0,2,1:T(8,128)S(1)} %get-tuple-element.20), channel_id=1, source_target_pairs={{0,1},{1,2},{2,3},{3,0},{4,5},{5,6},{6,7},{7,4},{8,9},{9,10},{10,1... | collective-permute-start | bytes 38024 | tf_op jit(solution)/shard_map/ppermute | solution.py:18
  16.9 4.1 %collective-permute-start.5 = (f32[8,1,6,66]{3,0,2,1:T(8,128)S(1)}, f32[8,1,6,66]{3,0,2,1:T(8,128)S(1)}, u32[]{:S(2)}, u32[]{:S(2)}) collective-permute-start(f32[8,1,6,66]{3,0,2,1:T(8,128)S(1)} %get-tuple-element.21), channel_id=1, source_target_pairs={{1,0},{2,1},{3,2},{0,3},{5,4},{6,5},{7,6},{4,7},{9,8},{10,9},{11,1... | collective-permute-start | bytes 38024 | tf_op jit(solution)/shard_map/ppermute | solution.py:19
  23.4 3.7 %collective-permute-start.6 = (f32[8,4,4,1]{3,0,2,1:T(8,128)S(1)}, f32[8,4,4,1]{3,0,2,1:T(8,128)S(1)}, u32[]{:S(2)}, u32[]{:S(2)}) collective-permute-start(f32[8,4,4,1]{3,0,2,1:T(8,128)S(1)} %get-tuple-element.34), channel_id=1, source_target_pairs={{0,8},{8,16},{16,24},{24,0},{1,9},{9,17},{17,25},{25,1},{2,10},{10... | collective-permute-start | bytes 1544 | tf_op jit(solution)/shard_map/ppermute | solution.py:18
  23.5 3.7 %collective-permute-start.7 = (f32[8,4,4,1]{3,0,2,1:T(8,128)S(1)}, f32[8,4,4,1]{3,0,2,1:T(8,128)S(1)}, u32[]{:S(2)}, u32[]{:S(2)}) collective-permute-start(f32[8,4,4,1]{3,0,2,1:T(8,128)S(1)} %get-tuple-element.35), channel_id=1, source_target_pairs={{8,0},{16,8},{24,16},{0,24},{9,1},{17,9},{25,17},{1,25},{10,2},{18... | collective-permute-start | bytes 1544 | tf_op jit(solution)/shard_map/ppermute | solution.py:19
  27.2 3.8 %collective-permute-start.8 = (f32[8,4,1,66]{3,0,2,1:T(8,128)S(1)}, f32[8,4,1,66]{3,0,2,1:T(8,128)S(1)}, u32[]{:S(2)}, u32[]{:S(2)}) collective-permute-start(f32[8,4,1,66]{3,0,2,1:T(8,128)S(1)} %get-tuple-element.26), channel_id=1, source_target_pairs={{0,4},{4,0},{1,5},{5,1},{2,6},{6,2},{3,7},{7,3},{8,12},{12,8},{9,1... | collective-permute-start | bytes 25352 | tf_op jit(solution)/shard_map/ppermute | solution.py:18
  28.1 3.8 %collective-permute-start.9 = (f32[8,4,1,66]{3,0,2,1:T(8,128)S(1)}, f32[8,4,1,66]{3,0,2,1:T(8,128)S(1)}, u32[]{:S(2)}, u32[]{:S(2)}) collective-permute-start(f32[8,4,1,66]{3,0,2,1:T(8,128)S(1)} %get-tuple-element.27), channel_id=1, source_target_pairs={{4,0},{0,4},{5,1},{1,5},{6,2},{2,6},{7,3},{3,7},{12,8},{8,12},{13,... | collective-permute-start | bytes 25352 | tf_op jit(solution)/shard_map/ppermute | solution.py:19
  32.0 5.7 %collective-permute-start.10 = (f32[8,1,6,66]{3,0,2,1:T(8,128)S(1)}, f32[8,1,6,66]{3,0,2,1:T(8,128)S(1)}, u32[]{:S(2)}, u32[]{:S(2)}) collective-permute-start(f32[8,1,6,66]{3,0,2,1:T(8,128)S(1)} %get-tuple-element.18), channel_id=1, source_target_pairs={{0,1},{1,2},{2,3},{3,0},{4,5},{5,6},{6,7},{7,4},{8,9},{9,10},{10,1... | collective-permute-start | bytes 38024 | tf_op jit(solution)/shard_map/ppermute | solution.py:18
  33.1 4.5 %collective-permute-start.11 = (f32[8,1,6,66]{3,0,2,1:T(8,128)S(1)}, f32[8,1,6,66]{3,0,2,1:T(8,128)S(1)}, u32[]{:S(2)}, u32[]{:S(2)}) collective-permute-start(f32[8,1,6,66]{3,0,2,1:T(8,128)S(1)} %get-tuple-element.19), channel_id=1, source_target_pairs={{1,0},{2,1},{3,2},{0,3},{5,4},{6,5},{7,6},{4,7},{9,8},{10,9},{11,1... | collective-permute-start | bytes 38024 | tf_op jit(solution)/shard_map/ppermute | solution.py:19
  40.1 3.7 %collective-permute-start.12 = (f32[8,4,4,1]{3,0,2,1:T(8,128)S(1)}, f32[8,4,4,1]{3,0,2,1:T(8,128)S(1)}, u32[]{:S(2)}, u32[]{:S(2)}) collective-permute-start(f32[8,4,4,1]{3,0,2,1:T(8,128)S(1)} %get-tuple-element.32), channel_id=1, source_target_pairs={{0,8},{8,16},{16,24},{24,0},{1,9},{9,17},{17,25},{25,1},{2,10},{10... | collective-permute-start | bytes 1544 | tf_op jit(solution)/shard_map/ppermute | solution.py:18
  40.1 4.2 %collective-permute-start.13 = (f32[8,4,4,1]{3,0,2,1:T(8,128)S(1)}, f32[8,4,4,1]{3,0,2,1:T(8,128)S(1)}, u32[]{:S(2)}, u32[]{:S(2)}) collective-permute-start(f32[8,4,4,1]{3,0,2,1:T(8,128)S(1)} %get-tuple-element.33), channel_id=1, source_target_pairs={{8,0},{16,8},{24,16},{0,24},{9,1},{17,9},{25,17},{1,25},{10,2},{18... | collective-permute-start | bytes 1544 | tf_op jit(solution)/shard_map/ppermute | solution.py:19
  44.5 3.8 %collective-permute-start.14 = (f32[8,4,1,66]{3,0,2,1:T(8,128)S(1)}, f32[8,4,1,66]{3,0,2,1:T(8,128)S(1)}, u32[]{:S(2)}, u32[]{:S(2)}) collective-permute-start(f32[8,4,1,66]{3,0,2,1:T(8,128)S(1)} %get-tuple-element.24), channel_id=1, source_target_pairs={{0,4},{4,0},{1,5},{5,1},{2,6},{6,2},{3,7},{7,3},{8,12},{12,8},{9,1... | collective-permute-start | bytes 25352 | tf_op jit(solution)/shard_map/ppermute | solution.py:18
  45.2 3.7 %collective-permute-start.15 = (f32[8,4,1,66]{3,0,2,1:T(8,128)S(1)}, f32[8,4,1,66]{3,0,2,1:T(8,128)S(1)}, u32[]{:S(2)}, u32[]{:S(2)}) collective-permute-start(f32[8,4,1,66]{3,0,2,1:T(8,128)S(1)} %get-tuple-element.25), channel_id=1, source_target_pairs={{4,0},{0,4},{5,1},{1,5},{6,2},{2,6},{7,3},{3,7},{12,8},{8,12},{13,... | collective-permute-start | bytes 25352 | tf_op jit(solution)/shard_map/ppermute | solution.py:19
  49.0 5.8 %collective-permute-start.16 = (f32[8,1,6,66]{3,0,2,1:T(8,128)S(1)}, f32[8,1,6,66]{3,0,2,1:T(8,128)S(1)}, u32[]{:S(2)}, u32[]{:S(2)}) collective-permute-start(f32[8,1,6,66]{3,0,2,1:T(8,128)S(1)} %get-tuple-element.16), channel_id=1, source_target_pairs={{0,1},{1,2},{2,3},{3,0},{4,5},{5,6},{6,7},{7,4},{8,9},{9,10},{10,1... | collective-permute-start | bytes 38024 | tf_op jit(solution)/shard_map/ppermute | solution.py:18
  50.1 4.7 %collective-permute-start.17 = (f32[8,1,6,66]{3,0,2,1:T(8,128)S(1)}, f32[8,1,6,66]{3,0,2,1:T(8,128)S(1)}, u32[]{:S(2)}, u32[]{:S(2)}) collective-permute-start(f32[8,1,6,66]{3,0,2,1:T(8,128)S(1)} %get-tuple-element.17), channel_id=1, source_target_pairs={{1,0},{2,1},{3,2},{0,3},{5,4},{6,5},{7,6},{4,7},{9,8},{10,9},{11,1... | collective-permute-start | bytes 38024 | tf_op jit(solution)/shard_map/ppermute | solution.py:19
  57.2 3.7 %collective-permute-start.18 = (f32[8,4,4,1]{3,0,2,1:T(8,128)S(1)}, f32[8,4,4,1]{3,0,2,1:T(8,128)S(1)}, u32[]{:S(2)}, u32[]{:S(2)}) collective-permute-start(f32[8,4,4,1]{3,0,2,1:T(8,128)S(1)} %get-tuple-element.30), channel_id=1, source_target_pairs={{0,8},{8,16},{16,24},{24,0},{1,9},{9,17},{17,25},{25,1},{2,10},{10... | collective-permute-start | bytes 1544 | tf_op jit(solution)/shard_map/ppermute | solution.py:18
  57.3 3.8 %collective-permute-start.19 = (f32[8,4,4,1]{3,0,2,1:T(8,128)S(1)}, f32[8,4,4,1]{3,0,2,1:T(8,128)S(1)}, u32[]{:S(2)}, u32[]{:S(2)}) collective-permute-start(f32[8,4,4,1]{3,0,2,1:T(8,128)S(1)} %get-tuple-element.31), channel_id=1, source_target_pairs={{8,0},{16,8},{24,16},{0,24},{9,1},{17,9},{25,17},{1,25},{10,2},{18... | collective-permute-start | bytes 1544 | tf_op jit(solution)/shard_map/ppermute | solution.py:19
  61.2 3.8 %collective-permute-start.20 = (f32[8,4,1,66]{3,0,2,1:T(8,128)S(1)}, f32[8,4,1,66]{3,0,2,1:T(8,128)S(1)}, u32[]{:S(2)}, u32[]{:S(2)}) collective-permute-start(f32[8,4,1,66]{3,0,2,1:T(8,128)S(1)} %get-tuple-element.22), channel_id=1, source_target_pairs={{0,4},{4,0},{1,5},{5,1},{2,6},{6,2},{3,7},{7,3},{8,12},{12,8},{9,1... | collective-permute-start | bytes 25352 | tf_op jit(solution)/shard_map/ppermute | solution.py:18
  63.0 3.7 %collective-permute-start.21 = (f32[8,4,1,66]{3,0,2,1:T(8,128)S(1)}, f32[8,4,1,66]{3,0,2,1:T(8,128)S(1)}, u32[]{:S(2)}, u32[]{:S(2)}) collective-permute-start(f32[8,4,1,66]{3,0,2,1:T(8,128)S(1)} %get-tuple-element.23), channel_id=1, source_target_pairs={{4,0},{0,4},{5,1},{1,5},{6,2},{2,6},{7,3},{3,7},{12,8},{8,12},{13,... | collective-permute-start | bytes 25352 | tf_op jit(solution)/shard_map/ppermute | solution.py:19
  66.8 5.9 %collective-permute-start.22 = (f32[8,1,6,66]{3,0,2,1:T(8,128)S(1)}, f32[8,1,6,66]{3,0,2,1:T(8,128)S(1)}, u32[]{:S(2)}, u32[]{:S(2)}) collective-permute-start(f32[8,1,6,66]{3,0,2,1:T(8,128)S(1)} %get-tuple-element.14), channel_id=1, source_target_pairs={{0,1},{1,2},{2,3},{3,0},{4,5},{5,6},{6,7},{7,4},{8,9},{9,10},{10,1... | collective-permute-start | bytes 38024 | tf_op jit(solution)/shard_map/ppermute | solution.py:18
  67.8 4.9 %collective-permute-start.23 = (f32[8,1,6,66]{3,0,2,1:T(8,128)S(1)}, f32[8,1,6,66]{3,0,2,1:T(8,128)S(1)}, u32[]{:S(2)}, u32[]{:S(2)}) collective-permute-start(f32[8,1,6,66]{3,0,2,1:T(8,128)S(1)} %get-tuple-element.15), channel_id=1, source_target_pairs={{1,0},{2,1},{3,2},{0,3},{5,4},{6,5},{7,6},{4,7},{9,8},{10,9},{11,1... | collective-permute-start | bytes 38024 | tf_op jit(solution)/shard_map/ppermute | solution.py:19
where the time goes:
time: 137 us; the launch traced here: 136 us
  blocking collectives  39.9 us (29%)
  starting transfers between devices  31.8 us (23%)
  waiting for transfers between devices  28.3 us (21%)
  between operations  16.2 us (12%)
  matrix products  7.47 us (5%)
  other arithmetic  6.85 us (5%)
  local copies, waits for them, and re-layouts  5.5 us (4%)
    psum x1, blocking collectives, local(): products = lax.psum(local_products, ('row', 'th', 'ph'))  39.9 us
    ppermute x12, waiting for transfers between devices, with_halo(): before = lax.ppermute(last, axis, up)  22 us
    ppermute x12, starting transfers between devices, with_halo(): after = lax.ppermute(first, axis, down)  21 us
    ppermute x12, starting transfers between devices, with_halo(): before = lax.ppermute(last, axis, up)  10.9 us
    ppermute x12, waiting for transfers between devices, with_halo(): after = lax.ppermute(first, axis, down)  6.21 us
    dot_general x4, matrix products, precondition(): jnp.einsum('pqbij,pqbj->pqbi', inverse, blocked, preferred_element_type=j...  4.7 us
  transfers between devices with their start and end apart: 24, of which 19 were waited for; matrix products, arithmetic and copies ran while one was open for 0% of the time, Pallas kernels for 0%

commit v1 on v0

v1 whole, which is shorter than its diff:
```python
import functools

import jax
import jax.numpy as jnp
from jax import lax
from jax.experimental import pallas as pl
from jax.experimental.pallas import tpu as pltpu
from jax.sharding import PartitionSpec as P

VARS = 8
BLK = 16
S = 4
LANES = VARS * BLK
GROUP = 8
VMEM_LIMIT = 24 * 1024 * 1024


def pairs_low(count):
    return [(i, i ^ 1) for i in range(count)]


def pairs_high(count):
    return [(i, (i + 1) % count if i % 2 else (i - 1) % count) for i in range(count)]


def to_rows(field):
    var, ph, th, radial = field.shape
    split = field.reshape(var, ph, th, radial // BLK, BLK).transpose(3, 1, 2, 0, 4)
    return split.reshape(-1, var * BLK)


def from_rows(rows, shape):
    var, ph, th, radial = shape
    split = rows.reshape(radial // BLK, ph, th, var, BLK).transpose(3, 1, 2, 0, 4)
    return split.reshape(shape)


def apply_blocks(field, inverse_ref, ph, th):
    rounded = field.astype(jnp.bfloat16)
    across = 2 * GROUP
    row = lax.broadcasted_iota(jnp.int32, (across, LANES), 0) % GROUP
    parts = []
    for first in range(0, field.shape[0], across):
        vectors = rounded[first : first + across]
        spread = jnp.concatenate(
            [jnp.where(row == m, vectors, jnp.zeros_like(vectors)) for m in range(GROUP)], axis=1
        )
        halves = []
        for half in range(2):
            blocks = []
            for m in range(GROUP):
                index = first + half * GROUP + m
                b, place = divmod(index, ph * th)
                p, t = divmod(place, th)
                blocks.append(inverse_ref[p, t, b])
            halves.append(jnp.concatenate(blocks, axis=1))
        matrix = jnp.concatenate(halves, axis=0)
        out = lax.dot_general(
            spread, matrix, (((1,), (1,)), ((), ())), preferred_element_type=jnp.float32
        )
        parts += [out[:GROUP, :LANES], out[GROUP:, LANES:]]
    return jnp.concatenate(parts, axis=0)


def pack_faces(field, d_ref, out_refs, flags_ref, ph, th):
    ph_a, ph_b, row_a, row_b, th_a, th_b = out_refs
    rows = field.shape[0]
    per = ph * th
    nb = rows // per
    cell = lax.broadcasted_iota(jnp.int32, (per, LANES), 1) % BLK
    odd_ph, odd_row, odd_th = flags_ref[0] == 1, flags_ref[1] == 1, flags_ref[2] == 1
    low = jnp.concatenate([field[b * per : b * per + th] for b in range(nb)], axis=0)
    high = jnp.concatenate([field[(b + 1) * per - th : (b + 1) * per] for b in range(nb)], axis=0)
    ph_a[...] = jnp.where(odd_ph, low, high)
    ph_b[...] = jnp.where(odd_ph, high, low)
    low = jnp.where(cell == BLK - 1, pltpu.roll(field[:per], BLK - 1, 1), 0.0)
    high = jnp.where(cell == 0, pltpu.roll(field[rows - per :], LANES - BLK + 1, 1), 0.0)
    row_a[...] = jnp.where(odd_row, low, high)
    if row_b is not None:
        row_b[...] = jnp.where(odd_row, high, low)
    low = d_ref[pl.ds(0, rows // th, stride=th), :]
    high = d_ref[pl.ds(th - 1, rows // th, stride=th), :]
    th_a[...] = jnp.where(odd_th, low, high)
    if th_b is not None:
        th_b[...] = jnp.where(odd_th, high, low)


def local_part(field, d_ref, krylov, conduct, diagonal, mixing_ref, ph, th):
    rows = field.shape[0]
    per = ph * th
    lane = lax.broadcasted_iota(jnp.int32, (rows, LANES), 1)
    row = lax.broadcasted_iota(jnp.int32, (rows, LANES), 0)
    cell = lane % BLK
    polar = row % th
    azimuth = (row // th) % ph
    mixed = field * mixing_ref[0:1, :]
    for m in range(1, VARS):
        mixed += pltpu.roll(field, LANES - BLK * m, 1) * mixing_ref[m : m + 1, :]
    zero = jnp.zeros((per, LANES), jnp.float32)
    from_low = pltpu.roll(field, LANES - BLK + 1, 1)
    from_low = jnp.concatenate([zero, from_low[: rows - per]], axis=0)
    from_high = pltpu.roll(field, BLK - 1, 1)
    from_high = jnp.concatenate([from_high[per:], zero], axis=0)
    total = jnp.where(cell == 0, from_low, pltpu.roll(field, 1, 1))
    total += jnp.where(cell == BLK - 1, from_high, pltpu.roll(field, LANES - 1, 1))
    total += jnp.where(polar == 0, 0.0, pltpu.roll(field, 1, 0))
    total += jnp.where(polar == th - 1, 0.0, pltpu.roll(field, rows - 1, 0))
    total += jnp.where(azimuth == 0, 0.0, pltpu.roll(field, th, 0))
    total += jnp.where(azimuth == ph - 1, 0.0, pltpu.roll(field, rows - th, 0))
    return field + mixed + conduct * (diagonal * field - total) - krylov


def add_faces(halo_ref, in_refs, flags_ref, ph, th):
    ph_a, ph_b, row_a, row_b, th_a, th_b = in_refs
    rows = halo_ref.shape[0]
    per = ph * th
    nb = rows // per
    odd_ph, odd_row, odd_th = flags_ref[0] == 1, flags_ref[1] == 1, flags_ref[2] == 1
    halo_ref[...] = jnp.zeros_like(halo_ref)

    def sides(odd, a, b, has_low, has_high):
        first = a[...]
        second = jnp.zeros_like(first) if b is None else b[...]
        low = jnp.where(odd, first, second)
        high = jnp.where(odd, second, first)
        if has_low is not None:
            low = jnp.where(has_low, low, 0.0)
            high = jnp.where(has_high, high, 0.0)
        return low, high

    low, high = sides(odd_ph, ph_a, ph_b, None, None)
    for b in range(nb):
        halo_ref[b * per : b * per + th, :] += low[b * th : (b + 1) * th]
        halo_ref[(b + 1) * per - th : (b + 1) * per, :] += high[b * th : (b + 1) * th]
    low, high = sides(odd_row, row_a, row_b, flags_ref[3] == 1, flags_ref[4] == 1)
    halo_ref[:per, :] += low
    halo_ref[rows - per :, :] += high
    low, high = sides(odd_th, th_a, th_b, flags_ref[5] == 1, flags_ref[6] == 1)
    halo_ref[pl.ds(0, rows // th, stride=th), :] += low
    halo_ref[pl.ds(th - 1, rows // th, stride=th), :] += high
    return halo_ref[...]


def fill(refs, present):
    refs = iter(refs)
    return [next(refs) if there else None for there in present]


def first_kernel(ph, th, present, flags_ref, krylov_ref, inverse_ref, d_ref, *faces):
    direction = apply_blocks(krylov_ref[...], inverse_ref, ph, th)
    d_ref[...] = direction
    pack_faces(direction, d_ref, fill(faces, present), flags_ref, ph, th)


def step_kernel(ph, th, present, flags_ref, krylov_ref, last_ref, conduct_ref, diagonal_ref, mixing_ref, inverse_ref, *rest):
    n = sum(present)
    in_faces, (next_ref, d_ref), out_faces, (halo_ref,) = rest[:n], rest[n : n + 2], rest[n + 2 : 2 * n + 2], rest[2 * n + 2 :]
    conduct = conduct_ref[...]
    local = local_part(last_ref[...], last_ref, krylov_ref[...], conduct, diagonal_ref[...], mixing_ref, ph, th)
    halo = add_faces(halo_ref, fill(in_faces, present), flags_ref, ph, th)
    krylov = local - conduct * halo
    next_ref[...] = krylov
    direction = apply_blocks(krylov, inverse_ref, ph, th)
    d_ref[...] = direction
    pack_faces(direction, d_ref, fill(out_faces, present), flags_ref, ph, th)


def last_kernel(ph, th, present, flags_ref, krylov_ref, last_ref, conduct_ref, diagonal_ref, mixing_ref, *rest):
    n = sum(present)
    older, in_faces, (next_ref, gram_ref), (halo_ref,) = rest[: S - 1], rest[S - 1 : S - 1 + n], rest[S - 1 + n : S + 1 + n], rest[S + 1 + n :]
    conduct = conduct_ref[...]
    newest = krylov_ref[...]
    local = local_part(last_ref[...], last_ref, newest, conduct, diagonal_ref[...], mixing_ref, ph, th)
    halo = add_faces(halo_ref, fill(in_faces, present), flags_ref, ph, th)
    final = local - conduct * halo
    next_ref[...] = final
    basis = [ref[...] for ref in older] + [newest, final]
    sums = []
    for i in range(S + 1):
        for j in range(i + 1):
            product = basis[i] * basis[j]
            sums.append(jnp.sum(product, axis=0, keepdims=True))
    sums += [jnp.zeros_like(sums[0])] * (-len(sums) % 8)
    stacked = jnp.concatenate(sums, axis=0)
    each = jnp.sum(stacked, axis=1, keepdims=True)
    lane = lax.broadcasted_iota(jnp.int32, stacked.shape, 1)
    row = lax.broadcasted_iota(jnp.int32, stacked.shape, 0)
    line = jnp.sum(jnp.where(lane == row, each, 0.0), axis=0, keepdims=True)
    gram_ref[...] = jnp.broadcast_to(line, gram_ref.shape)


def cholesky(matrix, order):
    lower = [[None] * order for _ in range(order)]
    for j in range(order):
        summed = matrix[j][j]
        for k in range(j):
            summed = summed - lower[j][k] * lower[j][k]
        lower[j][j] = jnp.sqrt(summed)
        for i in range(j + 1, order):
            summed = matrix[i][j]
            for k in range(j):
                summed = summed - lower[i][k] * lower[j][k]
            lower[i][j] = summed / lower[j][j]
    return lower


def small_solve(products):
    factor = cholesky(products, S + 1)
    upper = [[factor[j][i] if i <= j else None for j in range(S + 1)] for i in range(S + 1)]

    def plus(a, b):
        return b if a is None else a if b is None else a + b

    hess = [[plus(upper[i][j], upper[i][j + 1]) for j in range(S)] for i in range(S + 1)]

    def dot(j, k):
        total = None
        for i in range(S + 1):
            if hess[i][j] is not None and hess[i][k] is not None:
                total = plus(total, hess[i][j] * hess[i][k])
        return total

    normal = [[dot(j, k) for k in range(j + 1)] for j in range(S)]
    moment = [hess[0][j] * upper[0][0] for j in range(S)]
    lower = cholesky(normal, S)
    forward = []
    for i in range(S):
        summed = moment[i]
        for k in range(i):
            summed = summed - lower[i][k] * forward[k]
        forward.append(summed / lower[i][i])
    weights = [None] * S
    for i in reversed(range(S)):
        summed = forward[i]
        for k in range(i + 1, S):
            summed = summed - lower[k][i] * weights[k]
        weights[i] = summed / lower[i][i]
    return weights


def combine_kernel(gram_ref, *refs):
    krylov, directions, (correction_ref, residual_ref) = refs[: S + 1], refs[S + 1 : 2 * S + 1], refs[2 * S + 1 :]
    line = jnp.sum(gram_ref[...], axis=0, keepdims=True)
    products, place = [], 0
    for i in range(S + 1):
        products.append([])
        for j in range(i + 1):
            products[i].append(line[:, place : place + 1])
            place += 1
    weights = small_solve(products)
    basis = [ref[...] for ref in krylov]
    correction = jnp.zeros_like(basis[0])
    residual = basis[0]
    for j in range(S):
        correction = correction + weights[j] * directions[j][...]
        residual = residual - weights[j] * (basis[j + 1] + basis[j])
    correction_ref[...] = correction
    residual_ref[...] = residual


def call(kernel, outs, scratch, *args):
    specs = [
        pl.BlockSpec(memory_space=pltpu.SMEM if a.dtype == jnp.int32 else pltpu.VMEM) for a in args
    ]
    return pl.pallas_call(
        kernel,
        out_shape=outs,
        in_specs=specs,
        out_specs=[pl.BlockSpec(memory_space=pltpu.VMEM)] * len(outs),
        scratch_shapes=scratch,
        compiler_params=pltpu.CompilerParams(vmem_limit_bytes=VMEM_LIMIT),
    )(*args)


def local(right_side, conduct, coupling, inverse, face_codes):
    _, ph, th, radial = right_side.shape
    nb = radial // BLK
    per = ph * th
    rows = per * nb
    at = {axis: (lax.axis_index(axis), lax.axis_size(axis)) for axis in ("row", "th", "ph")}
    (row_at, row_n), (th_at, th_n), (ph_at, ph_n) = at["row"], at["th"], at["ph"]
    present = (True, True, True, row_n > 2, True, th_n > 2)
    flags = jnp.stack(
        [ph_at % 2, row_at % 2, th_at % 2, row_at > 0, row_at < row_n - 1, th_at > 0, th_at < th_n - 1]
    ).astype(jnp.int32)

    factor = (face_codes == 1).astype(jnp.float32) - (face_codes == 2).astype(jnp.float32)
    factor = factor.reshape(2, 1, per, 1)
    block = lax.broadcasted_iota(jnp.int32, (nb, per, LANES), 0)
    cell = lax.broadcasted_iota(jnp.int32, (nb, per, LANES), 2) % BLK
    ghost = jnp.where((block == 0) & (cell == 0) & (row_at == 0), factor[0], 0.0)
    ghost += jnp.where((block == nb - 1) & (cell == BLK - 1) & (row_at == row_n - 1), factor[1], 0.0)
    diagonal = (6.0 - ghost).reshape(rows, LANES)
    mixing = jnp.stack([jnp.diagonal(jnp.roll(coupling, -m, 1)) for m in range(VARS)])
    mixing = jnp.repeat(mixing, BLK, axis=1)
    conducts = to_rows(conduct)

    def shape(n):
        return jax.ShapeDtypeStruct((n, LANES), jnp.float32)

    face_rows = (nb * th, nb * th, per, per, rows // th, rows // th)
    faces = [shape(n) for n, there in zip(face_rows, present) if there]
    whole = shape(rows)

    def exchange(sent):
        plan = (("ph", pairs_low), ("ph", pairs_high), ("row", pairs_low), ("row", pairs_high), ("th", pairs_low), ("th", pairs_high))
        plan = [p for p, there in zip(plan, present) if there]
        taken = [None] * len(plan)
        order = sorted(range(len(plan)), key=lambda i: (plan[i][0] != "ph", plan[i][0] != "th", plan[i][1] is pairs_low))
        for i in order:
            axis, pairs = plan[i]
            taken[i] = lax.ppermute(sent[i], axis, pairs(lax.axis_size(axis)))
        return taken

    krylov = [to_rows(right_side)]
    direction, *sent = call(
        functools.partial(first_kernel, ph, th, present), [whole] + faces, [], flags, krylov[0], inverse
    )
    directions = [direction]
    halo = [pltpu.VMEM((rows, LANES), jnp.float32)]
    for _ in range(S - 1):
        taken = exchange(sent)
        following, direction, *sent = call(
            functools.partial(step_kernel, ph, th, present),
            [whole, whole] + faces,
            halo,
            flags, krylov[-1], directions[-1], conducts, diagonal, mixing, inverse, *taken,
        )
        krylov.append(following)
        directions.append(direction)
    taken = exchange(sent)
    devices = row_n * th_n * ph_n
    following, gram = call(
        functools.partial(last_kernel, ph, th, present),
        [whole, shape(devices)],
        halo,
        flags, krylov[-1], directions[-1], conducts, diagonal, mixing, *krylov[:-1], *taken,
    )
    krylov.append(following)
    gram = lax.all_to_all(gram, ("row", "th", "ph"), 0, 0, tiled=True)
    correction, residual = call(combine_kernel, [whole, whole], [], gram, *krylov, *directions)
    return from_rows(correction, right_side.shape), from_rows(residual, right_side.shape)


def solution(mesh):
    placed = (
        P(None, "ph", "th", "row"),
        P(None, "ph", "th", "row"),
        P(),
        P("ph", "th", "row", None, None),
        P(None, "ph", "th"),
    )
    return jax.shard_map(
        local,
        mesh=mesh,
        in_specs=placed,
        out_specs=(P(None, "ph", "th", "row"), P(None, "ph", "th", "row")),
        check_vma=False,
    )
```

time: 137 us -> 60.9 us (0.44)
  blocking collectives: 39.9 us -> 10.9 us
  waiting for transfers between devices: 28.3 us -> 9.7 us
  between operations: 16.2 us -> 0.92 us
  starting transfers between devices: 31.8 us -> 19.8 us
  matrix products: 7.47 us -> 0 us
  Pallas kernels: 0 us -> 6.89 us
  local copies, waits for them, and re-layouts: 5.5 us -> 12.1 us
  other arithmetic: 6.85 us -> 0.44 us
    psum x1 -> x0, blocking collectives: 39.9 us -> none  [local(): products = lax.psum(local_products, ('row', 'th', 'ph'))]
    ppermute x24 -> x20, waiting for transfers between devices: 28.3 us -> 9.7 us  [exchange(): taken[i] = lax.ppermute(sent[i], axis, pairs(lax.axis_size(axis)))]
    ppermute x24 -> x20, starting transfers between devices: 31.8 us -> 19.8 us  [exchange(): taken[i] = lax.ppermute(sent[i], axis, pairs(lax.axis_size(axis)))]
    all_to_all x0 -> x1, blocking collectives: none -> 10.9 us  [local(): gram = lax.all_to_all(gram, ('row', 'th', 'ph'), 0, 0, tiled=True)]
    dot_general x11 -> x0, matrix products: 7.47 us -> none  [the longest x4 4.7 us: precondition(): jnp.einsum('pqbij,pqbj->pqbi', inverse, blocked, preferred_element_type=j...]
    pallas_call x0 -> x6, Pallas kernels: none -> 6.89 us  [call(): pl.pallas_call(kernel, out_shape=outs, in_specs=specs, out_specs=[pl.Bloc...]
    gather x0 -> x8, local copies, waits for them, and re-layouts: none -> 5.08 us  [local(): jnp.diagonal(jnp.roll(coupling, -m, 1))]
    another operation x6 -> x0, other arithmetic: 2.18 us -> none  [the longest x3 1.12 us: local(): upper_factor = jnp.linalg.cholesky(products).T]
  transfers between devices with their start and end apart: 24 -> 20, of which waited for: 19 -> 7; matrix products, arithmetic and copies ran while one was open for 0% -> 12% of each run, Pallas kernels for 0% -> 0%
where the time goes in v1:
time: 60.9 us; the launch traced here: 60.7 us
  starting transfers between devices  19.8 us (33%)
  local copies, waits for them, and re-layouts  12.1 us (20%)
  blocking collectives  10.9 us (18%)
  waiting for transfers between devices  9.7 us (16%)
  Pallas kernels  6.89 us (11%)
  between operations  0.92 us (2%)
    ppermute x20, starting transfers between devices, exchange(): taken[i] = lax.ppermute(sent[i], axis, pairs(lax.axis_size(axis)))  19.8 us
    all_to_all x1, blocking collectives, local(): gram = lax.all_to_all(gram, ('row', 'th', 'ph'), 0, 0, tiled=True)  10.9 us
    ppermute x20, waiting for transfers between devices, exchange(): taken[i] = lax.ppermute(sent[i], axis, pairs(lax.axis_size(axis)))  9.7 us
    pallas_call x6, Pallas kernels, call(): pl.pallas_call(kernel, out_shape=outs, in_specs=specs, out_specs=[pl.Bloc...  6.89 us
    gather x8, local copies, waits for them, and re-layouts, local(): jnp.diagonal(jnp.roll(coupling, -m, 1))  5.08 us
    reshape x2, local copies, waits for them, and re-layouts, from_rows(): return split.reshape(shape)  1.62 us
    unnamed x10, local copies, waits for them, and re-layouts  1.61 us
    reshape x4, local copies, waits for them, and re-layouts, to_rows(): field.reshape(var, ph, th, radial // BLK, BLK).transpose(3, 1, 2, 0, 4)  1.53 us
  transfers between devices with their start and end apart: 20, of which 7 were waited for; matrix products, arithmetic and copies ran while one was open for 12% of the time, Pallas kernels for 0%

profile of v1, /device:TPU:0, one launch (start us, length us, event | category | flops | bytes accessed | tf_op | source)
XLA Modules:
  0.0 60.7 jit_solution(5205473616966704101)
XLA Ops:
  0.7 1.0 %reshape.45 = f32[8,4,4,4,16]{4,3,2,1,0:T(4,128)S(1)} reshape(f32[8,4,4,64]{3,2,1,0:T(4,128)} %param.5) | data formatting | bytes 65536 | tf_op jit(solution)/shard_map/reshape | solution.py:28
  1.7 0.2 copy.23
  1.9 0.1 reshape.46.krylov_ref.rest_0_.refs_0_
  2.1 0.1 stack.74.flags_ref
  2.1 1.6 %copy-done = bf16[4,4,4,128,128]{4,3,2,1,0:T(8,128)(2,1)S(1)} copy-done((bf16[4,4,4,128,128]{4,3,2,1,0:T(8,128)(2,1)S(1)}, bf16[4,4,4,128,128]{4,3,2,1,0:T(8,128)(2,1)}, u32[]{:S(2)}) %copy-start) | copy-done | bytes 2097176
  3.7 1.2 %shard_map.68 = (f32[64,128]{1,0:T(8,128)S(1)}, f32[16,128]{1,0:T(8,128)S(1)}, f32[16,128]{1,0:T(8,128)S(1)}, f32[16,128]{1,0:T(8,128)S(1)}, f32[16,128]{1,0:T(8,128)S(1)}, /*index=5*/f32[16,128]{1,0:T(8,128)S(1)}) custom-call(s32[7]{0:T(128)S(1)} %stack.74.flags_ref, f32[64,128]{1,0:T(8,128)S(1)} %reshape.46.krylov_ref.rest_0_.refs_0_, ...), custom_call_target="tpu_custom_call" | custom-call | tf_op jit(solution)/shard_map/pallas_call | solution.py:265
  5.0 3.1 %collective-permute-start = (f32[16,128]{1,0:T(8,128)S(1)}, f32[16,128]{1,0:T(8,128)S(1)}, u32[]{:S(2)}, u32[]{:S(2)}) collective-permute-start(f32[16,128]{1,0:T(8,128)S(1)} %get-tuple-element.34), channel_id=1, source_target_pairs={{0,1},{1,0},{2,3},{3,2},{4,5},{5,4},{6,7},{7,6},{8,9},{9,8},{10,11... | collective-permute-start | bytes 24584 | tf_op jit(solution)/shard_map/ppermute | solution.py:312
  8.0 2.5 %collective-permute-start.1 = (f32[16,128]{1,0:T(8,128)S(1)}, f32[16,128]{1,0:T(8,128)S(1)}, u32[]{:S(2)}, u32[]{:S(2)}) collective-permute-start(f32[16,128]{1,0:T(8,128)S(1)} %get-tuple-element.35), channel_id=1, source_target_pairs={{0,3},{1,2},{2,1},{3,0},{4,7},{5,6},{6,5},{7,4},{8,11},{9,10},{10,... | collective-permute-start | bytes 24584 | tf_op jit(solution)/shard_map/ppermute | solution.py:312
  10.5 1.6 %collective-permute-start.3 = (f32[16,128]{1,0:T(8,128)S(1)}, f32[16,128]{1,0:T(8,128)S(1)}, u32[]{:S(2)}, u32[]{:S(2)}) collective-permute-start(f32[16,128]{1,0:T(8,128)S(1)} %get-tuple-element.37), channel_id=1, source_target_pairs={{0,24},{8,16},{16,8},{24,0},{1,25},{9,17},{17,9},{25,1},{2,26},{10... | collective-permute-start | bytes 24584 | tf_op jit(solution)/shard_map/ppermute | solution.py:312
  12.1 1.5 %collective-permute-start.4 = (f32[16,128]{1,0:T(8,128)S(1)}, f32[16,128]{1,0:T(8,128)S(1)}, u32[]{:S(2)}, u32[]{:S(2)}) collective-permute-start(f32[16,128]{1,0:T(8,128)S(1)} %get-tuple-element.38), channel_id=1, source_target_pairs={{0,4},{4,0},{1,5},{5,1},{2,6},{6,2},{3,7},{7,3},{8,12},{12,8},{9,1... | collective-permute-start | bytes 24584 | tf_op jit(solution)/shard_map/ppermute | solution.py:312
  14.2 0.1 broadcast_in_dim.56
  14.3 0.1 broadcast_in_dim.58
  14.4 0.1 broadcast_in_dim.51
  14.5 0.1 broadcast_in_dim.53
  14.6 0.1 iota.69
  14.8 0.1 iota.61
  14.9 0.1 pad_maximum_fusion.3
  15.0 0.1 pad_maximum_fusion
  15.0 0.1 pad_maximum_fusion.1
  15.1 0.1 pad_maximum_fusion.2
  15.2 0.1 add_subtract_fusion.diagonal_ref
  15.3 0.2 reshape.47
  15.5 0.2 copy.22
  15.7 0.1 reshape.48.conduct_ref
  15.8 0.6 %gather_fusion = f32[8]{0:T(128)S(1)} fusion(f32[8,8]{1,0:T(8,128)S(1)} %copy-done.2, s32[8]{0:T(128)S(1)} %or_bitcast_fusion), kind=kCustom, calls=%fused_computation | custom fusion | bytes 128 | tf_op jit(solution)/shard_map/jit(diagonal)/cond/branch_0_fun/gather | solution.py:294
  16.4 0.6 %gather_fusion.1 = f32[8]{0:T(128)S(1)} fusion(f32[8,8]{1,0:T(8,128)S(1)} %get-tuple-element.82, s32[8]{0:T(128)S(1)} %or_bitcast_fusion), kind=kCustom, calls=%fused_computation.1 | custom fusion | bytes 128 | tf_op jit(solution)/shard_map/jit(diagonal)/cond/branch_0_fun/gather | solution.py:294
  17.1 0.6 %gather_fusion.2 = f32[8]{0:T(128)S(1)} fusion(f32[8,8]{1,0:T(8,128)S(1)} %get-tuple-element.84, s32[8]{0:T(128)S(1)} %or_bitcast_fusion), kind=kCustom, calls=%fused_computation.2 | custom fusion | bytes 128 | tf_op jit(solution)/shard_map/jit(diagonal)/cond/branch_0_fun/gather | solution.py:294
  17.7 0.6 %gather_fusion.3 = f32[8]{0:T(128)S(1)} fusion(f32[8,8]{1,0:T(8,128)S(1)} %get-tuple-element.86, s32[8]{0:T(128)S(1)} %or_bitcast_fusion), kind=kCustom, calls=%fused_computation.3 | custom fusion | bytes 128 | tf_op jit(solution)/shard_map/jit(diagonal)/cond/branch_0_fun/gather | solution.py:294
  18.4 0.6 %gather_fusion.4 = f32[8]{0:T(128)S(1)} fusion(f32[8,8]{1,0:T(8,128)S(1)} %pad_maximum_fusion.3, s32[8]{0:T(128)S(1)} %or_bitcast_fusion), kind=kCustom, calls=%fused_computation.4 | custom fusion | bytes 128 | tf_op jit(solution)/shard_map/jit(diagonal)/cond/branch_0_fun/gather | solution.py:294
  19.0 0.6 %gather_fusion.5 = f32[8]{0:T(128)S(1)} fusion(f32[8,8]{1,0:T(8,128)S(1)} %get-tuple-element.87, s32[8]{0:T(128)S(1)} %or_bitcast_fusion), kind=kCustom, calls=%fused_computation.5 | custom fusion | bytes 128 | tf_op jit(solution)/shard_map/jit(diagonal)/cond/branch_0_fun/gather | solution.py:294
  19.6 0.6 %gather_fusion.6 = f32[8]{0:T(128)S(1)} fusion(f32[8,8]{1,0:T(8,128)S(1)} %get-tuple-element.85, s32[8]{0:T(128)S(1)} %or_bitcast_fusion), kind=kCustom, calls=%fused_computation.6 | custom fusion | bytes 128 | tf_op jit(solution)/shard_map/jit(diagonal)/cond/branch_0_fun/gather | solution.py:294
  20.3 0.6 %gather_fusion.7 = f32[8]{0:T(128)S(1)} fusion(f32[8,8]{1,0:T(8,128)S(1)} %get-tuple-element.83, s32[8]{0:T(128)S(1)} %or_bitcast_fusion), kind=kCustom, calls=%fused_computation.7 | custom fusion | bytes 128 | tf_op jit(solution)/shard_map/jit(diagonal)/cond/branch_0_fun/gather | solution.py:294
  21.0 0.1 reshape.49.mixing_ref
  21.1 1.3 %shard_map.69 = (f32[64,128]{1,0:T(8,128)S(1)}, f32[64,128]{1,0:T(8,128)S(1)}, f32[16,128]{1,0:T(8,128)S(1)}, f32[16,128]{1,0:T(8,128)S(1)}, f32[16,128]{1,0:T(8...) custom-call(s32[7]{0:T(128)S(1)} %stack.74.flags_ref, f32[64,128]{1,0:T(8,128)S(1)} %reshape.46.krylov_ref.rest_0_.refs_0_, ...), custom_call_target="tpu_custom_call" | custom-call | tf_op jit(solution)/shard_map/pallas_call | solution.py:265
  22.4 0.7 %collective-permute-start.5 = (f32[16,128]{1,0:T(8,128)S(1)}, f32[16,128]{1,0:T(8,128)S(1)}, u32[]{:S(2)}, u32[]{:S(2)}) collective-permute-start(f32[16,128]{1,0:T(8,128)S(1)} %get-tuple-element.41), channel_id=1, source_target_pairs={{0,1},{1,0},{2,3},{3,2},{4,5},{5,4},{6,7},{7,6},{8,9},{9,8},{10,11... | collective-permute-start | bytes 24584 | tf_op jit(solution)/shard_map/ppermute | solution.py:312
  23.2 0.9 %collective-permute-start.6 = (f32[16,128]{1,0:T(8,128)S(1)}, f32[16,128]{1,0:T(8,128)S(1)}, u32[]{:S(2)}, u32[]{:S(2)}) collective-permute-start(f32[16,128]{1,0:T(8,128)S(1)} %get-tuple-element.42), channel_id=1, source_target_pairs={{0,3},{1,2},{2,1},{3,0},{4,7},{5,6},{6,5},{7,4},{8,11},{9,10},{10,... | collective-permute-start | bytes 24584 | tf_op jit(solution)/shard_map/ppermute | solution.py:312
  24.1 0.6 %collective-permute-start.8 = (f32[16,128]{1,0:T(8,128)S(1)}, f32[16,128]{1,0:T(8,128)S(1)}, u32[]{:S(2)}, u32[]{:S(2)}) collective-permute-start(f32[16,128]{1,0:T(8,128)S(1)} %get-tuple-element.44), channel_id=1, source_target_pairs={{0,24},{8,16},{16,8},{24,0},{1,25},{9,17},{17,9},{25,1},{2,26},{10... | collective-permute-start | bytes 24584 | tf_op jit(solution)/shard_map/ppermute | solution.py:312
  24.7 0.5 collective-permute-start.9
  25.2 0.9 %collective-permute-done.5.rest_0_ = f32[16,128]{1,0:T(8,128)S(1)} collective-permute-done((f32[16,128]{1,0:T(8,128)S(1)}, f32[16,128]{1,0:T(8,128)S(1)}, u32[]{:S(2)}, u32[]{:S(2)}) %collective-permute-start.5) | collective-permute-done | bytes 8224 | tf_op jit(solution)/shard_map/ppermute | solution.py:312
  26.1 2.5 %collective-permute-done.6.rest_1_ = f32[16,128]{1,0:T(8,128)S(1)} collective-permute-done((f32[16,128]{1,0:T(8,128)S(1)}, f32[16,128]{1,0:T(8,128)S(1)}, u32[]{:S(2)}, u32[]{:S(2)}) %collective-permute-start.6) | collective-permute-done | bytes 8224 | tf_op jit(solution)/shard_map/ppermute | solution.py:312
  28.6 1.3 %shard_map.70 = (f32[64,128]{1,0:T(8,128)S(1)}, f32[64,128]{1,0:T(8,128)S(1)}, f32[16,128]{1,0:T(8,128)S(1)}, f32[16,128]{1,0:T(8,128)S(1)}, f32[16,128]{1,0:T(8...) custom-call(s32[7]{0:T(128)S(1)} %stack.74.flags_ref, ...), custom_call_target="tpu_custom_call" | custom-call | tf_op jit(solution)/shard_map/pallas_call | solution.py:265
  29.9 0.7 %collective-permute-start.10 = (f32[16,128]{1,0:T(8,128)S(1)}, f32[16,128]{1,0:T(8,128)S(1)}, u32[]{:S(2)}, u32[]{:S(2)}) collective-permute-start(f32[16,128]{1,0:T(8,128)S(1)} %get-tuple-element.48), channel_id=1, source_target_pairs={{0,1},{1,0},{2,3},{3,2},{4,5},{5,4},{6,7},{7,6},{8,9},{9,8},{10,11... | collective-permute-start | bytes 24584 | tf_op jit(solution)/shard_map/ppermute | solution.py:312
  30.6 2.5 %collective-permute-start.11 = (f32[16,128]{1,0:T(8,128)S(1)}, f32[16,128]{1,0:T(8,128)S(1)}, u32[]{:S(2)}, u32[]{:S(2)}) collective-permute-start(f32[16,128]{1,0:T(8,128)S(1)} %get-tuple-element.49), channel_id=1, source_target_pairs={{0,3},{1,2},{2,1},{3,0},{4,7},{5,6},{6,5},{7,4},{8,11},{9,10},{10,... | collective-permute-start | bytes 24584 | tf_op jit(solution)/shard_map/ppermute | solution.py:312
  33.1 1.6 %collective-permute-start.13 = (f32[16,128]{1,0:T(8,128)S(1)}, f32[16,128]{1,0:T(8,128)S(1)}, u32[]{:S(2)}, u32[]{:S(2)}) collective-permute-start(f32[16,128]{1,0:T(8,128)S(1)} %get-tuple-element.51), channel_id=1, source_target_pairs={{0,24},{8,16},{16,8},{24,0},{1,25},{9,17},{17,9},{25,1},{2,26},{10... | collective-permute-start | bytes 24584 | tf_op jit(solution)/shard_map/ppermute | solution.py:312
  34.7 0.5 collective-permute-start.14
  35.2 0.9 %collective-permute-done.11.rest_1_ = f32[16,128]{1,0:T(8,128)S(1)} collective-permute-done((f32[16,128]{1,0:T(8,128)S(1)}, f32[16,128]{1,0:T(8,128)S(1)}, u32[]{:S(2)}, u32[]{:S(2)}) %collective-permute-start.11) | collective-permute-done | bytes 8224 | tf_op jit(solution)/shard_map/ppermute | solution.py:312
  36.1 0.1 collective-permute-done.13.rest_3_
  36.2 2.2 %collective-permute-done.14.rest_4_ = f32[16,128]{1,0:T(8,128)S(1)} collective-permute-done((f32[16,128]{1,0:T(8,128)S(1)}, f32[16,128]{1,0:T(8,128)S(1)}, u32[]{:S(2)}, u32[]{:S(2)}) %collective-permute-start.14) | collective-permute-done | bytes 8224 | tf_op jit(solution)/shard_map/ppermute | solution.py:312
  38.3 1.3 %shard_map.71 = (f32[64,128]{1,0:T(8,128)S(1)}, f32[64,128]{1,0:T(8,128)S(1)}, f32[16,128]{1,0:T(8,128)S(1)}, f32[16,128]{1,0:T(8,128)S(1)}, f32[16,128]{1,0:T(8...) custom-call(s32[7]{0:T(128)S(1)} %stack.74.flags_ref, ...), custom_call_target="tpu_custom_call" | custom-call | tf_op jit(solution)/shard_map/pallas_call | solution.py:265
  39.6 0.7 %collective-permute-start.15 = (f32[16,128]{1,0:T(8,128)S(1)}, f32[16,128]{1,0:T(8,128)S(1)}, u32[]{:S(2)}, u32[]{:S(2)}) collective-permute-start(f32[16,128]{1,0:T(8,128)S(1)} %get-tuple-element.55), channel_id=1, source_target_pairs={{0,1},{1,0},{2,3},{3,2},{4,5},{5,4},{6,7},{7,6},{8,9},{9,8},{10,11... | collective-permute-start | bytes 24584 | tf_op jit(solution)/shard_map/ppermute | solution.py:312
  40.4 0.9 %collective-permute-start.16 = (f32[16,128]{1,0:T(8,128)S(1)}, f32[16,128]{1,0:T(8,128)S(1)}, u32[]{:S(2)}, u32[]{:S(2)}) collective-permute-start(f32[16,128]{1,0:T(8,128)S(1)} %get-tuple-element.56), channel_id=1, source_target_pairs={{0,3},{1,2},{2,1},{3,0},{4,7},{5,6},{6,5},{7,4},{8,11},{9,10},{10,... | collective-permute-start | bytes 24584 | tf_op jit(solution)/shard_map/ppermute | solution.py:312
  41.3 0.9 %collective-permute-start.18 = (f32[16,128]{1,0:T(8,128)S(1)}, f32[16,128]{1,0:T(8,128)S(1)}, u32[]{:S(2)}, u32[]{:S(2)}) collective-permute-start(f32[16,128]{1,0:T(8,128)S(1)} %get-tuple-element.58), channel_id=1, source_target_pairs={{0,24},{8,16},{16,8},{24,0},{1,25},{9,17},{17,9},{25,1},{2,26},{10... | collective-permute-start | bytes 24584 | tf_op jit(solution)/shard_map/ppermute | solution.py:312
  42.2 0.5 collective-permute-start.19
  42.7 0.7 %collective-permute-done.15.rest_3_ = f32[16,128]{1,0:T(8,128)S(1)} collective-permute-done((f32[16,128]{1,0:T(8,128)S(1)}, f32[16,128]{1,0:T(8,128)S(1)}, u32[]{:S(2)}, u32[]{:S(2)}) %collective-permute-start.15) | collective-permute-done | bytes 8224 | tf_op jit(solution)/shard_map/ppermute | solution.py:312
  43.3 2.5 %collective-permute-done.16.rest_4_ = f32[16,128]{1,0:T(8,128)S(1)} collective-permute-done((f32[16,128]{1,0:T(8,128)S(1)}, f32[16,128]{1,0:T(8,128)S(1)}, u32[]{:S(2)}, u32[]{:S(2)}) %collective-permute-start.16) | collective-permute-done | bytes 8224 | tf_op jit(solution)/shard_map/ppermute | solution.py:312
  45.8 0.8 %shard_map.72 = (f32[64,128]{1,0:T(8,128)S(1)}, f32[32,128]{1,0:T(8,128)S(1)}) custom-call(s32[7]{0:T(128)S(1)} %stack.74.flags_ref, f32[64,128]{1,0:T(8,128)S(1)} %get-tuple-element.53.krylov_ref.refs_3_, f32[64,128]{1,0:T(8,128)S(1)} %get-tuple-element.54.last_ref.refs_8_, f32[64,128]{1,0:T(8,128)S(1)} %reshape.48.conduct_ref, ...), custom_call_target="tpu_custom_call" | custom-call | tf_op jit(solution)/shard_map/pallas_call | solution.py:265
  46.6 10.9 %all_to_all.11 = f32[32,1,128]{2,1,0:T(1,128)S(1)} all-to-all(f32[32,1,128]{2,1,0:T(1,128)S(1)} %bitcast.34), channel_id=1, replica_groups=mesh['row'=4,'th'=2,'ph'=4] {'row','th','ph'}, dimensions={0} | all-to-all | bytes 32768 | tf_op jit(solution)/shard_map/all_to_all | solution.py:340
  57.5 1.0 %shard_map.73 = (f32[64,128]{1,0:T(8,128)S(1)}, f32[64,128]{1,0:T(8,128)S(1)}) custom-call(f32[32,128]{1,0:T(8,128)S(1)} %bitcast.33, f32[64,128]{1,0:T(8,128)S(1)} %reshape.46.krylov_ref.rest_0_.refs_0_, f32[64,128]{1,0:T(8,128)S(1)} %get-tuple-element.39.krylov_ref.rest_1_.refs_1_, f32[64,128]{1,0:T(8,128)S(1)} %get-tuple-element.46.krylov_ref.rest_2_.refs_2_, ...), custom_call_target="tpu_custom_call" | custom-call | tf_op jit(solution)/shard_map/pallas_call | solution.py:265
  58.5 0.1 reshape.50
  58.6 0.2 copy.18
  58.8 0.8 %reshape.51 = f32[8,4,4,64]{3,2,1,0:T(4,128)} reshape(f32[8,4,4,4,16]{4,3,2,1,0:T(4,128)S(1)} %copy.18) | data formatting | bytes 65536 | tf_op jit(solution)/shard_map/reshape | solution.py:35
  59.6 0.1 reshape.52
  59.7 0.2 copy.19
  59.9 0.8 %reshape.53 = f32[8,4,4,64]{3,2,1,0:T(4,128)} reshape(f32[8,4,4,4,16]{4,3,2,1,0:T(4,128)S(1)} %copy.19) | data formatting | bytes 65536 | tf_op jit(solution)/shard_map/reshape | solution.py:35
  (46 shorter events, 0.9 us)
Async XLA Ops:
  0.6 13.0 %copy-start.2 = (f32[8,8]{1,0:T(8,128)S(1)}, f32[8,8]{1,0:T(8,128)}, u32[]{:S(2)}) copy-start(f32[8,8]{1,0:T(8,128)} %param.7) | copy-start | bytes 772
  0.6 13.6 %copy-start.4 = (s32[2,4,4]{2,1,0:T(4,128)S(1)}, s32[2,4,4]{2,1,0:T(4,128)}, u32[]{:S(2)}) copy-start(s32[2,4,4]{2,1,0:T(4,128)} %param.9) | copy-start | bytes 388
  0.7 14.7 %copy-start.3 = (f32[8,4,4,64]{3,2,1,0:T(4,128)S(1)}, f32[8,4,4,64]{3,2,1,0:T(4,128)}, u32[]{:S(2)}) copy-start(f32[8,4,4,64]{3,2,1,0:T(4,128)} %param.6) | copy-start | bytes 98308
  2.1 1.6 %copy-start = (bf16[4,4,4,128,128]{4,3,2,1,0:T(8,128)(2,1)S(1)}, bf16[4,4,4,128,128]{4,3,2,1,0:T(8,128)(2,1)}, u32[]{:S(2)}) copy-start(bf16[4,4,4,128,128]{4,3,2,1,0:T(8,128)(2,1)} %inverse_ref.7) | copy-start | bytes 6291460
  5.0 16.1 %collective-permute-start = (f32[16,128]{1,0:T(8,128)S(1)}, f32[16,128]{1,0:T(8,128)S(1)}, u32[]{:S(2)}, u32[]{:S(2)}) collective-permute-start(f32[16,128]{1,0:T(8,128)S(1)} %get-tuple-element.34), channel_id=1, source_target_pairs={{0,1},{1,0},{2,3},{3,2},{4,5},{5,4},{6,7},{7,6},{8,9},{9,8},{10,11... | collective-permute-start | bytes 24584 | tf_op jit(solution)/shard_map/ppermute | solution.py:312
  8.0 13.1 %collective-permute-start.1 = (f32[16,128]{1,0:T(8,128)S(1)}, f32[16,128]{1,0:T(8,128)S(1)}, u32[]{:S(2)}, u32[]{:S(2)}) collective-permute-start(f32[16,128]{1,0:T(8,128)S(1)} %get-tuple-element.35), channel_id=1, source_target_pairs={{0,3},{1,2},{2,1},{3,0},{4,7},{5,6},{6,5},{7,4},{8,11},{9,10},{10,... | collective-permute-start | bytes 24584 | tf_op jit(solution)/shard_map/ppermute | solution.py:312
  10.5 10.6 %collective-permute-start.2 = (f32[16,128]{1,0:T(8,128)S(1)}, f32[16,128]{1,0:T(8,128)S(1)}, u32[]{:S(2)}, u32[]{:S(2)}) collective-permute-start(f32[16,128]{1,0:T(8,128)S(1)} %get-tuple-element.36), channel_id=1, source_target_pairs={{0,8},{8,0},{16,24},{24,16},{1,9},{9,1},{17,25},{25,17},{2,10},{10... | collective-permute-start | bytes 24584 | tf_op jit(solution)/shard_map/ppermute | solution.py:312
  10.5 10.6 %collective-permute-start.3 = (f32[16,128]{1,0:T(8,128)S(1)}, f32[16,128]{1,0:T(8,128)S(1)}, u32[]{:S(2)}, u32[]{:S(2)}) collective-permute-start(f32[16,128]{1,0:T(8,128)S(1)} %get-tuple-element.37), channel_id=1, source_target_pairs={{0,24},{8,16},{16,8},{24,0},{1,25},{9,17},{17,9},{25,1},{2,26},{10... | collective-permute-start | bytes 24584 | tf_op jit(solution)/shard_map/ppermute | solution.py:312
  12.1 9.0 %collective-permute-start.4 = (f32[16,128]{1,0:T(8,128)S(1)}, f32[16,128]{1,0:T(8,128)S(1)}, u32[]{:S(2)}, u32[]{:S(2)}) collective-permute-start(f32[16,128]{1,0:T(8,128)S(1)} %get-tuple-element.38), channel_id=1, source_target_pairs={{0,4},{4,0},{1,5},{5,1},{2,6},{6,2},{3,7},{7,3},{8,12},{12,8},{9,1... | collective-permute-start | bytes 24584 | tf_op jit(solution)/shard_map/ppermute | solution.py:312
  15.8 5.3 %copy-start.1 = (bf16[4,4,4,128,128]{4,3,2,1,0:T(8,128)(2,1)S(1)}, bf16[4,4,4,128,128]{4,3,2,1,0:T(8,128)(2,1)}, u32[]{:S(2)}) copy-start(bf16[4,4,4,128,128]{4,3,2,1,0:T(8,128)(2,1)} %inverse_ref.7) | copy-start | bytes 6291460
  22.4 3.7 %collective-permute-start.5 = (f32[16,128]{1,0:T(8,128)S(1)}, f32[16,128]{1,0:T(8,128)S(1)}, u32[]{:S(2)}, u32[]{:S(2)}) collective-permute-start(f32[16,128]{1,0:T(8,128)S(1)} %get-tuple-element.41), channel_id=1, source_target_pairs={{0,1},{1,0},{2,3},{3,2},{4,5},{5,4},{6,7},{7,6},{8,9},{9,8},{10,11... | collective-permute-start | bytes 24584 | tf_op jit(solution)/shard_map/ppermute | solution.py:312
  23.2 5.4 %collective-permute-start.6 = (f32[16,128]{1,0:T(8,128)S(1)}, f32[16,128]{1,0:T(8,128)S(1)}, u32[]{:S(2)}, u32[]{:S(2)}) collective-permute-start(f32[16,128]{1,0:T(8,128)S(1)} %get-tuple-element.42), channel_id=1, source_target_pairs={{0,3},{1,2},{2,1},{3,0},{4,7},{5,6},{6,5},{7,4},{8,11},{9,10},{10,... | collective-permute-start | bytes 24584 | tf_op jit(solution)/shard_map/ppermute | solution.py:312
  24.1 4.6 %collective-permute-start.7 = (f32[16,128]{1,0:T(8,128)S(1)}, f32[16,128]{1,0:T(8,128)S(1)}, u32[]{:S(2)}, u32[]{:S(2)}) collective-permute-start(f32[16,128]{1,0:T(8,128)S(1)} %get-tuple-element.43), channel_id=1, source_target_pairs={{0,8},{8,0},{16,24},{24,16},{1,9},{9,1},{17,25},{25,17},{2,10},{10... | collective-permute-start | bytes 24584 | tf_op jit(solution)/shard_map/ppermute | solution.py:312
  24.1 4.6 %collective-permute-start.8 = (f32[16,128]{1,0:T(8,128)S(1)}, f32[16,128]{1,0:T(8,128)S(1)}, u32[]{:S(2)}, u32[]{:S(2)}) collective-permute-start(f32[16,128]{1,0:T(8,128)S(1)} %get-tuple-element.44), channel_id=1, source_target_pairs={{0,24},{8,16},{16,8},{24,0},{1,25},{9,17},{17,9},{25,1},{2,26},{10... | collective-permute-start | bytes 24584 | tf_op jit(solution)/shard_map/ppermute | solution.py:312
  24.7 3.9 %collective-permute-start.9 = (f32[16,128]{1,0:T(8,128)S(1)}, f32[16,128]{1,0:T(8,128)S(1)}, u32[]{:S(2)}, u32[]{:S(2)}) collective-permute-start(f32[16,128]{1,0:T(8,128)S(1)} %get-tuple-element.45), channel_id=1, source_target_pairs={{0,4},{4,0},{1,5},{5,1},{2,6},{6,2},{3,7},{7,3},{8,12},{12,8},{9,1... | collective-permute-start | bytes 24584 | tf_op jit(solution)/shard_map/ppermute | solution.py:312
  29.9 5.3 %collective-permute-start.10 = (f32[16,128]{1,0:T(8,128)S(1)}, f32[16,128]{1,0:T(8,128)S(1)}, u32[]{:S(2)}, u32[]{:S(2)}) collective-permute-start(f32[16,128]{1,0:T(8,128)S(1)} %get-tuple-element.48), channel_id=1, source_target_pairs={{0,1},{1,0},{2,3},{3,2},{4,5},{5,4},{6,7},{7,6},{8,9},{9,8},{10,11... | collective-permute-start | bytes 24584 | tf_op jit(solution)/shard_map/ppermute | solution.py:312
  30.6 5.4 %collective-permute-start.11 = (f32[16,128]{1,0:T(8,128)S(1)}, f32[16,128]{1,0:T(8,128)S(1)}, u32[]{:S(2)}, u32[]{:S(2)}) collective-permute-start(f32[16,128]{1,0:T(8,128)S(1)} %get-tuple-element.49), channel_id=1, source_target_pairs={{0,3},{1,2},{2,1},{3,0},{4,7},{5,6},{6,5},{7,4},{8,11},{9,10},{10,... | collective-permute-start | bytes 24584 | tf_op jit(solution)/shard_map/ppermute | solution.py:312
  33.1 3.0 %collective-permute-start.12 = (f32[16,128]{1,0:T(8,128)S(1)}, f32[16,128]{1,0:T(8,128)S(1)}, u32[]{:S(2)}, u32[]{:S(2)}) collective-permute-start(f32[16,128]{1,0:T(8,128)S(1)} %get-tuple-element.50), channel_id=1, source_target_pairs={{0,8},{8,0},{16,24},{24,16},{1,9},{9,1},{17,25},{25,17},{2,10},{10... | collective-permute-start | bytes 24584 | tf_op jit(solution)/shard_map/ppermute | solution.py:312
  33.1 3.1 %collective-permute-start.13 = (f32[16,128]{1,0:T(8,128)S(1)}, f32[16,128]{1,0:T(8,128)S(1)}, u32[]{:S(2)}, u32[]{:S(2)}) collective-permute-start(f32[16,128]{1,0:T(8,128)S(1)} %get-tuple-element.51), channel_id=1, source_target_pairs={{0,24},{8,16},{16,8},{24,0},{1,25},{9,17},{17,9},{25,1},{2,26},{10... | collective-permute-start | bytes 24584 | tf_op jit(solution)/shard_map/ppermute | solution.py:312
  34.7 3.7 %collective-permute-start.14 = (f32[16,128]{1,0:T(8,128)S(1)}, f32[16,128]{1,0:T(8,128)S(1)}, u32[]{:S(2)}, u32[]{:S(2)}) collective-permute-start(f32[16,128]{1,0:T(8,128)S(1)} %get-tuple-element.52), channel_id=1, source_target_pairs={{0,4},{4,0},{1,5},{5,1},{2,6},{6,2},{3,7},{7,3},{8,12},{12,8},{9,1... | collective-permute-start | bytes 24584 | tf_op jit(solution)/shard_map/ppermute | solution.py:312
  39.6 3.7 %collective-permute-start.15 = (f32[16,128]{1,0:T(8,128)S(1)}, f32[16,128]{1,0:T(8,128)S(1)}, u32[]{:S(2)}, u32[]{:S(2)}) collective-permute-start(f32[16,128]{1,0:T(8,128)S(1)} %get-tuple-element.55), channel_id=1, source_target_pairs={{0,1},{1,0},{2,3},{3,2},{4,5},{5,4},{6,7},{7,6},{8,9},{9,8},{10,11... | collective-permute-start | bytes 24584 | tf_op jit(solution)/shard_map/ppermute | solution.py:312
  40.4 5.4 %collective-permute-start.16 = (f32[16,128]{1,0:T(8,128)S(1)}, f32[16,128]{1,0:T(8,128)S(1)}, u32[]{:S(2)}, u32[]{:S(2)}) collective-permute-start(f32[16,128]{1,0:T(8,128)S(1)} %get-tuple-element.56), channel_id=1, source_target_pairs={{0,3},{1,2},{2,1},{3,0},{4,7},{5,6},{6,5},{7,4},{8,11},{9,10},{10,... | collective-permute-start | bytes 24584 | tf_op jit(solution)/shard_map/ppermute | solution.py:312
  41.3 4.6 %collective-permute-start.17 = (f32[16,128]{1,0:T(8,128)S(1)}, f32[16,128]{1,0:T(8,128)S(1)}, u32[]{:S(2)}, u32[]{:S(2)}) collective-permute-start(f32[16,128]{1,0:T(8,128)S(1)} %get-tuple-element.57), channel_id=1, source_target_pairs={{0,8},{8,0},{16,24},{24,16},{1,9},{9,1},{17,25},{25,17},{2,10},{10... | collective-permute-start | bytes 24584 | tf_op jit(solution)/shard_map/ppermute | solution.py:312
  41.3 4.6 %collective-permute-start.18 = (f32[16,128]{1,0:T(8,128)S(1)}, f32[16,128]{1,0:T(8,128)S(1)}, u32[]{:S(2)}, u32[]{:S(2)}) collective-permute-start(f32[16,128]{1,0:T(8,128)S(1)} %get-tuple-element.58), channel_id=1, source_target_pairs={{0,24},{8,16},{16,8},{24,0},{1,25},{9,17},{17,9},{25,1},{2,26},{10... | collective-permute-start | bytes 24584 | tf_op jit(solution)/shard_map/ppermute | solution.py:312
  42.2 3.7 %collective-permute-start.19 = (f32[16,128]{1,0:T(8,128)S(1)}, f32[16,128]{1,0:T(8,128)S(1)}, u32[]{:S(2)}, u32[]{:S(2)}) collective-permute-start(f32[16,128]{1,0:T(8,128)S(1)} %get-tuple-element.59), channel_id=1, source_target_pairs={{0,4},{4,0},{1,5},{5,1},{2,6},{6,2},{3,7},{7,3},{8,12},{12,8},{9,1... | collective-permute-start | bytes 24584 | tf_op jit(solution)/shard_map/ppermute | solution.py:312

commit v2 on v1

--- a/solution.py
+++ b/solution.py
@@ -23,43 +23,48 @@
     return [(i, (i + 1) % count if i % 2 else (i - 1) % count) for i in range(count)]
 
 
-def to_rows(field):
-    var, ph, th, radial = field.shape
-    split = field.reshape(var, ph, th, radial // BLK, BLK).transpose(3, 1, 2, 0, 4)
-    return split.reshape(-1, var * BLK)
-
-
-def from_rows(rows, shape):
-    var, ph, th, radial = shape
-    split = rows.reshape(radial // BLK, ph, th, var, BLK).transpose(3, 1, 2, 0, 4)
-    return split.reshape(shape)
-
-
-def apply_blocks(field, inverse_ref, ph, th):
-    rounded = field.astype(jnp.bfloat16)
-    across = 2 * GROUP
-    row = lax.broadcasted_iota(jnp.int32, (across, LANES), 0) % GROUP
-    parts = []
-    for first in range(0, field.shape[0], across):
-        vectors = rounded[first : first + across]
-        spread = jnp.concatenate(
-            [jnp.where(row == m, vectors, jnp.zeros_like(vectors)) for m in range(GROUP)], axis=1
+def to_rows(native_ref):
+    var, ph, th, radial = native_ref.shape
+    planes = [
+        jnp.concatenate([native_ref[v, p] for p in range(ph)], axis=0) for v in range(var)
+    ]
+    return jnp.concatenate(
+        [
+            jnp.concatenate([plane[:, r : r + BLK] for plane in planes], axis=1)
+            for r in range(0, radial, BLK)
+        ],
+        axis=0,
+    )
+
+
+def from_rows(rows, native_ref):
+    var, ph, th, radial = native_ref.shape
+    per = ph * th
+    for v in range(var):
+        plane = jnp.concatenate(
+            [rows[b * per : (b + 1) * per, v * BLK : (v + 1) * BLK] for b in range(radial // BLK)], axis=1
         )
-        halves = []
-        for half in range(2):
-            blocks = []
-            for m in range(GROUP):
-                index = first + half * GROUP + m
-                b, place = divmod(index, ph * th)
-                p, t = divmod(place, th)
-                blocks.append(inverse_ref[p, t, b])
-            halves.append(jnp.concatenate(blocks, axis=1))
-        matrix = jnp.concatenate(halves, axis=0)
-        out = lax.dot_general(
-            spread, matrix, (((1,), (1,)), ((), ())), preferred_element_type=jnp.float32
-        )
-        parts += [out[:GROUP, :LANES], out[GROUP:, LANES:]]
-    return jnp.concatenate(parts, axis=0)
+        for p in range(ph):
+            native_ref[v, p] = plane[p * th : (p + 1) * th]
+
+
+def apply_blocks(vectors, turned_ref, first):
+    rounded = vectors.astype(jnp.bfloat16)
+    row = lax.broadcasted_iota(jnp.int32, rounded.shape, 0) % GROUP
+    spread = jnp.concatenate(
+        [jnp.where(row == m, rounded, jnp.zeros_like(rounded)) for m in range(GROUP)], axis=1
+    )
+    halves = [
+        jnp.concatenate([turned_ref[first + half * GROUP + m] for m in range(GROUP)], axis=0) for half in range(2)
+    ]
+    out = jnp.dot(spread, jnp.concatenate(halves, axis=1), preferred_element_type=jnp.float32)
+    return jnp.concatenate([out[:GROUP, :LANES], out[GROUP:, LANES:]], axis=0)
+
+
+def apply_all(field, turned_ref):
+    return jnp.concatenate(
+        [apply_blocks(field[i : i + 2 * GROUP], turned_ref, i) for i in range(0, field.shape[0], 2 * GROUP)], axis=0
+    )
 
 
 def pack_faces(field, d_ref, out_refs, flags_ref, ph, th):
@@ -146,42 +151,90 @@
     return [next(refs) if there else None for there in present]
 
 
-def first_kernel(ph, th, present, flags_ref, krylov_ref, inverse_ref, d_ref, *faces):
-    direction = apply_blocks(krylov_ref[...], inverse_ref, ph, th)
-    d_ref[...] = direction
-    pack_faces(direction, d_ref, fill(faces, present), flags_ref, ph, th)
-
-
-def step_kernel(ph, th, present, flags_ref, krylov_ref, last_ref, conduct_ref, diagonal_ref, mixing_ref, inverse_ref, *rest):
+def first_kernel(ph, th, present, flags_ref, right_ref, conduct_ref, coupling_ref, codes_ref, inverse_ref, *rest):
+    n = sum(present)
+    krylov_ref, conducts_ref, diagonal_ref, mixing_ref, turned_ref, d_ref = rest[:6]
+    faces = fill(rest[6 : 6 + n], present)
+    right, conduct, coupling, codes, blocks, sems = rest[6 + n :]
+    per = ph * th
+    rows = d_ref.shape[0]
+    nb = rows // per
+    pairs = [(right_ref, right), (coupling_ref, coupling), (codes_ref, codes)]
+    pairs += [(inverse_ref.at[:, :, b], blocks.at[b]) for b in range(nb)] + [(conduct_ref, conduct)]
+    copies = [pltpu.make_async_copy(a, b, sems.at[i]) for i, (a, b) in enumerate(pairs)]
+    for copy in copies:
+        copy.start()
+
+    copies[0].wait()
+    krylov = to_rows(right)
+    krylov_ref[...] = krylov
+    copies[1].wait()
+    lane = lax.broadcasted_iota(jnp.int32, (1, LANES), 1)
+    for m in range(VARS):
+        line = jnp.zeros((1, LANES), jnp.float32)
+        for k in range(VARS):
+            line = jnp.where(lane // BLK == k, coupling[k, (k + m) % VARS], line)
+        mixing_ref[m : m + 1, :] = line
+    copies[2].wait()
+    cell = lax.broadcasted_iota(jnp.int32, (per, LANES), 1) % BLK
+    row = lax.broadcasted_iota(jnp.int32, (per, LANES), 0)
+    diagonal_ref[...] = jnp.full_like(diagonal_ref, 6.0)
+    for side, (edge, first, has) in enumerate(((0, 0, flags_ref[3]), (BLK - 1, rows - per, flags_ref[4]))):
+        factor = jnp.zeros((per, LANES), jnp.float32)
+        for i in range(per):
+            code = codes[side, i // th, i % th]
+            value = jnp.where(code == 1, 1.0, jnp.where(code == 2, -1.0, 0.0))
+            factor = jnp.where(row == i, value, factor)
+        factor = jnp.where((cell == edge) & (has == 0), factor, 0.0)
+        diagonal_ref[first : first + per, :] -= factor
+    for b in range(nb):
+        copies[3 + b].wait()
+        for i in range(per):
+            turned_ref[b * per + i] = blocks[b, i // th, i % th].T
+        for i in range(b * per, (b + 1) * per, 2 * GROUP):
+            d_ref[i : i + 2 * GROUP, :] = apply_blocks(krylov[i : i + 2 * GROUP], turned_ref, i)
+    pack_faces(d_ref[...], d_ref, faces, flags_ref, ph, th)
+    copies[3 + nb].wait()
+    conducts_ref[...] = to_rows(conduct)
+
+
+def local_kernel(ph, th, krylov_ref, last_ref, conduct_ref, diagonal_ref, mixing_ref, out_ref):
+    out_ref[...] = local_part(
+        last_ref[...], last_ref, krylov_ref[...], conduct_ref[...], diagonal_ref[...], mixing_ref, ph, th
+    )
+
+
+def gram_rows(left, right):
+    lines = [jnp.sum(a * b, axis=0, keepdims=True) for a, b in zip(left, right)]
+    return lines + [jnp.zeros_like(lines[0])] * (-len(lines) % 8)
+
+
+def gram_kernel(*refs):
+    basis = [ref[...] for ref in refs[:-1]]
+    left = [basis[i] for i in range(S) for _ in range(i + 1)]
+    right = [basis[j] for i in range(S) for j in range(i + 1)]
+    refs[-1][...] = jnp.concatenate(gram_rows(left, right), axis=0)
+
+
+def step_kernel(ph, th, present, flags_ref, local_ref, conduct_ref, turned_ref, *rest):
     n = sum(present)
     in_faces, (next_ref, d_ref), out_faces, (halo_ref,) = rest[:n], rest[n : n + 2], rest[n + 2 : 2 * n + 2], rest[2 * n + 2 :]
-    conduct = conduct_ref[...]
-    local = local_part(last_ref[...], last_ref, krylov_ref[...], conduct, diagonal_ref[...], mixing_ref, ph, th)
     halo = add_faces(halo_ref, fill(in_faces, present), flags_ref, ph, th)
-    krylov = local - conduct * halo
+    krylov = local_ref[...] - conduct_ref[...] * halo
     next_ref[...] = krylov
-    direction = apply_blocks(krylov, inverse_ref, ph, th)
+    direction = apply_all(krylov, turned_ref)
     d_ref[...] = direction
     pack_faces(direction, d_ref, fill(out_faces, present), flags_ref, ph, th)
 
 
-def last_kernel(ph, th, present, flags_ref, krylov_ref, last_ref, conduct_ref, diagonal_ref, mixing_ref, *rest):
+def last_kernel(ph, th, present, flags_ref, local_ref, conduct_ref, partial_ref, *rest):
     n = sum(present)
-    older, in_faces, (next_ref, gram_ref), (halo_ref,) = rest[: S - 1], rest[S - 1 : S - 1 + n], rest[S - 1 + n : S + 1 + n], rest[S + 1 + n :]
-    conduct = conduct_ref[...]
-    newest = krylov_ref[...]
-    local = local_part(last_ref[...], last_ref, newest, conduct, diagonal_ref[...], mixing_ref, ph, th)
+    older, in_faces, (next_ref, gram_ref), (halo_ref,) = rest[:S], rest[S : S + n], rest[S + n : S + 2 + n], rest[S + 2 + n :]
     halo = add_faces(halo_ref, fill(in_faces, present), flags_ref, ph, th)
-    final = local - conduct * halo
+    final = local_ref[...] - conduct_ref[...] * halo
     next_ref[...] = final
-    basis = [ref[...] for ref in older] + [newest, final]
-    sums = []
-    for i in range(S + 1):
-        for j in range(i + 1):
-            product = basis[i] * basis[j]
-            sums.append(jnp.sum(product, axis=0, keepdims=True))
-    sums += [jnp.zeros_like(sums[0])] * (-len(sums) % 8)
-    stacked = jnp.concatenate(sums, axis=0)
+    basis = [ref[...] for ref in older] + [final]
+    stacked = jnp.concatenate([partial_ref[...]] + gram_rows([final] * (S + 1), basis), axis=0)
     each = jnp.sum(stacked, axis=1, keepdims=True)
     lane = lax.broadcasted_iota(jnp.int32, stacked.shape, 1)
     row = lax.broadcasted_iota(jnp.int32, stacked.shape, 0)
@@ -238,38 +291,50 @@
     return weights
 
 
-def combine_kernel(gram_ref, *refs):
-    krylov, directions, (correction_ref, residual_ref) = refs[: S + 1], refs[S + 1 : 2 * S + 1], refs[2 * S + 1 :]
+def combine_kernel(partial_rows, gram_ref, *refs):
+    krylov, directions, rest = refs[: S + 1], refs[S + 1 : 2 * S + 1], refs[2 * S + 1 :]
+    correction_ref, residual_ref, correction, residual, sems = rest
     line = jnp.sum(gram_ref[...], axis=0, keepdims=True)
     products, place = [], 0
     for i in range(S + 1):
         products.append([])
+        place = partial_rows if i == S else place
         for j in range(i + 1):
             products[i].append(line[:, place : place + 1])
             place += 1
     weights = small_solve(products)
+    total = weights[0] * directions[0][...]
+    for j in range(1, S):
+        total = total + weights[j] * directions[j][...]
+    from_rows(total, correction)
+    first = pltpu.make_async_copy(correction, correction_ref, sems.at[0])
+    first.start()
     basis = [ref[...] for ref in krylov]
-    correction = jnp.zeros_like(basis[0])
-    residual = basis[0]
+    total = basis[0]
     for j in range(S):
-        correction = correction + weights[j] * directions[j][...]
-        residual = residual - weights[j] * (basis[j + 1] + basis[j])
-    correction_ref[...] = correction
-    residual_ref[...] = residual
-
-
-def call(kernel, outs, scratch, *args):
-    specs = [
-        pl.BlockSpec(memory_space=pltpu.SMEM if a.dtype == jnp.int32 else pltpu.VMEM) for a in args
-    ]
+        total = total - weights[j] * (basis[j + 1] + basis[j])
+    from_rows(total, residual)
+    second = pltpu.make_async_copy(residual, residual_ref, sems.at[1])
+    second.start()
+    first.wait()
+    second.wait()
+
+
+def call(kernel, outs, scratch, *args, stay=False):
+    def space(a):
+        if a.dtype == jnp.int32 and a.ndim == 1:
+            return pltpu.SMEM
+        return pltpu.HBM if stay and (a.ndim > 3 or a.shape[-1] != LANES) else pltpu.VMEM
+
+    placed = [pltpu.with_memory_space_constraint(a, pltpu.HBM) if space(a) == pltpu.HBM else a for a in args]
     return pl.pallas_call(
         kernel,
         out_shape=outs,
-        in_specs=specs,
-        out_specs=[pl.BlockSpec(memory_space=pltpu.VMEM)] * len(outs),
+        in_specs=[pl.BlockSpec(memory_space=space(a)) for a in args],
+        out_specs=[pl.BlockSpec(memory_space=space(a)) for a in outs],
         scratch_shapes=scratch,
         compiler_params=pltpu.CompilerParams(vmem_limit_bytes=VMEM_LIMIT),
-    )(*args)
+    )(*placed)
 
 
 def local(right_side, conduct, coupling, inverse, face_codes):
@@ -283,17 +348,6 @@
     flags = jnp.stack(
         [ph_at % 2, row_at % 2, th_at % 2, row_at > 0, row_at < row_n - 1, th_at > 0, th_at < th_n - 1]
     ).astype(jnp.int32)
-
-    factor = (face_codes == 1).astype(jnp.float32) - (face_codes == 2).astype(jnp.float32)
-    factor = factor.reshape(2, 1, per, 1)
-    block = lax.broadcasted_iota(jnp.int32, (nb, per, LANES), 0)
-    cell = lax.broadcasted_iota(jnp.int32, (nb, per, LANES), 2) % BLK
-    ghost = jnp.where((block == 0) & (cell == 0) & (row_at == 0), factor[0], 0.0)
-    ghost += jnp.where((block == nb - 1) & (cell == BLK - 1) & (row_at == row_n - 1), factor[1], 0.0)
-    diagonal = (6.0 - ghost).reshape(rows, LANES)
-    mixing = jnp.stack([jnp.diagonal(jnp.roll(coupling, -m, 1)) for m in range(VARS)])
-    mixing = jnp.repeat(mixing, BLK, axis=1)
-    conducts = to_rows(conduct)
 
     def shape(n):
         return jax.ShapeDtypeStruct((n, LANES), jnp.float32)
@@ -312,34 +366,58 @@
             taken[i] = lax.ppermute(sent[i], axis, pairs(lax.axis_size(axis)))
         return taken
 
-    krylov = [to_rows(right_side)]
-    direction, *sent = call(
-        functools.partial(first_kernel, ph, th, present), [whole] + faces, [], flags, krylov[0], inverse
-    )
-    directions = [direction]
+    field = pltpu.VMEM(right_side.shape, jnp.float32)
+    start, conducts, diagonal, mixing, turned, direction, *sent = call(
+        functools.partial(first_kernel, ph, th, present),
+        [whole, whole, whole, shape(VARS), jax.ShapeDtypeStruct((rows, LANES, LANES), jnp.bfloat16), whole] + faces,
+        [
+            field,
+            field,
+            pltpu.SMEM(coupling.shape, jnp.float32),
+            pltpu.SMEM(face_codes.shape, jnp.int32),
+            pltpu.VMEM((nb, ph, th, LANES, LANES), jnp.bfloat16),
+            pltpu.SemaphoreType.DMA((nb + 4,)),
+        ],
+        flags, right_side, conduct, coupling, face_codes, inverse,
+        stay=True,
+    )
+    krylov, directions = [start], [direction]
     halo = [pltpu.VMEM((rows, LANES), jnp.float32)]
-    for _ in range(S - 1):
+    for step in range(S):
         taken = exchange(sent)
-        following, direction, *sent = call(
-            functools.partial(step_kernel, ph, th, present),
-            [whole, whole] + faces,
-            halo,
-            flags, krylov[-1], directions[-1], conducts, diagonal, mixing, inverse, *taken,
+        (beside,) = call(
+            functools.partial(local_kernel, ph, th), [whole], [], krylov[-1], directions[-1], conducts, diagonal, mixing
         )
-        krylov.append(following)
-        directions.append(direction)
-    taken = exchange(sent)
-    devices = row_n * th_n * ph_n
+        if step < S - 1:
+            following, direction, *sent = call(
+                functools.partial(step_kernel, ph, th, present),
+                [whole, whole] + faces,
+                halo,
+                flags, beside, conducts, turned, *taken,
+            )
+            krylov.append(following)
+            directions.append(direction)
+    partial_rows = S * (S + 1) // 2
+    partial_rows += -partial_rows % 8
+    (partial,) = call(gram_kernel, [shape(partial_rows)], [], *krylov)
     following, gram = call(
         functools.partial(last_kernel, ph, th, present),
-        [whole, shape(devices)],
+        [whole, shape(row_n * th_n * ph_n)],
         halo,
-        flags, krylov[-1], directions[-1], conducts, diagonal, mixing, *krylov[:-1], *taken,
+        flags, beside, conducts, partial, *krylov, *taken,
     )
     krylov.append(following)
     gram = lax.all_to_all(gram, ("row", "th", "ph"), 0, 0, tiled=True)
-    correction, residual = call(combine_kernel, [whole, whole], [], gram, *krylov, *directions)
-    return from_rows(correction, right_side.shape), from_rows(residual, right_side.shape)
+    native = jax.ShapeDtypeStruct(right_side.shape, jnp.float32)
+    return tuple(
+        call(
+            functools.partial(combine_kernel, partial_rows),
+            [native, native],
+            [field, field, pltpu.SemaphoreType.DMA((2,))],
+            gram, *krylov, *directions,
+            stay=True,
+        )
+    )
 
 
 def solution(mesh):

time: 60.9 us -> 53.1 us (0.87)
  local copies, waits for them, and re-layouts: 12.1 us -> 0.09 us
  starting transfers between devices: 19.8 us -> 22.7 us
  Pallas kernels: 6.89 us -> 9.51 us
  waiting for transfers between devices: 9.7 us -> 7.99 us
  blocking collectives: 10.9 us -> 11.8 us
    gather x8 -> x0, local copies, waits for them, and re-layouts: 5.08 us -> none  [local(): jnp.diagonal(jnp.roll(coupling, -m, 1))]
    reshape x11 -> x0, local copies, waits for them, and re-layouts: 3.72 us -> none  [the longest x2 1.62 us: from_rows(): return split.reshape(shape)]
    ppermute x20, starting transfers between devices: 19.8 us -> 22.7 us  [exchange(): taken[i] = lax.ppermute(sent[i], axis, pairs(lax.axis_size(axis)))]
    pallas_call x6 -> x11, Pallas kernels: 6.89 us -> 9.51 us  [call(): pl.pallas_call(kernel, out_shape=outs, in_specs=[pl.BlockSpec(memory_spac...]
    ppermute x20, waiting for transfers between devices: 9.7 us -> 7.99 us  [exchange(): taken[i] = lax.ppermute(sent[i], axis, pairs(lax.axis_size(axis)))]
    unnamed x10 -> x0, local copies, waits for them, and re-layouts: 1.61 us -> none
    all_to_all x1, blocking collectives: 10.9 us -> 11.8 us  [local(): gram = lax.all_to_all(gram, ('row', 'th', 'ph'), 0, 0, tiled=True)]
  transfers between devices with their start and end apart: 20 -> 20, of which waited for: 7 -> 4; matrix products, arithmetic and copies ran while one was open for 12% -> 0% of each run, Pallas kernels for 0% -> 1%
where the time goes in v2:
time: 53.1 us; the launch traced here: 53 us
  starting transfers between devices  22.7 us (43%)
  blocking collectives  11.8 us (22%)
  Pallas kernels  9.51 us (18%)
  waiting for transfers between devices  7.99 us (15%)
  between operations  0.8 us (2%)
    ppermute x20, starting transfers between devices, exchange(): taken[i] = lax.ppermute(sent[i], axis, pairs(lax.axis_size(axis)))  22.7 us
    all_to_all x1, blocking collectives, local(): gram = lax.all_to_all(gram, ('row', 'th', 'ph'), 0, 0, tiled=True)  11.8 us
    pallas_call x11, Pallas kernels, call(): pl.pallas_call(kernel, out_shape=outs, in_specs=[pl.BlockSpec(memory_spac...  9.51 us
    ppermute x20, waiting for transfers between devices, exchange(): taken[i] = lax.ppermute(sent[i], axis, pairs(lax.axis_size(axis)))  7.99 us
  transfers between devices with their start and end apart: 20, of which 4 were waited for; matrix products, arithmetic and copies ran while one was open for 0% of the time, Pallas kernels for 1%

profile of v2, /device:TPU:0, one launch (start us, length us, event | category | flops | bytes accessed | tf_op | source)
XLA Modules:
  0.0 53.0 jit_solution(3207012715444445243)
XLA Ops:
  0.7 0.1 stack.47.flags_ref
  0.7 3.4 %shard_map.68 = (f32[64,128]{1,0:T(8,128)S(1)}, f32[64,128]{1,0:T(8,128)S(1)}, f32[64,128]{1,0:T(8,128)S(1)}, f32[8,128]{1,0:T(8,128)S(1)}, bf16[64,128,128]{2,1...) custom-call(s32[7]{0:T(128)S(1)} %stack.47.flags_ref, ...), custom_call_target="tpu_custom_call" | custom-call | tf_op jit(solution)/shard_map/pallas_call | solution.py:330
  4.1 3.1 %collective-permute-start = (f32[16,128]{1,0:T(8,128)S(1)}, f32[16,128]{1,0:T(8,128)S(1)}, u32[]{:S(2)}, u32[]{:S(2)}) collective-permute-start(f32[16,128]{1,0:T(8,128)S(1)} %get-tuple-element.42), channel_id=1, source_target_pairs={{0,1},{1,0},{2,3},{3,2},{4,5},{5,4},{6,7},{7,6},{8,9},{9,8},{10,11... | collective-permute-start | bytes 24584 | tf_op jit(solution)/shard_map/ppermute | solution.py:366
  7.2 2.5 %collective-permute-start.1 = (f32[16,128]{1,0:T(8,128)S(1)}, f32[16,128]{1,0:T(8,128)S(1)}, u32[]{:S(2)}, u32[]{:S(2)}) collective-permute-start(f32[16,128]{1,0:T(8,128)S(1)} %get-tuple-element.43), channel_id=1, source_target_pairs={{0,3},{1,2},{2,1},{3,0},{4,7},{5,6},{6,5},{7,4},{8,11},{9,10},{10,... | collective-permute-start | bytes 24584 | tf_op jit(solution)/shard_map/ppermute | solution.py:366
  9.7 0.0 collective-permute-start.2
  9.7 1.6 %collective-permute-start.3 = (f32[16,128]{1,0:T(8,128)S(1)}, f32[16,128]{1,0:T(8,128)S(1)}, u32[]{:S(2)}, u32[]{:S(2)}) collective-permute-start(f32[16,128]{1,0:T(8,128)S(1)} %get-tuple-element.45), channel_id=1, source_target_pairs={{0,24},{8,16},{16,8},{24,0},{1,25},{9,17},{17,9},{25,1},{2,26},{10... | collective-permute-start | bytes 24584 | tf_op jit(solution)/shard_map/ppermute | solution.py:366
  11.3 1.5 %collective-permute-start.4 = (f32[16,128]{1,0:T(8,128)S(1)}, f32[16,128]{1,0:T(8,128)S(1)}, u32[]{:S(2)}, u32[]{:S(2)}) collective-permute-start(f32[16,128]{1,0:T(8,128)S(1)} %get-tuple-element.46), channel_id=1, source_target_pairs={{0,4},{4,0},{1,5},{5,1},{2,6},{6,2},{3,7},{7,3},{8,12},{12,8},{9,1... | collective-permute-start | bytes 24584 | tf_op jit(solution)/shard_map/ppermute | solution.py:366
  12.8 0.2 shard_map.69.local_ref
  13.0 0.0 collective-permute-done.rest_0_
  13.0 0.0 collective-permute-done.1.rest_1_
  13.0 0.0 collective-permute-done.2.rest_2_
  13.0 0.0 collective-permute-done.3.rest_3_
  13.0 1.9 %collective-permute-done.4.rest_4_ = f32[16,128]{1,0:T(8,128)S(1)} collective-permute-done((f32[16,128]{1,0:T(8,128)S(1)}, f32[16,128]{1,0:T(8,128)S(1)}, u32[]{:S(2)}, u32[]{:S(2)}) %collective-permute-start.4) | collective-permute-done | bytes 8224 | tf_op jit(solution)/shard_map/ppermute | solution.py:366
  14.9 1.0 %shard_map.70 = (f32[64,128]{1,0:T(8,128)S(1)}, f32[64,128]{1,0:T(8,128)S(1)}, f32[16,128]{1,0:T(8,128)S(1)}, f32[16,128]{1,0:T(8,128)S(1)}, f32[16,128]{1,0:T(8...) custom-call(s32[7]{0:T(128)S(1)} %stack.47.flags_ref, f32[64,128]{1,0:T(8,128)S(1)} %shard_map.69.local_ref, ...), custom_call_target="tpu_custom_call" | custom-call | tf_op jit(solution)/shard_map/pallas_call | solution.py:330
  15.9 0.7 %collective-permute-start.5 = (f32[16,128]{1,0:T(8,128)S(1)}, f32[16,128]{1,0:T(8,128)S(1)}, u32[]{:S(2)}, u32[]{:S(2)}) collective-permute-start(f32[16,128]{1,0:T(8,128)S(1)} %get-tuple-element.49), channel_id=1, source_target_pairs={{0,1},{1,0},{2,3},{3,2},{4,5},{5,4},{6,7},{7,6},{8,9},{9,8},{10,11... | collective-permute-start | bytes 24584 | tf_op jit(solution)/shard_map/ppermute | solution.py:366
  16.6 0.9 %collective-permute-start.6 = (f32[16,128]{1,0:T(8,128)S(1)}, f32[16,128]{1,0:T(8,128)S(1)}, u32[]{:S(2)}, u32[]{:S(2)}) collective-permute-start(f32[16,128]{1,0:T(8,128)S(1)} %get-tuple-element.50), channel_id=1, source_target_pairs={{0,3},{1,2},{2,1},{3,0},{4,7},{5,6},{6,5},{7,4},{8,11},{9,10},{10,... | collective-permute-start | bytes 24584 | tf_op jit(solution)/shard_map/ppermute | solution.py:366
  17.5 0.0 collective-permute-start.7
  17.5 0.6 %collective-permute-start.8 = (f32[16,128]{1,0:T(8,128)S(1)}, f32[16,128]{1,0:T(8,128)S(1)}, u32[]{:S(2)}, u32[]{:S(2)}) collective-permute-start(f32[16,128]{1,0:T(8,128)S(1)} %get-tuple-element.52), channel_id=1, source_target_pairs={{0,24},{8,16},{16,8},{24,0},{1,25},{9,17},{17,9},{25,1},{2,26},{10... | collective-permute-start | bytes 24584 | tf_op jit(solution)/shard_map/ppermute | solution.py:366
  18.2 1.5 %collective-permute-start.9 = (f32[16,128]{1,0:T(8,128)S(1)}, f32[16,128]{1,0:T(8,128)S(1)}, u32[]{:S(2)}, u32[]{:S(2)}) collective-permute-start(f32[16,128]{1,0:T(8,128)S(1)} %get-tuple-element.53), channel_id=1, source_target_pairs={{0,4},{4,0},{1,5},{5,1},{2,6},{6,2},{3,7},{7,3},{8,12},{12,8},{9,1... | collective-permute-start | bytes 24584 | tf_op jit(solution)/shard_map/ppermute | solution.py:366
  19.7 0.2 shard_map.71.local_ref
  19.9 0.0 collective-permute-done.5.rest_0_
  19.9 2.2 %collective-permute-done.6.rest_1_ = f32[16,128]{1,0:T(8,128)S(1)} collective-permute-done((f32[16,128]{1,0:T(8,128)S(1)}, f32[16,128]{1,0:T(8,128)S(1)}, u32[]{:S(2)}, u32[]{:S(2)}) %collective-permute-start.6) | collective-permute-done | bytes 8224 | tf_op jit(solution)/shard_map/ppermute | solution.py:366
  22.1 0.0 collective-permute-done.7.rest_2_
  22.1 0.0 collective-permute-done.8.rest_3_
  22.1 0.0 collective-permute-done.9.rest_4_
  22.1 1.0 %shard_map.72 = (f32[64,128]{1,0:T(8,128)S(1)}, f32[64,128]{1,0:T(8,128)S(1)}, f32[16,128]{1,0:T(8,128)S(1)}, f32[16,128]{1,0:T(8,128)S(1)}, f32[16,128]{1,0:T(8...) custom-call(s32[7]{0:T(128)S(1)} %stack.47.flags_ref, f32[64,128]{1,0:T(8,128)S(1)} %shard_map.71.local_ref, ...), custom_call_target="tpu_custom_call" | custom-call | tf_op jit(solution)/shard_map/pallas_call | solution.py:330
  23.1 0.7 %collective-permute-start.10 = (f32[16,128]{1,0:T(8,128)S(1)}, f32[16,128]{1,0:T(8,128)S(1)}, u32[]{:S(2)}, u32[]{:S(2)}) collective-permute-start(f32[16,128]{1,0:T(8,128)S(1)} %get-tuple-element.56), channel_id=1, source_target_pairs={{0,1},{1,0},{2,3},{3,2},{4,5},{5,4},{6,7},{7,6},{8,9},{9,8},{10,11... | collective-permute-start | bytes 24584 | tf_op jit(solution)/shard_map/ppermute | solution.py:366
  23.7 2.5 %collective-permute-start.11 = (f32[16,128]{1,0:T(8,128)S(1)}, f32[16,128]{1,0:T(8,128)S(1)}, u32[]{:S(2)}, u32[]{:S(2)}) collective-permute-start(f32[16,128]{1,0:T(8,128)S(1)} %get-tuple-element.57), channel_id=1, source_target_pairs={{0,3},{1,2},{2,1},{3,0},{4,7},{5,6},{6,5},{7,4},{8,11},{9,10},{10,... | collective-permute-start | bytes 24584 | tf_op jit(solution)/shard_map/ppermute | solution.py:366
  26.2 0.0 collective-permute-start.12
  26.2 1.6 %collective-permute-start.13 = (f32[16,128]{1,0:T(8,128)S(1)}, f32[16,128]{1,0:T(8,128)S(1)}, u32[]{:S(2)}, u32[]{:S(2)}) collective-permute-start(f32[16,128]{1,0:T(8,128)S(1)} %get-tuple-element.59), channel_id=1, source_target_pairs={{0,24},{8,16},{16,8},{24,0},{1,25},{9,17},{17,9},{25,1},{2,26},{10... | collective-permute-start | bytes 24584 | tf_op jit(solution)/shard_map/ppermute | solution.py:366
  27.8 1.5 %collective-permute-start.14 = (f32[16,128]{1,0:T(8,128)S(1)}, f32[16,128]{1,0:T(8,128)S(1)}, u32[]{:S(2)}, u32[]{:S(2)}) collective-permute-start(f32[16,128]{1,0:T(8,128)S(1)} %get-tuple-element.60), channel_id=1, source_target_pairs={{0,4},{4,0},{1,5},{5,1},{2,6},{6,2},{3,7},{7,3},{8,12},{12,8},{9,1... | collective-permute-start | bytes 24584 | tf_op jit(solution)/shard_map/ppermute | solution.py:366
  29.3 0.2 shard_map.73.local_ref
  29.5 0.0 collective-permute-done.10.rest_0_
  29.5 0.0 collective-permute-done.11.rest_1_
  29.5 0.0 collective-permute-done.12.rest_2_
  29.5 0.0 collective-permute-done.13.rest_3_
  29.6 1.9 %collective-permute-done.14.rest_4_ = f32[16,128]{1,0:T(8,128)S(1)} collective-permute-done((f32[16,128]{1,0:T(8,128)S(1)}, f32[16,128]{1,0:T(8,128)S(1)}, u32[]{:S(2)}, u32[]{:S(2)}) %collective-permute-start.14) | collective-permute-done | bytes 8224 | tf_op jit(solution)/shard_map/ppermute | solution.py:366
  31.5 1.0 %shard_map.74 = (f32[64,128]{1,0:T(8,128)S(1)}, f32[64,128]{1,0:T(8,128)S(1)}, f32[16,128]{1,0:T(8,128)S(1)}, f32[16,128]{1,0:T(8,128)S(1)}, f32[16,128]{1,0:T(8...) custom-call(s32[7]{0:T(128)S(1)} %stack.47.flags_ref, f32[64,128]{1,0:T(8,128)S(1)} %shard_map.73.local_ref, ...), custom_call_target="tpu_custom_call" | custom-call | tf_op jit(solution)/shard_map/pallas_call | solution.py:330
  32.5 0.7 %collective-permute-start.15 = (f32[16,128]{1,0:T(8,128)S(1)}, f32[16,128]{1,0:T(8,128)S(1)}, u32[]{:S(2)}, u32[]{:S(2)}) collective-permute-start(f32[16,128]{1,0:T(8,128)S(1)} %get-tuple-element.63), channel_id=1, source_target_pairs={{0,1},{1,0},{2,3},{3,2},{4,5},{5,4},{6,7},{7,6},{8,9},{9,8},{10,11... | collective-permute-start | bytes 24584 | tf_op jit(solution)/shard_map/ppermute | solution.py:366
  33.2 0.9 %collective-permute-start.16 = (f32[16,128]{1,0:T(8,128)S(1)}, f32[16,128]{1,0:T(8,128)S(1)}, u32[]{:S(2)}, u32[]{:S(2)}) collective-permute-start(f32[16,128]{1,0:T(8,128)S(1)} %get-tuple-element.64), channel_id=1, source_target_pairs={{0,3},{1,2},{2,1},{3,0},{4,7},{5,6},{6,5},{7,4},{8,11},{9,10},{10,... | collective-permute-start | bytes 24584 | tf_op jit(solution)/shard_map/ppermute | solution.py:366
  34.1 0.0 collective-permute-start.17
  34.1 0.9 %collective-permute-start.18 = (f32[16,128]{1,0:T(8,128)S(1)}, f32[16,128]{1,0:T(8,128)S(1)}, u32[]{:S(2)}, u32[]{:S(2)}) collective-permute-start(f32[16,128]{1,0:T(8,128)S(1)} %get-tuple-element.66), channel_id=1, source_target_pairs={{0,24},{8,16},{16,8},{24,0},{1,25},{9,17},{17,9},{25,1},{2,26},{10... | collective-permute-start | bytes 24584 | tf_op jit(solution)/shard_map/ppermute | solution.py:366
  35.0 1.5 %collective-permute-start.19 = (f32[16,128]{1,0:T(8,128)S(1)}, f32[16,128]{1,0:T(8,128)S(1)}, u32[]{:S(2)}, u32[]{:S(2)}) collective-permute-start(f32[16,128]{1,0:T(8,128)S(1)} %get-tuple-element.67), channel_id=1, source_target_pairs={{0,4},{4,0},{1,5},{5,1},{2,6},{6,2},{3,7},{7,3},{8,12},{12,8},{9,1... | collective-permute-start | bytes 24584 | tf_op jit(solution)/shard_map/ppermute | solution.py:366
  36.6 0.2 shard_map.75.local_ref
  36.7 0.0 collective-permute-done.15.rest_4_
  36.7 1.9 %collective-permute-done.16.rest_5_ = f32[16,128]{1,0:T(8,128)S(1)} collective-permute-done((f32[16,128]{1,0:T(8,128)S(1)}, f32[16,128]{1,0:T(8,128)S(1)}, u32[]{:S(2)}, u32[]{:S(2)}) %collective-permute-start.16) | collective-permute-done | bytes 8224 | tf_op jit(solution)/shard_map/ppermute | solution.py:366
  38.6 0.0 collective-permute-done.17.rest_6_
  38.6 0.0 collective-permute-done.18.rest_7_
  38.6 0.0 collective-permute-done.19.rest_8_
  38.6 0.7 %shard_map.77 = (f32[64,128]{1,0:T(8,128)S(1)}, f32[32,128]{1,0:T(8,128)S(1)}) custom-call(s32[7]{0:T(128)S(1)} %stack.47.flags_ref, f32[64,128]{1,0:T(8,128)S(1)} %shard_map.75.local_ref, f32[64,128]{1,0:T(8,128)S(1)} %get-tuple-element.38.conduct_ref, f32[16,128]{1,0:T(8,128)S(1)} %shard_map.76.partial_ref, ...), custom_call_target="tpu_custom_call" | custom-call | tf_op jit(solution)/shard_map/pallas_call | solution.py:330
  39.3 11.8 %all_to_all.11 = f32[32,1,128]{2,1,0:T(1,128)S(1)} all-to-all(f32[32,1,128]{2,1,0:T(1,128)S(1)} %bitcast.12), channel_id=1, replica_groups=mesh['row'=4,'th'=2,'ph'=4] {'row','th','ph'}, dimensions={0} | all-to-all | bytes 32768 | tf_op jit(solution)/shard_map/all_to_all | solution.py:410
  51.1 1.8 %shard_map.78 = (f32[8,4,4,64]{3,2,1,0:T(4,128)}, f32[8,4,4,64]{3,2,1,0:T(4,128)}) custom-call(f32[32,128]{1,0:T(8,128)S(1)} %bitcast.11, f32[64,128]{1,0:T(8,128)S(1)} %get-tuple-element.36.krylov_ref.refs_0_.rest_0_, f32[64,128]{1,0:T(8,128)S(1)} %get-tuple-element.47.krylov_ref.refs_1_.rest_1_, ...), custom_call_target="tpu_custom_call" | custom-call | tf_op jit(solution)/shard_map/pallas_call | solution.py:330
  (1 shorter events, 0.0 us)
Async XLA Ops:
  4.1 8.9 %collective-permute-start = (f32[16,128]{1,0:T(8,128)S(1)}, f32[16,128]{1,0:T(8,128)S(1)}, u32[]{:S(2)}, u32[]{:S(2)}) collective-permute-start(f32[16,128]{1,0:T(8,128)S(1)} %get-tuple-element.42), channel_id=1, source_target_pairs={{0,1},{1,0},{2,3},{3,2},{4,5},{5,4},{6,7},{7,6},{8,9},{9,8},{10,11... | collective-permute-start | bytes 24584 | tf_op jit(solution)/shard_map/ppermute | solution.py:366
  7.2 5.8 %collective-permute-start.1 = (f32[16,128]{1,0:T(8,128)S(1)}, f32[16,128]{1,0:T(8,128)S(1)}, u32[]{:S(2)}, u32[]{:S(2)}) collective-permute-start(f32[16,128]{1,0:T(8,128)S(1)} %get-tuple-element.43), channel_id=1, source_target_pairs={{0,3},{1,2},{2,1},{3,0},{4,7},{5,6},{6,5},{7,4},{8,11},{9,10},{10,... | collective-permute-start | bytes 24584 | tf_op jit(solution)/shard_map/ppermute | solution.py:366
  9.7 3.3 %collective-permute-start.2 = (f32[16,128]{1,0:T(8,128)S(1)}, f32[16,128]{1,0:T(8,128)S(1)}, u32[]{:S(2)}, u32[]{:S(2)}) collective-permute-start(f32[16,128]{1,0:T(8,128)S(1)} %get-tuple-element.44), channel_id=1, source_target_pairs={{0,8},{8,0},{16,24},{24,16},{1,9},{9,1},{17,25},{25,17},{2,10},{10... | collective-permute-start | bytes 24584 | tf_op jit(solution)/shard_map/ppermute | solution.py:366
  9.7 3.3 %collective-permute-start.3 = (f32[16,128]{1,0:T(8,128)S(1)}, f32[16,128]{1,0:T(8,128)S(1)}, u32[]{:S(2)}, u32[]{:S(2)}) collective-permute-start(f32[16,128]{1,0:T(8,128)S(1)} %get-tuple-element.45), channel_id=1, source_target_pairs={{0,24},{8,16},{16,8},{24,0},{1,25},{9,17},{17,9},{25,1},{2,26},{10... | collective-permute-start | bytes 24584 | tf_op jit(solution)/shard_map/ppermute | solution.py:366
  11.3 3.7 %collective-permute-start.4 = (f32[16,128]{1,0:T(8,128)S(1)}, f32[16,128]{1,0:T(8,128)S(1)}, u32[]{:S(2)}, u32[]{:S(2)}) collective-permute-start(f32[16,128]{1,0:T(8,128)S(1)} %get-tuple-element.46), channel_id=1, source_target_pairs={{0,4},{4,0},{1,5},{5,1},{2,6},{6,2},{3,7},{7,3},{8,12},{12,8},{9,1... | collective-permute-start | bytes 24584 | tf_op jit(solution)/shard_map/ppermute | solution.py:366
  15.9 3.9 %collective-permute-start.5 = (f32[16,128]{1,0:T(8,128)S(1)}, f32[16,128]{1,0:T(8,128)S(1)}, u32[]{:S(2)}, u32[]{:S(2)}) collective-permute-start(f32[16,128]{1,0:T(8,128)S(1)} %get-tuple-element.49), channel_id=1, source_target_pairs={{0,1},{1,0},{2,3},{3,2},{4,5},{5,4},{6,7},{7,6},{8,9},{9,8},{10,11... | collective-permute-start | bytes 24584 | tf_op jit(solution)/shard_map/ppermute | solution.py:366
  16.6 5.4 %collective-permute-start.6 = (f32[16,128]{1,0:T(8,128)S(1)}, f32[16,128]{1,0:T(8,128)S(1)}, u32[]{:S(2)}, u32[]{:S(2)}) collective-permute-start(f32[16,128]{1,0:T(8,128)S(1)} %get-tuple-element.50), channel_id=1, source_target_pairs={{0,3},{1,2},{2,1},{3,0},{4,7},{5,6},{6,5},{7,4},{8,11},{9,10},{10,... | collective-permute-start | bytes 24584 | tf_op jit(solution)/shard_map/ppermute | solution.py:366
  17.5 4.6 %collective-permute-start.7 = (f32[16,128]{1,0:T(8,128)S(1)}, f32[16,128]{1,0:T(8,128)S(1)}, u32[]{:S(2)}, u32[]{:S(2)}) collective-permute-start(f32[16,128]{1,0:T(8,128)S(1)} %get-tuple-element.51), channel_id=1, source_target_pairs={{0,8},{8,0},{16,24},{24,16},{1,9},{9,1},{17,25},{25,17},{2,10},{10... | collective-permute-start | bytes 24584 | tf_op jit(solution)/shard_map/ppermute | solution.py:366
  17.5 4.6 %collective-permute-start.8 = (f32[16,128]{1,0:T(8,128)S(1)}, f32[16,128]{1,0:T(8,128)S(1)}, u32[]{:S(2)}, u32[]{:S(2)}) collective-permute-start(f32[16,128]{1,0:T(8,128)S(1)} %get-tuple-element.52), channel_id=1, source_target_pairs={{0,24},{8,16},{16,8},{24,0},{1,25},{9,17},{17,9},{25,1},{2,26},{10... | collective-permute-start | bytes 24584 | tf_op jit(solution)/shard_map/ppermute | solution.py:366
  18.2 3.9 %collective-permute-start.9 = (f32[16,128]{1,0:T(8,128)S(1)}, f32[16,128]{1,0:T(8,128)S(1)}, u32[]{:S(2)}, u32[]{:S(2)}) collective-permute-start(f32[16,128]{1,0:T(8,128)S(1)} %get-tuple-element.53), channel_id=1, source_target_pairs={{0,4},{4,0},{1,5},{5,1},{2,6},{6,2},{3,7},{7,3},{8,12},{12,8},{9,1... | collective-permute-start | bytes 24584 | tf_op jit(solution)/shard_map/ppermute | solution.py:366
  23.1 6.4 %collective-permute-start.10 = (f32[16,128]{1,0:T(8,128)S(1)}, f32[16,128]{1,0:T(8,128)S(1)}, u32[]{:S(2)}, u32[]{:S(2)}) collective-permute-start(f32[16,128]{1,0:T(8,128)S(1)} %get-tuple-element.56), channel_id=1, source_target_pairs={{0,1},{1,0},{2,3},{3,2},{4,5},{5,4},{6,7},{7,6},{8,9},{9,8},{10,11... | collective-permute-start | bytes 24584 | tf_op jit(solution)/shard_map/ppermute | solution.py:366
  23.7 5.8 %collective-permute-start.11 = (f32[16,128]{1,0:T(8,128)S(1)}, f32[16,128]{1,0:T(8,128)S(1)}, u32[]{:S(2)}, u32[]{:S(2)}) collective-permute-start(f32[16,128]{1,0:T(8,128)S(1)} %get-tuple-element.57), channel_id=1, source_target_pairs={{0,3},{1,2},{2,1},{3,0},{4,7},{5,6},{6,5},{7,4},{8,11},{9,10},{10,... | collective-permute-start | bytes 24584 | tf_op jit(solution)/shard_map/ppermute | solution.py:366
  26.2 3.3 %collective-permute-start.12 = (f32[16,128]{1,0:T(8,128)S(1)}, f32[16,128]{1,0:T(8,128)S(1)}, u32[]{:S(2)}, u32[]{:S(2)}) collective-permute-start(f32[16,128]{1,0:T(8,128)S(1)} %get-tuple-element.58), channel_id=1, source_target_pairs={{0,8},{8,0},{16,24},{24,16},{1,9},{9,1},{17,25},{25,17},{2,10},{10... | collective-permute-start | bytes 24584 | tf_op jit(solution)/shard_map/ppermute | solution.py:366
  26.2 3.3 %collective-permute-start.13 = (f32[16,128]{1,0:T(8,128)S(1)}, f32[16,128]{1,0:T(8,128)S(1)}, u32[]{:S(2)}, u32[]{:S(2)}) collective-permute-start(f32[16,128]{1,0:T(8,128)S(1)} %get-tuple-element.59), channel_id=1, source_target_pairs={{0,24},{8,16},{16,8},{24,0},{1,25},{9,17},{17,9},{25,1},{2,26},{10... | collective-permute-start | bytes 24584 | tf_op jit(solution)/shard_map/ppermute | solution.py:366
  27.8 3.7 %collective-permute-start.14 = (f32[16,128]{1,0:T(8,128)S(1)}, f32[16,128]{1,0:T(8,128)S(1)}, u32[]{:S(2)}, u32[]{:S(2)}) collective-permute-start(f32[16,128]{1,0:T(8,128)S(1)} %get-tuple-element.60), channel_id=1, source_target_pairs={{0,4},{4,0},{1,5},{5,1},{2,6},{6,2},{3,7},{7,3},{8,12},{12,8},{9,1... | collective-permute-start | bytes 24584 | tf_op jit(solution)/shard_map/ppermute | solution.py:366
  32.5 4.2 %collective-permute-start.15 = (f32[16,128]{1,0:T(8,128)S(1)}, f32[16,128]{1,0:T(8,128)S(1)}, u32[]{:S(2)}, u32[]{:S(2)}) collective-permute-start(f32[16,128]{1,0:T(8,128)S(1)} %get-tuple-element.63), channel_id=1, source_target_pairs={{0,1},{1,0},{2,3},{3,2},{4,5},{5,4},{6,7},{7,6},{8,9},{9,8},{10,11... | collective-permute-start | bytes 24584 | tf_op jit(solution)/shard_map/ppermute | solution.py:366
  33.2 5.4 %collective-permute-start.16 = (f32[16,128]{1,0:T(8,128)S(1)}, f32[16,128]{1,0:T(8,128)S(1)}, u32[]{:S(2)}, u32[]{:S(2)}) collective-permute-start(f32[16,128]{1,0:T(8,128)S(1)} %get-tuple-element.64), channel_id=1, source_target_pairs={{0,3},{1,2},{2,1},{3,0},{4,7},{5,6},{6,5},{7,4},{8,11},{9,10},{10,... | collective-permute-start | bytes 24584 | tf_op jit(solution)/shard_map/ppermute | solution.py:366
  34.1 4.6 %collective-permute-start.17 = (f32[16,128]{1,0:T(8,128)S(1)}, f32[16,128]{1,0:T(8,128)S(1)}, u32[]{:S(2)}, u32[]{:S(2)}) collective-permute-start(f32[16,128]{1,0:T(8,128)S(1)} %get-tuple-element.65), channel_id=1, source_target_pairs={{0,8},{8,0},{16,24},{24,16},{1,9},{9,1},{17,25},{25,17},{2,10},{10... | collective-permute-start | bytes 24584 | tf_op jit(solution)/shard_map/ppermute | solution.py:366
  34.1 4.6 %collective-permute-start.18 = (f32[16,128]{1,0:T(8,128)S(1)}, f32[16,128]{1,0:T(8,128)S(1)}, u32[]{:S(2)}, u32[]{:S(2)}) collective-permute-start(f32[16,128]{1,0:T(8,128)S(1)} %get-tuple-element.66), channel_id=1, source_target_pairs={{0,24},{8,16},{16,8},{24,0},{1,25},{9,17},{17,9},{25,1},{2,26},{10... | collective-permute-start | bytes 24584 | tf_op jit(solution)/shard_map/ppermute | solution.py:366
  35.0 3.7 %collective-permute-start.19 = (f32[16,128]{1,0:T(8,128)S(1)}, f32[16,128]{1,0:T(8,128)S(1)}, u32[]{:S(2)}, u32[]{:S(2)}) collective-permute-start(f32[16,128]{1,0:T(8,128)S(1)} %get-tuple-element.67), channel_id=1, source_target_pairs={{0,4},{4,0},{1,5},{5,1},{2,6},{6,2},{3,7},{7,3},{8,12},{12,8},{9,1... | collective-permute-start | bytes 24584 | tf_op jit(solution)/shard_map/ppermute | solution.py:366

commit v3 on v2

--- a/solution.py
+++ b/solution.py
@@ -67,27 +67,26 @@
     )
 
 
-def pack_faces(field, d_ref, out_refs, flags_ref, ph, th):
-    ph_a, ph_b, row_a, row_b, th_a, th_b = out_refs
+def pack_faces(field, d_ref, outs, flags_ref, ph, th):
     rows = field.shape[0]
     per = ph * th
     nb = rows // per
     cell = lax.broadcasted_iota(jnp.int32, (per, LANES), 1) % BLK
-    odd_ph, odd_row, odd_th = flags_ref[0] == 1, flags_ref[1] == 1, flags_ref[2] == 1
+    odd_ph, odd_row, odd_th = flags_ref[0:1, :] > 0.5, flags_ref[1:2, :] > 0.5, flags_ref[2:3, :] > 0.5
     low = jnp.concatenate([field[b * per : b * per + th] for b in range(nb)], axis=0)
     high = jnp.concatenate([field[(b + 1) * per - th : (b + 1) * per] for b in range(nb)], axis=0)
-    ph_a[...] = jnp.where(odd_ph, low, high)
-    ph_b[...] = jnp.where(odd_ph, high, low)
+    outs["ph_high"][...] = jnp.where(odd_ph, high, low)
+    outs["ph_low"][...] = jnp.where(odd_ph, low, high)
     low = jnp.where(cell == BLK - 1, pltpu.roll(field[:per], BLK - 1, 1), 0.0)
     high = jnp.where(cell == 0, pltpu.roll(field[rows - per :], LANES - BLK + 1, 1), 0.0)
-    row_a[...] = jnp.where(odd_row, low, high)
-    if row_b is not None:
-        row_b[...] = jnp.where(odd_row, high, low)
+    outs["row_low"][...] = jnp.where(odd_row, low, high)
+    if "row_high" in outs:
+        outs["row_high"][...] = jnp.where(odd_row, high, low)
     low = d_ref[pl.ds(0, rows // th, stride=th), :]
     high = d_ref[pl.ds(th - 1, rows // th, stride=th), :]
-    th_a[...] = jnp.where(odd_th, low, high)
-    if th_b is not None:
-        th_b[...] = jnp.where(odd_th, high, low)
+    outs["th_low"][...] = jnp.where(odd_th, low, high)
+    if "th_high" in outs:
+        outs["th_high"][...] = jnp.where(odd_th, high, low)
 
 
 def local_part(field, d_ref, krylov, conduct, diagonal, mixing_ref, ph, th):
@@ -115,46 +114,38 @@
     return field + mixed + conduct * (diagonal * field - total) - krylov
 
 
-def add_faces(halo_ref, in_refs, flags_ref, ph, th):
-    ph_a, ph_b, row_a, row_b, th_a, th_b = in_refs
+def add_faces(halo_ref, taken, flags_ref, ph, th):
     rows = halo_ref.shape[0]
     per = ph * th
     nb = rows // per
-    odd_ph, odd_row, odd_th = flags_ref[0] == 1, flags_ref[1] == 1, flags_ref[2] == 1
+    flag = [flags_ref[i : i + 1, :] > 0.5 for i in range(7)]
     halo_ref[...] = jnp.zeros_like(halo_ref)
 
-    def sides(odd, a, b, has_low, has_high):
-        first = a[...]
-        second = jnp.zeros_like(first) if b is None else b[...]
-        low = jnp.where(odd, first, second)
-        high = jnp.where(odd, second, first)
-        if has_low is not None:
-            low = jnp.where(has_low, low, 0.0)
-            high = jnp.where(has_high, high, 0.0)
-        return low, high
-
-    low, high = sides(odd_ph, ph_a, ph_b, None, None)
+    def sides(axis, odd, has_low=None, has_high=None):
+        first = taken[axis + "_low"][...]
+        second = taken[axis + "_high"][...] if axis + "_high" in taken else jnp.zeros_like(first)
+        low, high = jnp.where(odd, first, second), jnp.where(odd, second, first)
+        if has_low is None:
+            return low, high
+        return jnp.where(has_low, low, 0.0), jnp.where(has_high, high, 0.0)
+
+    low, high = sides("ph", flag[0])
     for b in range(nb):
         halo_ref[b * per : b * per + th, :] += low[b * th : (b + 1) * th]
         halo_ref[(b + 1) * per - th : (b + 1) * per, :] += high[b * th : (b + 1) * th]
-    low, high = sides(odd_row, row_a, row_b, flags_ref[3] == 1, flags_ref[4] == 1)
+    low, high = sides("row", flag[1], flag[3], flag[4])
     halo_ref[:per, :] += low
     halo_ref[rows - per :, :] += high
-    low, high = sides(odd_th, th_a, th_b, flags_ref[5] == 1, flags_ref[6] == 1)
+    low, high = sides("th", flag[2], flag[5], flag[6])
     halo_ref[pl.ds(0, rows // th, stride=th), :] += low
     halo_ref[pl.ds(th - 1, rows // th, stride=th), :] += high
     return halo_ref[...]
 
 
-def fill(refs, present):
-    refs = iter(refs)
-    return [next(refs) if there else None for there in present]
-
-
-def first_kernel(ph, th, present, flags_ref, right_ref, conduct_ref, coupling_ref, codes_ref, inverse_ref, *rest):
-    n = sum(present)
+def first_kernel(ph, th, names, flags_ref, right_ref, conduct_ref, coupling_ref, codes_ref, inverse_ref, *rest):
+    n = len(names)
     krylov_ref, conducts_ref, diagonal_ref, mixing_ref, turned_ref, d_ref = rest[:6]
-    faces = fill(rest[6 : 6 + n], present)
+    faces = dict(zip(names, rest[6 : 6 + n]))
     right, conduct, coupling, codes, blocks, sems = rest[6 + n :]
     per = ph * th
     rows = d_ref.shape[0]
@@ -179,13 +170,13 @@
     cell = lax.broadcasted_iota(jnp.int32, (per, LANES), 1) % BLK
     row = lax.broadcasted_iota(jnp.int32, (per, LANES), 0)
     diagonal_ref[...] = jnp.full_like(diagonal_ref, 6.0)
-    for side, (edge, first, has) in enumerate(((0, 0, flags_ref[3]), (BLK - 1, rows - per, flags_ref[4]))):
+    for side, (edge, first, has) in enumerate(((0, 0, 3), (BLK - 1, rows - per, 4))):
         factor = jnp.zeros((per, LANES), jnp.float32)
         for i in range(per):
             code = codes[side, i // th, i % th]
             value = jnp.where(code == 1, 1.0, jnp.where(code == 2, -1.0, 0.0))
             factor = jnp.where(row == i, value, factor)
-        factor = jnp.where((cell == edge) & (has == 0), factor, 0.0)
+        factor = jnp.where((cell == edge) & (flags_ref[has : has + 1, :] < 0.5), factor, 0.0)
         diagonal_ref[first : first + per, :] -= factor
     for b in range(nb):
         copies[3 + b].wait()
@@ -216,21 +207,20 @@
     refs[-1][...] = jnp.concatenate(gram_rows(left, right), axis=0)
 
 
-def step_kernel(ph, th, present, flags_ref, local_ref, conduct_ref, turned_ref, *rest):
-    n = sum(present)
-    in_faces, (next_ref, d_ref), out_faces, (halo_ref,) = rest[:n], rest[n : n + 2], rest[n + 2 : 2 * n + 2], rest[2 * n + 2 :]
-    halo = add_faces(halo_ref, fill(in_faces, present), flags_ref, ph, th)
+def step_kernel(ph, th, names, flags_ref, local_ref, conduct_ref, turned_ref, *rest):
+    n = len(names)
+    next_ref, d_ref, *sent, halo_ref = rest[n:]
+    halo = add_faces(halo_ref, dict(zip(names, rest)), flags_ref, ph, th)
     krylov = local_ref[...] - conduct_ref[...] * halo
     next_ref[...] = krylov
     direction = apply_all(krylov, turned_ref)
     d_ref[...] = direction
-    pack_faces(direction, d_ref, fill(out_faces, present), flags_ref, ph, th)
-
-
-def last_kernel(ph, th, present, flags_ref, local_ref, conduct_ref, partial_ref, *rest):
-    n = sum(present)
-    older, in_faces, (next_ref, gram_ref), (halo_ref,) = rest[:S], rest[S : S + n], rest[S + n : S + 2 + n], rest[S + 2 + n :]
-    halo = add_faces(halo_ref, fill(in_faces, present), flags_ref, ph, th)
+    pack_faces(direction, d_ref, dict(zip(names, sent)), flags_ref, ph, th)
+
+
+def last_kernel(ph, th, names, flags_ref, local_ref, conduct_ref, partial_ref, *rest):
+    older, taken, (next_ref, gram_ref, halo_ref) = rest[:S], rest[S : S + len(names)], rest[S + len(names) :]
+    halo = add_faces(halo_ref, dict(zip(names, taken)), flags_ref, ph, th)
     final = local_ref[...] - conduct_ref[...] * halo
     next_ref[...] = final
     basis = [ref[...] for ref in older] + [final]
@@ -322,8 +312,6 @@
 
 def call(kernel, outs, scratch, *args, stay=False):
     def space(a):
-        if a.dtype == jnp.int32 and a.ndim == 1:
-            return pltpu.SMEM
         return pltpu.HBM if stay and (a.ndim > 3 or a.shape[-1] != LANES) else pltpu.VMEM
 
     placed = [pltpu.with_memory_space_constraint(a, pltpu.HBM) if space(a) == pltpu.HBM else a for a in args]
@@ -344,31 +332,35 @@
     rows = per * nb
     at = {axis: (lax.axis_index(axis), lax.axis_size(axis)) for axis in ("row", "th", "ph")}
     (row_at, row_n), (th_at, th_n), (ph_at, ph_n) = at["row"], at["th"], at["ph"]
-    present = (True, True, True, row_n > 2, True, th_n > 2)
+    face_rows = {"ph_high": nb * th, "row_high": per, "ph_low": nb * th, "th_high": rows // th, "th_low": rows // th, "row_low": per}
+    if row_n == 2:
+        face_rows.pop("row_high")
+    if th_n == 2:
+        face_rows.pop("th_high")
+    names = tuple(face_rows)
     flags = jnp.stack(
-        [ph_at % 2, row_at % 2, th_at % 2, row_at > 0, row_at < row_n - 1, th_at > 0, th_at < th_n - 1]
-    ).astype(jnp.int32)
+        [ph_at % 2, row_at % 2, th_at % 2, row_at > 0, row_at < row_n - 1, th_at > 0, th_at < th_n - 1, 0]
+    ).astype(jnp.float32)
+    flags = jnp.broadcast_to(flags[:, None], (flags.shape[0], LANES))
 
     def shape(n):
         return jax.ShapeDtypeStruct((n, LANES), jnp.float32)
 
-    face_rows = (nb * th, nb * th, per, per, rows // th, rows // th)
-    faces = [shape(n) for n, there in zip(face_rows, present) if there]
+    faces = [shape(n) for n in face_rows.values()]
     whole = shape(rows)
 
+    plans = {"low": pairs_low, "high": pairs_high}
+
     def exchange(sent):
-        plan = (("ph", pairs_low), ("ph", pairs_high), ("row", pairs_low), ("row", pairs_high), ("th", pairs_low), ("th", pairs_high))
-        plan = [p for p, there in zip(plan, present) if there]
-        taken = [None] * len(plan)
-        order = sorted(range(len(plan)), key=lambda i: (plan[i][0] != "ph", plan[i][0] != "th", plan[i][1] is pairs_low))
-        for i in order:
-            axis, pairs = plan[i]
-            taken[i] = lax.ppermute(sent[i], axis, pairs(lax.axis_size(axis)))
+        taken = []
+        for name, array in zip(names, sent):
+            axis, side = name.split("_")
+            taken.append(lax.ppermute(array, axis, plans[side](lax.axis_size(axis))))
         return taken
 
     field = pltpu.VMEM(right_side.shape, jnp.float32)
     start, conducts, diagonal, mixing, turned, direction, *sent = call(
-        functools.partial(first_kernel, ph, th, present),
+        functools.partial(first_kernel, ph, th, names),
         [whole, whole, whole, shape(VARS), jax.ShapeDtypeStruct((rows, LANES, LANES), jnp.bfloat16), whole] + faces,
         [
             field,
@@ -390,7 +382,7 @@
         )
         if step < S - 1:
             following, direction, *sent = call(
-                functools.partial(step_kernel, ph, th, present),
+                functools.partial(step_kernel, ph, th, names),
                 [whole, whole] + faces,
                 halo,
                 flags, beside, conducts, turned, *taken,
@@ -401,7 +393,7 @@
     partial_rows += -partial_rows % 8
     (partial,) = call(gram_kernel, [shape(partial_rows)], [], *krylov)
     following, gram = call(
-        functools.partial(last_kernel, ph, th, present),
+        functools.partial(last_kernel, ph, th, names),
         [whole, shape(row_n * th_n * ph_n)],
         halo,
         flags, beside, conducts, partial, *krylov, *taken,

time: 53.1 us -> 46.6 us (0.88)
  Pallas kernels: 9.51 us -> 6.85 us
  waiting for transfers between devices: 7.99 us -> 6.07 us
  starting transfers between devices: 22.7 us -> 21.3 us
    pallas_call x11, Pallas kernels: 9.51 us -> 6.85 us  [call(): pl.pallas_call(kernel, out_shape=outs, in_specs=[pl.BlockSpec(memory_spac...]
    ppermute x20, waiting for transfers between devices: 7.99 us -> 6.07 us  [exchange(): taken.append(lax.ppermute(array, axis, plans[side](lax.axis_size(axis))))]
    ppermute x20, starting transfers between devices: 22.7 us -> 21.3 us  [exchange(): taken.append(lax.ppermute(array, axis, plans[side](lax.axis_size(axis))))]
    all_to_all x1, blocking collectives: 11.8 us -> 11.3 us  [local(): gram = lax.all_to_all(gram, ('row', 'th', 'ph'), 0, 0, tiled=True)]
  transfers between devices with their start and end apart: 20 -> 20, of which waited for: 4 -> 9; matrix products, arithmetic and copies ran while one was open for 0% -> 0% of each run, Pallas kernels for 1% -> 1%
where the time goes in v3:
time: 46.6 us; the launch traced here: 46.4 us
  starting transfers between devices  21.3 us (46%)
  blocking collectives  11.3 us (24%)
  Pallas kernels  6.85 us (15%)
  waiting for transfers between devices  6.07 us (13%)
  between operations  0.74 us (2%)
    ppermute x20, starting transfers between devices, exchange(): taken.append(lax.ppermute(array, axis, plans[side](lax.axis_size(axis))))  21.3 us
    all_to_all x1, blocking collectives, local(): gram = lax.all_to_all(gram, ('row', 'th', 'ph'), 0, 0, tiled=True)  11.3 us
    pallas_call x11, Pallas kernels, call(): pl.pallas_call(kernel, out_shape=outs, in_specs=[pl.BlockSpec(memory_spac...  6.85 us
    ppermute x20, waiting for transfers between devices, exchange(): taken.append(lax.ppermute(array, axis, plans[side](lax.axis_size(axis))))  6.07 us
  transfers between devices with their start and end apart: 20, of which 9 were waited for; matrix products, arithmetic and copies ran while one was open for 0% of the time, Pallas kernels for 1%

profile of v3, /device:TPU:0, one launch (start us, length us, event | category | flops | bytes accessed | tf_op | source)
XLA Modules:
  0.0 46.4 jit_solution(14168566191366221035)
XLA Ops:
  0.7 0.1 stack.43
  0.8 0.1 broadcast_in_dim.2.flags_ref
  0.8 2.8 %shard_map.68 = (f32[64,128]{1,0:T(8,128)S(1)}, f32[64,128]{1,0:T(8,128)S(1)}, f32[64,128]{1,0:T(8,128)S(1)}, f32[8,128]{1,0:T(8,128)S(1)}, bf16[64,128,128]{2,1...) custom-call(f32[8,128]{1,0:T(8,128)S(1)} %broadcast_in_dim.2.flags_r, ...), custom_call_target="tpu_custom_call" | custom-call | tf_op jit(solution)/shard_map/pallas_call | solution.py:318
  3.7 5.1 %collective-permute-start = (f32[16,128]{1,0:T(8,128)S(1)}, f32[16,128]{1,0:T(8,128)S(1)}, u32[]{:S(2)}, u32[]{:S(2)}) collective-permute-start(f32[16,128]{1,0:T(8,128)S(1)} %get-tuple-element.42), channel_id=1, source_target_pairs={{0,3},{1,2},{2,1},{3,0},{4,7},{5,6},{6,5},{7,4},{8,11},{9,10},{10,... | collective-permute-start | bytes 24584 | tf_op jit(solution)/shard_map/ppermute | solution.py:358
  8.8 0.7 %collective-permute-start.1 = (f32[16,128]{1,0:T(8,128)S(1)}, f32[16,128]{1,0:T(8,128)S(1)}, u32[]{:S(2)}, u32[]{:S(2)}) collective-permute-start(f32[16,128]{1,0:T(8,128)S(1)} %get-tuple-element.43), channel_id=1, source_target_pairs={{0,24},{8,16},{16,8},{24,0},{1,25},{9,17},{17,9},{25,1},{2,26},{10... | collective-permute-start | bytes 24584 | tf_op jit(solution)/shard_map/ppermute | solution.py:358
  9.4 0.0 collective-permute-start.2
  9.4 1.5 %collective-permute-start.3 = (f32[16,128]{1,0:T(8,128)S(1)}, f32[16,128]{1,0:T(8,128)S(1)}, u32[]{:S(2)}, u32[]{:S(2)}) collective-permute-start(f32[16,128]{1,0:T(8,128)S(1)} %get-tuple-element.45), channel_id=1, source_target_pairs={{0,4},{4,0},{1,5},{5,1},{2,6},{6,2},{3,7},{7,3},{8,12},{12,8},{9,1... | collective-permute-start | bytes 24584 | tf_op jit(solution)/shard_map/ppermute | solution.py:358
  10.9 0.7 %collective-permute-start.4 = (f32[16,128]{1,0:T(8,128)S(1)}, f32[16,128]{1,0:T(8,128)S(1)}, u32[]{:S(2)}, u32[]{:S(2)}) collective-permute-start(f32[16,128]{1,0:T(8,128)S(1)} %get-tuple-element.46), channel_id=1, source_target_pairs={{0,8},{8,0},{16,24},{24,16},{1,9},{9,1},{17,25},{25,17},{2,10},{10... | collective-permute-start | bytes 24584 | tf_op jit(solution)/shard_map/ppermute | solution.py:358
  11.6 0.2 shard_map.69.local_ref
  11.8 0.0 collective-permute-done.rest_0_
  11.8 0.1 collective-permute-done.1.rest_1_
  11.9 1.3 %collective-permute-done.2.rest_2_ = f32[16,128]{1,0:T(8,128)S(1)} collective-permute-done((f32[16,128]{1,0:T(8,128)S(1)}, f32[16,128]{1,0:T(8,128)S(1)}, u32[]{:S(2)}, u32[]{:S(2)}) %collective-permute-start.2) | collective-permute-done | bytes 8224 | tf_op jit(solution)/shard_map/ppermute | solution.py:358
  13.1 0.0 collective-permute-done.3.rest_3_
  13.1 0.0 collective-permute-done.4.rest_4_
  13.1 0.5 %shard_map.70 = (f32[64,128]{1,0:T(8,128)S(1)}, f32[64,128]{1,0:T(8,128)S(1)}, f32[16,128]{1,0:T(8,128)S(1)}, f32[16,128]{1,0:T(8,128)S(1)}, f32[16,128]{1,0:T(8...) custom-call(f32[8,128]{1,0:T(8,128)S(1)} %broadcast_in_dim.2.flags_ref, f32[64,128]{1,0:T(8,128)S(1)} %shard_map.69.local_ref, ...), custom_call_target="tpu_custom_call" | custom-call | tf_op jit(solution)/shard_map/pallas_call | solution.py:318
  13.6 1.1 %collective-permute-start.5 = (f32[16,128]{1,0:T(8,128)S(1)}, f32[16,128]{1,0:T(8,128)S(1)}, u32[]{:S(2)}, u32[]{:S(2)}) collective-permute-start(f32[16,128]{1,0:T(8,128)S(1)} %get-tuple-element.49), channel_id=1, source_target_pairs={{0,3},{1,2},{2,1},{3,0},{4,7},{5,6},{6,5},{7,4},{8,11},{9,10},{10,... | collective-permute-start | bytes 24584 | tf_op jit(solution)/shard_map/ppermute | solution.py:358
  14.7 0.0 collective-permute-start.6
  14.7 1.0 %collective-permute-start.7 = (f32[16,128]{1,0:T(8,128)S(1)}, f32[16,128]{1,0:T(8,128)S(1)}, u32[]{:S(2)}, u32[]{:S(2)}) collective-permute-start(f32[16,128]{1,0:T(8,128)S(1)} %get-tuple-element.51), channel_id=1, source_target_pairs={{0,1},{1,0},{2,3},{3,2},{4,5},{5,4},{6,7},{7,6},{8,9},{9,8},{10,11... | collective-permute-start | bytes 24584 | tf_op jit(solution)/shard_map/ppermute | solution.py:358
  15.7 1.5 %collective-permute-start.8 = (f32[16,128]{1,0:T(8,128)S(1)}, f32[16,128]{1,0:T(8,128)S(1)}, u32[]{:S(2)}, u32[]{:S(2)}) collective-permute-start(f32[16,128]{1,0:T(8,128)S(1)} %get-tuple-element.52), channel_id=1, source_target_pairs={{0,4},{4,0},{1,5},{5,1},{2,6},{6,2},{3,7},{7,3},{8,12},{12,8},{9,1... | collective-permute-start | bytes 24584 | tf_op jit(solution)/shard_map/ppermute | solution.py:358
  17.3 0.4 collective-permute-start.9
  17.6 0.2 shard_map.71.local_ref
  17.8 1.4 %collective-permute-done.5.rest_0_ = f32[16,128]{1,0:T(8,128)S(1)} collective-permute-done((f32[16,128]{1,0:T(8,128)S(1)}, f32[16,128]{1,0:T(8,128)S(1)}, u32[]{:S(2)}, u32[]{:S(2)}) %collective-permute-start.5) | collective-permute-done | bytes 8224 | tf_op jit(solution)/shard_map/ppermute | solution.py:358
  19.2 0.0 collective-permute-done.6.rest_1_
  19.2 0.0 collective-permute-done.7.rest_2_
  19.2 0.2 collective-permute-done.8.rest_3_
  19.4 0.0 collective-permute-done.9.rest_4_
  19.4 0.5 %shard_map.72 = (f32[64,128]{1,0:T(8,128)S(1)}, f32[64,128]{1,0:T(8,128)S(1)}, f32[16,128]{1,0:T(8,128)S(1)}, f32[16,128]{1,0:T(8,128)S(1)}, f32[16,128]{1,0:T(8...) custom-call(f32[8,128]{1,0:T(8,128)S(1)} %broadcast_in_dim.2.flags_ref, f32[64,128]{1,0:T(8,128)S(1)} %shard_map.71.local_ref, ...), custom_call_target="tpu_custom_call" | custom-call | tf_op jit(solution)/shard_map/pallas_call | solution.py:318
  19.9 2.8 %collective-permute-start.10 = (f32[16,128]{1,0:T(8,128)S(1)}, f32[16,128]{1,0:T(8,128)S(1)}, u32[]{:S(2)}, u32[]{:S(2)}) collective-permute-start(f32[16,128]{1,0:T(8,128)S(1)} %get-tuple-element.56), channel_id=1, source_target_pairs={{0,3},{1,2},{2,1},{3,0},{4,7},{5,6},{6,5},{7,4},{8,11},{9,10},{10,... | collective-permute-start | bytes 24584 | tf_op jit(solution)/shard_map/ppermute | solution.py:358
  22.7 0.4 collective-permute-start.11
  23.0 0.0 collective-permute-start.12
  23.0 1.5 %collective-permute-start.13 = (f32[16,128]{1,0:T(8,128)S(1)}, f32[16,128]{1,0:T(8,128)S(1)}, u32[]{:S(2)}, u32[]{:S(2)}) collective-permute-start(f32[16,128]{1,0:T(8,128)S(1)} %get-tuple-element.59), channel_id=1, source_target_pairs={{0,4},{4,0},{1,5},{5,1},{2,6},{6,2},{3,7},{7,3},{8,12},{12,8},{9,1... | collective-permute-start | bytes 24584 | tf_op jit(solution)/shard_map/ppermute | solution.py:358
  24.6 0.7 %collective-permute-start.14 = (f32[16,128]{1,0:T(8,128)S(1)}, f32[16,128]{1,0:T(8,128)S(1)}, u32[]{:S(2)}, u32[]{:S(2)}) collective-permute-start(f32[16,128]{1,0:T(8,128)S(1)} %get-tuple-element.60), channel_id=1, source_target_pairs={{0,8},{8,0},{16,24},{24,16},{1,9},{9,1},{17,25},{25,17},{2,10},{10... | collective-permute-start | bytes 24584 | tf_op jit(solution)/shard_map/ppermute | solution.py:358
  25.3 0.2 shard_map.73.local_ref
  25.4 0.0 collective-permute-done.10.rest_0_
  25.4 0.3 collective-permute-done.11.rest_1_
  25.7 1.0 %collective-permute-done.12.rest_2_ = f32[16,128]{1,0:T(8,128)S(1)} collective-permute-done((f32[16,128]{1,0:T(8,128)S(1)}, f32[16,128]{1,0:T(8,128)S(1)}, u32[]{:S(2)}, u32[]{:S(2)}) %collective-permute-start.12) | collective-permute-done | bytes 8224 | tf_op jit(solution)/shard_map/ppermute | solution.py:358
  26.7 0.1 collective-permute-done.13.rest_3_
  26.8 0.0 collective-permute-done.14.rest_4_
  26.8 0.5 %shard_map.74 = (f32[64,128]{1,0:T(8,128)S(1)}, f32[64,128]{1,0:T(8,128)S(1)}, f32[16,128]{1,0:T(8,128)S(1)}, f32[16,128]{1,0:T(8,128)S(1)}, f32[16,128]{1,0:T(8...) custom-call(f32[8,128]{1,0:T(8,128)S(1)} %broadcast_in_dim.2.flags_ref, f32[64,128]{1,0:T(8,128)S(1)} %shard_map.73.local_ref, ...), custom_call_target="tpu_custom_call" | custom-call | tf_op jit(solution)/shard_map/pallas_call | solution.py:318
  27.2 1.4 %collective-permute-start.15 = (f32[16,128]{1,0:T(8,128)S(1)}, f32[16,128]{1,0:T(8,128)S(1)}, u32[]{:S(2)}, u32[]{:S(2)}) collective-permute-start(f32[16,128]{1,0:T(8,128)S(1)} %get-tuple-element.63), channel_id=1, source_target_pairs={{0,3},{1,2},{2,1},{3,0},{4,7},{5,6},{6,5},{7,4},{8,11},{9,10},{10,... | collective-permute-start | bytes 24584 | tf_op jit(solution)/shard_map/ppermute | solution.py:358
  28.6 0.0 collective-permute-start.16
  28.6 0.9 %collective-permute-start.17 = (f32[16,128]{1,0:T(8,128)S(1)}, f32[16,128]{1,0:T(8,128)S(1)}, u32[]{:S(2)}, u32[]{:S(2)}) collective-permute-start(f32[16,128]{1,0:T(8,128)S(1)} %get-tuple-element.65), channel_id=1, source_target_pairs={{0,1},{1,0},{2,3},{3,2},{4,5},{5,4},{6,7},{7,6},{8,9},{9,8},{10,11... | collective-permute-start | bytes 24584 | tf_op jit(solution)/shard_map/ppermute | solution.py:358
  29.5 1.5 %collective-permute-start.18 = (f32[16,128]{1,0:T(8,128)S(1)}, f32[16,128]{1,0:T(8,128)S(1)}, u32[]{:S(2)}, u32[]{:S(2)}) collective-permute-start(f32[16,128]{1,0:T(8,128)S(1)} %get-tuple-element.66), channel_id=1, source_target_pairs={{0,4},{4,0},{1,5},{5,1},{2,6},{6,2},{3,7},{7,3},{8,12},{12,8},{9,1... | collective-permute-start | bytes 24584 | tf_op jit(solution)/shard_map/ppermute | solution.py:358
  31.1 0.2 collective-permute-start.19
  31.3 0.2 shard_map.75.local_ref
  31.4 1.3 %collective-permute-done.15.rest_4_ = f32[16,128]{1,0:T(8,128)S(1)} collective-permute-done((f32[16,128]{1,0:T(8,128)S(1)}, f32[16,128]{1,0:T(8,128)S(1)}, u32[]{:S(2)}, u32[]{:S(2)}) %collective-permute-start.15) | collective-permute-done | bytes 8224 | tf_op jit(solution)/shard_map/ppermute | solution.py:358
  32.7 0.0 collective-permute-done.16.rest_5_
  32.7 0.0 collective-permute-done.17.rest_6_
  32.7 0.5 %collective-permute-done.18.rest_7_ = f32[16,128]{1,0:T(8,128)S(1)} collective-permute-done((f32[16,128]{1,0:T(8,128)S(1)}, f32[16,128]{1,0:T(8,128)S(1)}, u32[]{:S(2)}, u32[]{:S(2)}) %collective-permute-start.18) | collective-permute-done | bytes 8224 | tf_op jit(solution)/shard_map/ppermute | solution.py:358
  33.2 0.0 collective-permute-done.19.rest_8_
  33.2 0.1 shard_map.77
  33.3 11.3 %all_to_all.11 = f32[32,1,128]{2,1,0:T(1,128)S(1)} all-to-all(f32[32,1,128]{2,1,0:T(1,128)S(1)} %bitcast.12), channel_id=1, replica_groups=mesh['row'=4,'th'=2,'ph'=4] {'row','th','ph'}, dimensions={0} | all-to-all | bytes 32768 | tf_op jit(solution)/shard_map/all_to_all | solution.py:402
  44.6 1.8 %shard_map.78 = (f32[8,4,4,64]{3,2,1,0:T(4,128)}, f32[8,4,4,64]{3,2,1,0:T(4,128)}) custom-call(f32[32,128]{1,0:T(8,128)S(1)} %bitcast.11, f32[64,128]{1,0:T(8,128)S(1)} %get-tuple-element.36.krylov_ref.refs_0_.rest_0_, f32[64,128]{1,0:T(8,128)S(1)} %get-tuple-element.47.krylov_ref.refs_1_.rest_1_, ...), custom_call_target="tpu_custom_call" | custom-call | tf_op jit(solution)/shard_map/pallas_call | solution.py:318
  (2 shorter events, 0.0 us)
Async XLA Ops:
  3.7 8.1 %collective-permute-start = (f32[16,128]{1,0:T(8,128)S(1)}, f32[16,128]{1,0:T(8,128)S(1)}, u32[]{:S(2)}, u32[]{:S(2)}) collective-permute-start(f32[16,128]{1,0:T(8,128)S(1)} %get-tuple-element.42), channel_id=1, source_target_pairs={{0,3},{1,2},{2,1},{3,0},{4,7},{5,6},{6,5},{7,4},{8,11},{9,10},{10,... | collective-permute-start | bytes 24584 | tf_op jit(solution)/shard_map/ppermute | solution.py:358
  8.8 3.1 %collective-permute-start.1 = (f32[16,128]{1,0:T(8,128)S(1)}, f32[16,128]{1,0:T(8,128)S(1)}, u32[]{:S(2)}, u32[]{:S(2)}) collective-permute-start(f32[16,128]{1,0:T(8,128)S(1)} %get-tuple-element.43), channel_id=1, source_target_pairs={{0,24},{8,16},{16,8},{24,0},{1,25},{9,17},{17,9},{25,1},{2,26},{10... | collective-permute-start | bytes 24584 | tf_op jit(solution)/shard_map/ppermute | solution.py:358
  9.4 3.7 %collective-permute-start.2 = (f32[16,128]{1,0:T(8,128)S(1)}, f32[16,128]{1,0:T(8,128)S(1)}, u32[]{:S(2)}, u32[]{:S(2)}) collective-permute-start(f32[16,128]{1,0:T(8,128)S(1)} %get-tuple-element.44), channel_id=1, source_target_pairs={{0,1},{1,0},{2,3},{3,2},{4,5},{5,4},{6,7},{7,6},{8,9},{9,8},{10,11... | collective-permute-start | bytes 24584 | tf_op jit(solution)/shard_map/ppermute | solution.py:358
  9.4 3.7 %collective-permute-start.3 = (f32[16,128]{1,0:T(8,128)S(1)}, f32[16,128]{1,0:T(8,128)S(1)}, u32[]{:S(2)}, u32[]{:S(2)}) collective-permute-start(f32[16,128]{1,0:T(8,128)S(1)} %get-tuple-element.45), channel_id=1, source_target_pairs={{0,4},{4,0},{1,5},{5,1},{2,6},{6,2},{3,7},{7,3},{8,12},{12,8},{9,1... | collective-permute-start | bytes 24584 | tf_op jit(solution)/shard_map/ppermute | solution.py:358
  10.9 2.2 %collective-permute-start.4 = (f32[16,128]{1,0:T(8,128)S(1)}, f32[16,128]{1,0:T(8,128)S(1)}, u32[]{:S(2)}, u32[]{:S(2)}) collective-permute-start(f32[16,128]{1,0:T(8,128)S(1)} %get-tuple-element.46), channel_id=1, source_target_pairs={{0,8},{8,0},{16,24},{24,16},{1,9},{9,1},{17,25},{25,17},{2,10},{10... | collective-permute-start | bytes 24584 | tf_op jit(solution)/shard_map/ppermute | solution.py:358
  13.6 5.5 %collective-permute-start.5 = (f32[16,128]{1,0:T(8,128)S(1)}, f32[16,128]{1,0:T(8,128)S(1)}, u32[]{:S(2)}, u32[]{:S(2)}) collective-permute-start(f32[16,128]{1,0:T(8,128)S(1)} %get-tuple-element.49), channel_id=1, source_target_pairs={{0,3},{1,2},{2,1},{3,0},{4,7},{5,6},{6,5},{7,4},{8,11},{9,10},{10,... | collective-permute-start | bytes 24584 | tf_op jit(solution)/shard_map/ppermute | solution.py:358
  14.7 4.4 %collective-permute-start.6 = (f32[16,128]{1,0:T(8,128)S(1)}, f32[16,128]{1,0:T(8,128)S(1)}, u32[]{:S(2)}, u32[]{:S(2)}) collective-permute-start(f32[16,128]{1,0:T(8,128)S(1)} %get-tuple-element.50), channel_id=1, source_target_pairs={{0,24},{8,16},{16,8},{24,0},{1,25},{9,17},{17,9},{25,1},{2,26},{10... | collective-permute-start | bytes 24584 | tf_op jit(solution)/shard_map/ppermute | solution.py:358
  14.7 4.4 %collective-permute-start.7 = (f32[16,128]{1,0:T(8,128)S(1)}, f32[16,128]{1,0:T(8,128)S(1)}, u32[]{:S(2)}, u32[]{:S(2)}) collective-permute-start(f32[16,128]{1,0:T(8,128)S(1)} %get-tuple-element.51), channel_id=1, source_target_pairs={{0,1},{1,0},{2,3},{3,2},{4,5},{5,4},{6,7},{7,6},{8,9},{9,8},{10,11... | collective-permute-start | bytes 24584 | tf_op jit(solution)/shard_map/ppermute | solution.py:358
  15.7 3.7 %collective-permute-start.8 = (f32[16,128]{1,0:T(8,128)S(1)}, f32[16,128]{1,0:T(8,128)S(1)}, u32[]{:S(2)}, u32[]{:S(2)}) collective-permute-start(f32[16,128]{1,0:T(8,128)S(1)} %get-tuple-element.52), channel_id=1, source_target_pairs={{0,4},{4,0},{1,5},{5,1},{2,6},{6,2},{3,7},{7,3},{8,12},{12,8},{9,1... | collective-permute-start | bytes 24584 | tf_op jit(solution)/shard_map/ppermute | solution.py:358
  17.3 2.1 %collective-permute-start.9 = (f32[16,128]{1,0:T(8,128)S(1)}, f32[16,128]{1,0:T(8,128)S(1)}, u32[]{:S(2)}, u32[]{:S(2)}) collective-permute-start(f32[16,128]{1,0:T(8,128)S(1)} %get-tuple-element.53), channel_id=1, source_target_pairs={{0,8},{8,0},{16,24},{24,16},{1,9},{9,1},{17,25},{25,17},{2,10},{10... | collective-permute-start | bytes 24584 | tf_op jit(solution)/shard_map/ppermute | solution.py:358
  19.9 5.6 %collective-permute-start.10 = (f32[16,128]{1,0:T(8,128)S(1)}, f32[16,128]{1,0:T(8,128)S(1)}, u32[]{:S(2)}, u32[]{:S(2)}) collective-permute-start(f32[16,128]{1,0:T(8,128)S(1)} %get-tuple-element.56), channel_id=1, source_target_pairs={{0,3},{1,2},{2,1},{3,0},{4,7},{5,6},{6,5},{7,4},{8,11},{9,10},{10,... | collective-permute-start | bytes 24584 | tf_op jit(solution)/shard_map/ppermute | solution.py:358
  22.7 3.1 %collective-permute-start.11 = (f32[16,128]{1,0:T(8,128)S(1)}, f32[16,128]{1,0:T(8,128)S(1)}, u32[]{:S(2)}, u32[]{:S(2)}) collective-permute-start(f32[16,128]{1,0:T(8,128)S(1)} %get-tuple-element.57), channel_id=1, source_target_pairs={{0,24},{8,16},{16,8},{24,0},{1,25},{9,17},{17,9},{25,1},{2,26},{10... | collective-permute-start | bytes 24584 | tf_op jit(solution)/shard_map/ppermute | solution.py:358
  23.0 3.7 %collective-permute-start.12 = (f32[16,128]{1,0:T(8,128)S(1)}, f32[16,128]{1,0:T(8,128)S(1)}, u32[]{:S(2)}, u32[]{:S(2)}) collective-permute-start(f32[16,128]{1,0:T(8,128)S(1)} %get-tuple-element.58), channel_id=1, source_target_pairs={{0,1},{1,0},{2,3},{3,2},{4,5},{5,4},{6,7},{7,6},{8,9},{9,8},{10,11... | collective-permute-start | bytes 24584 | tf_op jit(solution)/shard_map/ppermute | solution.py:358
  23.0 3.7 %collective-permute-start.13 = (f32[16,128]{1,0:T(8,128)S(1)}, f32[16,128]{1,0:T(8,128)S(1)}, u32[]{:S(2)}, u32[]{:S(2)}) collective-permute-start(f32[16,128]{1,0:T(8,128)S(1)} %get-tuple-element.59), channel_id=1, source_target_pairs={{0,4},{4,0},{1,5},{5,1},{2,6},{6,2},{3,7},{7,3},{8,12},{12,8},{9,1... | collective-permute-start | bytes 24584 | tf_op jit(solution)/shard_map/ppermute | solution.py:358
  24.6 2.2 %collective-permute-start.14 = (f32[16,128]{1,0:T(8,128)S(1)}, f32[16,128]{1,0:T(8,128)S(1)}, u32[]{:S(2)}, u32[]{:S(2)}) collective-permute-start(f32[16,128]{1,0:T(8,128)S(1)} %get-tuple-element.60), channel_id=1, source_target_pairs={{0,8},{8,0},{16,24},{24,16},{1,9},{9,1},{17,25},{25,17},{2,10},{10... | collective-permute-start | bytes 24584 | tf_op jit(solution)/shard_map/ppermute | solution.py:358
  27.2 5.5 %collective-permute-start.15 = (f32[16,128]{1,0:T(8,128)S(1)}, f32[16,128]{1,0:T(8,128)S(1)}, u32[]{:S(2)}, u32[]{:S(2)}) collective-permute-start(f32[16,128]{1,0:T(8,128)S(1)} %get-tuple-element.63), channel_id=1, source_target_pairs={{0,3},{1,2},{2,1},{3,0},{4,7},{5,6},{6,5},{7,4},{8,11},{9,10},{10,... | collective-permute-start | bytes 24584 | tf_op jit(solution)/shard_map/ppermute | solution.py:358
  28.6 4.1 %collective-permute-start.16 = (f32[16,128]{1,0:T(8,128)S(1)}, f32[16,128]{1,0:T(8,128)S(1)}, u32[]{:S(2)}, u32[]{:S(2)}) collective-permute-start(f32[16,128]{1,0:T(8,128)S(1)} %get-tuple-element.64), channel_id=1, source_target_pairs={{0,24},{8,16},{16,8},{24,0},{1,25},{9,17},{17,9},{25,1},{2,26},{10... | collective-permute-start | bytes 24584 | tf_op jit(solution)/shard_map/ppermute | solution.py:358
  28.6 4.1 %collective-permute-start.17 = (f32[16,128]{1,0:T(8,128)S(1)}, f32[16,128]{1,0:T(8,128)S(1)}, u32[]{:S(2)}, u32[]{:S(2)}) collective-permute-start(f32[16,128]{1,0:T(8,128)S(1)} %get-tuple-element.65), channel_id=1, source_target_pairs={{0,1},{1,0},{2,3},{3,2},{4,5},{5,4},{6,7},{7,6},{8,9},{9,8},{10,11... | collective-permute-start | bytes 24584 | tf_op jit(solution)/shard_map/ppermute | solution.py:358
  29.5 3.7 %collective-permute-start.18 = (f32[16,128]{1,0:T(8,128)S(1)}, f32[16,128]{1,0:T(8,128)S(1)}, u32[]{:S(2)}, u32[]{:S(2)}) collective-permute-start(f32[16,128]{1,0:T(8,128)S(1)} %get-tuple-element.66), channel_id=1, source_target_pairs={{0,4},{4,0},{1,5},{5,1},{2,6},{6,2},{3,7},{7,3},{8,12},{12,8},{9,1... | collective-permute-start | bytes 24584 | tf_op jit(solution)/shard_map/ppermute | solution.py:358
  31.1 2.1 %collective-permute-start.19 = (f32[16,128]{1,0:T(8,128)S(1)}, f32[16,128]{1,0:T(8,128)S(1)}, u32[]{:S(2)}, u32[]{:S(2)}) collective-permute-start(f32[16,128]{1,0:T(8,128)S(1)} %get-tuple-element.67), channel_id=1, source_target_pairs={{0,8},{8,0},{16,24},{24,16},{1,9},{9,1},{17,25},{25,17},{2,10},{10... | collective-permute-start | bytes 24584 | tf_op jit(solution)/shard_map/ppermute | solution.py:358

commit v4 on v3

--- a/solution.py
+++ b/solution.py
@@ -48,23 +48,42 @@
             native_ref[v, p] = plane[p * th : (p + 1) * th]
 
 
-def apply_blocks(vectors, turned_ref, first):
+def spread_rows(vectors):
     rounded = vectors.astype(jnp.bfloat16)
     row = lax.broadcasted_iota(jnp.int32, rounded.shape, 0) % GROUP
-    spread = jnp.concatenate(
+    return jnp.concatenate(
         [jnp.where(row == m, rounded, jnp.zeros_like(rounded)) for m in range(GROUP)], axis=1
     )
-    halves = [
-        jnp.concatenate([turned_ref[first + half * GROUP + m] for m in range(GROUP)], axis=0) for half in range(2)
-    ]
-    out = jnp.dot(spread, jnp.concatenate(halves, axis=1), preferred_element_type=jnp.float32)
+
+
+def own_halves(out):
     return jnp.concatenate([out[:GROUP, :LANES], out[GROUP:, LANES:]], axis=0)
 
 
-def apply_all(field, turned_ref):
-    return jnp.concatenate(
-        [apply_blocks(field[i : i + 2 * GROUP], turned_ref, i) for i in range(0, field.shape[0], 2 * GROUP)], axis=0
-    )
+def apply_stored(vectors, blocks):
+    halves = [jnp.concatenate(blocks[half * GROUP : (half + 1) * GROUP], axis=1) for half in range(2)]
+    out = lax.dot_general(
+        spread_rows(vectors),
+        jnp.concatenate(halves, axis=0),
+        (((1,), (1,)), ((), ())),
+        preferred_element_type=jnp.float32,
+    )
+    return own_halves(out)
+
+
+def apply_turned(field, turned_ref):
+    parts = []
+    for first in range(0, field.shape[0], 2 * GROUP):
+        halves = [
+            jnp.concatenate([turned_ref[first + half * GROUP + m] for m in range(GROUP)], axis=0) for half in range(2)
+        ]
+        out = jnp.dot(
+            spread_rows(field[first : first + 2 * GROUP]),
+            jnp.concatenate(halves, axis=1),
+            preferred_element_type=jnp.float32,
+        )
+        parts.append(own_halves(out))
+    return jnp.concatenate(parts, axis=0)
 
 
 def pack_faces(field, d_ref, outs, flags_ref, ph, th):
@@ -142,51 +161,65 @@
     return halo_ref[...]
 
 
-def first_kernel(ph, th, names, flags_ref, right_ref, conduct_ref, coupling_ref, codes_ref, inverse_ref, *rest):
-    n = len(names)
-    krylov_ref, conducts_ref, diagonal_ref, mixing_ref, turned_ref, d_ref = rest[:6]
-    faces = dict(zip(names, rest[6 : 6 + n]))
-    right, conduct, coupling, codes, blocks, sems = rest[6 + n :]
+def first_kernel(ph, th, names, sizes, right_ref, conduct_ref, coupling_ref, codes_ref, inverse_ref, *rest):
+    flags_ref, krylov_ref, conducts_ref, diagonal_ref, mixing_ref, held_ref, d_ref, *sent = rest[: 7 + len(names)]
+    right, conduct, coupling, codes, sems = rest[7 + len(names) :]
     per = ph * th
     rows = d_ref.shape[0]
-    nb = rows // per
-    pairs = [(right_ref, right), (coupling_ref, coupling), (codes_ref, codes)]
-    pairs += [(inverse_ref.at[:, :, b], blocks.at[b]) for b in range(nb)] + [(conduct_ref, conduct)]
+    pairs = [(right_ref, right), (coupling_ref, coupling), (codes_ref, codes), (conduct_ref, conduct)]
+    pairs += [(inverse_ref, held_ref)]
     copies = [pltpu.make_async_copy(a, b, sems.at[i]) for i, (a, b) in enumerate(pairs)]
     for copy in copies:
         copy.start()
 
+    def mix():
+        copies[1].wait()
+        lane = lax.broadcasted_iota(jnp.int32, (1, LANES), 1)
+        for m in range(VARS):
+            line = jnp.zeros((1, LANES), jnp.float32)
+            for k in range(VARS):
+                line = jnp.where(lane // BLK == k, coupling[k, (k + m) % VARS], line)
+            mixing_ref[m : m + 1, :] = line
+
+    def ghosts():
+        copies[2].wait()
+        cell = lax.broadcasted_iota(jnp.int32, (per, LANES), 1) % BLK
+        row = lax.broadcasted_iota(jnp.int32, (per, LANES), 0)
+        diagonal_ref[...] = jnp.full_like(diagonal_ref, 6.0)
+        for side, (edge, first, has) in enumerate(((0, 0, 3), (BLK - 1, rows - per, 4))):
+            factor = jnp.zeros((per, LANES), jnp.float32)
+            for i in range(per):
+                code = codes[side, i // th, i % th]
+                value = jnp.where(code == 1, 1.0, jnp.where(code == 2, -1.0, 0.0))
+                factor = jnp.where(row == i, value, factor)
+            factor = jnp.where((cell == edge) & (flags_ref[has : has + 1, :] < 0.5), factor, 0.0)
+            diagonal_ref[first : first + per, :] -= factor
+
+    def lay_out():
+        copies[3].wait()
+        conducts_ref[...] = to_rows(conduct)
+
+    (row_at, row_n), (th_at, th_n), (ph_at, ph_n) = [(lax.axis_index(axis), n) for axis, n in sizes]
+    values = [ph_at % 2, row_at % 2, th_at % 2, row_at > 0, row_at < row_n - 1, th_at > 0, th_at < th_n - 1]
+    for i, value in enumerate(values):
+        flags_ref[i : i + 1, :] = jnp.full((1, LANES), value.astype(jnp.float32))
     copies[0].wait()
-    krylov = to_rows(right)
-    krylov_ref[...] = krylov
-    copies[1].wait()
-    lane = lax.broadcasted_iota(jnp.int32, (1, LANES), 1)
-    for m in range(VARS):
-        line = jnp.zeros((1, LANES), jnp.float32)
-        for k in range(VARS):
-            line = jnp.where(lane // BLK == k, coupling[k, (k + m) % VARS], line)
-        mixing_ref[m : m + 1, :] = line
-    copies[2].wait()
-    cell = lax.broadcasted_iota(jnp.int32, (per, LANES), 1) % BLK
-    row = lax.broadcasted_iota(jnp.int32, (per, LANES), 0)
-    diagonal_ref[...] = jnp.full_like(diagonal_ref, 6.0)
-    for side, (edge, first, has) in enumerate(((0, 0, 3), (BLK - 1, rows - per, 4))):
-        factor = jnp.zeros((per, LANES), jnp.float32)
-        for i in range(per):
-            code = codes[side, i // th, i % th]
-            value = jnp.where(code == 1, 1.0, jnp.where(code == 2, -1.0, 0.0))
-            factor = jnp.where(row == i, value, factor)
-        factor = jnp.where((cell == edge) & (flags_ref[has : has + 1, :] < 0.5), factor, 0.0)
-        diagonal_ref[first : first + per, :] -= factor
-    for b in range(nb):
-        copies[3 + b].wait()
-        for i in range(per):
-            turned_ref[b * per + i] = blocks[b, i // th, i % th].T
-        for i in range(b * per, (b + 1) * per, 2 * GROUP):
-            d_ref[i : i + 2 * GROUP, :] = apply_blocks(krylov[i : i + 2 * GROUP], turned_ref, i)
-    pack_faces(d_ref[...], d_ref, faces, flags_ref, ph, th)
-    copies[3 + nb].wait()
-    conducts_ref[...] = to_rows(conduct)
+    krylov_ref[...] = to_rows(right)
+    mix()
+    ghosts()
+    lay_out()
+    copies[4].wait()
+    for first in range(0, rows, 2 * GROUP):
+        blocks = [held_ref[i % per // th, i % th, i // per] for i in range(first, first + 2 * GROUP)]
+        d_ref[first : first + 2 * GROUP, :] = apply_stored(krylov_ref[first : first + 2 * GROUP, :], blocks)
+    pack_faces(d_ref[...], d_ref, dict(zip(names, sent)), flags_ref, ph, th)
+
+
+def turn_kernel(held_ref, turned_ref):
+    ph, th = held_ref.shape[:2]
+    for i in range(turned_ref.shape[0]):
+        b, place = divmod(i, ph * th)
+        turned_ref[i] = held_ref[place // th, place % th, b].T
 
 
 def local_kernel(ph, th, krylov_ref, last_ref, conduct_ref, diagonal_ref, mixing_ref, out_ref):
@@ -213,7 +246,7 @@
     halo = add_faces(halo_ref, dict(zip(names, rest)), flags_ref, ph, th)
     krylov = local_ref[...] - conduct_ref[...] * halo
     next_ref[...] = krylov
-    direction = apply_all(krylov, turned_ref)
+    direction = apply_turned(krylov, turned_ref)
     d_ref[...] = direction
     pack_faces(direction, d_ref, dict(zip(names, sent)), flags_ref, ph, th)
 
@@ -232,52 +265,29 @@
     gram_ref[...] = jnp.broadcast_to(line, gram_ref.shape)
 
 
-def cholesky(matrix, order):
-    lower = [[None] * order for _ in range(order)]
-    for j in range(order):
-        summed = matrix[j][j]
-        for k in range(j):
-            summed = summed - lower[j][k] * lower[j][k]
-        lower[j][j] = jnp.sqrt(summed)
-        for i in range(j + 1, order):
-            summed = matrix[i][j]
-            for k in range(j):
-                summed = summed - lower[i][k] * lower[j][k]
-            lower[i][j] = summed / lower[j][j]
-    return lower
-
-
 def small_solve(products):
-    factor = cholesky(products, S + 1)
-    upper = [[factor[j][i] if i <= j else None for j in range(S + 1)] for i in range(S + 1)]
-
-    def plus(a, b):
-        return b if a is None else a if b is None else a + b
-
-    hess = [[plus(upper[i][j], upper[i][j + 1]) for j in range(S)] for i in range(S + 1)]
-
-    def dot(j, k):
-        total = None
-        for i in range(S + 1):
-            if hess[i][j] is not None and hess[i][k] is not None:
-                total = plus(total, hess[i][j] * hess[i][k])
-        return total
-
-    normal = [[dot(j, k) for k in range(j + 1)] for j in range(S)]
-    moment = [hess[0][j] * upper[0][0] for j in range(S)]
-    lower = cholesky(normal, S)
-    forward = []
-    for i in range(S):
-        summed = moment[i]
-        for k in range(i):
-            summed = summed - lower[i][k] * forward[k]
-        forward.append(summed / lower[i][i])
+    def entry(i, j):
+        return products[max(i, j)][min(i, j)]
+
+    def normal(j, k):
+        return (entry(j, k) + entry(j + 1, k + 1)) + (entry(j + 1, k) + entry(j, k + 1))
+
+    matrix = [[normal(j, k) for k in range(j + 1)] for j in range(S)]
+    moment = [entry(j, 0) + entry(j + 1, 0) for j in range(S)]
+    inverse = []
+    for j in range(S):
+        inverse.append(1.0 / matrix[j][j])
+        scaled = {i: matrix[i][j] * inverse[j] for i in range(j + 1, S)}
+        for i in range(j + 1, S):
+            for k in range(j + 1, i + 1):
+                matrix[i][k] = matrix[i][k] - scaled[i] * matrix[k][j]
+            moment[i] = moment[i] - scaled[i] * moment[j]
     weights = [None] * S
     for i in reversed(range(S)):
-        summed = forward[i]
+        summed = moment[i]
         for k in range(i + 1, S):
-            summed = summed - lower[k][i] * weights[k]
-        weights[i] = summed / lower[i][i]
+            summed = summed - matrix[k][i] * weights[k]
+        weights[i] = summed * inverse[i]
     return weights
 
 
@@ -290,7 +300,7 @@
         products.append([])
         place = partial_rows if i == S else place
         for j in range(i + 1):
-            products[i].append(line[:, place : place + 1])
+            products[i].append(jnp.broadcast_to(line[:, place : place + 1], line.shape))
             place += 1
     weights = small_solve(products)
     total = weights[0] * directions[0][...]
@@ -299,10 +309,9 @@
     from_rows(total, correction)
     first = pltpu.make_async_copy(correction, correction_ref, sems.at[0])
     first.start()
-    basis = [ref[...] for ref in krylov]
-    total = basis[0]
+    total = krylov[0][...]
     for j in range(S):
-        total = total - weights[j] * (basis[j + 1] + basis[j])
+        total = total - weights[j] * (krylov[j + 1][...] + krylov[j][...])
     from_rows(total, residual)
     second = pltpu.make_async_copy(residual, residual_ref, sems.at[1])
     second.start()
@@ -310,16 +319,16 @@
     second.wait()
 
 
-def call(kernel, outs, scratch, *args, stay=False):
-    def space(a):
-        return pltpu.HBM if stay and (a.ndim > 3 or a.shape[-1] != LANES) else pltpu.VMEM
-
-    placed = [pltpu.with_memory_space_constraint(a, pltpu.HBM) if space(a) == pltpu.HBM else a for a in args]
+def call(kernel, outs, scratch, *args, stay=()):
+    def spec(a):
+        return pl.BlockSpec(memory_space=pltpu.HBM if any(a is b for b in stay) else pltpu.VMEM)
+
+    placed = [pltpu.with_memory_space_constraint(a, pltpu.HBM) if any(a is b for b in stay) else a for a in args]
     return pl.pallas_call(
         kernel,
         out_shape=outs,
-        in_specs=[pl.BlockSpec(memory_space=space(a)) for a in args],
-        out_specs=[pl.BlockSpec(memory_space=space(a)) for a in outs],
+        in_specs=[spec(a) for a in args],
+        out_specs=[spec(a) for a in outs],
         scratch_shapes=scratch,
         compiler_params=pltpu.CompilerParams(vmem_limit_bytes=VMEM_LIMIT),
     )(*placed)
@@ -338,11 +347,6 @@
     if th_n == 2:
         face_rows.pop("th_high")
     names = tuple(face_rows)
-    flags = jnp.stack(
-        [ph_at % 2, row_at % 2, th_at % 2, row_at > 0, row_at < row_n - 1, th_at > 0, th_at < th_n - 1, 0]
-    ).astype(jnp.float32)
-    flags = jnp.broadcast_to(flags[:, None], (flags.shape[0], LANES))
-
     def shape(n):
         return jax.ShapeDtypeStruct((n, LANES), jnp.float32)
 
@@ -359,20 +363,20 @@
         return taken
 
     field = pltpu.VMEM(right_side.shape, jnp.float32)
-    start, conducts, diagonal, mixing, turned, direction, *sent = call(
-        functools.partial(first_kernel, ph, th, names),
-        [whole, whole, whole, shape(VARS), jax.ShapeDtypeStruct((rows, LANES, LANES), jnp.bfloat16), whole] + faces,
+    flags, start, conducts, diagonal, mixing, held, direction, *sent = call(
+        functools.partial(first_kernel, ph, th, names, (("row", row_n), ("th", th_n), ("ph", ph_n))),
+        [shape(VARS), whole, whole, whole, shape(VARS), jax.ShapeDtypeStruct(inverse.shape, jnp.bfloat16), whole] + faces,
         [
             field,
             field,
             pltpu.SMEM(coupling.shape, jnp.float32),
             pltpu.SMEM(face_codes.shape, jnp.int32),
-            pltpu.VMEM((nb, ph, th, LANES, LANES), jnp.bfloat16),
-            pltpu.SemaphoreType.DMA((nb + 4,)),
+            pltpu.SemaphoreType.DMA((5,)),
         ],
-        flags, right_side, conduct, coupling, face_codes, inverse,
-        stay=True,
-    )
+        right_side, conduct, coupling, face_codes, inverse,
+        stay=(right_side, conduct, coupling, face_codes, inverse),
+    )
+    (turned,) = call(turn_kernel, [jax.ShapeDtypeStruct((rows, LANES, LANES), jnp.bfloat16)], [], held)
     krylov, directions = [start], [direction]
     halo = [pltpu.VMEM((rows, LANES), jnp.float32)]
     for step in range(S):
@@ -400,14 +404,14 @@
     )
     krylov.append(following)
     gram = lax.all_to_all(gram, ("row", "th", "ph"), 0, 0, tiled=True)
-    native = jax.ShapeDtypeStruct(right_side.shape, jnp.float32)
+    native = [jax.ShapeDtypeStruct(right_side.shape, jnp.float32)] * 2
     return tuple(
         call(
             functools.partial(combine_kernel, partial_rows),
-            [native, native],
+            native,
             [field, field, pltpu.SemaphoreType.DMA((2,))],
             gram, *krylov, *directions,
-            stay=True,
+            stay=native,
         )
     )
 

time: 46.6 us -> 45.2 us (0.970)
  waiting for transfers between devices: 6.07 us -> 5.46 us
  Pallas kernels: 6.85 us -> 6.24 us
    pallas_call x11 -> x12, Pallas kernels: 6.85 us -> 6.24 us  [call(): pl.pallas_call(kernel, out_shape=outs, in_specs=[spec(a) for a in args],...]
    ppermute x20, waiting for transfers between devices: 6.07 us -> 5.46 us  [exchange(): taken.append(lax.ppermute(array, axis, plans[side](lax.axis_size(axis))))]
  transfers between devices with their start and end apart: 20 -> 20, of which waited for: 9 -> 8; matrix products, arithmetic and copies ran while one was open for 0% -> 0% of each run, Pallas kernels for 1% -> 3%
where the time goes in v4:
time: 45.2 us; the launch traced here: 45 us
  starting transfers between devices  21.3 us (47%)
  blocking collectives  11.3 us (25%)
  Pallas kernels  6.24 us (14%)
  waiting for transfers between devices  5.46 us (12%)
  between operations  0.72 us (2%)
    ppermute x20, starting transfers between devices, exchange(): taken.append(lax.ppermute(array, axis, plans[side](lax.axis_size(axis))))  21.3 us
    all_to_all x1, blocking collectives, local(): gram = lax.all_to_all(gram, ('row', 'th', 'ph'), 0, 0, tiled=True)  11.3 us
    pallas_call x12, Pallas kernels, call(): pl.pallas_call(kernel, out_shape=outs, in_specs=[spec(a) for a in args],...  6.24 us
    ppermute x20, waiting for transfers between devices, exchange(): taken.append(lax.ppermute(array, axis, plans[side](lax.axis_size(axis))))  5.46 us
  transfers between devices with their start and end apart: 20, of which 8 were waited for; matrix products, arithmetic and copies ran while one was open for 0% of the time, Pallas kernels for 3%

profile of v4, /device:TPU:0, one launch (start us, length us, event | category | flops | bytes accessed | tf_op | source)
XLA Modules:
  0.0 45.0 jit_solution(2375775241460265855)
XLA Ops:
  0.6 2.4 %shard_map.68 = (f32[8,128]{1,0:T(8,128)S(1)}, f32[64,128]{1,0:T(8,128)S(1)}, f32[64,128]{1,0:T(8,128)S(1)}, f32[64,128]{1,0:T(8,128)S(1)}, f32[8,128]{1,0:T(8,1...) custom-call(f32[8,4,4,64]{3,2,1,0:T(4,128)} %right_ref.1, ...), custom_call_target="tpu_custom_call" | custom-call | tf_op jit(solution)/shard_map/pallas_call | solution.py:327
  3.1 5.1 %collective-permute-start = (f32[16,128]{1,0:T(8,128)S(1)}, f32[16,128]{1,0:T(8,128)S(1)}, u32[]{:S(2)}, u32[]{:S(2)}) collective-permute-start(f32[16,128]{1,0:T(8,128)S(1)} %get-tuple-element.44), channel_id=1, source_target_pairs={{0,3},{1,2},{2,1},{3,0},{4,7},{5,6},{6,5},{7,4},{8,11},{9,10},{10,... | collective-permute-start | bytes 24584 | tf_op jit(solution)/shard_map/ppermute | solution.py:362
  8.2 0.7 %collective-permute-start.1 = (f32[16,128]{1,0:T(8,128)S(1)}, f32[16,128]{1,0:T(8,128)S(1)}, u32[]{:S(2)}, u32[]{:S(2)}) collective-permute-start(f32[16,128]{1,0:T(8,128)S(1)} %get-tuple-element.45), channel_id=1, source_target_pairs={{0,24},{8,16},{16,8},{24,0},{1,25},{9,17},{17,9},{25,1},{2,26},{10... | collective-permute-start | bytes 24584 | tf_op jit(solution)/shard_map/ppermute | solution.py:362
  8.9 0.0 collective-permute-start.2
  8.9 1.5 %collective-permute-start.3 = (f32[16,128]{1,0:T(8,128)S(1)}, f32[16,128]{1,0:T(8,128)S(1)}, u32[]{:S(2)}, u32[]{:S(2)}) collective-permute-start(f32[16,128]{1,0:T(8,128)S(1)} %get-tuple-element.47), channel_id=1, source_target_pairs={{0,4},{4,0},{1,5},{5,1},{2,6},{6,2},{3,7},{7,3},{8,12},{12,8},{9,1... | collective-permute-start | bytes 24584 | tf_op jit(solution)/shard_map/ppermute | solution.py:362
  10.4 0.7 %collective-permute-start.4 = (f32[16,128]{1,0:T(8,128)S(1)}, f32[16,128]{1,0:T(8,128)S(1)}, u32[]{:S(2)}, u32[]{:S(2)}) collective-permute-start(f32[16,128]{1,0:T(8,128)S(1)} %get-tuple-element.48), channel_id=1, source_target_pairs={{0,8},{8,0},{16,24},{24,16},{1,9},{9,1},{17,25},{25,17},{2,10},{10... | collective-permute-start | bytes 24584 | tf_op jit(solution)/shard_map/ppermute | solution.py:362
  11.1 0.6 %shard_map.70.turned_ref = bf16[64,128,128]{2,1,0:T(8,128)(2,1)S(1)} custom-call(bf16[4,4,4,128,128]{4,3,2,1,0:T(8,128)(2,1)S(1)} %get-tuple-element.43.held_ref), custom_call_target="tpu_custom_call" | custom-call | tf_op jit(solution)/shard_map/pallas_call | solution.py:327
  11.6 0.2 shard_map.69.local_ref
  11.8 0.0 collective-permute-done.rest_0_
  11.8 0.0 collective-permute-done.1.rest_1_
  11.8 0.7 %collective-permute-done.2.rest_2_ = f32[16,128]{1,0:T(8,128)S(1)} collective-permute-done((f32[16,128]{1,0:T(8,128)S(1)}, f32[16,128]{1,0:T(8,128)S(1)}, u32[]{:S(2)}, u32[]{:S(2)}) %collective-permute-start.2) | collective-permute-done | bytes 8224 | tf_op jit(solution)/shard_map/ppermute | solution.py:362
  12.6 0.0 collective-permute-done.3.rest_3_
  12.6 0.0 collective-permute-done.4.rest_4_
  12.6 0.5 %shard_map.71 = (f32[64,128]{1,0:T(8,128)S(1)}, f32[64,128]{1,0:T(8,128)S(1)}, f32[16,128]{1,0:T(8,128)S(1)}, f32[16,128]{1,0:T(8,128)S(1)}, f32[16,128]{1,0:T(8...) custom-call(f32[8,128]{1,0:T(8,128)S(1)} %get-tuple-element.37.flags_ref, f32[64,128]{1,0:T(8,128)S(1)} %shard_map.69.local_ref, ...), custom_call_target="tpu_custom_call" | custom-call | tf_op jit(solution)/shard_map/pallas_call | solution.py:327
  13.1 1.1 %collective-permute-start.5 = (f32[16,128]{1,0:T(8,128)S(1)}, f32[16,128]{1,0:T(8,128)S(1)}, u32[]{:S(2)}, u32[]{:S(2)}) collective-permute-start(f32[16,128]{1,0:T(8,128)S(1)} %get-tuple-element.51), channel_id=1, source_target_pairs={{0,3},{1,2},{2,1},{3,0},{4,7},{5,6},{6,5},{7,4},{8,11},{9,10},{10,... | collective-permute-start | bytes 24584 | tf_op jit(solution)/shard_map/ppermute | solution.py:362
  14.2 0.0 collective-permute-start.6
  14.2 1.0 %collective-permute-start.7 = (f32[16,128]{1,0:T(8,128)S(1)}, f32[16,128]{1,0:T(8,128)S(1)}, u32[]{:S(2)}, u32[]{:S(2)}) collective-permute-start(f32[16,128]{1,0:T(8,128)S(1)} %get-tuple-element.53), channel_id=1, source_target_pairs={{0,1},{1,0},{2,3},{3,2},{4,5},{5,4},{6,7},{7,6},{8,9},{9,8},{10,11... | collective-permute-start | bytes 24584 | tf_op jit(solution)/shard_map/ppermute | solution.py:362
  15.2 1.5 %collective-permute-start.8 = (f32[16,128]{1,0:T(8,128)S(1)}, f32[16,128]{1,0:T(8,128)S(1)}, u32[]{:S(2)}, u32[]{:S(2)}) collective-permute-start(f32[16,128]{1,0:T(8,128)S(1)} %get-tuple-element.54), channel_id=1, source_target_pairs={{0,4},{4,0},{1,5},{5,1},{2,6},{6,2},{3,7},{7,3},{8,12},{12,8},{9,1... | collective-permute-start | bytes 24584 | tf_op jit(solution)/shard_map/ppermute | solution.py:362
  16.7 0.4 collective-permute-start.9
  17.1 0.2 shard_map.72.local_ref
  17.2 1.4 %collective-permute-done.5.rest_0_ = f32[16,128]{1,0:T(8,128)S(1)} collective-permute-done((f32[16,128]{1,0:T(8,128)S(1)}, f32[16,128]{1,0:T(8,128)S(1)}, u32[]{:S(2)}, u32[]{:S(2)}) %collective-permute-start.5) | collective-permute-done | bytes 8224 | tf_op jit(solution)/shard_map/ppermute | solution.py:362
  18.6 0.0 collective-permute-done.6.rest_1_
  18.6 0.0 collective-permute-done.7.rest_2_
  18.6 0.2 collective-permute-done.8.rest_3_
  18.8 0.0 collective-permute-done.9.rest_4_
  18.8 0.5 %shard_map.73 = (f32[64,128]{1,0:T(8,128)S(1)}, f32[64,128]{1,0:T(8,128)S(1)}, f32[16,128]{1,0:T(8,128)S(1)}, f32[16,128]{1,0:T(8,128)S(1)}, f32[16,128]{1,0:T(8...) custom-call(f32[8,128]{1,0:T(8,128)S(1)} %get-tuple-element.37.flags_ref, f32[64,128]{1,0:T(8,128)S(1)} %shard_map.72.local_ref, ...), custom_call_target="tpu_custom_call" | custom-call | tf_op jit(solution)/shard_map/pallas_call | solution.py:327
  19.3 2.8 %collective-permute-start.10 = (f32[16,128]{1,0:T(8,128)S(1)}, f32[16,128]{1,0:T(8,128)S(1)}, u32[]{:S(2)}, u32[]{:S(2)}) collective-permute-start(f32[16,128]{1,0:T(8,128)S(1)} %get-tuple-element.58), channel_id=1, source_target_pairs={{0,3},{1,2},{2,1},{3,0},{4,7},{5,6},{6,5},{7,4},{8,11},{9,10},{10,... | collective-permute-start | bytes 24584 | tf_op jit(solution)/shard_map/ppermute | solution.py:362
  22.1 0.4 collective-permute-start.11
  22.5 0.0 collective-permute-start.12
  22.5 1.5 %collective-permute-start.13 = (f32[16,128]{1,0:T(8,128)S(1)}, f32[16,128]{1,0:T(8,128)S(1)}, u32[]{:S(2)}, u32[]{:S(2)}) collective-permute-start(f32[16,128]{1,0:T(8,128)S(1)} %get-tuple-element.61), channel_id=1, source_target_pairs={{0,4},{4,0},{1,5},{5,1},{2,6},{6,2},{3,7},{7,3},{8,12},{12,8},{9,1... | collective-permute-start | bytes 24584 | tf_op jit(solution)/shard_map/ppermute | solution.py:362
  24.0 0.7 %collective-permute-start.14 = (f32[16,128]{1,0:T(8,128)S(1)}, f32[16,128]{1,0:T(8,128)S(1)}, u32[]{:S(2)}, u32[]{:S(2)}) collective-permute-start(f32[16,128]{1,0:T(8,128)S(1)} %get-tuple-element.62), channel_id=1, source_target_pairs={{0,8},{8,0},{16,24},{24,16},{1,9},{9,1},{17,25},{25,17},{2,10},{10... | collective-permute-start | bytes 24584 | tf_op jit(solution)/shard_map/ppermute | solution.py:362
  24.7 0.2 shard_map.74.local_ref
  24.9 0.0 collective-permute-done.10.rest_0_
  24.9 0.3 collective-permute-done.11.rest_1_
  25.2 1.0 %collective-permute-done.12.rest_2_ = f32[16,128]{1,0:T(8,128)S(1)} collective-permute-done((f32[16,128]{1,0:T(8,128)S(1)}, f32[16,128]{1,0:T(8,128)S(1)}, u32[]{:S(2)}, u32[]{:S(2)}) %collective-permute-start.12) | collective-permute-done | bytes 8224 | tf_op jit(solution)/shard_map/ppermute | solution.py:362
  26.1 0.1 collective-permute-done.13.rest_3_
  26.2 0.0 collective-permute-done.14.rest_4_
  26.2 0.5 %shard_map.75 = (f32[64,128]{1,0:T(8,128)S(1)}, f32[64,128]{1,0:T(8,128)S(1)}, f32[16,128]{1,0:T(8,128)S(1)}, f32[16,128]{1,0:T(8,128)S(1)}, f32[16,128]{1,0:T(8...) custom-call(f32[8,128]{1,0:T(8,128)S(1)} %get-tuple-element.37.flags_ref, f32[64,128]{1,0:T(8,128)S(1)} %shard_map.74.local_ref, ...), custom_call_target="tpu_custom_call" | custom-call | tf_op jit(solution)/shard_map/pallas_call | solution.py:327
  26.7 1.4 %collective-permute-start.15 = (f32[16,128]{1,0:T(8,128)S(1)}, f32[16,128]{1,0:T(8,128)S(1)}, u32[]{:S(2)}, u32[]{:S(2)}) collective-permute-start(f32[16,128]{1,0:T(8,128)S(1)} %get-tuple-element.65), channel_id=1, source_target_pairs={{0,3},{1,2},{2,1},{3,0},{4,7},{5,6},{6,5},{7,4},{8,11},{9,10},{10,... | collective-permute-start | bytes 24584 | tf_op jit(solution)/shard_map/ppermute | solution.py:362
  28.0 0.0 collective-permute-start.16
  28.0 0.9 %collective-permute-start.17 = (f32[16,128]{1,0:T(8,128)S(1)}, f32[16,128]{1,0:T(8,128)S(1)}, u32[]{:S(2)}, u32[]{:S(2)}) collective-permute-start(f32[16,128]{1,0:T(8,128)S(1)} %get-tuple-element.67), channel_id=1, source_target_pairs={{0,1},{1,0},{2,3},{3,2},{4,5},{5,4},{6,7},{7,6},{8,9},{9,8},{10,11... | collective-permute-start | bytes 24584 | tf_op jit(solution)/shard_map/ppermute | solution.py:362
  29.0 1.5 %collective-permute-start.18 = (f32[16,128]{1,0:T(8,128)S(1)}, f32[16,128]{1,0:T(8,128)S(1)}, u32[]{:S(2)}, u32[]{:S(2)}) collective-permute-start(f32[16,128]{1,0:T(8,128)S(1)} %get-tuple-element.68), channel_id=1, source_target_pairs={{0,4},{4,0},{1,5},{5,1},{2,6},{6,2},{3,7},{7,3},{8,12},{12,8},{9,1... | collective-permute-start | bytes 24584 | tf_op jit(solution)/shard_map/ppermute | solution.py:362
  30.5 0.2 collective-permute-start.19
  30.7 0.2 shard_map.76.local_ref
  30.9 1.3 %collective-permute-done.15.rest_4_ = f32[16,128]{1,0:T(8,128)S(1)} collective-permute-done((f32[16,128]{1,0:T(8,128)S(1)}, f32[16,128]{1,0:T(8,128)S(1)}, u32[]{:S(2)}, u32[]{:S(2)}) %collective-permute-start.15) | collective-permute-done | bytes 8224 | tf_op jit(solution)/shard_map/ppermute | solution.py:362
  32.1 0.0 collective-permute-done.16.rest_5_
  32.1 0.0 collective-permute-done.17.rest_6_
  32.2 0.5 %collective-permute-done.18.rest_7_ = f32[16,128]{1,0:T(8,128)S(1)} collective-permute-done((f32[16,128]{1,0:T(8,128)S(1)}, f32[16,128]{1,0:T(8,128)S(1)}, u32[]{:S(2)}, u32[]{:S(2)}) %collective-permute-start.18) | collective-permute-done | bytes 8224 | tf_op jit(solution)/shard_map/ppermute | solution.py:362
  32.6 0.0 collective-permute-done.19.rest_8_
  32.6 0.1 shard_map.78
  32.8 11.3 %all_to_all.11 = f32[32,1,128]{2,1,0:T(1,128)S(1)} all-to-all(f32[32,1,128]{2,1,0:T(1,128)S(1)} %bitcast.5), channel_id=1, replica_groups=mesh['row'=4,'th'=2,'ph'=4] {'row','th','ph'}, dimensions={0} | all-to-all | bytes 32768 | tf_op jit(solution)/shard_map/all_to_all | solution.py:406
  44.0 1.0 %shard_map.79 = (f32[8,4,4,64]{3,2,1,0:T(4,128)}, f32[8,4,4,64]{3,2,1,0:T(4,128)}) custom-call(f32[32,128]{1,0:T(8,128)S(1)} %bitcast.4, f32[64,128]{1,0:T(8,128)S(1)} %get-tuple-element.38.krylov_ref.refs_0_.rest_0_, f32[64,128]{1,0:T(8,128)S(1)} %get-tuple-element.49.krylov_ref.refs_1_.rest_1_, f32[64,128]{1,0:T(8,128)S(1)} %get-tuple-element.56.krylov_ref.refs_2_.rest_2_, ...), custom_call_target="tpu_custom_call" | custom-call | tf_op jit(solution)/shard_map/pallas_call | solution.py:327
  (1 shorter events, 0.0 us)
Async XLA Ops:
  3.1 8.7 %collective-permute-start = (f32[16,128]{1,0:T(8,128)S(1)}, f32[16,128]{1,0:T(8,128)S(1)}, u32[]{:S(2)}, u32[]{:S(2)}) collective-permute-start(f32[16,128]{1,0:T(8,128)S(1)} %get-tuple-element.44), channel_id=1, source_target_pairs={{0,3},{1,2},{2,1},{3,0},{4,7},{5,6},{6,5},{7,4},{8,11},{9,10},{10,... | collective-permute-start | bytes 24584 | tf_op jit(solution)/shard_map/ppermute | solution.py:362
  8.2 3.6 %collective-permute-start.1 = (f32[16,128]{1,0:T(8,128)S(1)}, f32[16,128]{1,0:T(8,128)S(1)}, u32[]{:S(2)}, u32[]{:S(2)}) collective-permute-start(f32[16,128]{1,0:T(8,128)S(1)} %get-tuple-element.45), channel_id=1, source_target_pairs={{0,24},{8,16},{16,8},{24,0},{1,25},{9,17},{17,9},{25,1},{2,26},{10... | collective-permute-start | bytes 24584 | tf_op jit(solution)/shard_map/ppermute | solution.py:362
  8.9 3.7 %collective-permute-start.2 = (f32[16,128]{1,0:T(8,128)S(1)}, f32[16,128]{1,0:T(8,128)S(1)}, u32[]{:S(2)}, u32[]{:S(2)}) collective-permute-start(f32[16,128]{1,0:T(8,128)S(1)} %get-tuple-element.46), channel_id=1, source_target_pairs={{0,1},{1,0},{2,3},{3,2},{4,5},{5,4},{6,7},{7,6},{8,9},{9,8},{10,11... | collective-permute-start | bytes 24584 | tf_op jit(solution)/shard_map/ppermute | solution.py:362
  8.9 3.7 %collective-permute-start.3 = (f32[16,128]{1,0:T(8,128)S(1)}, f32[16,128]{1,0:T(8,128)S(1)}, u32[]{:S(2)}, u32[]{:S(2)}) collective-permute-start(f32[16,128]{1,0:T(8,128)S(1)} %get-tuple-element.47), channel_id=1, source_target_pairs={{0,4},{4,0},{1,5},{5,1},{2,6},{6,2},{3,7},{7,3},{8,12},{12,8},{9,1... | collective-permute-start | bytes 24584 | tf_op jit(solution)/shard_map/ppermute | solution.py:362
  10.4 2.2 %collective-permute-start.4 = (f32[16,128]{1,0:T(8,128)S(1)}, f32[16,128]{1,0:T(8,128)S(1)}, u32[]{:S(2)}, u32[]{:S(2)}) collective-permute-start(f32[16,128]{1,0:T(8,128)S(1)} %get-tuple-element.48), channel_id=1, source_target_pairs={{0,8},{8,0},{16,24},{24,16},{1,9},{9,1},{17,25},{25,17},{2,10},{10... | collective-permute-start | bytes 24584 | tf_op jit(solution)/shard_map/ppermute | solution.py:362
  13.1 5.5 %collective-permute-start.5 = (f32[16,128]{1,0:T(8,128)S(1)}, f32[16,128]{1,0:T(8,128)S(1)}, u32[]{:S(2)}, u32[]{:S(2)}) collective-permute-start(f32[16,128]{1,0:T(8,128)S(1)} %get-tuple-element.51), channel_id=1, source_target_pairs={{0,3},{1,2},{2,1},{3,0},{4,7},{5,6},{6,5},{7,4},{8,11},{9,10},{10,... | collective-permute-start | bytes 24584 | tf_op jit(solution)/shard_map/ppermute | solution.py:362
  14.2 4.4 %collective-permute-start.6 = (f32[16,128]{1,0:T(8,128)S(1)}, f32[16,128]{1,0:T(8,128)S(1)}, u32[]{:S(2)}, u32[]{:S(2)}) collective-permute-start(f32[16,128]{1,0:T(8,128)S(1)} %get-tuple-element.52), channel_id=1, source_target_pairs={{0,24},{8,16},{16,8},{24,0},{1,25},{9,17},{17,9},{25,1},{2,26},{10... | collective-permute-start | bytes 24584 | tf_op jit(solution)/shard_map/ppermute | solution.py:362
  14.2 4.4 %collective-permute-start.7 = (f32[16,128]{1,0:T(8,128)S(1)}, f32[16,128]{1,0:T(8,128)S(1)}, u32[]{:S(2)}, u32[]{:S(2)}) collective-permute-start(f32[16,128]{1,0:T(8,128)S(1)} %get-tuple-element.53), channel_id=1, source_target_pairs={{0,1},{1,0},{2,3},{3,2},{4,5},{5,4},{6,7},{7,6},{8,9},{9,8},{10,11... | collective-permute-start | bytes 24584 | tf_op jit(solution)/shard_map/ppermute | solution.py:362
  15.2 3.7 %collective-permute-start.8 = (f32[16,128]{1,0:T(8,128)S(1)}, f32[16,128]{1,0:T(8,128)S(1)}, u32[]{:S(2)}, u32[]{:S(2)}) collective-permute-start(f32[16,128]{1,0:T(8,128)S(1)} %get-tuple-element.54), channel_id=1, source_target_pairs={{0,4},{4,0},{1,5},{5,1},{2,6},{6,2},{3,7},{7,3},{8,12},{12,8},{9,1... | collective-permute-start | bytes 24584 | tf_op jit(solution)/shard_map/ppermute | solution.py:362
  16.7 2.1 %collective-permute-start.9 = (f32[16,128]{1,0:T(8,128)S(1)}, f32[16,128]{1,0:T(8,128)S(1)}, u32[]{:S(2)}, u32[]{:S(2)}) collective-permute-start(f32[16,128]{1,0:T(8,128)S(1)} %get-tuple-element.55), channel_id=1, source_target_pairs={{0,8},{8,0},{16,24},{24,16},{1,9},{9,1},{17,25},{25,17},{2,10},{10... | collective-permute-start | bytes 24584 | tf_op jit(solution)/shard_map/ppermute | solution.py:362
  19.3 5.6 %collective-permute-start.10 = (f32[16,128]{1,0:T(8,128)S(1)}, f32[16,128]{1,0:T(8,128)S(1)}, u32[]{:S(2)}, u32[]{:S(2)}) collective-permute-start(f32[16,128]{1,0:T(8,128)S(1)} %get-tuple-element.58), channel_id=1, source_target_pairs={{0,3},{1,2},{2,1},{3,0},{4,7},{5,6},{6,5},{7,4},{8,11},{9,10},{10,... | collective-permute-start | bytes 24584 | tf_op jit(solution)/shard_map/ppermute | solution.py:362
  22.1 3.1 %collective-permute-start.11 = (f32[16,128]{1,0:T(8,128)S(1)}, f32[16,128]{1,0:T(8,128)S(1)}, u32[]{:S(2)}, u32[]{:S(2)}) collective-permute-start(f32[16,128]{1,0:T(8,128)S(1)} %get-tuple-element.59), channel_id=1, source_target_pairs={{0,24},{8,16},{16,8},{24,0},{1,25},{9,17},{17,9},{25,1},{2,26},{10... | collective-permute-start | bytes 24584 | tf_op jit(solution)/shard_map/ppermute | solution.py:362
  22.5 3.7 %collective-permute-start.12 = (f32[16,128]{1,0:T(8,128)S(1)}, f32[16,128]{1,0:T(8,128)S(1)}, u32[]{:S(2)}, u32[]{:S(2)}) collective-permute-start(f32[16,128]{1,0:T(8,128)S(1)} %get-tuple-element.60), channel_id=1, source_target_pairs={{0,1},{1,0},{2,3},{3,2},{4,5},{5,4},{6,7},{7,6},{8,9},{9,8},{10,11... | collective-permute-start | bytes 24584 | tf_op jit(solution)/shard_map/ppermute | solution.py:362
  22.5 3.7 %collective-permute-start.13 = (f32[16,128]{1,0:T(8,128)S(1)}, f32[16,128]{1,0:T(8,128)S(1)}, u32[]{:S(2)}, u32[]{:S(2)}) collective-permute-start(f32[16,128]{1,0:T(8,128)S(1)} %get-tuple-element.61), channel_id=1, source_target_pairs={{0,4},{4,0},{1,5},{5,1},{2,6},{6,2},{3,7},{7,3},{8,12},{12,8},{9,1... | collective-permute-start | bytes 24584 | tf_op jit(solution)/shard_map/ppermute | solution.py:362
  24.0 2.2 %collective-permute-start.14 = (f32[16,128]{1,0:T(8,128)S(1)}, f32[16,128]{1,0:T(8,128)S(1)}, u32[]{:S(2)}, u32[]{:S(2)}) collective-permute-start(f32[16,128]{1,0:T(8,128)S(1)} %get-tuple-element.62), channel_id=1, source_target_pairs={{0,8},{8,0},{16,24},{24,16},{1,9},{9,1},{17,25},{25,17},{2,10},{10... | collective-permute-start | bytes 24584 | tf_op jit(solution)/shard_map/ppermute | solution.py:362
  26.7 5.5 %collective-permute-start.15 = (f32[16,128]{1,0:T(8,128)S(1)}, f32[16,128]{1,0:T(8,128)S(1)}, u32[]{:S(2)}, u32[]{:S(2)}) collective-permute-start(f32[16,128]{1,0:T(8,128)S(1)} %get-tuple-element.65), channel_id=1, source_target_pairs={{0,3},{1,2},{2,1},{3,0},{4,7},{5,6},{6,5},{7,4},{8,11},{9,10},{10,... | collective-permute-start | bytes 24584 | tf_op jit(solution)/shard_map/ppermute | solution.py:362
  28.0 4.1 %collective-permute-start.16 = (f32[16,128]{1,0:T(8,128)S(1)}, f32[16,128]{1,0:T(8,128)S(1)}, u32[]{:S(2)}, u32[]{:S(2)}) collective-permute-start(f32[16,128]{1,0:T(8,128)S(1)} %get-tuple-element.66), channel_id=1, source_target_pairs={{0,24},{8,16},{16,8},{24,0},{1,25},{9,17},{17,9},{25,1},{2,26},{10... | collective-permute-start | bytes 24584 | tf_op jit(solution)/shard_map/ppermute | solution.py:362
  28.0 4.1 %collective-permute-start.17 = (f32[16,128]{1,0:T(8,128)S(1)}, f32[16,128]{1,0:T(8,128)S(1)}, u32[]{:S(2)}, u32[]{:S(2)}) collective-permute-start(f32[16,128]{1,0:T(8,128)S(1)} %get-tuple-element.67), channel_id=1, source_target_pairs={{0,1},{1,0},{2,3},{3,2},{4,5},{5,4},{6,7},{7,6},{8,9},{9,8},{10,11... | collective-permute-start | bytes 24584 | tf_op jit(solution)/shard_map/ppermute | solution.py:362
  29.0 3.7 %collective-permute-start.18 = (f32[16,128]{1,0:T(8,128)S(1)}, f32[16,128]{1,0:T(8,128)S(1)}, u32[]{:S(2)}, u32[]{:S(2)}) collective-permute-start(f32[16,128]{1,0:T(8,128)S(1)} %get-tuple-element.68), channel_id=1, source_target_pairs={{0,4},{4,0},{1,5},{5,1},{2,6},{6,2},{3,7},{7,3},{8,12},{12,8},{9,1... | collective-permute-start | bytes 24584 | tf_op jit(solution)/shard_map/ppermute | solution.py:362
  30.5 2.1 %collective-permute-start.19 = (f32[16,128]{1,0:T(8,128)S(1)}, f32[16,128]{1,0:T(8,128)S(1)}, u32[]{:S(2)}, u32[]{:S(2)}) collective-permute-start(f32[16,128]{1,0:T(8,128)S(1)} %get-tuple-element.69), channel_id=1, source_target_pairs={{0,8},{8,0},{16,24},{24,16},{1,9},{9,1},{17,25},{25,17},{2,10},{10... | collective-permute-start | bytes 24584 | tf_op jit(solution)/shard_map/ppermute | solution.py:362

commit v5 on v4

v5 whole, which is shorter than its diff:
```python
import functools

import jax
import jax.numpy as jnp
from jax import lax
from jax.experimental import pallas as pl
from jax.experimental.pallas import tpu as pltpu
from jax.sharding import PartitionSpec as P

VARS = 8
BLK = 16
S = 4
LANES = VARS * BLK
GROUP = 8
VMEM_LIMIT = 24 * 1024 * 1024


def pairs_low(count):
    return [(i, i ^ 1) for i in range(count)]


def pairs_high(count):
    return [(i, (i + 1) % count if i % 2 else (i - 1) % count) for i in range(count)]


def to_rows(native_ref, turn_ref):
    var, ph, th, radial = native_ref.shape
    planes = [jnp.concatenate([native_ref[v, p] for p in range(ph)], axis=0) for v in range(var)]
    for b in range(radial // BLK):
        turn_ref[b * ph * th : (b + 1) * ph * th, :] = jnp.concatenate(
            [plane[:, b * BLK : (b + 1) * BLK] for plane in planes], axis=1
        )
    slab = turn_ref.shape[0] // th
    return jnp.concatenate([turn_ref[pl.ds(t, slab, stride=th), :] for t in range(th)], axis=0)


def from_rows(rows, native_ref, turn_ref):
    var, ph, th, radial = native_ref.shape
    slab = rows.shape[0] // th
    for t in range(th):
        turn_ref[pl.ds(t, slab, stride=th), :] = rows[t * slab : (t + 1) * slab]
    turned = turn_ref[...]
    per = ph * th
    for v in range(var):
        plane = jnp.concatenate(
            [turned[b * per : (b + 1) * per, v * BLK : (v + 1) * BLK] for b in range(radial // BLK)], axis=1
        )
        for p in range(ph):
            native_ref[v, p] = plane[p * th : (p + 1) * th]


def spread_rows(vectors):
    rounded = vectors.astype(jnp.bfloat16)
    row = lax.broadcasted_iota(jnp.int32, rounded.shape, 0) % GROUP
    return jnp.concatenate(
        [jnp.where(row == m, rounded, jnp.zeros_like(rounded)) for m in range(GROUP)], axis=1
    )


def own_halves(out):
    return jnp.concatenate([out[:GROUP, :LANES], out[GROUP:, LANES:]], axis=0)


def apply_stored(vectors, blocks):
    halves = [jnp.concatenate(blocks[half * GROUP : (half + 1) * GROUP], axis=1) for half in range(2)]
    out = lax.dot_general(
        spread_rows(vectors),
        jnp.concatenate(halves, axis=0),
        (((1,), (1,)), ((), ())),
        preferred_element_type=jnp.float32,
    )
    return own_halves(out)


def apply_turned(field_ref, turned_ref, out_ref, firsts):
    for first in firsts:
        halves = [
            jnp.concatenate([turned_ref[first + half * GROUP + m] for m in range(GROUP)], axis=0) for half in range(2)
        ]
        out = jnp.dot(
            spread_rows(field_ref[pl.ds(first, 2 * GROUP), :]),
            jnp.concatenate(halves, axis=1),
            preferred_element_type=jnp.float32,
        )
        out_ref[pl.ds(first, 2 * GROUP), :] = own_halves(out)


def pack_faces(d_ref, outs, flags_ref, ph, th):
    rows = d_ref.shape[0]
    slab = rows // th
    per = ph * th
    cell = lax.broadcasted_iota(jnp.int32, (per, LANES), 1) % BLK
    odd_ph, odd_row, odd_th = [flags_ref[i : i + 1, :] > 0.5 for i in range(3)]
    low = d_ref[pl.ds(0, rows // ph, stride=ph), :]
    high = d_ref[pl.ds(ph - 1, rows // ph, stride=ph), :]
    outs["ph_high"][...] = jnp.where(odd_ph, high, low)
    outs["ph_low"][...] = jnp.where(odd_ph, low, high)
    low = jnp.concatenate([d_ref[t * slab : t * slab + ph, :] for t in range(th)], axis=0)
    high = jnp.concatenate([d_ref[(t + 1) * slab - ph : (t + 1) * slab, :] for t in range(th)], axis=0)
    low = jnp.where(cell == BLK - 1, pltpu.roll(low, BLK - 1, 1), 0.0)
    high = jnp.where(cell == 0, pltpu.roll(high, LANES - BLK + 1, 1), 0.0)
    near = jnp.where(odd_row, low, high)
    outs["row_low"][...] = near[: per // 2] + pltpu.roll(near[per // 2 :], 1, 1)
    if "row_high" in outs:
        outs["row_high"][...] = jnp.where(odd_row, high, low)
    low, high = d_ref[:slab, :], d_ref[rows - slab :, :]
    outs["th_low"][...] = jnp.where(odd_th, low, high)
    if "th_high" in outs:
        outs["th_high"][...] = jnp.where(odd_th, high, low)


def local_part(field, krylov, conduct, diagonal, mixing_ref, ph, th):
    rows = field.shape[0]
    slab = rows // th
    nb = slab // ph
    lane = lax.broadcasted_iota(jnp.int32, (rows, LANES), 1)
    row = lax.broadcasted_iota(jnp.int32, (rows, LANES), 0)
    cell = lane % BLK
    azimuth = row % ph
    block = (row // ph) % nb
    mixed = field * mixing_ref[0:1, :]
    for m in range(1, VARS):
        mixed += pltpu.roll(field, LANES - BLK * m, 1) * mixing_ref[m : m + 1, :]
    from_low = pltpu.roll(pltpu.roll(field, LANES - BLK + 1, 1), ph, 0)
    from_high = pltpu.roll(pltpu.roll(field, BLK - 1, 1), rows - ph, 0)
    total = jnp.where(cell == 0, jnp.where(block == 0, 0.0, from_low), pltpu.roll(field, 1, 1))
    total += jnp.where(
        cell == BLK - 1, jnp.where(block == nb - 1, 0.0, from_high), pltpu.roll(field, LANES - 1, 1)
    )
    total += jnp.where(azimuth == 0, 0.0, pltpu.roll(field, 1, 0))
    total += jnp.where(azimuth == ph - 1, 0.0, pltpu.roll(field, rows - 1, 0))
    zero = jnp.zeros((slab, LANES), jnp.float32)
    total += jnp.concatenate([zero, field[: rows - slab]], axis=0)
    total += jnp.concatenate([field[slab:], zero], axis=0)
    return field + mixed + conduct * (diagonal * field - total) - krylov


def sides(axis, taken, flags_ref):
    parity, has_low, has_high = {"ph": (0, None, None), "row": (1, 3, 4), "th": (2, 5, 6)}[axis]
    odd = flags_ref[parity : parity + 1, :] > 0.5
    first = taken[axis + "_low"][...]
    if axis == "row":
        edge = jnp.where(odd, 0, BLK - 1)
        cell = lax.broadcasted_iota(jnp.int32, first.shape, 1) % BLK
        first = jnp.concatenate(
            [jnp.where(cell == edge, part, 0.0) for part in (first, pltpu.roll(first, LANES - 1, 1))], axis=0
        )
    second = taken[axis + "_high"][...] if axis + "_high" in taken else jnp.zeros_like(first)
    low, high = jnp.where(odd, first, second), jnp.where(odd, second, first)
    if has_low is None:
        return low, high
    low = jnp.where(flags_ref[has_low : has_low + 1, :] > 0.5, low, 0.0)
    return low, jnp.where(flags_ref[has_high : has_high + 1, :] > 0.5, high, 0.0)


def add_faces(halo_ref, taken, flags_ref, ph, th):
    rows = halo_ref.shape[0]
    slab = rows // th
    halo_ref[...] = jnp.zeros_like(halo_ref)
    low, high = sides("ph", taken, flags_ref)
    halo_ref[pl.ds(0, rows // ph, stride=ph), :] = low
    halo_ref[pl.ds(ph - 1, rows // ph, stride=ph), :] = high
    low, high = sides("row", taken, flags_ref)
    for t in range(th):
        halo_ref[t * slab : t * slab + ph, :] += low[t * ph : (t + 1) * ph]
        halo_ref[(t + 1) * slab - ph : (t + 1) * slab, :] += high[t * ph : (t + 1) * ph]


def split_slabs(th, th_n):
    if th_n > 2:
        return list(range(1, th - 1)), [0, th - 1]
    at = lax.axis_index("th")
    return [i + at for i in range(th - 1)], [(th - 1) * (1 - at)]


def groups_of(slabs, slab):
    return [
        pl.multiple_of(s * slab + i, 2 * GROUP) if not isinstance(s, int) else s * slab + i
        for s in slabs
        for i in range(0, slab, 2 * GROUP)
    ]


def first_kernel(ph, th, names, sizes, right_ref, conduct_ref, coupling_ref, codes_ref, inverse_ref, *rest):
    flags_ref, krylov_ref, conducts_ref, diagonal_ref, mixing_ref, held_ref, d_ref, *sent = rest[: 7 + len(names)]
    right, conduct, coupling, codes, turn, sems = rest[7 + len(names) :]
    rows = d_ref.shape[0]
    slab = rows // th
    pairs = [(right_ref, right), (coupling_ref, coupling), (codes_ref, codes), (conduct_ref, conduct)]
    parts = [pl.ds(t, th // 2) for t in range(0, th, th // 2)]
    pairs += [(inverse_ref.at[:, part], held_ref.at[:, part]) for part in parts]
    copies = [pltpu.make_async_copy(a, b, sems.at[i]) for i, (a, b) in enumerate(pairs)]
    for copy in copies:
        copy.start()

    def mix():
        copies[1].wait()
        lane = lax.broadcasted_iota(jnp.int32, (1, LANES), 1)
        for m in range(VARS):
            line = jnp.zeros((1, LANES), jnp.float32)
            for k in range(VARS):
                line = jnp.where(lane // BLK == k, coupling[k, (k + m) % VARS], line)
            mixing_ref[m : m + 1, :] = line

    def ghosts():
        copies[2].wait()
        cell = lax.broadcasted_iota(jnp.int32, (slab, LANES), 1) % BLK
        row = lax.broadcasted_iota(jnp.int32, (slab, LANES), 0)
        for t in range(th):
            diagonal = jnp.full((slab, LANES), 6.0, jnp.float32)
            for side, (edge, first, has) in enumerate(((0, 0, 3), (BLK - 1, slab - ph, 4))):
                factor = jnp.zeros((slab, LANES), jnp.float32)
                for p in range(ph):
                    code = codes[side, p, t]
                    value = jnp.where(code == 1, 1.0, jnp.where(code == 2, -1.0, 0.0))
                    factor = jnp.where(row == first + p, value, factor)
                diagonal -= jnp.where((cell == edge) & (flags_ref[has : has + 1, :] < 0.5), factor, 0.0)
            diagonal_ref[t * slab : (t + 1) * slab, :] = diagonal

    def lay_out():
        copies[3].wait()
        conducts_ref[...] = to_rows(conduct, turn)

    (row_at, row_n), (th_at, th_n), (ph_at, ph_n) = [(lax.axis_index(axis), n) for axis, n in sizes]
    values = [ph_at % 2, row_at % 2, th_at % 2, row_at > 0, row_at < row_n - 1, th_at > 0, th_at < th_n - 1]
    for i, value in enumerate(values):
        flags_ref[i : i + 1, :] = jnp.full((1, LANES), value.astype(jnp.float32))
    copies[0].wait()
    krylov_ref[...] = to_rows(right, turn)
    mix()
    ghosts()
    lay_out()
    for i, copy in enumerate(copies[4:]):
        copy.wait()
        for first in range(i * rows // 2, (i + 1) * rows // 2, 2 * GROUP):
            blocks = [held_ref[k % ph, k // slab, k % slab // ph] for k in range(first, first + 2 * GROUP)]
            d_ref[first : first + 2 * GROUP, :] = apply_stored(krylov_ref[first : first + 2 * GROUP, :], blocks)
    pack_faces(d_ref, dict(zip(names, sent)), flags_ref, ph, th)


def turn_kernel(held_ref, turned_ref):
    ph, th, nb = held_ref.shape[:3]
    for i in range(turned_ref.shape[0]):
        turned_ref[i] = held_ref[i % ph, i // (nb * ph), i % (nb * ph) // ph].T


def local_kernel(ph, th, krylov_ref, last_ref, conduct_ref, diagonal_ref, mixing_ref, out_ref):
    out_ref[...] = local_part(
        last_ref[...], krylov_ref[...], conduct_ref[...], diagonal_ref[...], mixing_ref, ph, th
    )


def gram_rows(left, right):
    lines = [jnp.sum(a * b, axis=0, keepdims=True) for a, b in zip(left, right)]
    return lines + [jnp.zeros_like(lines[0])] * (-len(lines) % 8)


def gram_kernel(*refs):
    basis = [ref[...] for ref in refs[:-1]]
    left = [basis[i] for i in range(S) for _ in range(i + 1)]
    right = [basis[j] for i in range(S) for j in range(i + 1)]
    refs[-1][...] = jnp.concatenate(gram_rows(left, right), axis=0)


def early_kernel(ph, th, th_n, names, flags_ref, local_ref, conduct_ref, turned_ref, *rest):
    next_ref, d_ref, halo_ref = rest[len(names) :]
    add_faces(halo_ref, dict(zip(names, rest)), flags_ref, ph, th)
    next_ref[...] = local_ref[...] - conduct_ref[...] * halo_ref[...]
    early, late = split_slabs(th, th_n)
    slab = d_ref.shape[0] // th
    apply_turned(next_ref, turned_ref, d_ref, groups_of(early, slab))
    for first in groups_of(late, slab):
        d_ref[pl.ds(first, 2 * GROUP), :] = jnp.zeros((2 * GROUP, LANES), jnp.float32)


def late_kernel(ph, th, th_n, names, late_names, flags_ref, early_ref, part_ref, conduct_ref, turned_ref, *rest):
    n = len(late_names)
    next_ref, d_ref, *sent = rest[n:]
    next_ref[...] = early_ref[...]
    d_ref[...] = part_ref[...]
    rows = d_ref.shape[0]
    slab = rows // th
    low, high = sides("th", dict(zip(late_names, rest)), flags_ref)
    _, late = split_slabs(th, th_n)
    faces = [low, high] if th_n > 2 else [low + high]
    for s, face in zip(late, faces):
        at = pl.ds(pl.multiple_of(s * slab, 2 * GROUP) if not isinstance(s, int) else s * slab, slab)
        next_ref[at, :] = early_ref[at, :] - conduct_ref[at, :] * face
    apply_turned(next_ref, turned_ref, d_ref, groups_of(late, slab))
    pack_faces(d_ref, dict(zip(names, sent)), flags_ref, ph, th)


def last_kernel(ph, th, names, flags_ref, local_ref, conduct_ref, partial_ref, *rest):
    older, taken, (next_ref, gram_ref, halo_ref) = rest[:S], rest[S : S + len(names)], rest[S + len(names) :]
    taken = dict(zip(names, taken))
    add_faces(halo_ref, taken, flags_ref, ph, th)
    low, high = sides("th", taken, flags_ref)
    rows = halo_ref.shape[0]
    slab = rows // th
    halo_ref[:slab, :] += low
    halo_ref[rows - slab :, :] += high
    final = local_ref[...] - conduct_ref[...] * halo_ref[...]
    next_ref[...] = final
    basis = [ref[...] for ref in older] + [final]
    stacked = jnp.concatenate([partial_ref[...]] + gram_rows([final] * (S + 1), basis), axis=0)
    each = jnp.sum(stacked, axis=1, keepdims=True)
    lane = lax.broadcasted_iota(jnp.int32, stacked.shape, 1)
    row = lax.broadcasted_iota(jnp.int32, stacked.shape, 0)
    line = jnp.sum(jnp.where(lane == row, each, 0.0), axis=0, keepdims=True)
    gram_ref[...] = jnp.broadcast_to(line, gram_ref.shape)


def small_solve(products):
    def entry(i, j):
        return products[max(i, j)][min(i, j)]

    def normal(j, k):
        return (entry(j, k) + entry(j + 1, k + 1)) + (entry(j + 1, k) + entry(j, k + 1))

    matrix = [[normal(j, k) for k in range(j + 1)] for j in range(S)]
    moment = [entry(j, 0) + entry(j + 1, 0) for j in range(S)]
    inverse = []
    for j in range(S):
        inverse.append(1.0 / matrix[j][j])
        scaled = {i: matrix[i][j] * inverse[j] for i in range(j + 1, S)}
        for i in range(j + 1, S):
            for k in range(j + 1, i + 1):
                matrix[i][k] = matrix[i][k] - scaled[i] * matrix[k][j]
            moment[i] = moment[i] - scaled[i] * moment[j]
    weights = [None] * S
    for i in reversed(range(S)):
        summed = moment[i]
        for k in range(i + 1, S):
            summed = summed - matrix[k][i] * weights[k]
        weights[i] = summed * inverse[i]
    return weights


def combine_kernel(partial_rows, gram_ref, *refs):
    krylov, directions, rest = refs[: S + 1], refs[S + 1 : 2 * S + 1], refs[2 * S + 1 :]
    correction_ref, residual_ref, correction, residual, turn, other_turn, sems = rest
    line = jnp.sum(gram_ref[...], axis=0, keepdims=True)
    products, place = [], 0
    for i in range(S + 1):
        products.append([])
        place = partial_rows if i == S else place
        for j in range(i + 1):
            products[i].append(jnp.broadcast_to(line[:, place : place + 1], line.shape))
            place += 1
    weights = small_solve(products)
    total = weights[0] * directions[0][...]
    for j in range(1, S):
        total = total + weights[j] * directions[j][...]
    left = krylov[0][...]
    for j in range(S):
        left = left - weights[j] * (krylov[j + 1][...] + krylov[j][...])
    from_rows(total, correction, turn)
    from_rows(left, residual, other_turn)
    copies = [
        pltpu.make_async_copy(correction, correction_ref, sems.at[0]),
        pltpu.make_async_copy(residual, residual_ref, sems.at[1]),
    ]
    for copy in copies:
        copy.start()
    for copy in copies:
        copy.wait()


def call(kernel, outs, scratch, *args, stay=()):
    def spec(a):
        return pl.BlockSpec(memory_space=pltpu.HBM if any(a is b for b in stay) else pltpu.VMEM)

    placed = [pltpu.with_memory_space_constraint(a, pltpu.HBM) if any(a is b for b in stay) else a for a in args]
    return pl.pallas_call(
        kernel,
        out_shape=outs,
        in_specs=[spec(a) for a in args],
        out_specs=[spec(a) for a in outs],
        scratch_shapes=scratch,
        compiler_params=pltpu.CompilerParams(vmem_limit_bytes=VMEM_LIMIT),
    )(*placed)


def local(right_side, conduct, coupling, inverse, face_codes):
    _, ph, th, radial = right_side.shape
    nb = radial // BLK
    per = ph * th
    rows = per * nb
    at = {axis: (lax.axis_index(axis), lax.axis_size(axis)) for axis in ("row", "th", "ph")}
    (row_at, row_n), (th_at, th_n), (ph_at, ph_n) = at["row"], at["th"], at["ph"]
    face_rows = {"ph_high": nb * th, "row_high": per, "ph_low": nb * th, "row_low": per // 2, "th_high": rows // th, "th_low": rows // th}
    if row_n == 2:
        face_rows.pop("row_high")
    if th_n == 2:
        face_rows.pop("th_high")
    names = tuple(face_rows)
    late_names = tuple(name for name in names if name[:2] == "th")
    def shape(n):
        return jax.ShapeDtypeStruct((n, LANES), jnp.float32)

    faces = [shape(n) for n in face_rows.values()]
    whole = shape(rows)

    plans = {"low": pairs_low, "high": pairs_high}

    def exchange(sent):
        taken = []
        for name, array in zip(names, sent):
            axis, side = name.split("_")
            taken.append(lax.ppermute(array, axis, plans[side](lax.axis_size(axis))))
        return taken

    field = pltpu.VMEM(right_side.shape, jnp.float32)
    turn = pltpu.VMEM((rows, LANES), jnp.float32)
    flags, start, conducts, diagonal, mixing, held, direction, *sent = call(
        functools.partial(first_kernel, ph, th, names, (("row", row_n), ("th", th_n), ("ph", ph_n))),
        [shape(VARS), whole, whole, whole, shape(VARS), jax.ShapeDtypeStruct(inverse.shape, jnp.bfloat16), whole] + faces,
        [
            field,
            field,
            pltpu.SMEM(coupling.shape, jnp.float32),
            pltpu.SMEM(face_codes.shape, jnp.int32),
            turn,
            pltpu.SemaphoreType.DMA((6,)),
        ],
        right_side, conduct, coupling, face_codes, inverse,
        stay=(right_side, conduct, coupling, face_codes, inverse),
    )
    (turned,) = call(turn_kernel, [jax.ShapeDtypeStruct((rows, LANES, LANES), jnp.bfloat16)], [], held)
    krylov, directions = [start], [direction]
    for step in range(S):
        taken = exchange(sent)
        (beside,) = call(
            functools.partial(local_kernel, ph, th), [whole], [], krylov[-1], directions[-1], conducts, diagonal, mixing
        )
        if step < S - 1:
            early_names, early_taken = zip(*[(n, t) for n, t in zip(names, taken) if n not in late_names])
            early, part = call(
                functools.partial(early_kernel, ph, th, th_n, early_names),
                [whole, whole],
                [turn],
                flags, beside, conducts, turned, *early_taken,
            )
            following, direction, *sent = call(
                functools.partial(late_kernel, ph, th, th_n, names, late_names),
                [whole, whole] + faces,
                [],
                flags, early, part, conducts, turned, *[t for n, t in zip(names, taken) if n in late_names],
            )
            krylov.append(following)
            directions.append(direction)
    partial_rows = S * (S + 1) // 2
    partial_rows += -partial_rows % 8
    (partial,) = call(gram_kernel, [shape(partial_rows)], [], *krylov)
    following, gram = call(
        functools.partial(last_kernel, ph, th, names),
        [whole, shape(row_n * th_n * ph_n)],
        [turn],
        flags, beside, conducts, partial, *krylov, *taken,
    )
    krylov.append(following)
    gram = lax.all_to_all(gram, ("row", "th", "ph"), 0, 0, tiled=True)
    native = [jax.ShapeDtypeStruct(right_side.shape, jnp.float32)] * 2
    return tuple(
        call(
            functools.partial(combine_kernel, partial_rows),
            native,
            [field, field, turn, turn, pltpu.SemaphoreType.DMA((2,))],
            gram, *krylov, *directions,
            stay=native,
        )
    )


def solution(mesh):
    placed = (
        P(None, "ph", "th", "row"),
        P(None, "ph", "th", "row"),
        P(),
        P("ph", "th", "row", None, None),
        P(None, "ph", "th"),
    )
    return jax.shard_map(
        local,
        mesh=mesh,
        in_specs=placed,
        out_specs=(P(None, "ph", "th", "row"), P(None, "ph", "th", "row")),
        check_vma=False,
    )
```

time: 45.2 us -> 44.6 us (0.987)
  waiting for transfers between devices: 5.46 us -> 4.46 us
  Pallas kernels: 6.24 us -> 6.72 us
    ppermute x20, waiting for transfers between devices: 5.46 us -> 4.46 us  [exchange(): taken.append(lax.ppermute(array, axis, plans[side](lax.axis_size(axis))))]
    pallas_call x12 -> x15, Pallas kernels: 6.24 us -> 6.72 us  [call(): pl.pallas_call(kernel, out_shape=outs, in_specs=[spec(a) for a in args],...]
  transfers between devices with their start and end apart: 20 -> 20, of which waited for: 8 -> 10; matrix products, arithmetic and copies ran while one was open for 0% -> 0% of each run, Pallas kernels for 3% -> 5%
where the time goes in v5:
time: 44.6 us; the launch traced here: 44.4 us
  starting transfers between devices  21.5 us (48%)
  blocking collectives  11 us (25%)
  Pallas kernels  6.72 us (15%)
  waiting for transfers between devices  4.46 us (10%)
  between operations  0.7 us (2%)
    ppermute x20, starting transfers between devices, exchange(): taken.append(lax.ppermute(array, axis, plans[side](lax.axis_size(axis))))  21.5 us
    all_to_all x1, blocking collectives, local(): gram = lax.all_to_all(gram, ('row', 'th', 'ph'), 0, 0, tiled=True)  11 us
    pallas_call x15, Pallas kernels, call(): pl.pallas_call(kernel, out_shape=outs, in_specs=[spec(a) for a in args],...  6.72 us
    ppermute x20, waiting for transfers between devices, exchange(): taken.append(lax.ppermute(array, axis, plans[side](lax.axis_size(axis))))  4.46 us
  transfers between devices with their start and end apart: 20, of which 10 were waited for; matrix products, arithmetic and copies ran while one was open for 0% of the time, Pallas kernels for 5%

profile of v5, /device:TPU:0, one launch (start us, length us, event | category | flops | bytes accessed | tf_op | source)
XLA Modules:
  0.0 44.4 jit_solution(17204183262332066479)
XLA Ops:
  0.6 2.3 %shard_map.68 = (f32[8,128]{1,0:T(8,128)S(1)}, f32[64,128]{1,0:T(8,128)S(1)}, f32[64,128]{1,0:T(8,128)S(1)}, f32[64,128]{1,0:T(8,128)S(1)}, f32[8,128]{1,0:T(8,1...) custom-call(f32[8,4,4,64]{3,2,1,0:T(4,128)} %right_ref.1, ...), custom_call_target="tpu_custom_call" | custom-call | tf_op jit(solution)/shard_map/pallas_call | solution.py:374
  2.9 5.1 %collective-permute-start = (f32[16,128]{1,0:T(8,128)S(1)}, f32[16,128]{1,0:T(8,128)S(1)}, u32[]{:S(2)}, u32[]{:S(2)}) collective-permute-start(f32[16,128]{1,0:T(8,128)S(1)} %get-tuple-element.50), channel_id=1, source_target_pairs={{0,3},{1,2},{2,1},{3,0},{4,7},{5,6},{6,5},{7,4},{8,11},{9,10},{10,... | collective-permute-start | bytes 24584 | tf_op jit(solution)/shard_map/ppermute | solution.py:410
  8.0 0.7 %collective-permute-start.1 = (f32[16,128]{1,0:T(8,128)S(1)}, f32[16,128]{1,0:T(8,128)S(1)}, u32[]{:S(2)}, u32[]{:S(2)}) collective-permute-start(f32[16,128]{1,0:T(8,128)S(1)} %get-tuple-element.51), channel_id=1, source_target_pairs={{0,24},{8,16},{16,8},{24,0},{1,25},{9,17},{17,9},{25,1},{2,26},{10... | collective-permute-start | bytes 24584 | tf_op jit(solution)/shard_map/ppermute | solution.py:410
  8.7 0.0 collective-permute-start.2
  8.7 1.5 %collective-permute-start.4 = (f32[16,128]{1,0:T(8,128)S(1)}, f32[16,128]{1,0:T(8,128)S(1)}, u32[]{:S(2)}, u32[]{:S(2)}) collective-permute-start(f32[16,128]{1,0:T(8,128)S(1)} %get-tuple-element.56), channel_id=1, source_target_pairs={{0,4},{4,0},{1,5},{5,1},{2,6},{6,2},{3,7},{7,3},{8,12},{12,8},{9,1... | collective-permute-start | bytes 24584 | tf_op jit(solution)/shard_map/ppermute | solution.py:410
  10.2 0.7 %collective-permute-start.3 = (f32[8,128]{1,0:T(8,128)S(1)}, f32[8,128]{1,0:T(8,128)S(1)}, u32[]{:S(2)}, u32[]{:S(2)}) collective-permute-start(f32[8,128]{1,0:T(8,128)S(1)} %get-tuple-element.53), channel_id=1, source_target_pairs={{0,8},{8,0},{16,24},{24,16},{1,9},{9,1},{17,25},{25,17},{2,10},{10... | collective-permute-start | bytes 12296 | tf_op jit(solution)/shard_map/ppermute | solution.py:410
  10.9 0.6 %shard_map.70.turned_ref = bf16[64,128,128]{2,1,0:T(8,128)(2,1)S(1)} custom-call(bf16[4,4,4,128,128]{4,3,2,1,0:T(8,128)(2,1)S(1)} %get-tuple-element.49.held_ref), custom_call_target="tpu_custom_call" | custom-call | tf_op jit(solution)/shard_map/pallas_call | solution.py:374
  11.5 0.2 shard_map.69.local_ref
  11.7 0.1 collective-permute-done.3.rest_3_
  11.7 0.0 collective-permute-done.rest_0_
  11.7 0.0 collective-permute-done.1.rest_1_
  11.7 0.7 %collective-permute-done.2.rest_2_ = f32[16,128]{1,0:T(8,128)S(1)} collective-permute-done((f32[16,128]{1,0:T(8,128)S(1)}, f32[16,128]{1,0:T(8,128)S(1)}, u32[]{:S(2)}, u32[]{:S(2)}) %collective-permute-start.2) | collective-permute-done | bytes 8224 | tf_op jit(solution)/shard_map/ppermute | solution.py:410
  12.4 0.3 shard_map.71
  12.7 0.0 collective-permute-done.4.rest_0_
  12.7 0.3 shard_map.72
  13.1 1.1 %collective-permute-start.5 = (f32[16,128]{1,0:T(8,128)S(1)}, f32[16,128]{1,0:T(8,128)S(1)}, u32[]{:S(2)}, u32[]{:S(2)}) collective-permute-start(f32[16,128]{1,0:T(8,128)S(1)} %get-tuple-element.59), channel_id=1, source_target_pairs={{0,3},{1,2},{2,1},{3,0},{4,7},{5,6},{6,5},{7,4},{8,11},{9,10},{10,... | collective-permute-start | bytes 24584 | tf_op jit(solution)/shard_map/ppermute | solution.py:410
  14.2 0.0 collective-permute-start.6
  14.2 0.6 %collective-permute-start.7 = (f32[16,128]{1,0:T(8,128)S(1)}, f32[16,128]{1,0:T(8,128)S(1)}, u32[]{:S(2)}, u32[]{:S(2)}) collective-permute-start(f32[16,128]{1,0:T(8,128)S(1)} %get-tuple-element.61), channel_id=1, source_target_pairs={{0,1},{1,0},{2,3},{3,2},{4,5},{5,4},{6,7},{7,6},{8,9},{9,8},{10,11... | collective-permute-start | bytes 24584 | tf_op jit(solution)/shard_map/ppermute | solution.py:410
  14.8 1.5 %collective-permute-start.9 = (f32[16,128]{1,0:T(8,128)S(1)}, f32[16,128]{1,0:T(8,128)S(1)}, u32[]{:S(2)}, u32[]{:S(2)}) collective-permute-start(f32[16,128]{1,0:T(8,128)S(1)} %get-tuple-element.65), channel_id=1, source_target_pairs={{0,4},{4,0},{1,5},{5,1},{2,6},{6,2},{3,7},{7,3},{8,12},{12,8},{9,1... | collective-permute-start | bytes 24584 | tf_op jit(solution)/shard_map/ppermute | solution.py:410
  16.3 0.8 %collective-permute-start.8 = (f32[8,128]{1,0:T(8,128)S(1)}, f32[8,128]{1,0:T(8,128)S(1)}, u32[]{:S(2)}, u32[]{:S(2)}) collective-permute-start(f32[8,128]{1,0:T(8,128)S(1)} %get-tuple-element.62), channel_id=1, source_target_pairs={{0,8},{8,0},{16,24},{24,16},{1,9},{9,1},{17,25},{25,17},{2,10},{10... | collective-permute-start | bytes 12296 | tf_op jit(solution)/shard_map/ppermute | solution.py:410
  17.1 0.2 shard_map.73.local_ref
  17.2 0.7 %collective-permute-done.8.rest_3_ = f32[8,128]{1,0:T(8,128)S(1)} collective-permute-done((f32[8,128]{1,0:T(8,128)S(1)}, f32[8,128]{1,0:T(8,128)S(1)}, u32[]{:S(2)}, u32[]{:S(2)}) %collective-permute-start.8) | collective-permute-done | bytes 4128 | tf_op jit(solution)/shard_map/ppermute | solution.py:410
  17.9 0.7 %collective-permute-done.5.rest_0_ = f32[16,128]{1,0:T(8,128)S(1)} collective-permute-done((f32[16,128]{1,0:T(8,128)S(1)}, f32[16,128]{1,0:T(8,128)S(1)}, u32[]{:S(2)}, u32[]{:S(2)}) %collective-permute-start.5) | collective-permute-done | bytes 8224 | tf_op jit(solution)/shard_map/ppermute | solution.py:410
  18.6 0.0 collective-permute-done.6.rest_1_
  18.6 0.0 collective-permute-done.7.rest_2_
  18.6 0.3 shard_map.74
  18.9 0.0 collective-permute-done.9.rest_0_
  18.9 0.3 shard_map.75
  19.3 2.3 %collective-permute-start.10 = (f32[16,128]{1,0:T(8,128)S(1)}, f32[16,128]{1,0:T(8,128)S(1)}, u32[]{:S(2)}, u32[]{:S(2)}) collective-permute-start(f32[16,128]{1,0:T(8,128)S(1)} %get-tuple-element.68), channel_id=1, source_target_pairs={{0,3},{1,2},{2,1},{3,0},{4,7},{5,6},{6,5},{7,4},{8,11},{9,10},{10,... | collective-permute-start | bytes 24584 | tf_op jit(solution)/shard_map/ppermute | solution.py:410
  21.6 0.3 collective-permute-start.11
  21.9 0.5 %collective-permute-start.12 = (f32[16,128]{1,0:T(8,128)S(1)}, f32[16,128]{1,0:T(8,128)S(1)}, u32[]{:S(2)}, u32[]{:S(2)}) collective-permute-start(f32[16,128]{1,0:T(8,128)S(1)} %get-tuple-element.70), channel_id=1, source_target_pairs={{0,1},{1,0},{2,3},{3,2},{4,5},{5,4},{6,7},{7,6},{8,9},{9,8},{10,11... | collective-permute-start | bytes 24584 | tf_op jit(solution)/shard_map/ppermute | solution.py:410
  22.4 1.2 %collective-permute-start.14 = (f32[16,128]{1,0:T(8,128)S(1)}, f32[16,128]{1,0:T(8,128)S(1)}, u32[]{:S(2)}, u32[]{:S(2)}) collective-permute-start(f32[16,128]{1,0:T(8,128)S(1)} %get-tuple-element.74), channel_id=1, source_target_pairs={{0,4},{4,0},{1,5},{5,1},{2,6},{6,2},{3,7},{7,3},{8,12},{12,8},{9,1... | collective-permute-start | bytes 24584 | tf_op jit(solution)/shard_map/ppermute | solution.py:410
  23.6 1.0 %collective-permute-start.13 = (f32[8,128]{1,0:T(8,128)S(1)}, f32[8,128]{1,0:T(8,128)S(1)}, u32[]{:S(2)}, u32[]{:S(2)}) collective-permute-start(f32[8,128]{1,0:T(8,128)S(1)} %get-tuple-element.71), channel_id=1, source_target_pairs={{0,8},{8,0},{16,24},{24,16},{1,9},{9,1},{17,25},{25,17},{2,10},{10... | collective-permute-start | bytes 12296 | tf_op jit(solution)/shard_map/ppermute | solution.py:410
  24.6 0.2 shard_map.76.local_ref
  24.7 0.7 %collective-permute-done.13.rest_3_ = f32[8,128]{1,0:T(8,128)S(1)} collective-permute-done((f32[8,128]{1,0:T(8,128)S(1)}, f32[8,128]{1,0:T(8,128)S(1)}, u32[]{:S(2)}, u32[]{:S(2)}) %collective-permute-start.13) | collective-permute-done | bytes 4128 | tf_op jit(solution)/shard_map/ppermute | solution.py:410
  25.4 0.0 collective-permute-done.10.rest_0_
  25.4 0.0 collective-permute-done.11.rest_1_
  25.4 0.2 collective-permute-done.12.rest_2_
  25.6 0.3 shard_map.77
  26.0 0.1 collective-permute-done.14.rest_0_
  26.1 0.3 shard_map.78
  26.4 1.3 %collective-permute-start.15 = (f32[16,128]{1,0:T(8,128)S(1)}, f32[16,128]{1,0:T(8,128)S(1)}, u32[]{:S(2)}, u32[]{:S(2)}) collective-permute-start(f32[16,128]{1,0:T(8,128)S(1)} %get-tuple-element.77), channel_id=1, source_target_pairs={{0,3},{1,2},{2,1},{3,0},{4,7},{5,6},{6,5},{7,4},{8,11},{9,10},{10,... | collective-permute-start | bytes 24584 | tf_op jit(solution)/shard_map/ppermute | solution.py:410
  27.8 0.3 collective-permute-start.16
  28.1 0.5 %collective-permute-start.17 = (f32[16,128]{1,0:T(8,128)S(1)}, f32[16,128]{1,0:T(8,128)S(1)}, u32[]{:S(2)}, u32[]{:S(2)}) collective-permute-start(f32[16,128]{1,0:T(8,128)S(1)} %get-tuple-element.79), channel_id=1, source_target_pairs={{0,1},{1,0},{2,3},{3,2},{4,5},{5,4},{6,7},{7,6},{8,9},{9,8},{10,11... | collective-permute-start | bytes 24584 | tf_op jit(solution)/shard_map/ppermute | solution.py:410
  28.5 1.3 %collective-permute-start.19 = (f32[16,128]{1,0:T(8,128)S(1)}, f32[16,128]{1,0:T(8,128)S(1)}, u32[]{:S(2)}, u32[]{:S(2)}) collective-permute-start(f32[16,128]{1,0:T(8,128)S(1)} %get-tuple-element.81), channel_id=1, source_target_pairs={{0,4},{4,0},{1,5},{5,1},{2,6},{6,2},{3,7},{7,3},{8,12},{12,8},{9,1... | collective-permute-start | bytes 24584 | tf_op jit(solution)/shard_map/ppermute | solution.py:410
  29.8 0.9 %collective-permute-start.18 = (f32[8,128]{1,0:T(8,128)S(1)}, f32[8,128]{1,0:T(8,128)S(1)}, u32[]{:S(2)}, u32[]{:S(2)}) collective-permute-start(f32[8,128]{1,0:T(8,128)S(1)} %get-tuple-element.80), channel_id=1, source_target_pairs={{0,8},{8,0},{16,24},{24,16},{1,9},{9,1},{17,25},{25,17},{2,10},{10... | collective-permute-start | bytes 12296 | tf_op jit(solution)/shard_map/ppermute | solution.py:410
  30.7 0.2 shard_map.79.local_ref
  30.9 0.6 %collective-permute-done.18.rest_7_ = f32[8,128]{1,0:T(8,128)S(1)} collective-permute-done((f32[8,128]{1,0:T(8,128)S(1)}, f32[8,128]{1,0:T(8,128)S(1)}, u32[]{:S(2)}, u32[]{:S(2)}) %collective-permute-start.18) | collective-permute-done | bytes 4128 | tf_op jit(solution)/shard_map/ppermute | solution.py:410
  31.5 0.4 collective-permute-done.15.rest_4_
  31.9 0.0 collective-permute-done.16.rest_5_
  31.9 0.0 collective-permute-done.17.rest_6_
  31.9 0.3 collective-permute-done.19.rest_8_
  32.2 0.2 shard_map.81
  32.4 11.0 %all_to_all.11 = f32[32,1,128]{2,1,0:T(1,128)S(1)} all-to-all(f32[32,1,128]{2,1,0:T(1,128)S(1)} %bitcast.5), channel_id=1, replica_groups=mesh['row'=4,'th'=2,'ph'=4] {'row','th','ph'}, dimensions={0} | all-to-all | bytes 32768 | tf_op jit(solution)/shard_map/all_to_all | solution.py:462
  43.5 1.0 %shard_map.82 = (f32[8,4,4,64]{3,2,1,0:T(4,128)}, f32[8,4,4,64]{3,2,1,0:T(4,128)}) custom-call(f32[32,128]{1,0:T(8,128)S(1)} %bitcast.4, f32[64,128]{1,0:T(8,128)S(1)} %get-tuple-element.44.krylov_ref.refs_0_.rest_0_, f32[64,128]{1,0:T(8,128)S(1)} %get-tuple-element.57.krylov_ref.refs_1_.rest_1_, f32[64,128]{1,0:T(8,128)S(1)} %get-tuple-element.66.krylov_ref.refs_2_.rest_2_, ...), custom_call_target="tpu_custom_call" | custom-call | tf_op jit(solution)/shard_map/pallas_call | solution.py:374
  (1 shorter events, 0.0 us)
Async XLA Ops:
  2.9 8.8 %collective-permute-start = (f32[16,128]{1,0:T(8,128)S(1)}, f32[16,128]{1,0:T(8,128)S(1)}, u32[]{:S(2)}, u32[]{:S(2)}) collective-permute-start(f32[16,128]{1,0:T(8,128)S(1)} %get-tuple-element.50), channel_id=1, source_target_pairs={{0,3},{1,2},{2,1},{3,0},{4,7},{5,6},{6,5},{7,4},{8,11},{9,10},{10,... | collective-permute-start | bytes 24584 | tf_op jit(solution)/shard_map/ppermute | solution.py:410
  8.0 3.7 %collective-permute-start.1 = (f32[16,128]{1,0:T(8,128)S(1)}, f32[16,128]{1,0:T(8,128)S(1)}, u32[]{:S(2)}, u32[]{:S(2)}) collective-permute-start(f32[16,128]{1,0:T(8,128)S(1)} %get-tuple-element.51), channel_id=1, source_target_pairs={{0,24},{8,16},{16,8},{24,0},{1,25},{9,17},{17,9},{25,1},{2,26},{10... | collective-permute-start | bytes 24584 | tf_op jit(solution)/shard_map/ppermute | solution.py:410
  8.7 3.7 %collective-permute-start.2 = (f32[16,128]{1,0:T(8,128)S(1)}, f32[16,128]{1,0:T(8,128)S(1)}, u32[]{:S(2)}, u32[]{:S(2)}) collective-permute-start(f32[16,128]{1,0:T(8,128)S(1)} %get-tuple-element.52), channel_id=1, source_target_pairs={{0,1},{1,0},{2,3},{3,2},{4,5},{5,4},{6,7},{7,6},{8,9},{9,8},{10,11... | collective-permute-start | bytes 24584 | tf_op jit(solution)/shard_map/ppermute | solution.py:410
  8.7 4.1 %collective-permute-start.4 = (f32[16,128]{1,0:T(8,128)S(1)}, f32[16,128]{1,0:T(8,128)S(1)}, u32[]{:S(2)}, u32[]{:S(2)}) collective-permute-start(f32[16,128]{1,0:T(8,128)S(1)} %get-tuple-element.56), channel_id=1, source_target_pairs={{0,4},{4,0},{1,5},{5,1},{2,6},{6,2},{3,7},{7,3},{8,12},{12,8},{9,1... | collective-permute-start | bytes 24584 | tf_op jit(solution)/shard_map/ppermute | solution.py:410
  10.2 1.5 %collective-permute-start.3 = (f32[8,128]{1,0:T(8,128)S(1)}, f32[8,128]{1,0:T(8,128)S(1)}, u32[]{:S(2)}, u32[]{:S(2)}) collective-permute-start(f32[8,128]{1,0:T(8,128)S(1)} %get-tuple-element.53), channel_id=1, source_target_pairs={{0,8},{8,0},{16,24},{24,16},{1,9},{9,1},{17,25},{25,17},{2,10},{10... | collective-permute-start | bytes 12296 | tf_op jit(solution)/shard_map/ppermute | solution.py:410
  13.1 5.5 %collective-permute-start.5 = (f32[16,128]{1,0:T(8,128)S(1)}, f32[16,128]{1,0:T(8,128)S(1)}, u32[]{:S(2)}, u32[]{:S(2)}) collective-permute-start(f32[16,128]{1,0:T(8,128)S(1)} %get-tuple-element.59), channel_id=1, source_target_pairs={{0,3},{1,2},{2,1},{3,0},{4,7},{5,6},{6,5},{7,4},{8,11},{9,10},{10,... | collective-permute-start | bytes 24584 | tf_op jit(solution)/shard_map/ppermute | solution.py:410
  14.2 4.4 %collective-permute-start.6 = (f32[16,128]{1,0:T(8,128)S(1)}, f32[16,128]{1,0:T(8,128)S(1)}, u32[]{:S(2)}, u32[]{:S(2)}) collective-permute-start(f32[16,128]{1,0:T(8,128)S(1)} %get-tuple-element.60), channel_id=1, source_target_pairs={{0,24},{8,16},{16,8},{24,0},{1,25},{9,17},{17,9},{25,1},{2,26},{10... | collective-permute-start | bytes 24584 | tf_op jit(solution)/shard_map/ppermute | solution.py:410
  14.2 4.4 %collective-permute-start.7 = (f32[16,128]{1,0:T(8,128)S(1)}, f32[16,128]{1,0:T(8,128)S(1)}, u32[]{:S(2)}, u32[]{:S(2)}) collective-permute-start(f32[16,128]{1,0:T(8,128)S(1)} %get-tuple-element.61), channel_id=1, source_target_pairs={{0,1},{1,0},{2,3},{3,2},{4,5},{5,4},{6,7},{7,6},{8,9},{9,8},{10,11... | collective-permute-start | bytes 24584 | tf_op jit(solution)/shard_map/ppermute | solution.py:410
  14.8 4.1 %collective-permute-start.9 = (f32[16,128]{1,0:T(8,128)S(1)}, f32[16,128]{1,0:T(8,128)S(1)}, u32[]{:S(2)}, u32[]{:S(2)}) collective-permute-start(f32[16,128]{1,0:T(8,128)S(1)} %get-tuple-element.65), channel_id=1, source_target_pairs={{0,4},{4,0},{1,5},{5,1},{2,6},{6,2},{3,7},{7,3},{8,12},{12,8},{9,1... | collective-permute-start | bytes 24584 | tf_op jit(solution)/shard_map/ppermute | solution.py:410
  16.3 1.6 %collective-permute-start.8 = (f32[8,128]{1,0:T(8,128)S(1)}, f32[8,128]{1,0:T(8,128)S(1)}, u32[]{:S(2)}, u32[]{:S(2)}) collective-permute-start(f32[8,128]{1,0:T(8,128)S(1)} %get-tuple-element.62), channel_id=1, source_target_pairs={{0,8},{8,0},{16,24},{24,16},{1,9},{9,1},{17,25},{25,17},{2,10},{10... | collective-permute-start | bytes 12296 | tf_op jit(solution)/shard_map/ppermute | solution.py:410
  19.3 6.1 %collective-permute-start.10 = (f32[16,128]{1,0:T(8,128)S(1)}, f32[16,128]{1,0:T(8,128)S(1)}, u32[]{:S(2)}, u32[]{:S(2)}) collective-permute-start(f32[16,128]{1,0:T(8,128)S(1)} %get-tuple-element.68), channel_id=1, source_target_pairs={{0,3},{1,2},{2,1},{3,0},{4,7},{5,6},{6,5},{7,4},{8,11},{9,10},{10,... | collective-permute-start | bytes 24584 | tf_op jit(solution)/shard_map/ppermute | solution.py:410
  21.6 3.8 %collective-permute-start.11 = (f32[16,128]{1,0:T(8,128)S(1)}, f32[16,128]{1,0:T(8,128)S(1)}, u32[]{:S(2)}, u32[]{:S(2)}) collective-permute-start(f32[16,128]{1,0:T(8,128)S(1)} %get-tuple-element.69), channel_id=1, source_target_pairs={{0,24},{8,16},{16,8},{24,0},{1,25},{9,17},{17,9},{25,1},{2,26},{10... | collective-permute-start | bytes 24584 | tf_op jit(solution)/shard_map/ppermute | solution.py:410
  21.9 3.7 %collective-permute-start.12 = (f32[16,128]{1,0:T(8,128)S(1)}, f32[16,128]{1,0:T(8,128)S(1)}, u32[]{:S(2)}, u32[]{:S(2)}) collective-permute-start(f32[16,128]{1,0:T(8,128)S(1)} %get-tuple-element.70), channel_id=1, source_target_pairs={{0,1},{1,0},{2,3},{3,2},{4,5},{5,4},{6,7},{7,6},{8,9},{9,8},{10,11... | collective-permute-start | bytes 24584 | tf_op jit(solution)/shard_map/ppermute | solution.py:410
  22.4 3.7 %collective-permute-start.14 = (f32[16,128]{1,0:T(8,128)S(1)}, f32[16,128]{1,0:T(8,128)S(1)}, u32[]{:S(2)}, u32[]{:S(2)}) collective-permute-start(f32[16,128]{1,0:T(8,128)S(1)} %get-tuple-element.74), channel_id=1, source_target_pairs={{0,4},{4,0},{1,5},{5,1},{2,6},{6,2},{3,7},{7,3},{8,12},{12,8},{9,1... | collective-permute-start | bytes 24584 | tf_op jit(solution)/shard_map/ppermute | solution.py:410
  23.6 1.8 %collective-permute-start.13 = (f32[8,128]{1,0:T(8,128)S(1)}, f32[8,128]{1,0:T(8,128)S(1)}, u32[]{:S(2)}, u32[]{:S(2)}) collective-permute-start(f32[8,128]{1,0:T(8,128)S(1)} %get-tuple-element.71), channel_id=1, source_target_pairs={{0,8},{8,0},{16,24},{24,16},{1,9},{9,1},{17,25},{25,17},{2,10},{10... | collective-permute-start | bytes 12296 | tf_op jit(solution)/shard_map/ppermute | solution.py:410
  26.4 5.5 %collective-permute-start.15 = (f32[16,128]{1,0:T(8,128)S(1)}, f32[16,128]{1,0:T(8,128)S(1)}, u32[]{:S(2)}, u32[]{:S(2)}) collective-permute-start(f32[16,128]{1,0:T(8,128)S(1)} %get-tuple-element.77), channel_id=1, source_target_pairs={{0,3},{1,2},{2,1},{3,0},{4,7},{5,6},{6,5},{7,4},{8,11},{9,10},{10,... | collective-permute-start | bytes 24584 | tf_op jit(solution)/shard_map/ppermute | solution.py:410
  27.8 4.1 %collective-permute-start.16 = (f32[16,128]{1,0:T(8,128)S(1)}, f32[16,128]{1,0:T(8,128)S(1)}, u32[]{:S(2)}, u32[]{:S(2)}) collective-permute-start(f32[16,128]{1,0:T(8,128)S(1)} %get-tuple-element.78), channel_id=1, source_target_pairs={{0,24},{8,16},{16,8},{24,0},{1,25},{9,17},{17,9},{25,1},{2,26},{10... | collective-permute-start | bytes 24584 | tf_op jit(solution)/shard_map/ppermute | solution.py:410
  28.1 3.8 %collective-permute-start.17 = (f32[16,128]{1,0:T(8,128)S(1)}, f32[16,128]{1,0:T(8,128)S(1)}, u32[]{:S(2)}, u32[]{:S(2)}) collective-permute-start(f32[16,128]{1,0:T(8,128)S(1)} %get-tuple-element.79), channel_id=1, source_target_pairs={{0,1},{1,0},{2,3},{3,2},{4,5},{5,4},{6,7},{7,6},{8,9},{9,8},{10,11... | collective-permute-start | bytes 24584 | tf_op jit(solution)/shard_map/ppermute | solution.py:410
  28.5 3.7 %collective-permute-start.19 = (f32[16,128]{1,0:T(8,128)S(1)}, f32[16,128]{1,0:T(8,128)S(1)}, u32[]{:S(2)}, u32[]{:S(2)}) collective-permute-start(f32[16,128]{1,0:T(8,128)S(1)} %get-tuple-element.81), channel_id=1, source_target_pairs={{0,4},{4,0},{1,5},{5,1},{2,6},{6,2},{3,7},{7,3},{8,12},{12,8},{9,1... | collective-permute-start | bytes 24584 | tf_op jit(solution)/shard_map/ppermute | solution.py:410
  29.8 1.7 %collective-permute-start.18 = (f32[8,128]{1,0:T(8,128)S(1)}, f32[8,128]{1,0:T(8,128)S(1)}, u32[]{:S(2)}, u32[]{:S(2)}) collective-permute-start(f32[8,128]{1,0:T(8,128)S(1)} %get-tuple-element.80), channel_id=1, source_target_pairs={{0,8},{8,0},{16,24},{24,16},{1,9},{9,1},{17,25},{25,17},{2,10},{10... | collective-permute-start | bytes 12296 | tf_op jit(solution)/shard_map/ppermute | solution.py:410

commit v6 on v5

--- a/solution.py
+++ b/solution.py
@@ -97,10 +97,12 @@
     outs["ph_low"][...] = jnp.where(odd_ph, low, high)
     low = jnp.concatenate([d_ref[t * slab : t * slab + ph, :] for t in range(th)], axis=0)
     high = jnp.concatenate([d_ref[(t + 1) * slab - ph : (t + 1) * slab, :] for t in range(th)], axis=0)
+    half = per // 2
+    low_next = jnp.where(cell[half:] == 0, pltpu.roll(low[half:], BLK, 1), 0.0)
+    high_next = jnp.where(cell[half:] == 1, pltpu.roll(high[half:], LANES - BLK + 2, 1), 0.0)
     low = jnp.where(cell == BLK - 1, pltpu.roll(low, BLK - 1, 1), 0.0)
     high = jnp.where(cell == 0, pltpu.roll(high, LANES - BLK + 1, 1), 0.0)
-    near = jnp.where(odd_row, low, high)
-    outs["row_low"][...] = near[: per // 2] + pltpu.roll(near[per // 2 :], 1, 1)
+    outs["row_low"][...] = jnp.where(odd_row, low[:half] + low_next, high[:half] + high_next)
     if "row_high" in outs:
         outs["row_high"][...] = jnp.where(odd_row, high, low)
     low, high = d_ref[:slab, :], d_ref[rows - slab :, :]

time: 44.6 us -> 44.4 us (level)
  no operation moved by 1% of the time
where the time goes in v6:
time: 44.4 us; the launch traced here: 44.2 us
  starting transfers between devices  21.5 us (48%)
  blocking collectives  11 us (25%)
  Pallas kernels  6.46 us (15%)
  waiting for transfers between devices  4.46 us (10%)
  between operations  0.7 us (2%)
    ppermute x20, starting transfers between devices, exchange(): taken.append(lax.ppermute(array, axis, plans[side](lax.axis_size(axis))))  21.5 us
    all_to_all x1, blocking collectives, local(): gram = lax.all_to_all(gram, ('row', 'th', 'ph'), 0, 0, tiled=True)  11 us
    pallas_call x15, Pallas kernels, call(): pl.pallas_call(kernel, out_shape=outs, in_specs=[spec(a) for a in args],...  6.46 us
    ppermute x20, waiting for transfers between devices, exchange(): taken.append(lax.ppermute(array, axis, plans[side](lax.axis_size(axis))))  4.46 us
  transfers between devices with their start and end apart: 20, of which 10 were waited for; matrix products, arithmetic and copies ran while one was open for 0% of the time, Pallas kernels for 5%

profile of v6, /device:TPU:0, one launch (start us, length us, event | category | flops | bytes accessed | tf_op | source)
XLA Modules:
  0.0 44.2 jit_solution(8414232193953381239)
XLA Ops:
  0.6 2.2 %shard_map.68 = (f32[8,128]{1,0:T(8,128)S(1)}, f32[64,128]{1,0:T(8,128)S(1)}, f32[64,128]{1,0:T(8,128)S(1)}, f32[64,128]{1,0:T(8,128)S(1)}, f32[8,128]{1,0:T(8,1...) custom-call(f32[8,4,4,64]{3,2,1,0:T(4,128)} %right_ref.1, ...), custom_call_target="tpu_custom_call" | custom-call | tf_op jit(solution)/shard_map/pallas_call | solution.py:376
  2.9 5.1 %collective-permute-start = (f32[16,128]{1,0:T(8,128)S(1)}, f32[16,128]{1,0:T(8,128)S(1)}, u32[]{:S(2)}, u32[]{:S(2)}) collective-permute-start(f32[16,128]{1,0:T(8,128)S(1)} %get-tuple-element.50), channel_id=1, source_target_pairs={{0,3},{1,2},{2,1},{3,0},{4,7},{5,6},{6,5},{7,4},{8,11},{9,10},{10,... | collective-permute-start | bytes 24584 | tf_op jit(solution)/shard_map/ppermute | solution.py:412
  8.0 0.7 %collective-permute-start.1 = (f32[16,128]{1,0:T(8,128)S(1)}, f32[16,128]{1,0:T(8,128)S(1)}, u32[]{:S(2)}, u32[]{:S(2)}) collective-permute-start(f32[16,128]{1,0:T(8,128)S(1)} %get-tuple-element.51), channel_id=1, source_target_pairs={{0,24},{8,16},{16,8},{24,0},{1,25},{9,17},{17,9},{25,1},{2,26},{10... | collective-permute-start | bytes 24584 | tf_op jit(solution)/shard_map/ppermute | solution.py:412
  8.6 0.0 collective-permute-start.2
  8.6 1.5 %collective-permute-start.4 = (f32[16,128]{1,0:T(8,128)S(1)}, f32[16,128]{1,0:T(8,128)S(1)}, u32[]{:S(2)}, u32[]{:S(2)}) collective-permute-start(f32[16,128]{1,0:T(8,128)S(1)} %get-tuple-element.56), channel_id=1, source_target_pairs={{0,4},{4,0},{1,5},{5,1},{2,6},{6,2},{3,7},{7,3},{8,12},{12,8},{9,1... | collective-permute-start | bytes 24584 | tf_op jit(solution)/shard_map/ppermute | solution.py:412
  10.1 0.7 %collective-permute-start.3 = (f32[8,128]{1,0:T(8,128)S(1)}, f32[8,128]{1,0:T(8,128)S(1)}, u32[]{:S(2)}, u32[]{:S(2)}) collective-permute-start(f32[8,128]{1,0:T(8,128)S(1)} %get-tuple-element.53), channel_id=1, source_target_pairs={{0,8},{8,0},{16,24},{24,16},{1,9},{9,1},{17,25},{25,17},{2,10},{10... | collective-permute-start | bytes 12296 | tf_op jit(solution)/shard_map/ppermute | solution.py:412
  10.8 0.6 %shard_map.70.turned_ref = bf16[64,128,128]{2,1,0:T(8,128)(2,1)S(1)} custom-call(bf16[4,4,4,128,128]{4,3,2,1,0:T(8,128)(2,1)S(1)} %get-tuple-element.49.held_ref), custom_call_target="tpu_custom_call" | custom-call | tf_op jit(solution)/shard_map/pallas_call | solution.py:376
  11.4 0.2 shard_map.69.local_ref
  11.6 0.1 collective-permute-done.3.rest_3_
  11.6 0.0 collective-permute-done.rest_0_
  11.6 0.0 collective-permute-done.1.rest_1_
  11.6 0.7 %collective-permute-done.2.rest_2_ = f32[16,128]{1,0:T(8,128)S(1)} collective-permute-done((f32[16,128]{1,0:T(8,128)S(1)}, f32[16,128]{1,0:T(8,128)S(1)}, u32[]{:S(2)}, u32[]{:S(2)}) %collective-permute-start.2) | collective-permute-done | bytes 8224 | tf_op jit(solution)/shard_map/ppermute | solution.py:412
  12.3 0.3 shard_map.71
  12.7 0.0 collective-permute-done.4.rest_0_
  12.7 0.3 shard_map.72
  13.0 1.1 %collective-permute-start.5 = (f32[16,128]{1,0:T(8,128)S(1)}, f32[16,128]{1,0:T(8,128)S(1)}, u32[]{:S(2)}, u32[]{:S(2)}) collective-permute-start(f32[16,128]{1,0:T(8,128)S(1)} %get-tuple-element.59), channel_id=1, source_target_pairs={{0,3},{1,2},{2,1},{3,0},{4,7},{5,6},{6,5},{7,4},{8,11},{9,10},{10,... | collective-permute-start | bytes 24584 | tf_op jit(solution)/shard_map/ppermute | solution.py:412
  14.0 0.0 collective-permute-start.6
  14.1 0.7 %collective-permute-start.7 = (f32[16,128]{1,0:T(8,128)S(1)}, f32[16,128]{1,0:T(8,128)S(1)}, u32[]{:S(2)}, u32[]{:S(2)}) collective-permute-start(f32[16,128]{1,0:T(8,128)S(1)} %get-tuple-element.61), channel_id=1, source_target_pairs={{0,1},{1,0},{2,3},{3,2},{4,5},{5,4},{6,7},{7,6},{8,9},{9,8},{10,11... | collective-permute-start | bytes 24584 | tf_op jit(solution)/shard_map/ppermute | solution.py:412
  14.7 1.5 %collective-permute-start.9 = (f32[16,128]{1,0:T(8,128)S(1)}, f32[16,128]{1,0:T(8,128)S(1)}, u32[]{:S(2)}, u32[]{:S(2)}) collective-permute-start(f32[16,128]{1,0:T(8,128)S(1)} %get-tuple-element.65), channel_id=1, source_target_pairs={{0,4},{4,0},{1,5},{5,1},{2,6},{6,2},{3,7},{7,3},{8,12},{12,8},{9,1... | collective-permute-start | bytes 24584 | tf_op jit(solution)/shard_map/ppermute | solution.py:412
  16.3 0.7 %collective-permute-start.8 = (f32[8,128]{1,0:T(8,128)S(1)}, f32[8,128]{1,0:T(8,128)S(1)}, u32[]{:S(2)}, u32[]{:S(2)}) collective-permute-start(f32[8,128]{1,0:T(8,128)S(1)} %get-tuple-element.62), channel_id=1, source_target_pairs={{0,8},{8,0},{16,24},{24,16},{1,9},{9,1},{17,25},{25,17},{2,10},{10... | collective-permute-start | bytes 12296 | tf_op jit(solution)/shard_map/ppermute | solution.py:412
  17.0 0.2 shard_map.73.local_ref
  17.1 0.7 %collective-permute-done.8.rest_3_ = f32[8,128]{1,0:T(8,128)S(1)} collective-permute-done((f32[8,128]{1,0:T(8,128)S(1)}, f32[8,128]{1,0:T(8,128)S(1)}, u32[]{:S(2)}, u32[]{:S(2)}) %collective-permute-start.8) | collective-permute-done | bytes 4128 | tf_op jit(solution)/shard_map/ppermute | solution.py:412
  17.8 0.7 %collective-permute-done.5.rest_0_ = f32[16,128]{1,0:T(8,128)S(1)} collective-permute-done((f32[16,128]{1,0:T(8,128)S(1)}, f32[16,128]{1,0:T(8,128)S(1)}, u32[]{:S(2)}, u32[]{:S(2)}) %collective-permute-start.5) | collective-permute-done | bytes 8224 | tf_op jit(solution)/shard_map/ppermute | solution.py:412
  18.5 0.0 collective-permute-done.6.rest_1_
  18.5 0.0 collective-permute-done.7.rest_2_
  18.5 0.3 shard_map.74
  18.8 0.0 collective-permute-done.9.rest_0_
  18.8 0.3 shard_map.75
  19.1 2.3 %collective-permute-start.10 = (f32[16,128]{1,0:T(8,128)S(1)}, f32[16,128]{1,0:T(8,128)S(1)}, u32[]{:S(2)}, u32[]{:S(2)}) collective-permute-start(f32[16,128]{1,0:T(8,128)S(1)} %get-tuple-element.68), channel_id=1, source_target_pairs={{0,3},{1,2},{2,1},{3,0},{4,7},{5,6},{6,5},{7,4},{8,11},{9,10},{10,... | collective-permute-start | bytes 24584 | tf_op jit(solution)/shard_map/ppermute | solution.py:412
  21.4 0.3 collective-permute-start.11
  21.7 0.5 %collective-permute-start.12 = (f32[16,128]{1,0:T(8,128)S(1)}, f32[16,128]{1,0:T(8,128)S(1)}, u32[]{:S(2)}, u32[]{:S(2)}) collective-permute-start(f32[16,128]{1,0:T(8,128)S(1)} %get-tuple-element.70), channel_id=1, source_target_pairs={{0,1},{1,0},{2,3},{3,2},{4,5},{5,4},{6,7},{7,6},{8,9},{9,8},{10,11... | collective-permute-start | bytes 24584 | tf_op jit(solution)/shard_map/ppermute | solution.py:412
  22.2 1.2 %collective-permute-start.14 = (f32[16,128]{1,0:T(8,128)S(1)}, f32[16,128]{1,0:T(8,128)S(1)}, u32[]{:S(2)}, u32[]{:S(2)}) collective-permute-start(f32[16,128]{1,0:T(8,128)S(1)} %get-tuple-element.74), channel_id=1, source_target_pairs={{0,4},{4,0},{1,5},{5,1},{2,6},{6,2},{3,7},{7,3},{8,12},{12,8},{9,1... | collective-permute-start | bytes 24584 | tf_op jit(solution)/shard_map/ppermute | solution.py:412
  23.4 1.0 %collective-permute-start.13 = (f32[8,128]{1,0:T(8,128)S(1)}, f32[8,128]{1,0:T(8,128)S(1)}, u32[]{:S(2)}, u32[]{:S(2)}) collective-permute-start(f32[8,128]{1,0:T(8,128)S(1)} %get-tuple-element.71), channel_id=1, source_target_pairs={{0,8},{8,0},{16,24},{24,16},{1,9},{9,1},{17,25},{25,17},{2,10},{10... | collective-permute-start | bytes 12296 | tf_op jit(solution)/shard_map/ppermute | solution.py:412
  24.4 0.2 shard_map.76.local_ref
  24.6 0.7 %collective-permute-done.13.rest_3_ = f32[8,128]{1,0:T(8,128)S(1)} collective-permute-done((f32[8,128]{1,0:T(8,128)S(1)}, f32[8,128]{1,0:T(8,128)S(1)}, u32[]{:S(2)}, u32[]{:S(2)}) %collective-permute-start.13) | collective-permute-done | bytes 4128 | tf_op jit(solution)/shard_map/ppermute | solution.py:412
  25.2 0.0 collective-permute-done.10.rest_0_
  25.2 0.0 collective-permute-done.11.rest_1_
  25.2 0.2 collective-permute-done.12.rest_2_
  25.5 0.3 shard_map.77
  25.8 0.1 collective-permute-done.14.rest_0_
  25.9 0.3 shard_map.78
  26.2 1.3 %collective-permute-start.15 = (f32[16,128]{1,0:T(8,128)S(1)}, f32[16,128]{1,0:T(8,128)S(1)}, u32[]{:S(2)}, u32[]{:S(2)}) collective-permute-start(f32[16,128]{1,0:T(8,128)S(1)} %get-tuple-element.77), channel_id=1, source_target_pairs={{0,3},{1,2},{2,1},{3,0},{4,7},{5,6},{6,5},{7,4},{8,11},{9,10},{10,... | collective-permute-start | bytes 24584 | tf_op jit(solution)/shard_map/ppermute | solution.py:412
  27.5 0.3 collective-permute-start.16
  27.8 0.5 %collective-permute-start.17 = (f32[16,128]{1,0:T(8,128)S(1)}, f32[16,128]{1,0:T(8,128)S(1)}, u32[]{:S(2)}, u32[]{:S(2)}) collective-permute-start(f32[16,128]{1,0:T(8,128)S(1)} %get-tuple-element.79), channel_id=1, source_target_pairs={{0,1},{1,0},{2,3},{3,2},{4,5},{5,4},{6,7},{7,6},{8,9},{9,8},{10,11... | collective-permute-start | bytes 24584 | tf_op jit(solution)/shard_map/ppermute | solution.py:412
  28.3 1.3 %collective-permute-start.19 = (f32[16,128]{1,0:T(8,128)S(1)}, f32[16,128]{1,0:T(8,128)S(1)}, u32[]{:S(2)}, u32[]{:S(2)}) collective-permute-start(f32[16,128]{1,0:T(8,128)S(1)} %get-tuple-element.81), channel_id=1, source_target_pairs={{0,4},{4,0},{1,5},{5,1},{2,6},{6,2},{3,7},{7,3},{8,12},{12,8},{9,1... | collective-permute-start | bytes 24584 | tf_op jit(solution)/shard_map/ppermute | solution.py:412
  29.6 0.9 %collective-permute-start.18 = (f32[8,128]{1,0:T(8,128)S(1)}, f32[8,128]{1,0:T(8,128)S(1)}, u32[]{:S(2)}, u32[]{:S(2)}) collective-permute-start(f32[8,128]{1,0:T(8,128)S(1)} %get-tuple-element.80), channel_id=1, source_target_pairs={{0,8},{8,0},{16,24},{24,16},{1,9},{9,1},{17,25},{25,17},{2,10},{10... | collective-permute-start | bytes 12296 | tf_op jit(solution)/shard_map/ppermute | solution.py:412
  30.5 0.2 shard_map.79.local_ref
  30.7 0.6 %collective-permute-done.18.rest_7_ = f32[8,128]{1,0:T(8,128)S(1)} collective-permute-done((f32[8,128]{1,0:T(8,128)S(1)}, f32[8,128]{1,0:T(8,128)S(1)}, u32[]{:S(2)}, u32[]{:S(2)}) %collective-permute-start.18) | collective-permute-done | bytes 4128 | tf_op jit(solution)/shard_map/ppermute | solution.py:412
  31.3 0.4 collective-permute-done.15.rest_4_
  31.6 0.0 collective-permute-done.16.rest_5_
  31.7 0.0 collective-permute-done.17.rest_6_
  31.7 0.3 collective-permute-done.19.rest_8_
  32.0 0.2 shard_map.81
  32.2 11.0 %all_to_all.11 = f32[32,1,128]{2,1,0:T(1,128)S(1)} all-to-all(f32[32,1,128]{2,1,0:T(1,128)S(1)} %bitcast.5), channel_id=1, replica_groups=mesh['row'=4,'th'=2,'ph'=4] {'row','th','ph'}, dimensions={0} | all-to-all | bytes 32768 | tf_op jit(solution)/shard_map/all_to_all | solution.py:464
  43.2 1.0 %shard_map.82 = (f32[8,4,4,64]{3,2,1,0:T(4,128)}, f32[8,4,4,64]{3,2,1,0:T(4,128)}) custom-call(f32[32,128]{1,0:T(8,128)S(1)} %bitcast.4, f32[64,128]{1,0:T(8,128)S(1)} %get-tuple-element.44.krylov_ref.refs_0_.rest_0_, f32[64,128]{1,0:T(8,128)S(1)} %get-tuple-element.57.krylov_ref.refs_1_.rest_1_, f32[64,128]{1,0:T(8,128)S(1)} %get-tuple-element.66.krylov_ref.refs_2_.rest_2_, ...), custom_call_target="tpu_custom_call" | custom-call | tf_op jit(solution)/shard_map/pallas_call | solution.py:376
  (1 shorter events, 0.0 us)
Async XLA Ops:
  2.9 8.8 %collective-permute-start = (f32[16,128]{1,0:T(8,128)S(1)}, f32[16,128]{1,0:T(8,128)S(1)}, u32[]{:S(2)}, u32[]{:S(2)}) collective-permute-start(f32[16,128]{1,0:T(8,128)S(1)} %get-tuple-element.50), channel_id=1, source_target_pairs={{0,3},{1,2},{2,1},{3,0},{4,7},{5,6},{6,5},{7,4},{8,11},{9,10},{10,... | collective-permute-start | bytes 24584 | tf_op jit(solution)/shard_map/ppermute | solution.py:412
  8.0 3.7 %collective-permute-start.1 = (f32[16,128]{1,0:T(8,128)S(1)}, f32[16,128]{1,0:T(8,128)S(1)}, u32[]{:S(2)}, u32[]{:S(2)}) collective-permute-start(f32[16,128]{1,0:T(8,128)S(1)} %get-tuple-element.51), channel_id=1, source_target_pairs={{0,24},{8,16},{16,8},{24,0},{1,25},{9,17},{17,9},{25,1},{2,26},{10... | collective-permute-start | bytes 24584 | tf_op jit(solution)/shard_map/ppermute | solution.py:412
  8.6 3.7 %collective-permute-start.2 = (f32[16,128]{1,0:T(8,128)S(1)}, f32[16,128]{1,0:T(8,128)S(1)}, u32[]{:S(2)}, u32[]{:S(2)}) collective-permute-start(f32[16,128]{1,0:T(8,128)S(1)} %get-tuple-element.52), channel_id=1, source_target_pairs={{0,1},{1,0},{2,3},{3,2},{4,5},{5,4},{6,7},{7,6},{8,9},{9,8},{10,11... | collective-permute-start | bytes 24584 | tf_op jit(solution)/shard_map/ppermute | solution.py:412
  8.6 4.1 %collective-permute-start.4 = (f32[16,128]{1,0:T(8,128)S(1)}, f32[16,128]{1,0:T(8,128)S(1)}, u32[]{:S(2)}, u32[]{:S(2)}) collective-permute-start(f32[16,128]{1,0:T(8,128)S(1)} %get-tuple-element.56), channel_id=1, source_target_pairs={{0,4},{4,0},{1,5},{5,1},{2,6},{6,2},{3,7},{7,3},{8,12},{12,8},{9,1... | collective-permute-start | bytes 24584 | tf_op jit(solution)/shard_map/ppermute | solution.py:412
  10.1 1.5 %collective-permute-start.3 = (f32[8,128]{1,0:T(8,128)S(1)}, f32[8,128]{1,0:T(8,128)S(1)}, u32[]{:S(2)}, u32[]{:S(2)}) collective-permute-start(f32[8,128]{1,0:T(8,128)S(1)} %get-tuple-element.53), channel_id=1, source_target_pairs={{0,8},{8,0},{16,24},{24,16},{1,9},{9,1},{17,25},{25,17},{2,10},{10... | collective-permute-start | bytes 12296 | tf_op jit(solution)/shard_map/ppermute | solution.py:412
  13.0 5.5 %collective-permute-start.5 = (f32[16,128]{1,0:T(8,128)S(1)}, f32[16,128]{1,0:T(8,128)S(1)}, u32[]{:S(2)}, u32[]{:S(2)}) collective-permute-start(f32[16,128]{1,0:T(8,128)S(1)} %get-tuple-element.59), channel_id=1, source_target_pairs={{0,3},{1,2},{2,1},{3,0},{4,7},{5,6},{6,5},{7,4},{8,11},{9,10},{10,... | collective-permute-start | bytes 24584 | tf_op jit(solution)/shard_map/ppermute | solution.py:412
  14.0 4.4 %collective-permute-start.6 = (f32[16,128]{1,0:T(8,128)S(1)}, f32[16,128]{1,0:T(8,128)S(1)}, u32[]{:S(2)}, u32[]{:S(2)}) collective-permute-start(f32[16,128]{1,0:T(8,128)S(1)} %get-tuple-element.60), channel_id=1, source_target_pairs={{0,24},{8,16},{16,8},{24,0},{1,25},{9,17},{17,9},{25,1},{2,26},{10... | collective-permute-start | bytes 24584 | tf_op jit(solution)/shard_map/ppermute | solution.py:412
  14.1 4.4 %collective-permute-start.7 = (f32[16,128]{1,0:T(8,128)S(1)}, f32[16,128]{1,0:T(8,128)S(1)}, u32[]{:S(2)}, u32[]{:S(2)}) collective-permute-start(f32[16,128]{1,0:T(8,128)S(1)} %get-tuple-element.61), channel_id=1, source_target_pairs={{0,1},{1,0},{2,3},{3,2},{4,5},{5,4},{6,7},{7,6},{8,9},{9,8},{10,11... | collective-permute-start | bytes 24584 | tf_op jit(solution)/shard_map/ppermute | solution.py:412
  14.7 4.1 %collective-permute-start.9 = (f32[16,128]{1,0:T(8,128)S(1)}, f32[16,128]{1,0:T(8,128)S(1)}, u32[]{:S(2)}, u32[]{:S(2)}) collective-permute-start(f32[16,128]{1,0:T(8,128)S(1)} %get-tuple-element.65), channel_id=1, source_target_pairs={{0,4},{4,0},{1,5},{5,1},{2,6},{6,2},{3,7},{7,3},{8,12},{12,8},{9,1... | collective-permute-start | bytes 24584 | tf_op jit(solution)/shard_map/ppermute | solution.py:412
  16.3 1.5 %collective-permute-start.8 = (f32[8,128]{1,0:T(8,128)S(1)}, f32[8,128]{1,0:T(8,128)S(1)}, u32[]{:S(2)}, u32[]{:S(2)}) collective-permute-start(f32[8,128]{1,0:T(8,128)S(1)} %get-tuple-element.62), channel_id=1, source_target_pairs={{0,8},{8,0},{16,24},{24,16},{1,9},{9,1},{17,25},{25,17},{2,10},{10... | collective-permute-start | bytes 12296 | tf_op jit(solution)/shard_map/ppermute | solution.py:412
  19.1 6.1 %collective-permute-start.10 = (f32[16,128]{1,0:T(8,128)S(1)}, f32[16,128]{1,0:T(8,128)S(1)}, u32[]{:S(2)}, u32[]{:S(2)}) collective-permute-start(f32[16,128]{1,0:T(8,128)S(1)} %get-tuple-element.68), channel_id=1, source_target_pairs={{0,3},{1,2},{2,1},{3,0},{4,7},{5,6},{6,5},{7,4},{8,11},{9,10},{10,... | collective-permute-start | bytes 24584 | tf_op jit(solution)/shard_map/ppermute | solution.py:412
  21.4 3.8 %collective-permute-start.11 = (f32[16,128]{1,0:T(8,128)S(1)}, f32[16,128]{1,0:T(8,128)S(1)}, u32[]{:S(2)}, u32[]{:S(2)}) collective-permute-start(f32[16,128]{1,0:T(8,128)S(1)} %get-tuple-element.69), channel_id=1, source_target_pairs={{0,24},{8,16},{16,8},{24,0},{1,25},{9,17},{17,9},{25,1},{2,26},{10... | collective-permute-start | bytes 24584 | tf_op jit(solution)/shard_map/ppermute | solution.py:412
  21.7 3.7 %collective-permute-start.12 = (f32[16,128]{1,0:T(8,128)S(1)}, f32[16,128]{1,0:T(8,128)S(1)}, u32[]{:S(2)}, u32[]{:S(2)}) collective-permute-start(f32[16,128]{1,0:T(8,128)S(1)} %get-tuple-element.70), channel_id=1, source_target_pairs={{0,1},{1,0},{2,3},{3,2},{4,5},{5,4},{6,7},{7,6},{8,9},{9,8},{10,11... | collective-permute-start | bytes 24584 | tf_op jit(solution)/shard_map/ppermute | solution.py:412
  22.2 3.7 %collective-permute-start.14 = (f32[16,128]{1,0:T(8,128)S(1)}, f32[16,128]{1,0:T(8,128)S(1)}, u32[]{:S(2)}, u32[]{:S(2)}) collective-permute-start(f32[16,128]{1,0:T(8,128)S(1)} %get-tuple-element.74), channel_id=1, source_target_pairs={{0,4},{4,0},{1,5},{5,1},{2,6},{6,2},{3,7},{7,3},{8,12},{12,8},{9,1... | collective-permute-start | bytes 24584 | tf_op jit(solution)/shard_map/ppermute | solution.py:412
  23.4 1.8 %collective-permute-start.13 = (f32[8,128]{1,0:T(8,128)S(1)}, f32[8,128]{1,0:T(8,128)S(1)}, u32[]{:S(2)}, u32[]{:S(2)}) collective-permute-start(f32[8,128]{1,0:T(8,128)S(1)} %get-tuple-element.71), channel_id=1, source_target_pairs={{0,8},{8,0},{16,24},{24,16},{1,9},{9,1},{17,25},{25,17},{2,10},{10... | collective-permute-start | bytes 12296 | tf_op jit(solution)/shard_map/ppermute | solution.py:412
  26.2 5.5 %collective-permute-start.15 = (f32[16,128]{1,0:T(8,128)S(1)}, f32[16,128]{1,0:T(8,128)S(1)}, u32[]{:S(2)}, u32[]{:S(2)}) collective-permute-start(f32[16,128]{1,0:T(8,128)S(1)} %get-tuple-element.77), channel_id=1, source_target_pairs={{0,3},{1,2},{2,1},{3,0},{4,7},{5,6},{6,5},{7,4},{8,11},{9,10},{10,... | collective-permute-start | bytes 24584 | tf_op jit(solution)/shard_map/ppermute | solution.py:412
  27.5 4.1 %collective-permute-start.16 = (f32[16,128]{1,0:T(8,128)S(1)}, f32[16,128]{1,0:T(8,128)S(1)}, u32[]{:S(2)}, u32[]{:S(2)}) collective-permute-start(f32[16,128]{1,0:T(8,128)S(1)} %get-tuple-element.78), channel_id=1, source_target_pairs={{0,24},{8,16},{16,8},{24,0},{1,25},{9,17},{17,9},{25,1},{2,26},{10... | collective-permute-start | bytes 24584 | tf_op jit(solution)/shard_map/ppermute | solution.py:412
  27.8 3.8 %collective-permute-start.17 = (f32[16,128]{1,0:T(8,128)S(1)}, f32[16,128]{1,0:T(8,128)S(1)}, u32[]{:S(2)}, u32[]{:S(2)}) collective-permute-start(f32[16,128]{1,0:T(8,128)S(1)} %get-tuple-element.79), channel_id=1, source_target_pairs={{0,1},{1,0},{2,3},{3,2},{4,5},{5,4},{6,7},{7,6},{8,9},{9,8},{10,11... | collective-permute-start | bytes 24584 | tf_op jit(solution)/shard_map/ppermute | solution.py:412
  28.3 3.7 %collective-permute-start.19 = (f32[16,128]{1,0:T(8,128)S(1)}, f32[16,128]{1,0:T(8,128)S(1)}, u32[]{:S(2)}, u32[]{:S(2)}) collective-permute-start(f32[16,128]{1,0:T(8,128)S(1)} %get-tuple-element.81), channel_id=1, source_target_pairs={{0,4},{4,0},{1,5},{5,1},{2,6},{6,2},{3,7},{7,3},{8,12},{12,8},{9,1... | collective-permute-start | bytes 24584 | tf_op jit(solution)/shard_map/ppermute | solution.py:412
  29.6 1.7 %collective-permute-start.18 = (f32[8,128]{1,0:T(8,128)S(1)}, f32[8,128]{1,0:T(8,128)S(1)}, u32[]{:S(2)}, u32[]{:S(2)}) collective-permute-start(f32[8,128]{1,0:T(8,128)S(1)} %get-tuple-element.80), channel_id=1, source_target_pairs={{0,8},{8,0},{16,24},{24,16},{1,9},{9,1},{17,25},{25,17},{2,10},{10... | collective-permute-start | bytes 12296 | tf_op jit(solution)/shard_map/ppermute | solution.py:412

commit v7 on v5

--- a/solution.py
+++ b/solution.py
@@ -88,25 +88,45 @@
 def pack_faces(d_ref, outs, flags_ref, ph, th):
     rows = d_ref.shape[0]
     slab = rows // th
-    per = ph * th
-    cell = lax.broadcasted_iota(jnp.int32, (per, LANES), 1) % BLK
     odd_ph, odd_row, odd_th = [flags_ref[i : i + 1, :] > 0.5 for i in range(3)]
     low = d_ref[pl.ds(0, rows // ph, stride=ph), :]
     high = d_ref[pl.ds(ph - 1, rows // ph, stride=ph), :]
     outs["ph_high"][...] = jnp.where(odd_ph, high, low)
     outs["ph_low"][...] = jnp.where(odd_ph, low, high)
-    low = jnp.concatenate([d_ref[t * slab : t * slab + ph, :] for t in range(th)], axis=0)
-    high = jnp.concatenate([d_ref[(t + 1) * slab - ph : (t + 1) * slab, :] for t in range(th)], axis=0)
-    low = jnp.where(cell == BLK - 1, pltpu.roll(low, BLK - 1, 1), 0.0)
-    high = jnp.where(cell == 0, pltpu.roll(high, LANES - BLK + 1, 1), 0.0)
-    near = jnp.where(odd_row, low, high)
-    outs["row_low"][...] = near[: per // 2] + pltpu.roll(near[per // 2 :], 1, 1)
     if "row_high" in outs:
-        outs["row_high"][...] = jnp.where(odd_row, high, low)
+        for t in range(th):
+            low, high = radial_edges(d_ref, t, slab, ph)
+            outs["row_high"][t * ph : (t + 1) * ph, :] = jnp.where(odd_row, high, low)
     low, high = d_ref[:slab, :], d_ref[rows - slab :, :]
     outs["th_low"][...] = jnp.where(odd_th, low, high)
     if "th_high" in outs:
         outs["th_high"][...] = jnp.where(odd_th, high, low)
+
+
+def radial_edges(d_ref, t, slab, ph):
+    return d_ref[t * slab : t * slab + ph, :], d_ref[(t + 1) * slab - ph : (t + 1) * slab, :]
+
+
+def near_kernel(ph, th, flags_ref, d_ref, out_ref):
+    slab = d_ref.shape[0] // th
+    half = out_ref.shape[0]
+    low, high = [jnp.concatenate(side, axis=0) for side in zip(*[radial_edges(d_ref, t, slab, ph) for t in range(th)])]
+    cell = lax.broadcasted_iota(jnp.int32, (half, LANES), 1) % BLK
+    low = jnp.where(cell == BLK - 1, pltpu.roll(low[:half], BLK - 1, 1), 0.0) + jnp.where(
+        cell == 0, pltpu.roll(low[half:], BLK, 1), 0.0
+    )
+    high = jnp.where(cell == 0, pltpu.roll(high[:half], LANES - BLK + 1, 1), 0.0) + jnp.where(
+        cell == 1, pltpu.roll(high[half:], LANES - BLK + 2, 1), 0.0
+    )
+    out_ref[...] = jnp.where(flags_ref[1:2, :] > 0.5, low, high)
+
+
+def across_kernel(flags_ref, face_ref, out_ref):
+    face = face_ref[...]
+    cell = lax.broadcasted_iota(jnp.int32, face.shape, 1) % BLK
+    below = jnp.where(cell == 0, pltpu.roll(face, LANES - BLK + 1, 1), 0.0)
+    above = jnp.where(cell == BLK - 1, pltpu.roll(face, BLK - 1, 1), 0.0)
+    out_ref[...] = jnp.where(flags_ref[1:2, :] > 0.5, above, below)
 
 
 def local_part(field, krylov, conduct, diagonal, mixing_ref, ph, th):
@@ -395,25 +415,31 @@
         face_rows.pop("th_high")
     names = tuple(face_rows)
     late_names = tuple(name for name in names if name[:2] == "th")
+    packed = tuple(name for name in names if name != "row_low")
     def shape(n):
         return jax.ShapeDtypeStruct((n, LANES), jnp.float32)
 
-    faces = [shape(n) for n in face_rows.values()]
+    faces = [shape(face_rows[name]) for name in packed]
     whole = shape(rows)
 
     plans = {"low": pairs_low, "high": pairs_high}
 
-    def exchange(sent):
+    def exchange(sent, direction):
+        (near,) = call(functools.partial(near_kernel, ph, th), [shape(face_rows["row_low"])], [], flags, direction)
+        sent = dict(zip(packed, sent), row_low=near)
         taken = []
-        for name, array in zip(names, sent):
+        for name in names:
             axis, side = name.split("_")
-            taken.append(lax.ppermute(array, axis, plans[side](lax.axis_size(axis))))
+            face = lax.ppermute(sent[name], axis, plans[side](lax.axis_size(axis)))
+            if name == "row_high":
+                (face,) = call(across_kernel, [shape(per)], [], flags, face)
+            taken.append(face)
         return taken
 
     field = pltpu.VMEM(right_side.shape, jnp.float32)
     turn = pltpu.VMEM((rows, LANES), jnp.float32)
     flags, start, conducts, diagonal, mixing, held, direction, *sent = call(
-        functools.partial(first_kernel, ph, th, names, (("row", row_n), ("th", th_n), ("ph", ph_n))),
+        functools.partial(first_kernel, ph, th, packed, (("row", row_n), ("th", th_n), ("ph", ph_n))),
         [shape(VARS), whole, whole, whole, shape(VARS), jax.ShapeDtypeStruct(inverse.shape, jnp.bfloat16), whole] + faces,
         [
             field,
@@ -429,7 +455,7 @@
     (turned,) = call(turn_kernel, [jax.ShapeDtypeStruct((rows, LANES, LANES), jnp.bfloat16)], [], held)
     krylov, directions = [start], [direction]
     for step in range(S):
-        taken = exchange(sent)
+        taken = exchange(sent, directions[-1])
         (beside,) = call(
             functools.partial(local_kernel, ph, th), [whole], [], krylov[-1], directions[-1], conducts, diagonal, mixing
         )
@@ -442,7 +468,7 @@
                 flags, beside, conducts, turned, *early_taken,
             )
             following, direction, *sent = call(
-                functools.partial(late_kernel, ph, th, th_n, names, late_names),
+                functools.partial(late_kernel, ph, th, th_n, packed, late_names),
                 [whole, whole] + faces,
                 [],
                 flags, early, part, conducts, turned, *[t for n, t in zip(names, taken) if n in late_names],

time: 44.6 us -> 44.1 us (0.989)
  starting transfers between devices: 21.5 us -> 19.6 us
  waiting for transfers between devices: 4.46 us -> 6.27 us
  blocking collectives: 11 us -> 10.5 us
    ppermute x20, starting transfers between devices: 21.5 us -> 19.6 us  [exchange(): face = lax.ppermute(sent[name], axis, plans[side](lax.axis_size(axis)))]
    ppermute x20, waiting for transfers between devices: 4.46 us -> 6.27 us  [exchange(): face = lax.ppermute(sent[name], axis, plans[side](lax.axis_size(axis)))]
    all_to_all x1, blocking collectives: 11 us -> 10.5 us  [local(): gram = lax.all_to_all(gram, ('row', 'th', 'ph'), 0, 0, tiled=True)]
    pallas_call x15 -> x23, Pallas kernels: 6.72 us -> 6.78 us  [call(): pl.pallas_call(kernel, out_shape=outs, in_specs=[spec(a) for a in args],...]
  transfers between devices with their start and end apart: 20 -> 20, of which waited for: 10 -> 12; matrix products, arithmetic and copies ran while one was open for 0% -> 0% of each run, Pallas kernels for 5% -> 7%
where the time goes in v7:
time: 44.1 us; the launch traced here: 43.9 us
  starting transfers between devices  19.6 us (44%)
  blocking collectives  10.5 us (24%)
  Pallas kernels  6.78 us (15%)
  waiting for transfers between devices  6.27 us (14%)
  between operations  0.75 us (2%)
    ppermute x20, starting transfers between devices, exchange(): face = lax.ppermute(sent[name], axis, plans[side](lax.axis_size(axis)))  19.6 us
    all_to_all x1, blocking collectives, local(): gram = lax.all_to_all(gram, ('row', 'th', 'ph'), 0, 0, tiled=True)  10.5 us
    pallas_call x23, Pallas kernels, call(): pl.pallas_call(kernel, out_shape=outs, in_specs=[spec(a) for a in args],...  6.78 us
    ppermute x20, waiting for transfers between devices, exchange(): face = lax.ppermute(sent[name], axis, plans[side](lax.axis_size(axis)))  6.27 us
  transfers between devices with their start and end apart: 20, of which 12 were waited for; matrix products, arithmetic and copies ran while one was open for 0% of the time, Pallas kernels for 7%

profile of v7, /device:TPU:0, one launch (start us, length us, event | category | flops | bytes accessed | tf_op | source)
XLA Modules:
  0.0 43.9 jit_solution(15652856075067227155)
XLA Ops:
  0.6 2.1 %shard_map.68 = (f32[8,128]{1,0:T(8,128)S(1)}, f32[64,128]{1,0:T(8,128)S(1)}, f32[64,128]{1,0:T(8,128)S(1)}, f32[64,128]{1,0:T(8,128)S(1)}, f32[8,128]{1,0:T(8,1...) custom-call(f32[8,4,4,64]{3,2,1,0:T(4,128)} %right_ref.1, ...), custom_call_target="tpu_custom_call" | custom-call | tf_op jit(solution)/shard_map/pallas_call | solution.py:394
  2.8 2.4 %collective-permute-start.1 = (f32[16,128]{1,0:T(8,128)S(1)}, f32[16,128]{1,0:T(8,128)S(1)}, u32[]{:S(2)}, u32[]{:S(2)}) collective-permute-start(f32[16,128]{1,0:T(8,128)S(1)} %get-tuple-element.47), channel_id=1, source_target_pairs={{0,24},{8,16},{16,8},{24,0},{1,25},{9,17},{17,9},{25,1},{2,26},{10... | collective-permute-start | bytes 24584 | tf_op jit(solution)/shard_map/ppermute | solution.py:433
  5.2 3.6 %collective-permute-start = (f32[16,128]{1,0:T(8,128)S(1)}, f32[16,128]{1,0:T(8,128)S(1)}, u32[]{:S(2)}, u32[]{:S(2)}) collective-permute-start(f32[16,128]{1,0:T(8,128)S(1)} %get-tuple-element.46), channel_id=1, source_target_pairs={{0,3},{1,2},{2,1},{3,0},{4,7},{5,6},{6,5},{7,4},{8,11},{9,10},{10,... | collective-permute-start | bytes 24584 | tf_op jit(solution)/shard_map/ppermute | solution.py:433
  8.8 0.0 collective-permute-start.2
  8.8 1.5 %collective-permute-start.4 = (f32[16,128]{1,0:T(8,128)S(1)}, f32[16,128]{1,0:T(8,128)S(1)}, u32[]{:S(2)}, u32[]{:S(2)}) collective-permute-start(f32[16,128]{1,0:T(8,128)S(1)} %get-tuple-element.51), channel_id=1, source_target_pairs={{0,4},{4,0},{1,5},{5,1},{2,6},{6,2},{3,7},{7,3},{8,12},{12,8},{9,1... | collective-permute-start | bytes 24584 | tf_op jit(solution)/shard_map/ppermute | solution.py:433
  10.3 0.1 shard_map.72
  10.4 0.2 collective-permute-start.3
  10.6 0.6 %shard_map.70.turned_ref = bf16[64,128,128]{2,1,0:T(8,128)(2,1)S(1)} custom-call(bf16[4,4,4,128,128]{4,3,2,1,0:T(8,128)(2,1)S(1)} %get-tuple-element.45.held_ref), custom_call_target="tpu_custom_call" | custom-call | tf_op jit(solution)/shard_map/pallas_call | solution.py:394
  11.2 0.2 shard_map.69.local_ref
  11.3 0.0 collective-permute-done.1.face_ref
  11.4 0.1 shard_map.71.rest_1_
  11.4 0.2 collective-permute-done.3.rest_3_
  11.6 0.0 collective-permute-done.rest_0_
  11.6 0.9 %collective-permute-done.2.rest_2_ = f32[16,128]{1,0:T(8,128)S(1)} collective-permute-done((f32[16,128]{1,0:T(8,128)S(1)}, f32[16,128]{1,0:T(8,128)S(1)}, u32[]{:S(2)}, u32[]{:S(2)}) %collective-permute-start.2) | collective-permute-done | bytes 8224 | tf_op jit(solution)/shard_map/ppermute | solution.py:433
  12.5 0.3 shard_map.73
  12.8 0.0 collective-permute-done.4.rest_0_
  12.8 0.2 shard_map.74
  13.0 0.0 collective-permute-start.6
  13.0 1.9 %collective-permute-start.5 = (f32[16,128]{1,0:T(8,128)S(1)}, f32[16,128]{1,0:T(8,128)S(1)}, u32[]{:S(2)}, u32[]{:S(2)}) collective-permute-start(f32[16,128]{1,0:T(8,128)S(1)} %get-tuple-element.54), channel_id=1, source_target_pairs={{0,3},{1,2},{2,1},{3,0},{4,7},{5,6},{6,5},{7,4},{8,11},{9,10},{10,... | collective-permute-start | bytes 24584 | tf_op jit(solution)/shard_map/ppermute | solution.py:433
  14.9 0.0 collective-permute-start.7
  14.9 1.5 %collective-permute-start.9 = (f32[16,128]{1,0:T(8,128)S(1)}, f32[16,128]{1,0:T(8,128)S(1)}, u32[]{:S(2)}, u32[]{:S(2)}) collective-permute-start(f32[16,128]{1,0:T(8,128)S(1)} %get-tuple-element.59), channel_id=1, source_target_pairs={{0,4},{4,0},{1,5},{5,1},{2,6},{6,2},{3,7},{7,3},{8,12},{12,8},{9,1... | collective-permute-start | bytes 24584 | tf_op jit(solution)/shard_map/ppermute | solution.py:433
  16.4 0.1 shard_map.77
  16.5 0.2 collective-permute-start.8
  16.6 0.2 shard_map.75.local_ref
  16.8 0.0 collective-permute-done.6.face_ref
  16.8 0.1 shard_map.76.rest_1_
  16.9 0.8 %collective-permute-done.8.rest_3_ = f32[8,128]{1,0:T(8,128)S(1)} collective-permute-done((f32[8,128]{1,0:T(8,128)S(1)}, f32[8,128]{1,0:T(8,128)S(1)}, u32[]{:S(2)}, u32[]{:S(2)}) %collective-permute-start.8) | collective-permute-done | bytes 4128 | tf_op jit(solution)/shard_map/ppermute | solution.py:433
  17.7 0.9 %collective-permute-done.5.rest_0_ = f32[16,128]{1,0:T(8,128)S(1)} collective-permute-done((f32[16,128]{1,0:T(8,128)S(1)}, f32[16,128]{1,0:T(8,128)S(1)}, u32[]{:S(2)}, u32[]{:S(2)}) %collective-permute-start.5) | collective-permute-done | bytes 8224 | tf_op jit(solution)/shard_map/ppermute | solution.py:433
  18.5 0.1 collective-permute-done.7.rest_2_
  18.6 0.3 shard_map.78
  19.0 0.0 collective-permute-done.9.rest_0_
  19.0 0.2 shard_map.79
  19.2 0.5 %collective-permute-start.11 = (f32[16,128]{1,0:T(8,128)S(1)}, f32[16,128]{1,0:T(8,128)S(1)}, u32[]{:S(2)}, u32[]{:S(2)}) collective-permute-start(f32[16,128]{1,0:T(8,128)S(1)} %get-tuple-element.63), channel_id=1, source_target_pairs={{0,24},{8,16},{16,8},{24,0},{1,25},{9,17},{17,9},{25,1},{2,26},{10... | collective-permute-start | bytes 24584 | tf_op jit(solution)/shard_map/ppermute | solution.py:433
  19.7 2.1 %collective-permute-start.10 = (f32[16,128]{1,0:T(8,128)S(1)}, f32[16,128]{1,0:T(8,128)S(1)}, u32[]{:S(2)}, u32[]{:S(2)}) collective-permute-start(f32[16,128]{1,0:T(8,128)S(1)} %get-tuple-element.62), channel_id=1, source_target_pairs={{0,3},{1,2},{2,1},{3,0},{4,7},{5,6},{6,5},{7,4},{8,11},{9,10},{10,... | collective-permute-start | bytes 24584 | tf_op jit(solution)/shard_map/ppermute | solution.py:433
  21.9 0.3 collective-permute-start.12
  22.2 1.3 %collective-permute-start.14 = (f32[16,128]{1,0:T(8,128)S(1)}, f32[16,128]{1,0:T(8,128)S(1)}, u32[]{:S(2)}, u32[]{:S(2)}) collective-permute-start(f32[16,128]{1,0:T(8,128)S(1)} %get-tuple-element.67), channel_id=1, source_target_pairs={{0,4},{4,0},{1,5},{5,1},{2,6},{6,2},{3,7},{7,3},{8,12},{12,8},{9,1... | collective-permute-start | bytes 24584 | tf_op jit(solution)/shard_map/ppermute | solution.py:433
  23.5 0.1 shard_map.82
  23.6 0.1 collective-permute-start.13
  23.6 0.2 shard_map.80.local_ref
  23.8 0.0 collective-permute-done.11.face_ref
  23.8 0.1 shard_map.81.rest_1_
  23.9 0.9 %collective-permute-done.13.rest_3_ = f32[8,128]{1,0:T(8,128)S(1)} collective-permute-done((f32[8,128]{1,0:T(8,128)S(1)}, f32[8,128]{1,0:T(8,128)S(1)}, u32[]{:S(2)}, u32[]{:S(2)}) %collective-permute-start.13) | collective-permute-done | bytes 4128 | tf_op jit(solution)/shard_map/ppermute | solution.py:433
  24.7 0.4 collective-permute-done.10.rest_0_
  25.2 0.4 collective-permute-done.12.rest_2_
  25.5 0.3 shard_map.83
  25.8 0.0 collective-permute-done.14.rest_0_
  25.9 0.2 shard_map.84
  26.1 0.1 collective-permute-start.16
  26.1 2.0 %collective-permute-start.15 = (f32[16,128]{1,0:T(8,128)S(1)}, f32[16,128]{1,0:T(8,128)S(1)}, u32[]{:S(2)}, u32[]{:S(2)}) collective-permute-start(f32[16,128]{1,0:T(8,128)S(1)} %get-tuple-element.70), channel_id=1, source_target_pairs={{0,3},{1,2},{2,1},{3,0},{4,7},{5,6},{6,5},{7,4},{8,11},{9,10},{10,... | collective-permute-start | bytes 24584 | tf_op jit(solution)/shard_map/ppermute | solution.py:433
  28.2 0.5 %collective-permute-start.17 = (f32[16,128]{1,0:T(8,128)S(1)}, f32[16,128]{1,0:T(8,128)S(1)}, u32[]{:S(2)}, u32[]{:S(2)}) collective-permute-start(f32[16,128]{1,0:T(8,128)S(1)} %get-tuple-element.72), channel_id=1, source_target_pairs={{0,1},{1,0},{2,3},{3,2},{4,5},{5,4},{6,7},{7,6},{8,9},{9,8},{10,11... | collective-permute-start | bytes 24584 | tf_op jit(solution)/shard_map/ppermute | solution.py:433
  28.6 1.4 %collective-permute-start.19 = (f32[16,128]{1,0:T(8,128)S(1)}, f32[16,128]{1,0:T(8,128)S(1)}, u32[]{:S(2)}, u32[]{:S(2)}) collective-permute-start(f32[16,128]{1,0:T(8,128)S(1)} %get-tuple-element.73), channel_id=1, source_target_pairs={{0,4},{4,0},{1,5},{5,1},{2,6},{6,2},{3,7},{7,3},{8,12},{12,8},{9,1... | collective-permute-start | bytes 24584 | tf_op jit(solution)/shard_map/ppermute | solution.py:433
  30.1 0.1 shard_map.88
  30.1 0.0 collective-permute-start.18
  30.1 0.2 shard_map.85.local_ref
  30.4 0.0 collective-permute-done.16.face_ref
  30.4 0.1 shard_map.87.rest_5_
  30.4 0.8 %collective-permute-done.18.rest_7_ = f32[8,128]{1,0:T(8,128)S(1)} collective-permute-done((f32[8,128]{1,0:T(8,128)S(1)}, f32[8,128]{1,0:T(8,128)S(1)}, u32[]{:S(2)}, u32[]{:S(2)}) %collective-permute-start.18) | collective-permute-done | bytes 4128 | tf_op jit(solution)/shard_map/ppermute | solution.py:433
  31.3 0.3 collective-permute-done.15.rest_4_
  31.6 0.2 collective-permute-done.17.rest_6_
  31.8 0.5 %collective-permute-done.19.rest_8_ = f32[16,128]{1,0:T(8,128)S(1)} collective-permute-done((f32[16,128]{1,0:T(8,128)S(1)}, f32[16,128]{1,0:T(8,128)S(1)}, u32[]{:S(2)}, u32[]{:S(2)}) %collective-permute-start.19) | collective-permute-done | bytes 8224 | tf_op jit(solution)/shard_map/ppermute | solution.py:433
  32.3 0.2 shard_map.89
  32.5 10.5 %all_to_all.11 = f32[32,1,128]{2,1,0:T(1,128)S(1)} all-to-all(f32[32,1,128]{2,1,0:T(1,128)S(1)} %bitcast.5), channel_id=1, replica_groups=mesh['row'=4,'th'=2,'ph'=4] {'row','th','ph'}, dimensions={0} | all-to-all | bytes 32768 | tf_op jit(solution)/shard_map/all_to_all | solution.py:488
  42.9 1.0 %shard_map.90 = (f32[8,4,4,64]{3,2,1,0:T(4,128)}, f32[8,4,4,64]{3,2,1,0:T(4,128)}) custom-call(f32[32,128]{1,0:T(8,128)S(1)} %bitcast.4, f32[64,128]{1,0:T(8,128)S(1)} %get-tuple-element.40.krylov_ref.refs_0_.rest_0_, f32[64,128]{1,0:T(8,128)S(1)} %get-tuple-element.52.krylov_ref.refs_1_.rest_1_, f32[64,128]{1,0:T(8,128)S(1)} %get-tuple-element.60.krylov_ref.refs_2_.rest_2_, ...), custom_call_target="tpu_custom_call" | custom-call | tf_op jit(solution)/shard_map/pallas_call | solution.py:394
  (1 shorter events, 0.0 us)
Async XLA Ops:
  2.8 8.6 %collective-permute-start.1 = (f32[16,128]{1,0:T(8,128)S(1)}, f32[16,128]{1,0:T(8,128)S(1)}, u32[]{:S(2)}, u32[]{:S(2)}) collective-permute-start(f32[16,128]{1,0:T(8,128)S(1)} %get-tuple-element.47), channel_id=1, source_target_pairs={{0,24},{8,16},{16,8},{24,0},{1,25},{9,17},{17,9},{25,1},{2,26},{10... | collective-permute-start | bytes 24584 | tf_op jit(solution)/shard_map/ppermute | solution.py:433
  5.2 6.4 %collective-permute-start = (f32[16,128]{1,0:T(8,128)S(1)}, f32[16,128]{1,0:T(8,128)S(1)}, u32[]{:S(2)}, u32[]{:S(2)}) collective-permute-start(f32[16,128]{1,0:T(8,128)S(1)} %get-tuple-element.46), channel_id=1, source_target_pairs={{0,3},{1,2},{2,1},{3,0},{4,7},{5,6},{6,5},{7,4},{8,11},{9,10},{10,... | collective-permute-start | bytes 24584 | tf_op jit(solution)/shard_map/ppermute | solution.py:433
  8.8 3.7 %collective-permute-start.2 = (f32[16,128]{1,0:T(8,128)S(1)}, f32[16,128]{1,0:T(8,128)S(1)}, u32[]{:S(2)}, u32[]{:S(2)}) collective-permute-start(f32[16,128]{1,0:T(8,128)S(1)} %get-tuple-element.48), channel_id=1, source_target_pairs={{0,1},{1,0},{2,3},{3,2},{4,5},{5,4},{6,7},{7,6},{8,9},{9,8},{10,11... | collective-permute-start | bytes 24584 | tf_op jit(solution)/shard_map/ppermute | solution.py:433
  8.8 4.0 %collective-permute-start.4 = (f32[16,128]{1,0:T(8,128)S(1)}, f32[16,128]{1,0:T(8,128)S(1)}, u32[]{:S(2)}, u32[]{:S(2)}) collective-permute-start(f32[16,128]{1,0:T(8,128)S(1)} %get-tuple-element.51), channel_id=1, source_target_pairs={{0,4},{4,0},{1,5},{5,1},{2,6},{6,2},{3,7},{7,3},{8,12},{12,8},{9,1... | collective-permute-start | bytes 24584 | tf_op jit(solution)/shard_map/ppermute | solution.py:433
  10.4 1.2 %collective-permute-start.3 = (f32[8,128]{1,0:T(8,128)S(1)}, f32[8,128]{1,0:T(8,128)S(1)}, u32[]{:S(2)}, u32[]{:S(2)}) collective-permute-start(f32[8,128]{1,0:T(8,128)S(1)} %shard_map.72), channel_id=1, source_target_pairs={{0,8},{8,0},{16,24},{24,16},{1,9},{9,1},{17,25},{25,17},{2,10},{10... | collective-permute-start | bytes 12296 | tf_op jit(solution)/shard_map/ppermute | solution.py:433
  13.0 3.8 %collective-permute-start.6 = (f32[16,128]{1,0:T(8,128)S(1)}, f32[16,128]{1,0:T(8,128)S(1)}, u32[]{:S(2)}, u32[]{:S(2)}) collective-permute-start(f32[16,128]{1,0:T(8,128)S(1)} %get-tuple-element.55), channel_id=1, source_target_pairs={{0,24},{8,16},{16,8},{24,0},{1,25},{9,17},{17,9},{25,1},{2,26},{10... | collective-permute-start | bytes 24584 | tf_op jit(solution)/shard_map/ppermute | solution.py:433
  13.0 5.5 %collective-permute-start.5 = (f32[16,128]{1,0:T(8,128)S(1)}, f32[16,128]{1,0:T(8,128)S(1)}, u32[]{:S(2)}, u32[]{:S(2)}) collective-permute-start(f32[16,128]{1,0:T(8,128)S(1)} %get-tuple-element.54), channel_id=1, source_target_pairs={{0,3},{1,2},{2,1},{3,0},{4,7},{5,6},{6,5},{7,4},{8,11},{9,10},{10,... | collective-permute-start | bytes 24584 | tf_op jit(solution)/shard_map/ppermute | solution.py:433
  14.9 3.7 %collective-permute-start.7 = (f32[16,128]{1,0:T(8,128)S(1)}, f32[16,128]{1,0:T(8,128)S(1)}, u32[]{:S(2)}, u32[]{:S(2)}) collective-permute-start(f32[16,128]{1,0:T(8,128)S(1)} %get-tuple-element.56), channel_id=1, source_target_pairs={{0,1},{1,0},{2,3},{3,2},{4,5},{5,4},{6,7},{7,6},{8,9},{9,8},{10,11... | collective-permute-start | bytes 24584 | tf_op jit(solution)/shard_map/ppermute | solution.py:433
  14.9 4.1 %collective-permute-start.9 = (f32[16,128]{1,0:T(8,128)S(1)}, f32[16,128]{1,0:T(8,128)S(1)}, u32[]{:S(2)}, u32[]{:S(2)}) collective-permute-start(f32[16,128]{1,0:T(8,128)S(1)} %get-tuple-element.59), channel_id=1, source_target_pairs={{0,4},{4,0},{1,5},{5,1},{2,6},{6,2},{3,7},{7,3},{8,12},{12,8},{9,1... | collective-permute-start | bytes 24584 | tf_op jit(solution)/shard_map/ppermute | solution.py:433
  16.5 1.2 %collective-permute-start.8 = (f32[8,128]{1,0:T(8,128)S(1)}, f32[8,128]{1,0:T(8,128)S(1)}, u32[]{:S(2)}, u32[]{:S(2)}) collective-permute-start(f32[8,128]{1,0:T(8,128)S(1)} %shard_map.77), channel_id=1, source_target_pairs={{0,8},{8,0},{16,24},{24,16},{1,9},{9,1},{17,25},{25,17},{2,10},{10... | collective-permute-start | bytes 12296 | tf_op jit(solution)/shard_map/ppermute | solution.py:433
  19.2 4.6 %collective-permute-start.11 = (f32[16,128]{1,0:T(8,128)S(1)}, f32[16,128]{1,0:T(8,128)S(1)}, u32[]{:S(2)}, u32[]{:S(2)}) collective-permute-start(f32[16,128]{1,0:T(8,128)S(1)} %get-tuple-element.63), channel_id=1, source_target_pairs={{0,24},{8,16},{16,8},{24,0},{1,25},{9,17},{17,9},{25,1},{2,26},{10... | collective-permute-start | bytes 24584 | tf_op jit(solution)/shard_map/ppermute | solution.py:433
  19.7 5.4 %collective-permute-start.10 = (f32[16,128]{1,0:T(8,128)S(1)}, f32[16,128]{1,0:T(8,128)S(1)}, u32[]{:S(2)}, u32[]{:S(2)}) collective-permute-start(f32[16,128]{1,0:T(8,128)S(1)} %get-tuple-element.62), channel_id=1, source_target_pairs={{0,3},{1,2},{2,1},{3,0},{4,7},{5,6},{6,5},{7,4},{8,11},{9,10},{10,... | collective-permute-start | bytes 24584 | tf_op jit(solution)/shard_map/ppermute | solution.py:433
  21.9 3.7 %collective-permute-start.12 = (f32[16,128]{1,0:T(8,128)S(1)}, f32[16,128]{1,0:T(8,128)S(1)}, u32[]{:S(2)}, u32[]{:S(2)}) collective-permute-start(f32[16,128]{1,0:T(8,128)S(1)} %get-tuple-element.64), channel_id=1, source_target_pairs={{0,1},{1,0},{2,3},{3,2},{4,5},{5,4},{6,7},{7,6},{8,9},{9,8},{10,11... | collective-permute-start | bytes 24584 | tf_op jit(solution)/shard_map/ppermute | solution.py:433
  22.2 3.7 %collective-permute-start.14 = (f32[16,128]{1,0:T(8,128)S(1)}, f32[16,128]{1,0:T(8,128)S(1)}, u32[]{:S(2)}, u32[]{:S(2)}) collective-permute-start(f32[16,128]{1,0:T(8,128)S(1)} %get-tuple-element.67), channel_id=1, source_target_pairs={{0,4},{4,0},{1,5},{5,1},{2,6},{6,2},{3,7},{7,3},{8,12},{12,8},{9,1... | collective-permute-start | bytes 24584 | tf_op jit(solution)/shard_map/ppermute | solution.py:433
  23.6 1.2 %collective-permute-start.13 = (f32[8,128]{1,0:T(8,128)S(1)}, f32[8,128]{1,0:T(8,128)S(1)}, u32[]{:S(2)}, u32[]{:S(2)}) collective-permute-start(f32[8,128]{1,0:T(8,128)S(1)} %shard_map.82), channel_id=1, source_target_pairs={{0,8},{8,0},{16,24},{24,16},{1,9},{9,1},{17,25},{25,17},{2,10},{10... | collective-permute-start | bytes 12296 | tf_op jit(solution)/shard_map/ppermute | solution.py:433
  26.1 4.3 %collective-permute-start.16 = (f32[16,128]{1,0:T(8,128)S(1)}, f32[16,128]{1,0:T(8,128)S(1)}, u32[]{:S(2)}, u32[]{:S(2)}) collective-permute-start(f32[16,128]{1,0:T(8,128)S(1)} %get-tuple-element.71), channel_id=1, source_target_pairs={{0,24},{8,16},{16,8},{24,0},{1,25},{9,17},{17,9},{25,1},{2,26},{10... | collective-permute-start | bytes 24584 | tf_op jit(solution)/shard_map/ppermute | solution.py:433
  26.1 5.5 %collective-permute-start.15 = (f32[16,128]{1,0:T(8,128)S(1)}, f32[16,128]{1,0:T(8,128)S(1)}, u32[]{:S(2)}, u32[]{:S(2)}) collective-permute-start(f32[16,128]{1,0:T(8,128)S(1)} %get-tuple-element.70), channel_id=1, source_target_pairs={{0,3},{1,2},{2,1},{3,0},{4,7},{5,6},{6,5},{7,4},{8,11},{9,10},{10,... | collective-permute-start | bytes 24584 | tf_op jit(solution)/shard_map/ppermute | solution.py:433
  28.2 3.7 %collective-permute-start.17 = (f32[16,128]{1,0:T(8,128)S(1)}, f32[16,128]{1,0:T(8,128)S(1)}, u32[]{:S(2)}, u32[]{:S(2)}) collective-permute-start(f32[16,128]{1,0:T(8,128)S(1)} %get-tuple-element.72), channel_id=1, source_target_pairs={{0,1},{1,0},{2,3},{3,2},{4,5},{5,4},{6,7},{7,6},{8,9},{9,8},{10,11... | collective-permute-start | bytes 24584 | tf_op jit(solution)/shard_map/ppermute | solution.py:433
  28.6 3.7 %collective-permute-start.19 = (f32[16,128]{1,0:T(8,128)S(1)}, f32[16,128]{1,0:T(8,128)S(1)}, u32[]{:S(2)}, u32[]{:S(2)}) collective-permute-start(f32[16,128]{1,0:T(8,128)S(1)} %get-tuple-element.73), channel_id=1, source_target_pairs={{0,4},{4,0},{1,5},{5,1},{2,6},{6,2},{3,7},{7,3},{8,12},{12,8},{9,1... | collective-permute-start | bytes 24584 | tf_op jit(solution)/shard_map/ppermute | solution.py:433
  30.1 1.2 %collective-permute-start.18 = (f32[8,128]{1,0:T(8,128)S(1)}, f32[8,128]{1,0:T(8,128)S(1)}, u32[]{:S(2)}, u32[]{:S(2)}) collective-permute-start(f32[8,128]{1,0:T(8,128)S(1)} %shard_map.88), channel_id=1, source_target_pairs={{0,8},{8,0},{16,24},{24,16},{1,9},{9,1},{17,25},{25,17},{2,10},{10... | collective-permute-start | bytes 12296 | tf_op jit(solution)/shard_map/ppermute | solution.py:433

commit v8 on v7

--- a/solution.py
+++ b/solution.py
@@ -121,12 +121,26 @@
     out_ref[...] = jnp.where(flags_ref[1:2, :] > 0.5, low, high)
 
 
-def across_kernel(flags_ref, face_ref, out_ref):
-    face = face_ref[...]
-    cell = lax.broadcasted_iota(jnp.int32, face.shape, 1) % BLK
-    below = jnp.where(cell == 0, pltpu.roll(face, LANES - BLK + 1, 1), 0.0)
-    above = jnp.where(cell == BLK - 1, pltpu.roll(face, BLK - 1, 1), 0.0)
-    out_ref[...] = jnp.where(flags_ref[1:2, :] > 0.5, above, below)
+def radial_kernel(ph, th, names, flags_ref, local_ref, conduct_ref, *rest):
+    taken, out_ref = dict(zip(names, rest)), rest[-1]
+    slab = out_ref.shape[0] // th
+    odd, has_low, has_high = [flags_ref[i : i + 1, :] > 0.5 for i in (1, 3, 4)]
+    near = taken["row_low"][...]
+    edge = lax.broadcasted_iota(jnp.int32, near.shape, 1) % BLK == jnp.where(odd, 0, BLK - 1)
+    near = jnp.concatenate([jnp.where(edge, part, 0.0) for part in (near, pltpu.roll(near, LANES - 1, 1))], axis=0)
+    below = above = jnp.zeros_like(near)
+    if "row_high" in taken:
+        face = taken["row_high"][...]
+        cell = lax.broadcasted_iota(jnp.int32, face.shape, 1) % BLK
+        below = jnp.where(cell == 0, pltpu.roll(face, LANES - BLK + 1, 1), 0.0)
+        above = jnp.where(cell == BLK - 1, pltpu.roll(face, BLK - 1, 1), 0.0)
+    low = jnp.where(has_low, jnp.where(odd, near, below), 0.0)
+    high = jnp.where(has_high, jnp.where(odd, above, near), 0.0)
+    out_ref[...] = local_ref[...]
+    for t in range(th):
+        for first, side in ((t * slab, low), ((t + 1) * slab - ph, high)):
+            at = pl.ds(first, ph)
+            out_ref[at, :] = local_ref[at, :] - conduct_ref[at, :] * side[t * ph : (t + 1) * ph]
 
 
 def local_part(field, krylov, conduct, diagonal, mixing_ref, ph, th):
@@ -156,15 +170,9 @@
 
 
 def sides(axis, taken, flags_ref):
-    parity, has_low, has_high = {"ph": (0, None, None), "row": (1, 3, 4), "th": (2, 5, 6)}[axis]
+    parity, has_low, has_high = {"ph": (0, None, None), "th": (2, 5, 6)}[axis]
     odd = flags_ref[parity : parity + 1, :] > 0.5
     first = taken[axis + "_low"][...]
-    if axis == "row":
-        edge = jnp.where(odd, 0, BLK - 1)
-        cell = lax.broadcasted_iota(jnp.int32, first.shape, 1) % BLK
-        first = jnp.concatenate(
-            [jnp.where(cell == edge, part, 0.0) for part in (first, pltpu.roll(first, LANES - 1, 1))], axis=0
-        )
     second = taken[axis + "_high"][...] if axis + "_high" in taken else jnp.zeros_like(first)
     low, high = jnp.where(odd, first, second), jnp.where(odd, second, first)
     if has_low is None:
@@ -173,17 +181,13 @@
     return low, jnp.where(flags_ref[has_high : has_high + 1, :] > 0.5, high, 0.0)
 
 
-def add_faces(halo_ref, taken, flags_ref, ph, th):
-    rows = halo_ref.shape[0]
-    slab = rows // th
-    halo_ref[...] = jnp.zeros_like(halo_ref)
+def take_azimuthal(out_ref, local_ref, conduct_ref, taken, flags_ref, ph):
+    rows = out_ref.shape[0]
     low, high = sides("ph", taken, flags_ref)
-    halo_ref[pl.ds(0, rows // ph, stride=ph), :] = low
-    halo_ref[pl.ds(ph - 1, rows // ph, stride=ph), :] = high
-    low, high = sides("row", taken, flags_ref)
-    for t in range(th):
-        halo_ref[t * slab : t * slab + ph, :] += low[t * ph : (t + 1) * ph]
-        halo_ref[(t + 1) * slab - ph : (t + 1) * slab, :] += high[t * ph : (t + 1) * ph]
+    out_ref[...] = local_ref[...]
+    for first, side in ((0, low), (ph - 1, high)):
+        at = pl.ds(first, rows // ph, stride=ph)
+        out_ref[at, :] = local_ref[at, :] - conduct_ref[at, :] * side
 
 
 def split_slabs(th, th_n):
@@ -202,8 +206,8 @@
 
 
 def first_kernel(ph, th, names, sizes, right_ref, conduct_ref, coupling_ref, codes_ref, inverse_ref, *rest):
-    flags_ref, krylov_ref, conducts_ref, diagonal_ref, mixing_ref, held_ref, d_ref, *sent = rest[: 7 + len(names)]
-    right, conduct, coupling, codes, turn, sems = rest[7 + len(names) :]
+    flags_ref, krylov_ref, conducts_ref, diagonal_ref, mixing_ref, held_ref, right, d_ref, *sent = rest[: 8 + len(names)]
+    conduct, coupling, codes, turn, sems = rest[8 + len(names) :]
     rows = d_ref.shape[0]
     slab = rows // th
     pairs = [(right_ref, right), (coupling_ref, coupling), (codes_ref, codes), (conduct_ref, conduct)]
@@ -264,10 +268,13 @@
         turned_ref[i] = held_ref[i % ph, i // (nb * ph), i % (nb * ph) // ph].T
 
 
-def local_kernel(ph, th, krylov_ref, last_ref, conduct_ref, diagonal_ref, mixing_ref, out_ref):
+def local_kernel(ph, th, count, krylov_ref, last_ref, conduct_ref, diagonal_ref, mixing_ref, *rest):
+    fields, (out_ref, *natives), turns = rest[:count], rest[count : 2 * count + 1], rest[2 * count + 1 :]
     out_ref[...] = local_part(
         last_ref[...], krylov_ref[...], conduct_ref[...], diagonal_ref[...], mixing_ref, ph, th
     )
+    for field_ref, native_ref, turn_ref in zip(fields, natives, turns):
+        from_rows(field_ref[...], native_ref, turn_ref)
 
 
 def gram_rows(left, right):
@@ -283,9 +290,8 @@
 
 
 def early_kernel(ph, th, th_n, names, flags_ref, local_ref, conduct_ref, turned_ref, *rest):
-    next_ref, d_ref, halo_ref = rest[len(names) :]
-    add_faces(halo_ref, dict(zip(names, rest)), flags_ref, ph, th)
-    next_ref[...] = local_ref[...] - conduct_ref[...] * halo_ref[...]
+    next_ref, d_ref = rest[len(names) :]
+    take_azimuthal(next_ref, local_ref, conduct_ref, dict(zip(names, rest)), flags_ref, ph)
     early, late = split_slabs(th, th_n)
     slab = d_ref.shape[0] // th
     apply_turned(next_ref, turned_ref, d_ref, groups_of(early, slab))
@@ -311,16 +317,15 @@
 
 
 def last_kernel(ph, th, names, flags_ref, local_ref, conduct_ref, partial_ref, *rest):
-    older, taken, (next_ref, gram_ref, halo_ref) = rest[:S], rest[S : S + len(names)], rest[S + len(names) :]
+    older, taken, (next_ref, gram_ref) = rest[:S], rest[S : S + len(names)], rest[S + len(names) :]
     taken = dict(zip(names, taken))
-    add_faces(halo_ref, taken, flags_ref, ph, th)
+    take_azimuthal(next_ref, local_ref, conduct_ref, taken, flags_ref, ph)
     low, high = sides("th", taken, flags_ref)
-    rows = halo_ref.shape[0]
+    rows = next_ref.shape[0]
     slab = rows // th
-    halo_ref[:slab, :] += low
-    halo_ref[rows - slab :, :] += high
-    final = local_ref[...] - conduct_ref[...] * halo_ref[...]
-    next_ref[...] = final
+    for at, side in ((pl.ds(0, slab), low), (pl.ds(rows - slab, slab), high)):
+        next_ref[at, :] = next_ref[at, :] - conduct_ref[at, :] * side
+    final = next_ref[...]
     basis = [ref[...] for ref in older] + [final]
     stacked = jnp.concatenate([partial_ref[...]] + gram_rows([final] * (S + 1), basis), axis=0)
     each = jnp.sum(stacked, axis=1, keepdims=True)
@@ -356,9 +361,11 @@
     return weights
 
 
-def combine_kernel(partial_rows, gram_ref, *refs):
-    krylov, directions, rest = refs[: S + 1], refs[S + 1 : 2 * S + 1], refs[2 * S + 1 :]
-    correction_ref, residual_ref, correction, residual, turn, other_turn, sems = rest
+def combine_kernel(partial_rows, gram_ref, final_ref, *refs):
+    krylov, directions, rest = refs[:S], refs[S : 2 * S], refs[2 * S :]
+    correction_ref, residual_ref, correction, residual, newest, turn, sems = rest
+    from_rows(final_ref[...], newest, turn)
+    krylov = [*krylov, newest]
     line = jnp.sum(gram_ref[...], axis=0, keepdims=True)
     products, place = [], 0
     for i in range(S + 1):
@@ -368,14 +375,16 @@
             products[i].append(jnp.broadcast_to(line[:, place : place + 1], line.shape))
             place += 1
     weights = small_solve(products)
-    total = weights[0] * directions[0][...]
-    for j in range(1, S):
-        total = total + weights[j] * directions[j][...]
-    left = krylov[0][...]
-    for j in range(S):
-        left = left - weights[j] * (krylov[j + 1][...] + krylov[j][...])
-    from_rows(total, correction, turn)
-    from_rows(left, residual, other_turn)
+    weights = [weight[:, : correction.shape[-1]] for weight in weights]
+    for v in range(correction.shape[0]):
+        total = weights[0] * directions[0][v]
+        left = krylov[0][v]
+        for j in range(S):
+            if j:
+                total = total + weights[j] * directions[j][v]
+            left = left - weights[j] * (krylov[j + 1][v] + krylov[j][v])
+        correction[v] = total
+        residual[v] = left
     copies = [
         pltpu.make_async_copy(correction, correction_ref, sems.at[0]),
         pltpu.make_async_copy(residual, residual_ref, sems.at[1]),
@@ -416,6 +425,8 @@
     names = tuple(face_rows)
     late_names = tuple(name for name in names if name[:2] == "th")
     packed = tuple(name for name in names if name != "row_low")
+    early_names = tuple(name for name in names if name[:2] == "ph")
+    radial_names = tuple(name for name in names if name[:3] == "row")
     def shape(n):
         return jax.ShapeDtypeStruct((n, LANES), jnp.float32)
 
@@ -430,19 +441,16 @@
         taken = []
         for name in names:
             axis, side = name.split("_")
-            face = lax.ppermute(sent[name], axis, plans[side](lax.axis_size(axis)))
-            if name == "row_high":
-                (face,) = call(across_kernel, [shape(per)], [], flags, face)
-            taken.append(face)
+            taken.append(lax.ppermute(sent[name], axis, plans[side](lax.axis_size(axis))))
         return taken
 
     field = pltpu.VMEM(right_side.shape, jnp.float32)
+    native = jax.ShapeDtypeStruct(right_side.shape, jnp.float32)
     turn = pltpu.VMEM((rows, LANES), jnp.float32)
-    flags, start, conducts, diagonal, mixing, held, direction, *sent = call(
+    flags, start, conducts, diagonal, mixing, held, right_native, direction, *sent = call(
         functools.partial(first_kernel, ph, th, packed, (("row", row_n), ("th", th_n), ("ph", ph_n))),
-        [shape(VARS), whole, whole, whole, shape(VARS), jax.ShapeDtypeStruct(inverse.shape, jnp.bfloat16), whole] + faces,
+        [shape(VARS), whole, whole, whole, shape(VARS), jax.ShapeDtypeStruct(inverse.shape, jnp.bfloat16), native, whole] + faces,
         [
-            field,
             field,
             pltpu.SMEM(coupling.shape, jnp.float32),
             pltpu.SMEM(face_codes.shape, jnp.int32),
@@ -454,24 +462,39 @@
     )
     (turned,) = call(turn_kernel, [jax.ShapeDtypeStruct((rows, LANES, LANES), jnp.bfloat16)], [], held)
     krylov, directions = [start], [direction]
+    krylov_native, direction_native = [right_native], []
     for step in range(S):
         taken = exchange(sent, directions[-1])
+        ready = [] if step == 0 else [krylov[-1], directions[-1]] + directions[:1] * (step == 1)
+        beside, *laid = call(
+            functools.partial(local_kernel, ph, th, len(ready)),
+            [whole] + [native] * len(ready),
+            [turn] * len(ready),
+            krylov[-1], directions[-1], conducts, diagonal, mixing, *ready,
+        )
+        if laid:
+            krylov_native.append(laid[0])
+            direction_native += laid[:0:-1]
+        taken = dict(zip(names, taken))
+
+        def of(some):
+            return [taken[name] for name in some]
+
         (beside,) = call(
-            functools.partial(local_kernel, ph, th), [whole], [], krylov[-1], directions[-1], conducts, diagonal, mixing
+            functools.partial(radial_kernel, ph, th, radial_names), [whole], [], flags, beside, conducts, *of(radial_names)
         )
         if step < S - 1:
-            early_names, early_taken = zip(*[(n, t) for n, t in zip(names, taken) if n not in late_names])
             early, part = call(
                 functools.partial(early_kernel, ph, th, th_n, early_names),
                 [whole, whole],
-                [turn],
-                flags, beside, conducts, turned, *early_taken,
+                [],
+                flags, beside, conducts, turned, *of(early_names),
             )
             following, direction, *sent = call(
                 functools.partial(late_kernel, ph, th, th_n, packed, late_names),
                 [whole, whole] + faces,
                 [],
-                flags, early, part, conducts, turned, *[t for n, t in zip(names, taken) if n in late_names],
+                flags, early, part, conducts, turned, *of(late_names),
             )
             krylov.append(following)
             directions.append(direction)
@@ -479,21 +502,21 @@
     partial_rows += -partial_rows % 8
     (partial,) = call(gram_kernel, [shape(partial_rows)], [], *krylov)
     following, gram = call(
-        functools.partial(last_kernel, ph, th, names),
+        functools.partial(last_kernel, ph, th, early_names + late_names),
         [whole, shape(row_n * th_n * ph_n)],
-        [turn],
-        flags, beside, conducts, partial, *krylov, *taken,
+        [],
+        flags, beside, conducts, partial, *krylov, *of(early_names + late_names),
     )
     krylov.append(following)
     gram = lax.all_to_all(gram, ("row", "th", "ph"), 0, 0, tiled=True)
-    native = [jax.ShapeDtypeStruct(right_side.shape, jnp.float32)] * 2
+    results = [native, jax.ShapeDtypeStruct(right_side.shape, jnp.float32)]
     return tuple(
         call(
             functools.partial(combine_kernel, partial_rows),
-            native,
-            [field, field, turn, turn, pltpu.SemaphoreType.DMA((2,))],
-            gram, *krylov, *directions,
-            stay=native,
+            results,
+            [field, field, field, turn, pltpu.SemaphoreType.DMA((2,))],
+            gram, following, *krylov_native, *direction_native,
+            stay=results,
         )
     )
 

time: 44.1 us -> 43.9 us (level)
  transfers between devices with their start and end apart: 20 -> 20, of which waited for: 12 -> 13; matrix products, arithmetic and copies ran while one was open for 0% -> 0% of each run, Pallas kernels for 7% -> 8%
where the time goes in v8:
time: 43.9 us; the launch traced here: 43.7 us
  starting transfers between devices  19.5 us (44%)
  blocking collectives  10.4 us (24%)
  Pallas kernels  7.06 us (16%)
  waiting for transfers between devices  6.01 us (14%)
  between operations  0.73 us (2%)
    ppermute x20, starting transfers between devices, exchange(): lax.ppermute(sent[name], axis, plans[side](lax.axis_size(axis)))  19.5 us
    all_to_all x1, blocking collectives, local(): gram = lax.all_to_all(gram, ('row', 'th', 'ph'), 0, 0, tiled=True)  10.4 us
    pallas_call x23, Pallas kernels, call(): pl.pallas_call(kernel, out_shape=outs, in_specs=[spec(a) for a in args],...  7.06 us
    ppermute x20, waiting for transfers between devices, exchange(): lax.ppermute(sent[name], axis, plans[side](lax.axis_size(axis)))  6.01 us
  transfers between devices with their start and end apart: 20, of which 13 were waited for; matrix products, arithmetic and copies ran while one was open for 0% of the time, Pallas kernels for 8%

profile of v8, /device:TPU:0, one launch (start us, length us, event | category | flops | bytes accessed | tf_op | source)
XLA Modules:
  0.0 43.7 jit_solution(18382230120935320607)
XLA Ops:
  0.6 2.1 %shard_map.68 = (f32[8,128]{1,0:T(8,128)S(1)}, f32[64,128]{1,0:T(8,128)S(1)}, f32[64,128]{1,0:T(8,128)S(1)}, f32[64,128]{1,0:T(8,128)S(1)}, f32[8,128]{1,0:T(8,1...) custom-call(f32[8,4,4,64]{3,2,1,0:T(4,128)} %right_ref.1, ...), custom_call_target="tpu_custom_call" | custom-call | tf_op jit(solution)/shard_map/pallas_call | solution.py:403
  2.8 2.4 %collective-permute-start = (f32[16,128]{1,0:T(8,128)S(1)}, f32[16,128]{1,0:T(8,128)S(1)}, u32[]{:S(2)}, u32[]{:S(2)}) collective-permute-start(f32[16,128]{1,0:T(8,128)S(1)} %get-tuple-element.56), channel_id=1, source_target_pairs={{0,24},{8,16},{16,8},{24,0},{1,25},{9,17},{17,9},{25,1},{2,26},{10... | collective-permute-start | bytes 24584 | tf_op jit(solution)/shard_map/ppermute | solution.py:444
  5.2 3.6 %collective-permute-start.2 = (f32[16,128]{1,0:T(8,128)S(1)}, f32[16,128]{1,0:T(8,128)S(1)}, u32[]{:S(2)}, u32[]{:S(2)}) collective-permute-start(f32[16,128]{1,0:T(8,128)S(1)} %get-tuple-element.58), channel_id=1, source_target_pairs={{0,3},{1,2},{2,1},{3,0},{4,7},{5,6},{6,5},{7,4},{8,11},{9,10},{10,... | collective-permute-start | bytes 24584 | tf_op jit(solution)/shard_map/ppermute | solution.py:444
  8.8 0.0 collective-permute-start.3
  8.8 1.5 %collective-permute-start.4 = (f32[16,128]{1,0:T(8,128)S(1)}, f32[16,128]{1,0:T(8,128)S(1)}, u32[]{:S(2)}, u32[]{:S(2)}) collective-permute-start(f32[16,128]{1,0:T(8,128)S(1)} %get-tuple-element.62), channel_id=1, source_target_pairs={{0,4},{4,0},{1,5},{5,1},{2,6},{6,2},{3,7},{7,3},{8,12},{12,8},{9,1... | collective-permute-start | bytes 24584 | tf_op jit(solution)/shard_map/ppermute | solution.py:444
  10.4 0.1 shard_map.70
  10.4 0.2 collective-permute-start.1
  10.6 0.6 %shard_map.72.turned_ref = bf16[64,128,128]{2,1,0:T(8,128)(2,1)S(1)} custom-call(bf16[4,4,4,128,128]{4,3,2,1,0:T(8,128)(2,1)S(1)} %get-tuple-element.57.held_ref), custom_call_target="tpu_custom_call" | custom-call | tf_op jit(solution)/shard_map/pallas_call | solution.py:403
  11.2 0.2 shard_map.69.local_ref
  11.3 0.2 collective-permute-done.1.rest_1_
  11.6 0.0 collective-permute-done.rest_0_
  11.6 0.1 shard_map.71.local_ref
  11.7 0.0 collective-permute-done.2.rest_0_
  11.7 0.8 %collective-permute-done.3.rest_1_ = f32[16,128]{1,0:T(8,128)S(1)} collective-permute-done((f32[16,128]{1,0:T(8,128)S(1)}, f32[16,128]{1,0:T(8,128)S(1)}, u32[]{:S(2)}, u32[]{:S(2)}) %collective-permute-start.3) | collective-permute-done | bytes 8224 | tf_op jit(solution)/shard_map/ppermute | solution.py:444
  12.5 0.3 shard_map.73
  12.8 0.0 collective-permute-done.4.rest_0_
  12.8 0.2 shard_map.74
  13.0 0.0 collective-permute-start.5
  13.0 1.9 %collective-permute-start.7 = (f32[16,128]{1,0:T(8,128)S(1)}, f32[16,128]{1,0:T(8,128)S(1)}, u32[]{:S(2)}, u32[]{:S(2)}) collective-permute-start(f32[16,128]{1,0:T(8,128)S(1)} %get-tuple-element.67), channel_id=1, source_target_pairs={{0,3},{1,2},{2,1},{3,0},{4,7},{5,6},{6,5},{7,4},{8,11},{9,10},{10,... | collective-permute-start | bytes 24584 | tf_op jit(solution)/shard_map/ppermute | solution.py:444
  14.9 0.0 collective-permute-start.8
  14.9 1.5 %collective-permute-start.9 = (f32[16,128]{1,0:T(8,128)S(1)}, f32[16,128]{1,0:T(8,128)S(1)}, u32[]{:S(2)}, u32[]{:S(2)}) collective-permute-start(f32[16,128]{1,0:T(8,128)S(1)} %get-tuple-element.71), channel_id=1, source_target_pairs={{0,4},{4,0},{1,5},{5,1},{2,6},{6,2},{3,7},{7,3},{8,12},{12,8},{9,1... | collective-permute-start | bytes 24584 | tf_op jit(solution)/shard_map/ppermute | solution.py:444
  16.4 0.1 shard_map.76
  16.5 0.2 collective-permute-start.6
  16.6 0.3 shard_map.75
  17.0 0.7 %collective-permute-done.6.rest_1_ = f32[8,128]{1,0:T(8,128)S(1)} collective-permute-done((f32[8,128]{1,0:T(8,128)S(1)}, f32[8,128]{1,0:T(8,128)S(1)}, u32[]{:S(2)}, u32[]{:S(2)}) %collective-permute-start.6) | collective-permute-done | bytes 4128 | tf_op jit(solution)/shard_map/ppermute | solution.py:444
  17.7 0.0 collective-permute-done.5.rest_0_
  17.7 0.1 shard_map.77.local_ref
  17.7 0.8 %collective-permute-done.7.rest_0_ = f32[16,128]{1,0:T(8,128)S(1)} collective-permute-done((f32[16,128]{1,0:T(8,128)S(1)}, f32[16,128]{1,0:T(8,128)S(1)}, u32[]{:S(2)}, u32[]{:S(2)}) %collective-permute-start.7) | collective-permute-done | bytes 8224 | tf_op jit(solution)/shard_map/ppermute | solution.py:444
  18.5 0.1 collective-permute-done.8.rest_1_
  18.6 0.3 shard_map.78
  18.9 0.0 collective-permute-done.9.rest_0_
  19.0 0.2 shard_map.79
  19.2 0.6 %collective-permute-start.10 = (f32[16,128]{1,0:T(8,128)S(1)}, f32[16,128]{1,0:T(8,128)S(1)}, u32[]{:S(2)}, u32[]{:S(2)}) collective-permute-start(f32[16,128]{1,0:T(8,128)S(1)} %get-tuple-element.75), channel_id=1, source_target_pairs={{0,24},{8,16},{16,8},{24,0},{1,25},{9,17},{17,9},{25,1},{2,26},{10... | collective-permute-start | bytes 24584 | tf_op jit(solution)/shard_map/ppermute | solution.py:444
  19.8 2.2 %collective-permute-start.12 = (f32[16,128]{1,0:T(8,128)S(1)}, f32[16,128]{1,0:T(8,128)S(1)}, u32[]{:S(2)}, u32[]{:S(2)}) collective-permute-start(f32[16,128]{1,0:T(8,128)S(1)} %get-tuple-element.76), channel_id=1, source_target_pairs={{0,3},{1,2},{2,1},{3,0},{4,7},{5,6},{6,5},{7,4},{8,11},{9,10},{10,... | collective-permute-start | bytes 24584 | tf_op jit(solution)/shard_map/ppermute | solution.py:444
  22.0 0.4 collective-permute-start.13
  22.3 1.2 %collective-permute-start.14 = (f32[16,128]{1,0:T(8,128)S(1)}, f32[16,128]{1,0:T(8,128)S(1)}, u32[]{:S(2)}, u32[]{:S(2)}) collective-permute-start(f32[16,128]{1,0:T(8,128)S(1)} %get-tuple-element.80), channel_id=1, source_target_pairs={{0,4},{4,0},{1,5},{5,1},{2,6},{6,2},{3,7},{7,3},{8,12},{12,8},{9,1... | collective-permute-start | bytes 24584 | tf_op jit(solution)/shard_map/ppermute | solution.py:444
  23.5 0.1 shard_map.81
  23.6 0.1 collective-permute-start.11
  23.6 0.3 shard_map.80
  23.9 0.8 %collective-permute-done.11.rest_1_ = f32[8,128]{1,0:T(8,128)S(1)} collective-permute-done((f32[8,128]{1,0:T(8,128)S(1)}, f32[8,128]{1,0:T(8,128)S(1)}, u32[]{:S(2)}, u32[]{:S(2)}) %collective-permute-start.11) | collective-permute-done | bytes 4128 | tf_op jit(solution)/shard_map/ppermute | solution.py:444
  24.7 0.0 collective-permute-done.10.rest_0_
  24.7 0.1 shard_map.82.local_ref
  24.8 0.4 collective-permute-done.12.rest_0_
  25.2 0.4 collective-permute-done.13.rest_1_
  25.6 0.3 shard_map.83
  25.9 0.1 collective-permute-done.14.rest_0_
  26.0 0.2 shard_map.84
  26.2 0.0 collective-permute-start.15
  26.2 1.9 %collective-permute-start.17 = (f32[16,128]{1,0:T(8,128)S(1)}, f32[16,128]{1,0:T(8,128)S(1)}, u32[]{:S(2)}, u32[]{:S(2)}) collective-permute-start(f32[16,128]{1,0:T(8,128)S(1)} %get-tuple-element.85), channel_id=1, source_target_pairs={{0,3},{1,2},{2,1},{3,0},{4,7},{5,6},{6,5},{7,4},{8,11},{9,10},{10,... | collective-permute-start | bytes 24584 | tf_op jit(solution)/shard_map/ppermute | solution.py:444
  28.2 0.5 %collective-permute-start.18 = (f32[16,128]{1,0:T(8,128)S(1)}, f32[16,128]{1,0:T(8,128)S(1)}, u32[]{:S(2)}, u32[]{:S(2)}) collective-permute-start(f32[16,128]{1,0:T(8,128)S(1)} %get-tuple-element.86), channel_id=1, source_target_pairs={{0,1},{1,0},{2,3},{3,2},{4,5},{5,4},{6,7},{7,6},{8,9},{9,8},{10,11... | collective-permute-start | bytes 24584 | tf_op jit(solution)/shard_map/ppermute | solution.py:444
  28.6 1.4 %collective-permute-start.19 = (f32[16,128]{1,0:T(8,128)S(1)}, f32[16,128]{1,0:T(8,128)S(1)}, u32[]{:S(2)}, u32[]{:S(2)}) collective-permute-start(f32[16,128]{1,0:T(8,128)S(1)} %get-tuple-element.87), channel_id=1, source_target_pairs={{0,4},{4,0},{1,5},{5,1},{2,6},{6,2},{3,7},{7,3},{8,12},{12,8},{9,1... | collective-permute-start | bytes 24584 | tf_op jit(solution)/shard_map/ppermute | solution.py:444
  30.0 0.1 shard_map.86
  30.1 0.0 collective-permute-start.16
  30.2 0.3 shard_map.85
  30.5 0.8 %collective-permute-done.16.rest_1_ = f32[8,128]{1,0:T(8,128)S(1)} collective-permute-done((f32[8,128]{1,0:T(8,128)S(1)}, f32[8,128]{1,0:T(8,128)S(1)}, u32[]{:S(2)}, u32[]{:S(2)}) %collective-permute-start.16) | collective-permute-done | bytes 4128 | tf_op jit(solution)/shard_map/ppermute | solution.py:444
  31.3 0.0 collective-permute-done.15.rest_0_
  31.3 0.1 shard_map.87.local_ref
  31.4 0.4 collective-permute-done.17.rest_4_
  31.8 0.1 collective-permute-done.18.rest_5_
  31.9 0.4 collective-permute-done.19.rest_6_
  32.3 0.1 shard_map.89
  32.4 10.4 %all_to_all.11 = f32[32,1,128]{2,1,0:T(1,128)S(1)} all-to-all(f32[32,1,128]{2,1,0:T(1,128)S(1)} %bitcast.5), channel_id=1, replica_groups=mesh['row'=4,'th'=2,'ph'=4] {'row','th','ph'}, dimensions={0} | all-to-all | bytes 32768 | tf_op jit(solution)/shard_map/all_to_all | solution.py:511
  42.9 0.9 %shard_map.90 = (f32[8,4,4,64]{3,2,1,0:T(4,128)}, f32[8,4,4,64]{3,2,1,0:T(4,128)}) custom-call(f32[32,128]{1,0:T(8,128)S(1)} %bitcast.4, f32[64,128]{1,0:T(8,128)S(1)} %get-tuple-element.89.final_ref, f32[8,4,4,64]{3,2,1,0:T(4,128)S(1)} %get-tuple-element.90.refs_0_, f32[8,4,4,64]{3,2,1,0:T(4,128)S(1)} %get-tuple-element.91.refs_1_, ...), custom_call_target="tpu_custom_call" | custom-call | tf_op jit(solution)/shard_map/pallas_call | solution.py:403
  (1 shorter events, 0.0 us)
Async XLA Ops:
  2.8 8.8 %collective-permute-start = (f32[16,128]{1,0:T(8,128)S(1)}, f32[16,128]{1,0:T(8,128)S(1)}, u32[]{:S(2)}, u32[]{:S(2)}) collective-permute-start(f32[16,128]{1,0:T(8,128)S(1)} %get-tuple-element.56), channel_id=1, source_target_pairs={{0,24},{8,16},{16,8},{24,0},{1,25},{9,17},{17,9},{25,1},{2,26},{10... | collective-permute-start | bytes 24584 | tf_op jit(solution)/shard_map/ppermute | solution.py:444
  5.2 6.5 %collective-permute-start.2 = (f32[16,128]{1,0:T(8,128)S(1)}, f32[16,128]{1,0:T(8,128)S(1)}, u32[]{:S(2)}, u32[]{:S(2)}) collective-permute-start(f32[16,128]{1,0:T(8,128)S(1)} %get-tuple-element.58), channel_id=1, source_target_pairs={{0,3},{1,2},{2,1},{3,0},{4,7},{5,6},{6,5},{7,4},{8,11},{9,10},{10,... | collective-permute-start | bytes 24584 | tf_op jit(solution)/shard_map/ppermute | solution.py:444
  8.8 3.7 %collective-permute-start.3 = (f32[16,128]{1,0:T(8,128)S(1)}, f32[16,128]{1,0:T(8,128)S(1)}, u32[]{:S(2)}, u32[]{:S(2)}) collective-permute-start(f32[16,128]{1,0:T(8,128)S(1)} %get-tuple-element.59), channel_id=1, source_target_pairs={{0,1},{1,0},{2,3},{3,2},{4,5},{5,4},{6,7},{7,6},{8,9},{9,8},{10,11... | collective-permute-start | bytes 24584 | tf_op jit(solution)/shard_map/ppermute | solution.py:444
  8.8 4.0 %collective-permute-start.4 = (f32[16,128]{1,0:T(8,128)S(1)}, f32[16,128]{1,0:T(8,128)S(1)}, u32[]{:S(2)}, u32[]{:S(2)}) collective-permute-start(f32[16,128]{1,0:T(8,128)S(1)} %get-tuple-element.62), channel_id=1, source_target_pairs={{0,4},{4,0},{1,5},{5,1},{2,6},{6,2},{3,7},{7,3},{8,12},{12,8},{9,1... | collective-permute-start | bytes 24584 | tf_op jit(solution)/shard_map/ppermute | solution.py:444
  10.4 1.2 %collective-permute-start.1 = (f32[8,128]{1,0:T(8,128)S(1)}, f32[8,128]{1,0:T(8,128)S(1)}, u32[]{:S(2)}, u32[]{:S(2)}) collective-permute-start(f32[8,128]{1,0:T(8,128)S(1)} %shard_map.70), channel_id=1, source_target_pairs={{0,8},{8,0},{16,24},{24,16},{1,9},{9,1},{17,25},{25,17},{2,10},{10... | collective-permute-start | bytes 12296 | tf_op jit(solution)/shard_map/ppermute | solution.py:444
  13.0 4.6 %collective-permute-start.5 = (f32[16,128]{1,0:T(8,128)S(1)}, f32[16,128]{1,0:T(8,128)S(1)}, u32[]{:S(2)}, u32[]{:S(2)}) collective-permute-start(f32[16,128]{1,0:T(8,128)S(1)} %get-tuple-element.66), channel_id=1, source_target_pairs={{0,24},{8,16},{16,8},{24,0},{1,25},{9,17},{17,9},{25,1},{2,26},{10... | collective-permute-start | bytes 24584 | tf_op jit(solution)/shard_map/ppermute | solution.py:444
  13.0 5.5 %collective-permute-start.7 = (f32[16,128]{1,0:T(8,128)S(1)}, f32[16,128]{1,0:T(8,128)S(1)}, u32[]{:S(2)}, u32[]{:S(2)}) collective-permute-start(f32[16,128]{1,0:T(8,128)S(1)} %get-tuple-element.67), channel_id=1, source_target_pairs={{0,3},{1,2},{2,1},{3,0},{4,7},{5,6},{6,5},{7,4},{8,11},{9,10},{10,... | collective-permute-start | bytes 24584 | tf_op jit(solution)/shard_map/ppermute | solution.py:444
  14.9 3.7 %collective-permute-start.8 = (f32[16,128]{1,0:T(8,128)S(1)}, f32[16,128]{1,0:T(8,128)S(1)}, u32[]{:S(2)}, u32[]{:S(2)}) collective-permute-start(f32[16,128]{1,0:T(8,128)S(1)} %get-tuple-element.68), channel_id=1, source_target_pairs={{0,1},{1,0},{2,3},{3,2},{4,5},{5,4},{6,7},{7,6},{8,9},{9,8},{10,11... | collective-permute-start | bytes 24584 | tf_op jit(solution)/shard_map/ppermute | solution.py:444
  14.9 4.1 %collective-permute-start.9 = (f32[16,128]{1,0:T(8,128)S(1)}, f32[16,128]{1,0:T(8,128)S(1)}, u32[]{:S(2)}, u32[]{:S(2)}) collective-permute-start(f32[16,128]{1,0:T(8,128)S(1)} %get-tuple-element.71), channel_id=1, source_target_pairs={{0,4},{4,0},{1,5},{5,1},{2,6},{6,2},{3,7},{7,3},{8,12},{12,8},{9,1... | collective-permute-start | bytes 24584 | tf_op jit(solution)/shard_map/ppermute | solution.py:444
  16.5 1.2 %collective-permute-start.6 = (f32[8,128]{1,0:T(8,128)S(1)}, f32[8,128]{1,0:T(8,128)S(1)}, u32[]{:S(2)}, u32[]{:S(2)}) collective-permute-start(f32[8,128]{1,0:T(8,128)S(1)} %shard_map.76), channel_id=1, source_target_pairs={{0,8},{8,0},{16,24},{24,16},{1,9},{9,1},{17,25},{25,17},{2,10},{10... | collective-permute-start | bytes 12296 | tf_op jit(solution)/shard_map/ppermute | solution.py:444
  19.2 5.6 %collective-permute-start.10 = (f32[16,128]{1,0:T(8,128)S(1)}, f32[16,128]{1,0:T(8,128)S(1)}, u32[]{:S(2)}, u32[]{:S(2)}) collective-permute-start(f32[16,128]{1,0:T(8,128)S(1)} %get-tuple-element.75), channel_id=1, source_target_pairs={{0,24},{8,16},{16,8},{24,0},{1,25},{9,17},{17,9},{25,1},{2,26},{10... | collective-permute-start | bytes 24584 | tf_op jit(solution)/shard_map/ppermute | solution.py:444
  19.8 5.5 %collective-permute-start.12 = (f32[16,128]{1,0:T(8,128)S(1)}, f32[16,128]{1,0:T(8,128)S(1)}, u32[]{:S(2)}, u32[]{:S(2)}) collective-permute-start(f32[16,128]{1,0:T(8,128)S(1)} %get-tuple-element.76), channel_id=1, source_target_pairs={{0,3},{1,2},{2,1},{3,0},{4,7},{5,6},{6,5},{7,4},{8,11},{9,10},{10,... | collective-permute-start | bytes 24584 | tf_op jit(solution)/shard_map/ppermute | solution.py:444
  22.0 3.7 %collective-permute-start.13 = (f32[16,128]{1,0:T(8,128)S(1)}, f32[16,128]{1,0:T(8,128)S(1)}, u32[]{:S(2)}, u32[]{:S(2)}) collective-permute-start(f32[16,128]{1,0:T(8,128)S(1)} %get-tuple-element.77), channel_id=1, source_target_pairs={{0,1},{1,0},{2,3},{3,2},{4,5},{5,4},{6,7},{7,6},{8,9},{9,8},{10,11... | collective-permute-start | bytes 24584 | tf_op jit(solution)/shard_map/ppermute | solution.py:444
  22.3 3.7 %collective-permute-start.14 = (f32[16,128]{1,0:T(8,128)S(1)}, f32[16,128]{1,0:T(8,128)S(1)}, u32[]{:S(2)}, u32[]{:S(2)}) collective-permute-start(f32[16,128]{1,0:T(8,128)S(1)} %get-tuple-element.80), channel_id=1, source_target_pairs={{0,4},{4,0},{1,5},{5,1},{2,6},{6,2},{3,7},{7,3},{8,12},{12,8},{9,1... | collective-permute-start | bytes 24584 | tf_op jit(solution)/shard_map/ppermute | solution.py:444
  23.6 1.2 %collective-permute-start.11 = (f32[8,128]{1,0:T(8,128)S(1)}, f32[8,128]{1,0:T(8,128)S(1)}, u32[]{:S(2)}, u32[]{:S(2)}) collective-permute-start(f32[8,128]{1,0:T(8,128)S(1)} %shard_map.81), channel_id=1, source_target_pairs={{0,8},{8,0},{16,24},{24,16},{1,9},{9,1},{17,25},{25,17},{2,10},{10... | collective-permute-start | bytes 12296 | tf_op jit(solution)/shard_map/ppermute | solution.py:444
  26.2 5.1 %collective-permute-start.15 = (f32[16,128]{1,0:T(8,128)S(1)}, f32[16,128]{1,0:T(8,128)S(1)}, u32[]{:S(2)}, u32[]{:S(2)}) collective-permute-start(f32[16,128]{1,0:T(8,128)S(1)} %get-tuple-element.84), channel_id=1, source_target_pairs={{0,24},{8,16},{16,8},{24,0},{1,25},{9,17},{17,9},{25,1},{2,26},{10... | collective-permute-start | bytes 24584 | tf_op jit(solution)/shard_map/ppermute | solution.py:444
  26.2 5.6 %collective-permute-start.17 = (f32[16,128]{1,0:T(8,128)S(1)}, f32[16,128]{1,0:T(8,128)S(1)}, u32[]{:S(2)}, u32[]{:S(2)}) collective-permute-start(f32[16,128]{1,0:T(8,128)S(1)} %get-tuple-element.85), channel_id=1, source_target_pairs={{0,3},{1,2},{2,1},{3,0},{4,7},{5,6},{6,5},{7,4},{8,11},{9,10},{10,... | collective-permute-start | bytes 24584 | tf_op jit(solution)/shard_map/ppermute | solution.py:444
  28.2 3.7 %collective-permute-start.18 = (f32[16,128]{1,0:T(8,128)S(1)}, f32[16,128]{1,0:T(8,128)S(1)}, u32[]{:S(2)}, u32[]{:S(2)}) collective-permute-start(f32[16,128]{1,0:T(8,128)S(1)} %get-tuple-element.86), channel_id=1, source_target_pairs={{0,1},{1,0},{2,3},{3,2},{4,5},{5,4},{6,7},{7,6},{8,9},{9,8},{10,11... | collective-permute-start | bytes 24584 | tf_op jit(solution)/shard_map/ppermute | solution.py:444
  28.6 3.7 %collective-permute-start.19 = (f32[16,128]{1,0:T(8,128)S(1)}, f32[16,128]{1,0:T(8,128)S(1)}, u32[]{:S(2)}, u32[]{:S(2)}) collective-permute-start(f32[16,128]{1,0:T(8,128)S(1)} %get-tuple-element.87), channel_id=1, source_target_pairs={{0,4},{4,0},{1,5},{5,1},{2,6},{6,2},{3,7},{7,3},{8,12},{12,8},{9,1... | collective-permute-start | bytes 24584 | tf_op jit(solution)/shard_map/ppermute | solution.py:444
  30.1 1.2 %collective-permute-start.16 = (f32[8,128]{1,0:T(8,128)S(1)}, f32[8,128]{1,0:T(8,128)S(1)}, u32[]{:S(2)}, u32[]{:S(2)}) collective-permute-start(f32[8,128]{1,0:T(8,128)S(1)} %shard_map.86), channel_id=1, source_target_pairs={{0,8},{8,0},{16,24},{24,16},{1,9},{9,1},{17,25},{25,17},{2,10},{10... | collective-permute-start | bytes 12296 | tf_op jit(solution)/shard_map/ppermute | solution.py:444

commit v9 on v8

--- a/solution.py
+++ b/solution.py
@@ -286,7 +286,15 @@
     basis = [ref[...] for ref in refs[:-1]]
     left = [basis[i] for i in range(S) for _ in range(i + 1)]
     right = [basis[j] for i in range(S) for j in range(i + 1)]
-    refs[-1][...] = jnp.concatenate(gram_rows(left, right), axis=0)
+    refs[-1][...] = jnp.broadcast_to(in_lanes(gram_rows(left, right), 0), refs[-1].shape)
+
+
+def in_lanes(lines, first):
+    stacked = jnp.concatenate(lines, axis=0)
+    each = jnp.sum(stacked, axis=1, keepdims=True)
+    lane = lax.broadcasted_iota(jnp.int32, stacked.shape, 1)
+    row = lax.broadcasted_iota(jnp.int32, stacked.shape, 0)
+    return jnp.sum(jnp.where(lane == row + first, each, 0.0), axis=0, keepdims=True)
 
 
 def early_kernel(ph, th, th_n, names, flags_ref, local_ref, conduct_ref, turned_ref, *rest):
@@ -316,7 +324,7 @@
     pack_faces(d_ref, dict(zip(names, sent)), flags_ref, ph, th)
 
 
-def last_kernel(ph, th, names, flags_ref, local_ref, conduct_ref, partial_ref, *rest):
+def last_kernel(ph, th, names, first, flags_ref, local_ref, conduct_ref, partial_ref, *rest):
     older, taken, (next_ref, gram_ref) = rest[:S], rest[S : S + len(names)], rest[S + len(names) :]
     taken = dict(zip(names, taken))
     take_azimuthal(next_ref, local_ref, conduct_ref, taken, flags_ref, ph)
@@ -327,11 +335,7 @@
         next_ref[at, :] = next_ref[at, :] - conduct_ref[at, :] * side
     final = next_ref[...]
     basis = [ref[...] for ref in older] + [final]
-    stacked = jnp.concatenate([partial_ref[...]] + gram_rows([final] * (S + 1), basis), axis=0)
-    each = jnp.sum(stacked, axis=1, keepdims=True)
-    lane = lax.broadcasted_iota(jnp.int32, stacked.shape, 1)
-    row = lax.broadcasted_iota(jnp.int32, stacked.shape, 0)
-    line = jnp.sum(jnp.where(lane == row, each, 0.0), axis=0, keepdims=True)
+    line = partial_ref[0:1, :] + in_lanes(gram_rows([final] * (S + 1), basis), first)
     gram_ref[...] = jnp.broadcast_to(line, gram_ref.shape)
 
 
@@ -500,9 +504,9 @@
             directions.append(direction)
     partial_rows = S * (S + 1) // 2
     partial_rows += -partial_rows % 8
-    (partial,) = call(gram_kernel, [shape(partial_rows)], [], *krylov)
+    (partial,) = call(gram_kernel, [shape(GROUP)], [], *krylov)
     following, gram = call(
-        functools.partial(last_kernel, ph, th, early_names + late_names),
+        functools.partial(last_kernel, ph, th, early_names + late_names, partial_rows),
         [whole, shape(row_n * th_n * ph_n)],
         [],
         flags, beside, conducts, partial, *krylov, *of(early_names + late_names),

time: 43.9 us -> 43.9 us (level)
  no operation moved by 1% of the time
where the time goes in v9:
time: 43.9 us; the launch traced here: 43.7 us
  starting transfers between devices  19.5 us (44%)
  blocking collectives  10.4 us (24%)
  Pallas kernels  7.14 us (16%)
  waiting for transfers between devices  5.93 us (14%)
  between operations  0.73 us (2%)
    ppermute x20, starting transfers between devices, exchange(): lax.ppermute(sent[name], axis, plans[side](lax.axis_size(axis)))  19.5 us
    all_to_all x1, blocking collectives, local(): gram = lax.all_to_all(gram, ('row', 'th', 'ph'), 0, 0, tiled=True)  10.4 us
    pallas_call x23, Pallas kernels, call(): pl.pallas_call(kernel, out_shape=outs, in_specs=[spec(a) for a in args],...  7.14 us
    ppermute x20, waiting for transfers between devices, exchange(): lax.ppermute(sent[name], axis, plans[side](lax.axis_size(axis)))  5.93 us
  transfers between devices with their start and end apart: 20, of which 13 were waited for; matrix products, arithmetic and copies ran while one was open for 0% of the time, Pallas kernels for 8%

profile of v9, /device:TPU:0, one launch (start us, length us, event | category | flops | bytes accessed | tf_op | source)
XLA Modules:
  0.0 43.7 jit_solution(8900560644363205200)
XLA Ops:
  0.6 2.1 %shard_map.68 = (f32[8,128]{1,0:T(8,128)S(1)}, f32[64,128]{1,0:T(8,128)S(1)}, f32[64,128]{1,0:T(8,128)S(1)}, f32[64,128]{1,0:T(8,128)S(1)}, f32[8,128]{1,0:T(8,1...) custom-call(f32[8,4,4,64]{3,2,1,0:T(4,128)} %right_ref.1, ...), custom_call_target="tpu_custom_call" | custom-call | tf_op jit(solution)/shard_map/pallas_call | solution.py:407
  2.8 2.4 %collective-permute-start = (f32[16,128]{1,0:T(8,128)S(1)}, f32[16,128]{1,0:T(8,128)S(1)}, u32[]{:S(2)}, u32[]{:S(2)}) collective-permute-start(f32[16,128]{1,0:T(8,128)S(1)} %get-tuple-element.56), channel_id=1, source_target_pairs={{0,24},{8,16},{16,8},{24,0},{1,25},{9,17},{17,9},{25,1},{2,26},{10... | collective-permute-start | bytes 24584 | tf_op jit(solution)/shard_map/ppermute | solution.py:448
  5.2 3.6 %collective-permute-start.2 = (f32[16,128]{1,0:T(8,128)S(1)}, f32[16,128]{1,0:T(8,128)S(1)}, u32[]{:S(2)}, u32[]{:S(2)}) collective-permute-start(f32[16,128]{1,0:T(8,128)S(1)} %get-tuple-element.58), channel_id=1, source_target_pairs={{0,3},{1,2},{2,1},{3,0},{4,7},{5,6},{6,5},{7,4},{8,11},{9,10},{10,... | collective-permute-start | bytes 24584 | tf_op jit(solution)/shard_map/ppermute | solution.py:448
  8.8 0.0 collective-permute-start.3
  8.8 1.5 %collective-permute-start.4 = (f32[16,128]{1,0:T(8,128)S(1)}, f32[16,128]{1,0:T(8,128)S(1)}, u32[]{:S(2)}, u32[]{:S(2)}) collective-permute-start(f32[16,128]{1,0:T(8,128)S(1)} %get-tuple-element.62), channel_id=1, source_target_pairs={{0,4},{4,0},{1,5},{5,1},{2,6},{6,2},{3,7},{7,3},{8,12},{12,8},{9,1... | collective-permute-start | bytes 24584 | tf_op jit(solution)/shard_map/ppermute | solution.py:448
  10.4 0.1 shard_map.70
  10.4 0.2 collective-permute-start.1
  10.6 0.6 %shard_map.72.turned_ref = bf16[64,128,128]{2,1,0:T(8,128)(2,1)S(1)} custom-call(bf16[4,4,4,128,128]{4,3,2,1,0:T(8,128)(2,1)S(1)} %get-tuple-element.57.held_ref), custom_call_target="tpu_custom_call" | custom-call | tf_op jit(solution)/shard_map/pallas_call | solution.py:407
  11.2 0.2 shard_map.69.local_ref
  11.3 0.2 collective-permute-done.1.rest_1_
  11.6 0.0 collective-permute-done.rest_0_
  11.6 0.1 shard_map.71.local_ref
  11.7 0.0 collective-permute-done.2.rest_0_
  11.7 0.8 %collective-permute-done.3.rest_1_ = f32[16,128]{1,0:T(8,128)S(1)} collective-permute-done((f32[16,128]{1,0:T(8,128)S(1)}, f32[16,128]{1,0:T(8,128)S(1)}, u32[]{:S(2)}, u32[]{:S(2)}) %collective-permute-start.3) | collective-permute-done | bytes 8224 | tf_op jit(solution)/shard_map/ppermute | solution.py:448
  12.5 0.3 shard_map.73
  12.8 0.0 collective-permute-done.4.rest_0_
  12.8 0.2 shard_map.74
  13.0 0.0 collective-permute-start.5
  13.0 1.9 %collective-permute-start.7 = (f32[16,128]{1,0:T(8,128)S(1)}, f32[16,128]{1,0:T(8,128)S(1)}, u32[]{:S(2)}, u32[]{:S(2)}) collective-permute-start(f32[16,128]{1,0:T(8,128)S(1)} %get-tuple-element.67), channel_id=1, source_target_pairs={{0,3},{1,2},{2,1},{3,0},{4,7},{5,6},{6,5},{7,4},{8,11},{9,10},{10,... | collective-permute-start | bytes 24584 | tf_op jit(solution)/shard_map/ppermute | solution.py:448
  14.9 0.0 collective-permute-start.8
  14.9 1.5 %collective-permute-start.9 = (f32[16,128]{1,0:T(8,128)S(1)}, f32[16,128]{1,0:T(8,128)S(1)}, u32[]{:S(2)}, u32[]{:S(2)}) collective-permute-start(f32[16,128]{1,0:T(8,128)S(1)} %get-tuple-element.71), channel_id=1, source_target_pairs={{0,4},{4,0},{1,5},{5,1},{2,6},{6,2},{3,7},{7,3},{8,12},{12,8},{9,1... | collective-permute-start | bytes 24584 | tf_op jit(solution)/shard_map/ppermute | solution.py:448
  16.4 0.1 shard_map.76
  16.5 0.2 collective-permute-start.6
  16.6 0.3 shard_map.75
  17.0 0.7 %collective-permute-done.6.rest_1_ = f32[8,128]{1,0:T(8,128)S(1)} collective-permute-done((f32[8,128]{1,0:T(8,128)S(1)}, f32[8,128]{1,0:T(8,128)S(1)}, u32[]{:S(2)}, u32[]{:S(2)}) %collective-permute-start.6) | collective-permute-done | bytes 4128 | tf_op jit(solution)/shard_map/ppermute | solution.py:448
  17.7 0.0 collective-permute-done.5.rest_0_
  17.7 0.1 shard_map.77.local_ref
  17.7 0.8 %collective-permute-done.7.rest_0_ = f32[16,128]{1,0:T(8,128)S(1)} collective-permute-done((f32[16,128]{1,0:T(8,128)S(1)}, f32[16,128]{1,0:T(8,128)S(1)}, u32[]{:S(2)}, u32[]{:S(2)}) %collective-permute-start.7) | collective-permute-done | bytes 8224 | tf_op jit(solution)/shard_map/ppermute | solution.py:448
  18.5 0.1 collective-permute-done.8.rest_1_
  18.6 0.3 shard_map.78
  18.9 0.0 collective-permute-done.9.rest_0_
  19.0 0.2 shard_map.79
  19.2 0.6 %collective-permute-start.10 = (f32[16,128]{1,0:T(8,128)S(1)}, f32[16,128]{1,0:T(8,128)S(1)}, u32[]{:S(2)}, u32[]{:S(2)}) collective-permute-start(f32[16,128]{1,0:T(8,128)S(1)} %get-tuple-element.75), channel_id=1, source_target_pairs={{0,24},{8,16},{16,8},{24,0},{1,25},{9,17},{17,9},{25,1},{2,26},{10... | collective-permute-start | bytes 24584 | tf_op jit(solution)/shard_map/ppermute | solution.py:448
  19.8 2.2 %collective-permute-start.12 = (f32[16,128]{1,0:T(8,128)S(1)}, f32[16,128]{1,0:T(8,128)S(1)}, u32[]{:S(2)}, u32[]{:S(2)}) collective-permute-start(f32[16,128]{1,0:T(8,128)S(1)} %get-tuple-element.76), channel_id=1, source_target_pairs={{0,3},{1,2},{2,1},{3,0},{4,7},{5,6},{6,5},{7,4},{8,11},{9,10},{10,... | collective-permute-start | bytes 24584 | tf_op jit(solution)/shard_map/ppermute | solution.py:448
  22.0 0.4 collective-permute-start.13
  22.3 1.2 %collective-permute-start.14 = (f32[16,128]{1,0:T(8,128)S(1)}, f32[16,128]{1,0:T(8,128)S(1)}, u32[]{:S(2)}, u32[]{:S(2)}) collective-permute-start(f32[16,128]{1,0:T(8,128)S(1)} %get-tuple-element.80), channel_id=1, source_target_pairs={{0,4},{4,0},{1,5},{5,1},{2,6},{6,2},{3,7},{7,3},{8,12},{12,8},{9,1... | collective-permute-start | bytes 24584 | tf_op jit(solution)/shard_map/ppermute | solution.py:448
  23.5 0.1 shard_map.81
  23.6 0.1 collective-permute-start.11
  23.6 0.3 shard_map.80
  23.9 0.8 %collective-permute-done.11.rest_1_ = f32[8,128]{1,0:T(8,128)S(1)} collective-permute-done((f32[8,128]{1,0:T(8,128)S(1)}, f32[8,128]{1,0:T(8,128)S(1)}, u32[]{:S(2)}, u32[]{:S(2)}) %collective-permute-start.11) | collective-permute-done | bytes 4128 | tf_op jit(solution)/shard_map/ppermute | solution.py:448
  24.7 0.0 collective-permute-done.10.rest_0_
  24.7 0.1 shard_map.82.local_ref
  24.8 0.4 collective-permute-done.12.rest_0_
  25.2 0.4 collective-permute-done.13.rest_1_
  25.6 0.3 shard_map.83
  25.9 0.1 collective-permute-done.14.rest_0_
  26.0 0.2 shard_map.84
  26.2 0.0 collective-permute-start.15
  26.2 1.9 %collective-permute-start.17 = (f32[16,128]{1,0:T(8,128)S(1)}, f32[16,128]{1,0:T(8,128)S(1)}, u32[]{:S(2)}, u32[]{:S(2)}) collective-permute-start(f32[16,128]{1,0:T(8,128)S(1)} %get-tuple-element.85), channel_id=1, source_target_pairs={{0,3},{1,2},{2,1},{3,0},{4,7},{5,6},{6,5},{7,4},{8,11},{9,10},{10,... | collective-permute-start | bytes 24584 | tf_op jit(solution)/shard_map/ppermute | solution.py:448
  28.2 0.5 %collective-permute-start.18 = (f32[16,128]{1,0:T(8,128)S(1)}, f32[16,128]{1,0:T(8,128)S(1)}, u32[]{:S(2)}, u32[]{:S(2)}) collective-permute-start(f32[16,128]{1,0:T(8,128)S(1)} %get-tuple-element.86), channel_id=1, source_target_pairs={{0,1},{1,0},{2,3},{3,2},{4,5},{5,4},{6,7},{7,6},{8,9},{9,8},{10,11... | collective-permute-start | bytes 24584 | tf_op jit(solution)/shard_map/ppermute | solution.py:448
  28.6 1.4 %collective-permute-start.19 = (f32[16,128]{1,0:T(8,128)S(1)}, f32[16,128]{1,0:T(8,128)S(1)}, u32[]{:S(2)}, u32[]{:S(2)}) collective-permute-start(f32[16,128]{1,0:T(8,128)S(1)} %get-tuple-element.87), channel_id=1, source_target_pairs={{0,4},{4,0},{1,5},{5,1},{2,6},{6,2},{3,7},{7,3},{8,12},{12,8},{9,1... | collective-permute-start | bytes 24584 | tf_op jit(solution)/shard_map/ppermute | solution.py:448
  30.0 0.1 shard_map.86
  30.1 0.0 collective-permute-start.16
  30.1 0.1 shard_map.88.partial_ref
  30.3 0.3 shard_map.85
  30.6 0.7 %collective-permute-done.16.rest_1_ = f32[8,128]{1,0:T(8,128)S(1)} collective-permute-done((f32[8,128]{1,0:T(8,128)S(1)}, f32[8,128]{1,0:T(8,128)S(1)}, u32[]{:S(2)}, u32[]{:S(2)}) %collective-permute-start.16) | collective-permute-done | bytes 4128 | tf_op jit(solution)/shard_map/ppermute | solution.py:448
  31.3 0.0 collective-permute-done.15.rest_0_
  31.3 0.1 shard_map.87.local_ref
  31.4 0.4 collective-permute-done.17.rest_4_
  31.8 0.1 collective-permute-done.18.rest_5_
  31.9 0.4 collective-permute-done.19.rest_6_
  32.3 0.1 shard_map.89
  32.4 10.4 %all_to_all.11 = f32[32,1,128]{2,1,0:T(1,128)S(1)} all-to-all(f32[32,1,128]{2,1,0:T(1,128)S(1)} %bitcast.5), channel_id=1, replica_groups=mesh['row'=4,'th'=2,'ph'=4] {'row','th','ph'}, dimensions={0} | all-to-all | bytes 32768 | tf_op jit(solution)/shard_map/all_to_all | solution.py:515
  42.9 0.9 %shard_map.90 = (f32[8,4,4,64]{3,2,1,0:T(4,128)}, f32[8,4,4,64]{3,2,1,0:T(4,128)}) custom-call(f32[32,128]{1,0:T(8,128)S(1)} %bitcast.4, f32[64,128]{1,0:T(8,128)S(1)} %get-tuple-element.89.final_ref, f32[8,4,4,64]{3,2,1,0:T(4,128)S(1)} %get-tuple-element.90.refs_0_, f32[8,4,4,64]{3,2,1,0:T(4,128)S(1)} %get-tuple-element.91.refs_1_, ...), custom_call_target="tpu_custom_call" | custom-call | tf_op jit(solution)/shard_map/pallas_call | solution.py:407
Async XLA Ops:
  2.8 8.8 %collective-permute-start = (f32[16,128]{1,0:T(8,128)S(1)}, f32[16,128]{1,0:T(8,128)S(1)}, u32[]{:S(2)}, u32[]{:S(2)}) collective-permute-start(f32[16,128]{1,0:T(8,128)S(1)} %get-tuple-element.56), channel_id=1, source_target_pairs={{0,24},{8,16},{16,8},{24,0},{1,25},{9,17},{17,9},{25,1},{2,26},{10... | collective-permute-start | bytes 24584 | tf_op jit(solution)/shard_map/ppermute | solution.py:448
  5.2 6.5 %collective-permute-start.2 = (f32[16,128]{1,0:T(8,128)S(1)}, f32[16,128]{1,0:T(8,128)S(1)}, u32[]{:S(2)}, u32[]{:S(2)}) collective-permute-start(f32[16,128]{1,0:T(8,128)S(1)} %get-tuple-element.58), channel_id=1, source_target_pairs={{0,3},{1,2},{2,1},{3,0},{4,7},{5,6},{6,5},{7,4},{8,11},{9,10},{10,... | collective-permute-start | bytes 24584 | tf_op jit(solution)/shard_map/ppermute | solution.py:448
  8.8 3.7 %collective-permute-start.3 = (f32[16,128]{1,0:T(8,128)S(1)}, f32[16,128]{1,0:T(8,128)S(1)}, u32[]{:S(2)}, u32[]{:S(2)}) collective-permute-start(f32[16,128]{1,0:T(8,128)S(1)} %get-tuple-element.59), channel_id=1, source_target_pairs={{0,1},{1,0},{2,3},{3,2},{4,5},{5,4},{6,7},{7,6},{8,9},{9,8},{10,11... | collective-permute-start | bytes 24584 | tf_op jit(solution)/shard_map/ppermute | solution.py:448
  8.8 4.0 %collective-permute-start.4 = (f32[16,128]{1,0:T(8,128)S(1)}, f32[16,128]{1,0:T(8,128)S(1)}, u32[]{:S(2)}, u32[]{:S(2)}) collective-permute-start(f32[16,128]{1,0:T(8,128)S(1)} %get-tuple-element.62), channel_id=1, source_target_pairs={{0,4},{4,0},{1,5},{5,1},{2,6},{6,2},{3,7},{7,3},{8,12},{12,8},{9,1... | collective-permute-start | bytes 24584 | tf_op jit(solution)/shard_map/ppermute | solution.py:448
  10.4 1.2 %collective-permute-start.1 = (f32[8,128]{1,0:T(8,128)S(1)}, f32[8,128]{1,0:T(8,128)S(1)}, u32[]{:S(2)}, u32[]{:S(2)}) collective-permute-start(f32[8,128]{1,0:T(8,128)S(1)} %shard_map.70), channel_id=1, source_target_pairs={{0,8},{8,0},{16,24},{24,16},{1,9},{9,1},{17,25},{25,17},{2,10},{10... | collective-permute-start | bytes 12296 | tf_op jit(solution)/shard_map/ppermute | solution.py:448
  13.0 4.6 %collective-permute-start.5 = (f32[16,128]{1,0:T(8,128)S(1)}, f32[16,128]{1,0:T(8,128)S(1)}, u32[]{:S(2)}, u32[]{:S(2)}) collective-permute-start(f32[16,128]{1,0:T(8,128)S(1)} %get-tuple-element.66), channel_id=1, source_target_pairs={{0,24},{8,16},{16,8},{24,0},{1,25},{9,17},{17,9},{25,1},{2,26},{10... | collective-permute-start | bytes 24584 | tf_op jit(solution)/shard_map/ppermute | solution.py:448
  13.0 5.5 %collective-permute-start.7 = (f32[16,128]{1,0:T(8,128)S(1)}, f32[16,128]{1,0:T(8,128)S(1)}, u32[]{:S(2)}, u32[]{:S(2)}) collective-permute-start(f32[16,128]{1,0:T(8,128)S(1)} %get-tuple-element.67), channel_id=1, source_target_pairs={{0,3},{1,2},{2,1},{3,0},{4,7},{5,6},{6,5},{7,4},{8,11},{9,10},{10,... | collective-permute-start | bytes 24584 | tf_op jit(solution)/shard_map/ppermute | solution.py:448
  14.9 3.7 %collective-permute-start.8 = (f32[16,128]{1,0:T(8,128)S(1)}, f32[16,128]{1,0:T(8,128)S(1)}, u32[]{:S(2)}, u32[]{:S(2)}) collective-permute-start(f32[16,128]{1,0:T(8,128)S(1)} %get-tuple-element.68), channel_id=1, source_target_pairs={{0,1},{1,0},{2,3},{3,2},{4,5},{5,4},{6,7},{7,6},{8,9},{9,8},{10,11... | collective-permute-start | bytes 24584 | tf_op jit(solution)/shard_map/ppermute | solution.py:448
  14.9 4.1 %collective-permute-start.9 = (f32[16,128]{1,0:T(8,128)S(1)}, f32[16,128]{1,0:T(8,128)S(1)}, u32[]{:S(2)}, u32[]{:S(2)}) collective-permute-start(f32[16,128]{1,0:T(8,128)S(1)} %get-tuple-element.71), channel_id=1, source_target_pairs={{0,4},{4,0},{1,5},{5,1},{2,6},{6,2},{3,7},{7,3},{8,12},{12,8},{9,1... | collective-permute-start | bytes 24584 | tf_op jit(solution)/shard_map/ppermute | solution.py:448
  16.5 1.2 %collective-permute-start.6 = (f32[8,128]{1,0:T(8,128)S(1)}, f32[8,128]{1,0:T(8,128)S(1)}, u32[]{:S(2)}, u32[]{:S(2)}) collective-permute-start(f32[8,128]{1,0:T(8,128)S(1)} %shard_map.76), channel_id=1, source_target_pairs={{0,8},{8,0},{16,24},{24,16},{1,9},{9,1},{17,25},{25,17},{2,10},{10... | collective-permute-start | bytes 12296 | tf_op jit(solution)/shard_map/ppermute | solution.py:448
  19.2 5.6 %collective-permute-start.10 = (f32[16,128]{1,0:T(8,128)S(1)}, f32[16,128]{1,0:T(8,128)S(1)}, u32[]{:S(2)}, u32[]{:S(2)}) collective-permute-start(f32[16,128]{1,0:T(8,128)S(1)} %get-tuple-element.75), channel_id=1, source_target_pairs={{0,24},{8,16},{16,8},{24,0},{1,25},{9,17},{17,9},{25,1},{2,26},{10... | collective-permute-start | bytes 24584 | tf_op jit(solution)/shard_map/ppermute | solution.py:448
  19.8 5.5 %collective-permute-start.12 = (f32[16,128]{1,0:T(8,128)S(1)}, f32[16,128]{1,0:T(8,128)S(1)}, u32[]{:S(2)}, u32[]{:S(2)}) collective-permute-start(f32[16,128]{1,0:T(8,128)S(1)} %get-tuple-element.76), channel_id=1, source_target_pairs={{0,3},{1,2},{2,1},{3,0},{4,7},{5,6},{6,5},{7,4},{8,11},{9,10},{10,... | collective-permute-start | bytes 24584 | tf_op jit(solution)/shard_map/ppermute | solution.py:448
  22.0 3.7 %collective-permute-start.13 = (f32[16,128]{1,0:T(8,128)S(1)}, f32[16,128]{1,0:T(8,128)S(1)}, u32[]{:S(2)}, u32[]{:S(2)}) collective-permute-start(f32[16,128]{1,0:T(8,128)S(1)} %get-tuple-element.77), channel_id=1, source_target_pairs={{0,1},{1,0},{2,3},{3,2},{4,5},{5,4},{6,7},{7,6},{8,9},{9,8},{10,11... | collective-permute-start | bytes 24584 | tf_op jit(solution)/shard_map/ppermute | solution.py:448
  22.3 3.7 %collective-permute-start.14 = (f32[16,128]{1,0:T(8,128)S(1)}, f32[16,128]{1,0:T(8,128)S(1)}, u32[]{:S(2)}, u32[]{:S(2)}) collective-permute-start(f32[16,128]{1,0:T(8,128)S(1)} %get-tuple-element.80), channel_id=1, source_target_pairs={{0,4},{4,0},{1,5},{5,1},{2,6},{6,2},{3,7},{7,3},{8,12},{12,8},{9,1... | collective-permute-start | bytes 24584 | tf_op jit(solution)/shard_map/ppermute | solution.py:448
  23.6 1.2 %collective-permute-start.11 = (f32[8,128]{1,0:T(8,128)S(1)}, f32[8,128]{1,0:T(8,128)S(1)}, u32[]{:S(2)}, u32[]{:S(2)}) collective-permute-start(f32[8,128]{1,0:T(8,128)S(1)} %shard_map.81), channel_id=1, source_target_pairs={{0,8},{8,0},{16,24},{24,16},{1,9},{9,1},{17,25},{25,17},{2,10},{10... | collective-permute-start | bytes 12296 | tf_op jit(solution)/shard_map/ppermute | solution.py:448
  26.2 5.1 %collective-permute-start.15 = (f32[16,128]{1,0:T(8,128)S(1)}, f32[16,128]{1,0:T(8,128)S(1)}, u32[]{:S(2)}, u32[]{:S(2)}) collective-permute-start(f32[16,128]{1,0:T(8,128)S(1)} %get-tuple-element.84), channel_id=1, source_target_pairs={{0,24},{8,16},{16,8},{24,0},{1,25},{9,17},{17,9},{25,1},{2,26},{10... | collective-permute-start | bytes 24584 | tf_op jit(solution)/shard_map/ppermute | solution.py:448
  26.2 5.6 %collective-permute-start.17 = (f32[16,128]{1,0:T(8,128)S(1)}, f32[16,128]{1,0:T(8,128)S(1)}, u32[]{:S(2)}, u32[]{:S(2)}) collective-permute-start(f32[16,128]{1,0:T(8,128)S(1)} %get-tuple-element.85), channel_id=1, source_target_pairs={{0,3},{1,2},{2,1},{3,0},{4,7},{5,6},{6,5},{7,4},{8,11},{9,10},{10,... | collective-permute-start | bytes 24584 | tf_op jit(solution)/shard_map/ppermute | solution.py:448
  28.2 3.7 %collective-permute-start.18 = (f32[16,128]{1,0:T(8,128)S(1)}, f32[16,128]{1,0:T(8,128)S(1)}, u32[]{:S(2)}, u32[]{:S(2)}) collective-permute-start(f32[16,128]{1,0:T(8,128)S(1)} %get-tuple-element.86), channel_id=1, source_target_pairs={{0,1},{1,0},{2,3},{3,2},{4,5},{5,4},{6,7},{7,6},{8,9},{9,8},{10,11... | collective-permute-start | bytes 24584 | tf_op jit(solution)/shard_map/ppermute | solution.py:448
  28.6 3.7 %collective-permute-start.19 = (f32[16,128]{1,0:T(8,128)S(1)}, f32[16,128]{1,0:T(8,128)S(1)}, u32[]{:S(2)}, u32[]{:S(2)}) collective-permute-start(f32[16,128]{1,0:T(8,128)S(1)} %get-tuple-element.87), channel_id=1, source_target_pairs={{0,4},{4,0},{1,5},{5,1},{2,6},{6,2},{3,7},{7,3},{8,12},{12,8},{9,1... | collective-permute-start | bytes 24584 | tf_op jit(solution)/shard_map/ppermute | solution.py:448
  30.1 1.2 %collective-permute-start.16 = (f32[8,128]{1,0:T(8,128)S(1)}, f32[8,128]{1,0:T(8,128)S(1)}, u32[]{:S(2)}, u32[]{:S(2)}) collective-permute-start(f32[8,128]{1,0:T(8,128)S(1)} %shard_map.86), channel_id=1, source_target_pairs={{0,8},{8,0},{16,24},{24,16},{1,9},{9,1},{17,25},{25,17},{2,10},{10... | collective-permute-start | bytes 12296 | tf_op jit(solution)/shard_map/ppermute | solution.py:448

commit v10 on v9

--- a/solution.py
+++ b/solution.py
@@ -421,7 +421,7 @@
     rows = per * nb
     at = {axis: (lax.axis_index(axis), lax.axis_size(axis)) for axis in ("row", "th", "ph")}
     (row_at, row_n), (th_at, th_n), (ph_at, ph_n) = at["row"], at["th"], at["ph"]
-    face_rows = {"ph_high": nb * th, "row_high": per, "ph_low": nb * th, "row_low": per // 2, "th_high": rows // th, "th_low": rows // th}
+    face_rows = {"ph_low": nb * th, "row_high": per, "ph_high": nb * th, "row_low": per // 2, "th_high": rows // th, "th_low": rows // th}
     if row_n == 2:
         face_rows.pop("row_high")
     if th_n == 2:

time: 43.9 us -> 44 us (level)
    all_to_all x1, blocking collectives: 10.4 us -> 10 us  [local(): gram = lax.all_to_all(gram, ('row', 'th', 'ph'), 0, 0, tiled=True)]
  transfers between devices with their start and end apart: 20 -> 20, of which waited for: 13 -> 10; matrix products, arithmetic and copies ran while one was open for 0% -> 0% of each run, Pallas kernels for 8% -> 8%
where the time goes in v10:
time: 44 us; the launch traced here: 43.8 us
  starting transfers between devices  19.6 us (45%)
  blocking collectives  10 us (23%)
  Pallas kernels  7.15 us (16%)
  waiting for transfers between devices  6.27 us (14%)
  between operations  0.76 us (2%)
    ppermute x20, starting transfers between devices, exchange(): lax.ppermute(sent[name], axis, plans[side](lax.axis_size(axis)))  19.6 us
    all_to_all x1, blocking collectives, local(): gram = lax.all_to_all(gram, ('row', 'th', 'ph'), 0, 0, tiled=True)  10 us
    pallas_call x23, Pallas kernels, call(): pl.pallas_call(kernel, out_shape=outs, in_specs=[spec(a) for a in args],...  7.15 us
    ppermute x20, waiting for transfers between devices, exchange(): lax.ppermute(sent[name], axis, plans[side](lax.axis_size(axis)))  6.27 us
  transfers between devices with their start and end apart: 20, of which 10 were waited for; matrix products, arithmetic and copies ran while one was open for 0% of the time, Pallas kernels for 8%

profile of v10, /device:TPU:0, one launch (start us, length us, event | category | flops | bytes accessed | tf_op | source)
XLA Modules:
  0.0 43.8 jit_solution(9838794670296280729)
XLA Ops:
  0.6 2.1 %shard_map.68 = (f32[8,128]{1,0:T(8,128)S(1)}, f32[64,128]{1,0:T(8,128)S(1)}, f32[64,128]{1,0:T(8,128)S(1)}, f32[64,128]{1,0:T(8,128)S(1)}, f32[8,128]{1,0:T(8,1...) custom-call(f32[8,4,4,64]{3,2,1,0:T(4,128)} %right_ref.1, ...), custom_call_target="tpu_custom_call" | custom-call | tf_op jit(solution)/shard_map/pallas_call | solution.py:407
  2.8 2.4 %collective-permute-start = (f32[16,128]{1,0:T(8,128)S(1)}, f32[16,128]{1,0:T(8,128)S(1)}, u32[]{:S(2)}, u32[]{:S(2)}) collective-permute-start(f32[16,128]{1,0:T(8,128)S(1)} %get-tuple-element.56), channel_id=1, source_target_pairs={{0,24},{8,16},{16,8},{24,0},{1,25},{9,17},{17,9},{25,1},{2,26},{10... | collective-permute-start | bytes 24584 | tf_op jit(solution)/shard_map/ppermute | solution.py:448
  5.2 1.6 %collective-permute-start.2 = (f32[16,128]{1,0:T(8,128)S(1)}, f32[16,128]{1,0:T(8,128)S(1)}, u32[]{:S(2)}, u32[]{:S(2)}) collective-permute-start(f32[16,128]{1,0:T(8,128)S(1)} %get-tuple-element.58), channel_id=1, source_target_pairs={{0,1},{1,0},{2,3},{3,2},{4,5},{5,4},{6,7},{7,6},{8,9},{9,8},{10,11... | collective-permute-start | bytes 24584 | tf_op jit(solution)/shard_map/ppermute | solution.py:448
  6.8 2.5 %collective-permute-start.3 = (f32[16,128]{1,0:T(8,128)S(1)}, f32[16,128]{1,0:T(8,128)S(1)}, u32[]{:S(2)}, u32[]{:S(2)}) collective-permute-start(f32[16,128]{1,0:T(8,128)S(1)} %get-tuple-element.59), channel_id=1, source_target_pairs={{0,3},{1,2},{2,1},{3,0},{4,7},{5,6},{6,5},{7,4},{8,11},{9,10},{10,... | collective-permute-start | bytes 24584 | tf_op jit(solution)/shard_map/ppermute | solution.py:448
  9.3 1.5 %collective-permute-start.4 = (f32[16,128]{1,0:T(8,128)S(1)}, f32[16,128]{1,0:T(8,128)S(1)}, u32[]{:S(2)}, u32[]{:S(2)}) collective-permute-start(f32[16,128]{1,0:T(8,128)S(1)} %get-tuple-element.62), channel_id=1, source_target_pairs={{0,4},{4,0},{1,5},{5,1},{2,6},{6,2},{3,7},{7,3},{8,12},{12,8},{9,1... | collective-permute-start | bytes 24584 | tf_op jit(solution)/shard_map/ppermute | solution.py:448
  10.8 0.1 shard_map.70
  10.9 0.0 collective-permute-start.1
  10.9 0.6 %shard_map.72.turned_ref = bf16[64,128,128]{2,1,0:T(8,128)(2,1)S(1)} custom-call(bf16[4,4,4,128,128]{4,3,2,1,0:T(8,128)(2,1)S(1)} %get-tuple-element.57.held_ref), custom_call_target="tpu_custom_call" | custom-call | tf_op jit(solution)/shard_map/pallas_call | solution.py:407
  11.5 0.2 shard_map.69.local_ref
  11.7 0.4 collective-permute-done.1.rest_1_
  12.0 0.0 collective-permute-done.rest_0_
  12.0 0.1 shard_map.71.local_ref
  12.1 0.0 collective-permute-done.2.rest_0_
  12.1 0.1 collective-permute-done.3.rest_1_
  12.3 0.3 shard_map.73
  12.6 0.4 collective-permute-done.4.rest_0_
  12.9 0.2 shard_map.74
  13.1 0.0 collective-permute-start.5
  13.1 0.7 %collective-permute-start.7 = (f32[16,128]{1,0:T(8,128)S(1)}, f32[16,128]{1,0:T(8,128)S(1)}, u32[]{:S(2)}, u32[]{:S(2)}) collective-permute-start(f32[16,128]{1,0:T(8,128)S(1)} %get-tuple-element.67), channel_id=1, source_target_pairs={{0,1},{1,0},{2,3},{3,2},{4,5},{5,4},{6,7},{7,6},{8,9},{9,8},{10,11... | collective-permute-start | bytes 24584 | tf_op jit(solution)/shard_map/ppermute | solution.py:448
  13.9 1.5 %collective-permute-start.8 = (f32[16,128]{1,0:T(8,128)S(1)}, f32[16,128]{1,0:T(8,128)S(1)}, u32[]{:S(2)}, u32[]{:S(2)}) collective-permute-start(f32[16,128]{1,0:T(8,128)S(1)} %get-tuple-element.68), channel_id=1, source_target_pairs={{0,3},{1,2},{2,1},{3,0},{4,7},{5,6},{6,5},{7,4},{8,11},{9,10},{10,... | collective-permute-start | bytes 24584 | tf_op jit(solution)/shard_map/ppermute | solution.py:448
  15.4 1.5 %collective-permute-start.9 = (f32[16,128]{1,0:T(8,128)S(1)}, f32[16,128]{1,0:T(8,128)S(1)}, u32[]{:S(2)}, u32[]{:S(2)}) collective-permute-start(f32[16,128]{1,0:T(8,128)S(1)} %get-tuple-element.71), channel_id=1, source_target_pairs={{0,4},{4,0},{1,5},{5,1},{2,6},{6,2},{3,7},{7,3},{8,12},{12,8},{9,1... | collective-permute-start | bytes 24584 | tf_op jit(solution)/shard_map/ppermute | solution.py:448
  16.9 0.1 shard_map.76
  17.0 0.1 collective-permute-start.6
  17.1 0.3 shard_map.75
  17.4 0.8 %collective-permute-done.6.rest_1_ = f32[8,128]{1,0:T(8,128)S(1)} collective-permute-done((f32[8,128]{1,0:T(8,128)S(1)}, f32[8,128]{1,0:T(8,128)S(1)}, u32[]{:S(2)}, u32[]{:S(2)}) %collective-permute-start.6) | collective-permute-done | bytes 4128 | tf_op jit(solution)/shard_map/ppermute | solution.py:448
  18.2 0.0 collective-permute-done.5.rest_0_
  18.2 0.1 shard_map.77.local_ref
  18.3 0.0 collective-permute-done.7.rest_0_
  18.3 1.1 %collective-permute-done.8.rest_1_ = f32[16,128]{1,0:T(8,128)S(1)} collective-permute-done((f32[16,128]{1,0:T(8,128)S(1)}, f32[16,128]{1,0:T(8,128)S(1)}, u32[]{:S(2)}, u32[]{:S(2)}) %collective-permute-start.8) | collective-permute-done | bytes 8224 | tf_op jit(solution)/shard_map/ppermute | solution.py:448
  19.3 0.3 shard_map.78
  19.7 0.0 collective-permute-done.9.rest_0_
  19.7 0.2 shard_map.79
  19.9 0.3 collective-permute-start.10
  20.1 0.6 %collective-permute-start.12 = (f32[16,128]{1,0:T(8,128)S(1)}, f32[16,128]{1,0:T(8,128)S(1)}, u32[]{:S(2)}, u32[]{:S(2)}) collective-permute-start(f32[16,128]{1,0:T(8,128)S(1)} %get-tuple-element.76), channel_id=1, source_target_pairs={{0,1},{1,0},{2,3},{3,2},{4,5},{5,4},{6,7},{7,6},{8,9},{9,8},{10,11... | collective-permute-start | bytes 24584 | tf_op jit(solution)/shard_map/ppermute | solution.py:448
  20.7 1.7 %collective-permute-start.13 = (f32[16,128]{1,0:T(8,128)S(1)}, f32[16,128]{1,0:T(8,128)S(1)}, u32[]{:S(2)}, u32[]{:S(2)}) collective-permute-start(f32[16,128]{1,0:T(8,128)S(1)} %get-tuple-element.77), channel_id=1, source_target_pairs={{0,3},{1,2},{2,1},{3,0},{4,7},{5,6},{6,5},{7,4},{8,11},{9,10},{10,... | collective-permute-start | bytes 24584 | tf_op jit(solution)/shard_map/ppermute | solution.py:448
  22.4 1.3 %collective-permute-start.14 = (f32[16,128]{1,0:T(8,128)S(1)}, f32[16,128]{1,0:T(8,128)S(1)}, u32[]{:S(2)}, u32[]{:S(2)}) collective-permute-start(f32[16,128]{1,0:T(8,128)S(1)} %get-tuple-element.80), channel_id=1, source_target_pairs={{0,4},{4,0},{1,5},{5,1},{2,6},{6,2},{3,7},{7,3},{8,12},{12,8},{9,1... | collective-permute-start | bytes 24584 | tf_op jit(solution)/shard_map/ppermute | solution.py:448
  23.7 0.1 shard_map.81
  23.8 0.0 collective-permute-start.11
  23.8 0.3 shard_map.80
  24.1 0.9 %collective-permute-done.11.rest_1_ = f32[8,128]{1,0:T(8,128)S(1)} collective-permute-done((f32[8,128]{1,0:T(8,128)S(1)}, f32[8,128]{1,0:T(8,128)S(1)}, u32[]{:S(2)}, u32[]{:S(2)}) %collective-permute-start.11) | collective-permute-done | bytes 4128 | tf_op jit(solution)/shard_map/ppermute | solution.py:448
  24.9 0.0 collective-permute-done.10.rest_0_
  24.9 0.1 shard_map.82.local_ref
  25.0 0.0 collective-permute-done.12.rest_0_
  25.0 1.1 %collective-permute-done.13.rest_1_ = f32[16,128]{1,0:T(8,128)S(1)} collective-permute-done((f32[16,128]{1,0:T(8,128)S(1)}, f32[16,128]{1,0:T(8,128)S(1)}, u32[]{:S(2)}, u32[]{:S(2)}) %collective-permute-start.13) | collective-permute-done | bytes 8224 | tf_op jit(solution)/shard_map/ppermute | solution.py:448
  26.2 0.3 shard_map.83
  26.5 0.0 collective-permute-done.14.rest_0_
  26.5 0.2 shard_map.84
  26.7 0.0 collective-permute-start.15
  26.7 0.3 collective-permute-start.17
  27.0 2.1 %collective-permute-start.18 = (f32[16,128]{1,0:T(8,128)S(1)}, f32[16,128]{1,0:T(8,128)S(1)}, u32[]{:S(2)}, u32[]{:S(2)}) collective-permute-start(f32[16,128]{1,0:T(8,128)S(1)} %get-tuple-element.86), channel_id=1, source_target_pairs={{0,3},{1,2},{2,1},{3,0},{4,7},{5,6},{6,5},{7,4},{8,11},{9,10},{10,... | collective-permute-start | bytes 24584 | tf_op jit(solution)/shard_map/ppermute | solution.py:448
  29.1 1.5 %collective-permute-start.19 = (f32[16,128]{1,0:T(8,128)S(1)}, f32[16,128]{1,0:T(8,128)S(1)}, u32[]{:S(2)}, u32[]{:S(2)}) collective-permute-start(f32[16,128]{1,0:T(8,128)S(1)} %get-tuple-element.87), channel_id=1, source_target_pairs={{0,4},{4,0},{1,5},{5,1},{2,6},{6,2},{3,7},{7,3},{8,12},{12,8},{9,1... | collective-permute-start | bytes 24584 | tf_op jit(solution)/shard_map/ppermute | solution.py:448
  30.6 0.1 shard_map.86
  30.7 0.0 collective-permute-start.16
  30.7 0.1 shard_map.88.partial_ref
  30.8 0.3 shard_map.85
  31.1 0.7 %collective-permute-done.16.rest_1_ = f32[8,128]{1,0:T(8,128)S(1)} collective-permute-done((f32[8,128]{1,0:T(8,128)S(1)}, f32[8,128]{1,0:T(8,128)S(1)}, u32[]{:S(2)}, u32[]{:S(2)}) %collective-permute-start.16) | collective-permute-done | bytes 4128 | tf_op jit(solution)/shard_map/ppermute | solution.py:448
  31.9 0.0 collective-permute-done.15.rest_0_
  31.9 0.1 shard_map.87.local_ref
  31.9 0.0 collective-permute-done.17.rest_4_
  32.0 0.5 %collective-permute-done.18.rest_5_ = f32[16,128]{1,0:T(8,128)S(1)} collective-permute-done((f32[16,128]{1,0:T(8,128)S(1)}, f32[16,128]{1,0:T(8,128)S(1)}, u32[]{:S(2)}, u32[]{:S(2)}) %collective-permute-start.18) | collective-permute-done | bytes 8224 | tf_op jit(solution)/shard_map/ppermute | solution.py:448
  32.5 0.3 collective-permute-done.19.rest_6_
  32.8 0.1 shard_map.89
  32.9 10.0 %all_to_all.11 = f32[32,1,128]{2,1,0:T(1,128)S(1)} all-to-all(f32[32,1,128]{2,1,0:T(1,128)S(1)} %bitcast.5), channel_id=1, replica_groups=mesh['row'=4,'th'=2,'ph'=4] {'row','th','ph'}, dimensions={0} | all-to-all | bytes 32768 | tf_op jit(solution)/shard_map/all_to_all | solution.py:515
  42.9 0.9 %shard_map.90 = (f32[8,4,4,64]{3,2,1,0:T(4,128)}, f32[8,4,4,64]{3,2,1,0:T(4,128)}) custom-call(f32[32,128]{1,0:T(8,128)S(1)} %bitcast.4, f32[64,128]{1,0:T(8,128)S(1)} %get-tuple-element.89.final_ref, f32[8,4,4,64]{3,2,1,0:T(4,128)S(1)} %get-tuple-element.90.refs_0_, f32[8,4,4,64]{3,2,1,0:T(4,128)S(1)} %get-tuple-element.91.refs_1_, ...), custom_call_target="tpu_custom_call" | custom-call | tf_op jit(solution)/shard_map/pallas_call | solution.py:407
Async XLA Ops:
  2.8 9.3 %collective-permute-start = (f32[16,128]{1,0:T(8,128)S(1)}, f32[16,128]{1,0:T(8,128)S(1)}, u32[]{:S(2)}, u32[]{:S(2)}) collective-permute-start(f32[16,128]{1,0:T(8,128)S(1)} %get-tuple-element.56), channel_id=1, source_target_pairs={{0,24},{8,16},{16,8},{24,0},{1,25},{9,17},{17,9},{25,1},{2,26},{10... | collective-permute-start | bytes 24584 | tf_op jit(solution)/shard_map/ppermute | solution.py:448
  5.2 6.9 %collective-permute-start.2 = (f32[16,128]{1,0:T(8,128)S(1)}, f32[16,128]{1,0:T(8,128)S(1)}, u32[]{:S(2)}, u32[]{:S(2)}) collective-permute-start(f32[16,128]{1,0:T(8,128)S(1)} %get-tuple-element.58), channel_id=1, source_target_pairs={{0,1},{1,0},{2,3},{3,2},{4,5},{5,4},{6,7},{7,6},{8,9},{9,8},{10,11... | collective-permute-start | bytes 24584 | tf_op jit(solution)/shard_map/ppermute | solution.py:448
  6.8 5.4 %collective-permute-start.3 = (f32[16,128]{1,0:T(8,128)S(1)}, f32[16,128]{1,0:T(8,128)S(1)}, u32[]{:S(2)}, u32[]{:S(2)}) collective-permute-start(f32[16,128]{1,0:T(8,128)S(1)} %get-tuple-element.59), channel_id=1, source_target_pairs={{0,3},{1,2},{2,1},{3,0},{4,7},{5,6},{6,5},{7,4},{8,11},{9,10},{10,... | collective-permute-start | bytes 24584 | tf_op jit(solution)/shard_map/ppermute | solution.py:448
  9.3 3.7 %collective-permute-start.4 = (f32[16,128]{1,0:T(8,128)S(1)}, f32[16,128]{1,0:T(8,128)S(1)}, u32[]{:S(2)}, u32[]{:S(2)}) collective-permute-start(f32[16,128]{1,0:T(8,128)S(1)} %get-tuple-element.62), channel_id=1, source_target_pairs={{0,4},{4,0},{1,5},{5,1},{2,6},{6,2},{3,7},{7,3},{8,12},{12,8},{9,1... | collective-permute-start | bytes 24584 | tf_op jit(solution)/shard_map/ppermute | solution.py:448
  10.9 1.2 %collective-permute-start.1 = (f32[8,128]{1,0:T(8,128)S(1)}, f32[8,128]{1,0:T(8,128)S(1)}, u32[]{:S(2)}, u32[]{:S(2)}) collective-permute-start(f32[8,128]{1,0:T(8,128)S(1)} %shard_map.70), channel_id=1, source_target_pairs={{0,8},{8,0},{16,24},{24,16},{1,9},{9,1},{17,25},{25,17},{2,10},{10... | collective-permute-start | bytes 12296 | tf_op jit(solution)/shard_map/ppermute | solution.py:448
  13.1 5.1 %collective-permute-start.5 = (f32[16,128]{1,0:T(8,128)S(1)}, f32[16,128]{1,0:T(8,128)S(1)}, u32[]{:S(2)}, u32[]{:S(2)}) collective-permute-start(f32[16,128]{1,0:T(8,128)S(1)} %get-tuple-element.66), channel_id=1, source_target_pairs={{0,24},{8,16},{16,8},{24,0},{1,25},{9,17},{17,9},{25,1},{2,26},{10... | collective-permute-start | bytes 24584 | tf_op jit(solution)/shard_map/ppermute | solution.py:448
  13.1 5.1 %collective-permute-start.7 = (f32[16,128]{1,0:T(8,128)S(1)}, f32[16,128]{1,0:T(8,128)S(1)}, u32[]{:S(2)}, u32[]{:S(2)}) collective-permute-start(f32[16,128]{1,0:T(8,128)S(1)} %get-tuple-element.67), channel_id=1, source_target_pairs={{0,1},{1,0},{2,3},{3,2},{4,5},{5,4},{6,7},{7,6},{8,9},{9,8},{10,11... | collective-permute-start | bytes 24584 | tf_op jit(solution)/shard_map/ppermute | solution.py:448
  13.9 5.4 %collective-permute-start.8 = (f32[16,128]{1,0:T(8,128)S(1)}, f32[16,128]{1,0:T(8,128)S(1)}, u32[]{:S(2)}, u32[]{:S(2)}) collective-permute-start(f32[16,128]{1,0:T(8,128)S(1)} %get-tuple-element.68), channel_id=1, source_target_pairs={{0,3},{1,2},{2,1},{3,0},{4,7},{5,6},{6,5},{7,4},{8,11},{9,10},{10,... | collective-permute-start | bytes 24584 | tf_op jit(solution)/shard_map/ppermute | solution.py:448
  15.4 4.2 %collective-permute-start.9 = (f32[16,128]{1,0:T(8,128)S(1)}, f32[16,128]{1,0:T(8,128)S(1)}, u32[]{:S(2)}, u32[]{:S(2)}) collective-permute-start(f32[16,128]{1,0:T(8,128)S(1)} %get-tuple-element.71), channel_id=1, source_target_pairs={{0,4},{4,0},{1,5},{5,1},{2,6},{6,2},{3,7},{7,3},{8,12},{12,8},{9,1... | collective-permute-start | bytes 24584 | tf_op jit(solution)/shard_map/ppermute | solution.py:448
  17.0 1.2 %collective-permute-start.6 = (f32[8,128]{1,0:T(8,128)S(1)}, f32[8,128]{1,0:T(8,128)S(1)}, u32[]{:S(2)}, u32[]{:S(2)}) collective-permute-start(f32[8,128]{1,0:T(8,128)S(1)} %shard_map.76), channel_id=1, source_target_pairs={{0,8},{8,0},{16,24},{24,16},{1,9},{9,1},{17,25},{25,17},{2,10},{10... | collective-permute-start | bytes 12296 | tf_op jit(solution)/shard_map/ppermute | solution.py:448
  19.9 5.1 %collective-permute-start.10 = (f32[16,128]{1,0:T(8,128)S(1)}, f32[16,128]{1,0:T(8,128)S(1)}, u32[]{:S(2)}, u32[]{:S(2)}) collective-permute-start(f32[16,128]{1,0:T(8,128)S(1)} %get-tuple-element.75), channel_id=1, source_target_pairs={{0,24},{8,16},{16,8},{24,0},{1,25},{9,17},{17,9},{25,1},{2,26},{10... | collective-permute-start | bytes 24584 | tf_op jit(solution)/shard_map/ppermute | solution.py:448
  20.1 4.9 %collective-permute-start.12 = (f32[16,128]{1,0:T(8,128)S(1)}, f32[16,128]{1,0:T(8,128)S(1)}, u32[]{:S(2)}, u32[]{:S(2)}) collective-permute-start(f32[16,128]{1,0:T(8,128)S(1)} %get-tuple-element.76), channel_id=1, source_target_pairs={{0,1},{1,0},{2,3},{3,2},{4,5},{5,4},{6,7},{7,6},{8,9},{9,8},{10,11... | collective-permute-start | bytes 24584 | tf_op jit(solution)/shard_map/ppermute | solution.py:448
  20.7 5.4 %collective-permute-start.13 = (f32[16,128]{1,0:T(8,128)S(1)}, f32[16,128]{1,0:T(8,128)S(1)}, u32[]{:S(2)}, u32[]{:S(2)}) collective-permute-start(f32[16,128]{1,0:T(8,128)S(1)} %get-tuple-element.77), channel_id=1, source_target_pairs={{0,3},{1,2},{2,1},{3,0},{4,7},{5,6},{6,5},{7,4},{8,11},{9,10},{10,... | collective-permute-start | bytes 24584 | tf_op jit(solution)/shard_map/ppermute | solution.py:448
  22.4 4.1 %collective-permute-start.14 = (f32[16,128]{1,0:T(8,128)S(1)}, f32[16,128]{1,0:T(8,128)S(1)}, u32[]{:S(2)}, u32[]{:S(2)}) collective-permute-start(f32[16,128]{1,0:T(8,128)S(1)} %get-tuple-element.80), channel_id=1, source_target_pairs={{0,4},{4,0},{1,5},{5,1},{2,6},{6,2},{3,7},{7,3},{8,12},{12,8},{9,1... | collective-permute-start | bytes 24584 | tf_op jit(solution)/shard_map/ppermute | solution.py:448
  23.8 1.2 %collective-permute-start.11 = (f32[8,128]{1,0:T(8,128)S(1)}, f32[8,128]{1,0:T(8,128)S(1)}, u32[]{:S(2)}, u32[]{:S(2)}) collective-permute-start(f32[8,128]{1,0:T(8,128)S(1)} %shard_map.81), channel_id=1, source_target_pairs={{0,8},{8,0},{16,24},{24,16},{1,9},{9,1},{17,25},{25,17},{2,10},{10... | collective-permute-start | bytes 12296 | tf_op jit(solution)/shard_map/ppermute | solution.py:448
  26.7 5.2 %collective-permute-start.15 = (f32[16,128]{1,0:T(8,128)S(1)}, f32[16,128]{1,0:T(8,128)S(1)}, u32[]{:S(2)}, u32[]{:S(2)}) collective-permute-start(f32[16,128]{1,0:T(8,128)S(1)} %get-tuple-element.84), channel_id=1, source_target_pairs={{0,24},{8,16},{16,8},{24,0},{1,25},{9,17},{17,9},{25,1},{2,26},{10... | collective-permute-start | bytes 24584 | tf_op jit(solution)/shard_map/ppermute | solution.py:448
  26.7 5.2 %collective-permute-start.17 = (f32[16,128]{1,0:T(8,128)S(1)}, f32[16,128]{1,0:T(8,128)S(1)}, u32[]{:S(2)}, u32[]{:S(2)}) collective-permute-start(f32[16,128]{1,0:T(8,128)S(1)} %get-tuple-element.85), channel_id=1, source_target_pairs={{0,1},{1,0},{2,3},{3,2},{4,5},{5,4},{6,7},{7,6},{8,9},{9,8},{10,11... | collective-permute-start | bytes 24584 | tf_op jit(solution)/shard_map/ppermute | solution.py:448
  27.0 5.4 %collective-permute-start.18 = (f32[16,128]{1,0:T(8,128)S(1)}, f32[16,128]{1,0:T(8,128)S(1)}, u32[]{:S(2)}, u32[]{:S(2)}) collective-permute-start(f32[16,128]{1,0:T(8,128)S(1)} %get-tuple-element.86), channel_id=1, source_target_pairs={{0,3},{1,2},{2,1},{3,0},{4,7},{5,6},{6,5},{7,4},{8,11},{9,10},{10,... | collective-permute-start | bytes 24584 | tf_op jit(solution)/shard_map/ppermute | solution.py:448
  29.1 3.7 %collective-permute-start.19 = (f32[16,128]{1,0:T(8,128)S(1)}, f32[16,128]{1,0:T(8,128)S(1)}, u32[]{:S(2)}, u32[]{:S(2)}) collective-permute-start(f32[16,128]{1,0:T(8,128)S(1)} %get-tuple-element.87), channel_id=1, source_target_pairs={{0,4},{4,0},{1,5},{5,1},{2,6},{6,2},{3,7},{7,3},{8,12},{12,8},{9,1... | collective-permute-start | bytes 24584 | tf_op jit(solution)/shard_map/ppermute | solution.py:448
  30.7 1.2 %collective-permute-start.16 = (f32[8,128]{1,0:T(8,128)S(1)}, f32[8,128]{1,0:T(8,128)S(1)}, u32[]{:S(2)}, u32[]{:S(2)}) collective-permute-start(f32[8,128]{1,0:T(8,128)S(1)} %shard_map.86), channel_id=1, source_target_pairs={{0,8},{8,0},{16,24},{24,16},{1,9},{9,1},{17,25},{25,17},{2,10},{10... | collective-permute-start | bytes 12296 | tf_op jit(solution)/shard_map/ppermute | solution.py:448
